TPU v7x, 32 devices: a whole 2x2x4 slice. The times are simulated.
32 devices in a mesh: dp: 4 (over y, core), row: 2 (over x), col: 4 (over z).
Axes of the slice: x: 2, y: 2, z: 4, core: 2. Of those that a mesh axis runs over, the one named last changes fastest.
Arguments:
- tokens: bfloat16 [16384, 2048], P(('dp', 'col'), 'row'), may hold values from -6 to 6
- cotangent: bfloat16 [16384, 2048], P(('dp', 'col'), 'row')
- prefix: int32 [8], P('dp'), may hold values from 204 to 1024
- query_weight: float32 [2048, 2048], P('row', 'col'), may hold values from -0.5 to 0.5
- key_projection: float32 [2048, 512], P('row'), may hold values from -0.5 to 0.5
- value_projection: float32 [2048, 512], P('row'), may hold values from -0.125 to 0.125
- out_weight: float32 [2048, 2048], P('col', 'row'), may hold values from -1.5 to 1.5
- gate_weight: float32 [2048, 8192], P('row', 'col'), may hold values from -0.125 to 0.125
- up_weight: float32 [2048, 8192], P('row', 'col'), may hold values from -0.125 to 0.125
- down_weight: float32 [8192, 2048], P('col', 'row'), may hold values from -0.375 to 0.375
- norm_gains: float32 [2, 2048], P(None, 'row')
- query_moment: float32 [2048, 2048], P('row', 'col'), may hold values from -0.0005128985 to 0.0005128985
- key_first_moment: float32 [2048, 512], P('row'), may hold values from -0.0005128985 to 0.0005128985
- value_first_moment: float32 [2048, 512], P('row'), may hold values from -0.0005128985 to 0.0005128985
- out_moment: float32 [2048, 2048], P('col', 'row'), may hold values from -0.00012822462 to 0.00012822462
- gate_moment: float32 [2048, 8192], P('row', 'col'), may hold values from -0.0005128985 to 0.0005128985
- up_moment: float32 [2048, 8192], P('row', 'col'), may hold values from -0.0005128985 to 0.0005128985
- down_moment: float32 [8192, 2048], P('col', 'row'), may hold values from -0.00017951446 to 0.00017951446
- gains_moment: float32 [2, 2048], P(None, 'row'), may hold values from -0.0005128985 to 0.0005128985
- query_square: float32 [2048, 2048], P('row', 'col'), may hold values from 1.6441554e-08 to 6.5766216e-08
- key_second_moment: float32 [2048, 512], P('row'), may hold values from 1.6441554e-08 to 6.5766216e-08
- value_second_moment: float32 [2048, 512], P('row'), may hold values from 1.6441554e-08 to 6.5766216e-08
- out_square: float32 [2048, 2048], P('col', 'row'), may hold values from 4.932466e-10 to 1.9729864e-09
- gate_square: float32 [2048, 8192], P('row', 'col'), may hold values from 1.6441554e-08 to 6.5766216e-08
- up_square: float32 [2048, 8192], P('row', 'col'), may hold values from 1.6441554e-08 to 6.5766216e-08
- down_square: float32 [8192, 2048], P('col', 'row'), may hold values from 9.864932e-10 to 3.945973e-09
- gains_square: float32 [2, 2048], P(None, 'row'), may hold values from 1.6441554e-08 to 6.5766216e-08
Outputs:
- layer_out: bfloat16 [16384, 2048], P(('dp', 'col'), 'row')
- input_grad: bfloat16 [16384, 2048], P(('dp', 'col'), 'row')
- query_grad: float32 [2048, 2048], P('row', 'col')
- key_grad: float32 [2048, 512], P('row')
- value_grad: float32 [2048, 512], P('row')
- out_grad: float32 [2048, 2048], P('col', 'row')
- gate_grad: float32 [2048, 8192], P('row', 'col')
- up_grad: float32 [2048, 8192], P('row', 'col')
- down_grad: float32 [8192, 2048], P('col', 'row')
- gains_grad: float32 [2, 2048], P(None, 'row')
- query_next: float32 [2048, 2048], P('row', 'col')
- key_next: float32 [2048, 512], P('row')
- value_next: float32 [2048, 512], P('row')
- out_next: float32 [2048, 2048], P('col', 'row')
- gate_next: float32 [2048, 8192], P('row', 'col')
- up_next: float32 [2048, 8192], P('row', 'col')
- down_next: float32 [8192, 2048], P('col', 'row')
- gains_next: float32 [2, 2048], P(None, 'row')
- query_variance: float32 [2048, 2048], P('row', 'col')
- key_variance: float32 [2048, 512], P('row')
- value_variance: float32 [2048, 512], P('row')
- out_variance: float32 [2048, 2048], P('col', 'row')
- gate_variance: float32 [2048, 8192], P('row', 'col')
- up_variance: float32 [2048, 8192], P('row', 'col')
- down_variance: float32 [8192, 2048], P('col', 'row')
- gains_variance: float32 [2, 2048], P(None, 'row')
- grad_norm: float32 [], replicated
Inputs may be any that keep to these rules, and one draw needn't show every extreme that they name: prefix[s] leading tokens of sequence s are visible to every token of that sequence.
All inputs are finite; a program needn't handle non-finite values.
Results may differ from a plain program's by a relative error of at most 0.025.
The roundings to bfloat16 on the way count: a program that leaves them out, or rounds other values in their place, can miss the bound.
Values may be sent and summed in bfloat16 or wider, within the bound.
No kernel may reach another device: no remote copies, remote signals or barrier semaphores. Data moves between devices by JAX's collectives and lax.ppermute only.
A program may use at most 576 MiB of HBM per device.

v0:
```python
import jax
import jax.numpy as jnp
from jax import lax
from jax.sharding import PartitionSpec as P

MODEL_WIDTH = 2048
QUERY_HEADS = 32
KEY_VALUE_HEADS = 8
HEAD_SIZE = 64
SEQUENCE_LENGTH = 2048
STEP = 5


EPS_NORM = 1e-05
RESID = 0.22
ATTN_SCALE = 1.0 / 64.0
THETA = 10000000.0
LEARN = 0.1
GAINS_LEARN = 0.5
BETA_ONE = 0.5
BETA_TWO = 0.5
ADAM_EPS = 1e-08
DECAY = 0.1
CLIP = 1.0


def matrix_multiply(left_side, right_side):
    return jnp.dot(left_side, right_side, preferred_element_type=jnp.float32)


def left_product(left_side, right_side):
    return lax.dot_general(
        left_side, right_side, (((0,), (0,)), ((), ())), preferred_element_type=jnp.float32
    )


def right_product(left_side, right_side):
    return lax.dot_general(
        left_side, right_side, (((1,), (1,)), ((), ())), preferred_element_type=jnp.float32
    )


def width_total(values):
    return lax.psum(values, "row")


def gather_tokens(values):
    return lax.all_gather(values, "col", axis=0, tiled=True)


def sum_tokens(term, tok_rows):
    return lax.psum_scatter(
        term(jnp.int32(0), lax.axis_size("col") * tok_rows).astype(jnp.bfloat16),
        "col",
        scatter_dimension=0,
        tiled=True,
    ).astype(jnp.float32)


def fetch_weights(first, second, third, fourth, fifth):
    return (
        lax.all_gather(first, "row", axis=0, tiled=True),
        lax.all_gather(second, "row", axis=0, tiled=True),
        lax.all_gather(third, "row", axis=0, tiled=True),
        lax.all_gather(fourth, "row", axis=1, tiled=True),
        lax.all_gather(fifth, "row", axis=1, tiled=True),
    )


def enter_rows(values):
    return lax.all_to_all(values, "row", split_axis=0, concat_axis=1, tiled=True)


def leave_rows(values):
    return lax.all_to_all(
        values.astype(jnp.bfloat16), "row", split_axis=1, concat_axis=0, tiled=True
    ).astype(values.dtype)


def reduce_rows(first, second, third, fourth, fifth):
    return (
        lax.psum_scatter(first.astype(jnp.bfloat16), "row", scatter_dimension=0, tiled=True).astype(
            jnp.float32
        ),
        lax.psum_scatter(
            second.astype(jnp.bfloat16), "row", scatter_dimension=0, tiled=True
        ).astype(jnp.float32),
        lax.psum_scatter(third.astype(jnp.bfloat16), "row", scatter_dimension=1, tiled=True).astype(
            jnp.float32
        ),
        lax.psum_scatter(
            fourth.astype(jnp.bfloat16), "row", scatter_dimension=0, tiled=True
        ).astype(jnp.float32),
        lax.psum_scatter(fifth.astype(jnp.bfloat16), "row", scatter_dimension=1, tiled=True).astype(
            jnp.float32
        ),
    )


def rope_tables(length):
    half_width = HEAD_SIZE // 2
    frequency = THETA ** (-(jnp.arange(half_width, dtype=jnp.float32) * 2.0 / HEAD_SIZE))
    angles = jnp.arange(length, dtype=jnp.float32)[:, None] * frequency[None, :]
    angles = jnp.concatenate([angles, angles], axis=1)
    return (jnp.cos(angles), jnp.sin(angles))


def rotate(values):
    half_width = values.shape[-1] // 2
    return jnp.concatenate([-values[..., half_width:], values[..., :half_width]], axis=-1)


def rope(values, cosine_table, sine_table):
    return values * cosine_table[:, None, :] + rotate(values) * sine_table[:, None, :]


def rope_back(gradient, cosine_table, sine_table):
    return gradient * cosine_table[:, None, :] - rotate(gradient * sine_table[:, None, :])


def rms_forward(values, gain_row):
    squares = width_total(jnp.sum(values * values, axis=1))
    factor = lax.rsqrt(squares[:, None] / MODEL_WIDTH + EPS_NORM)
    normed = values * factor
    return ((normed * gain_row).astype(jnp.bfloat16), normed, factor)


def rms_backward(grad_normed, normed, factor, gain_row):
    weighted = grad_normed * gain_row
    inner_sum = width_total(jnp.sum(weighted * normed, axis=1))
    grad_input = factor * (weighted - normed * (inner_sum[:, None] / MODEL_WIDTH))
    return (grad_input, jnp.sum(grad_normed * normed, axis=0))


def attend_sequence(
    heads_of_queries, heads_of_keys, heads_of_values, prefix_length, rows_per_block
):
    length = heads_of_keys.shape[0]
    key_place = jnp.arange(length)

    def one_block(inputs):
        query_block, positions = inputs
        scores = jnp.einsum(
            "qhgd,khd->hgqk", query_block, heads_of_keys, preferred_element_type=jnp.float32
        )
        visible = (key_place[None, :] <= positions[:, None]) | (key_place[None, :] < prefix_length)
        scores = jnp.where(visible, scores, -1e30)
        row_max = jnp.max(scores, axis=-1, keepdims=True)
        exponent = jnp.exp(scores - row_max)
        total_sum = jnp.sum(exponent, axis=-1, keepdims=True)
        probability = (exponent / total_sum).astype(jnp.bfloat16)
        result = jnp.einsum(
            "hgqk,khd->qhgd", probability, heads_of_values, preferred_element_type=jnp.float32
        )
        return (result, row_max[..., 0] + jnp.log(total_sum[..., 0]))

    block_count = length // rows_per_block
    shaped = heads_of_queries.reshape((block_count, rows_per_block) + heads_of_queries.shape[1:])
    positions = jnp.arange(length).reshape(block_count, rows_per_block)
    result, logsum = lax.map(one_block, (shaped, positions))
    return (result.reshape(heads_of_queries.shape), logsum)


def attend_back(
    heads_of_queries,
    heads_of_keys,
    heads_of_values,
    prefix_length,
    logsum,
    grad_heads,
    rows_per_block,
):
    length = heads_of_keys.shape[0]
    key_place = jnp.arange(length)
    block_count = length // rows_per_block

    def one_block(carried, inputs):
        query_block, grad_block, logsum_block, positions = inputs
        scores = jnp.einsum(
            "qhgd,khd->hgqk", query_block, heads_of_keys, preferred_element_type=jnp.float32
        )
        visible = (key_place[None, :] <= positions[:, None]) | (key_place[None, :] < prefix_length)
        scores = jnp.where(visible, scores, -1e30)
        probability = jnp.exp(scores - logsum_block[..., None])
        grad_prob = jnp.einsum(
            "qhgd,khd->hgqk", grad_block, heads_of_values, preferred_element_type=jnp.float32
        )
        delta_sum = jnp.sum(probability * grad_prob, axis=-1, keepdims=True)
        grad_scores = (probability * (grad_prob - delta_sum)).astype(jnp.bfloat16)
        grad_query = jnp.einsum(
            "hgqk,khd->qhgd", grad_scores, heads_of_keys, preferred_element_type=jnp.float32
        )
        grad_keys = jnp.einsum(
            "hgqk,qhgd->khd", grad_scores, query_block, preferred_element_type=jnp.float32
        )
        grad_values = jnp.einsum(
            "hgqk,qhgd->khd",
            probability.astype(jnp.bfloat16),
            grad_block,
            preferred_element_type=jnp.float32,
        )
        return ((carried[0] + grad_keys, carried[1] + grad_values), grad_query)

    block_shape = (block_count, rows_per_block) + heads_of_queries.shape[1:]
    initial = (
        jnp.zeros(heads_of_keys.shape, jnp.float32),
        jnp.zeros(heads_of_values.shape, jnp.float32),
    )
    positions = jnp.arange(length).reshape(block_count, rows_per_block)
    inputs = (
        heads_of_queries.reshape(block_shape),
        grad_heads.reshape(block_shape),
        logsum,
        positions,
    )
    (grad_keys, grad_values), grad_query = lax.scan(one_block, initial, inputs)
    return (grad_query.reshape(heads_of_queries.shape), grad_keys, grad_values)


def adam(weight, gradient, moment_one, moment_two, decay_rate, learn_rate):
    moment_new = BETA_ONE * moment_one + (1.0 - BETA_ONE) * gradient
    square_new = BETA_TWO * moment_two + (1.0 - BETA_TWO) * gradient * gradient
    moment_hat = moment_new / (1.0 - BETA_ONE**STEP)
    square_hat = square_new / (1.0 - BETA_TWO**STEP)
    return (
        weight
        - learn_rate * (moment_hat / (jnp.sqrt(square_hat) + ADAM_EPS) + decay_rate * weight),
        square_new,
    )


def shards(
    tokens,
    cotangent,
    prefix,
    query_weight,
    key_projection,
    value_projection,
    out_weight,
    gate_weight,
    up_weight,
    down_weight,
    norm_gains,
    query_moment,
    key_first_moment,
    value_first_moment,
    out_moment,
    gate_moment,
    up_moment,
    down_moment,
    gains_moment,
    query_square,
    key_second_moment,
    value_second_moment,
    out_square,
    gate_square,
    up_square,
    down_square,
    gains_square,
):
    tok_rows = tokens.shape[0]
    query_cols = query_weight.shape[1]
    kv_all = key_projection.shape[1]
    ffn_cols = gate_weight.shape[1]
    row_size = lax.axis_size("row")
    col_size = lax.axis_size("col")
    row_index = lax.axis_index("row")
    col_index = lax.axis_index("col")
    tok_count = tok_rows * col_size
    seq_count = prefix.shape[0]
    group_width = QUERY_HEADS // KEY_VALUE_HEADS
    rows_per_block = min(512, SEQUENCE_LENGTH)
    col_heads = query_cols // HEAD_SIZE
    frame_used = max(1, col_heads // group_width)
    frame_start = col_index * col_heads // group_width
    frame_width = frame_used * HEAD_SIZE
    key_here = lax.dynamic_slice_in_dim(key_projection, frame_start * HEAD_SIZE, frame_width, 1)
    value_here = lax.dynamic_slice_in_dim(value_projection, frame_start * HEAD_SIZE, frame_width, 1)
    query_mat = query_weight.astype(jnp.bfloat16)
    kv_mat = (
        jnp.stack([key_here, value_here], axis=1)
        .astype(jnp.bfloat16)
        .reshape(key_here.shape[0], 2 * frame_width)
    )
    out_mat = out_weight.astype(jnp.bfloat16)
    ffn_mat = (
        jnp.stack([gate_weight, up_weight], axis=1)
        .astype(jnp.bfloat16)
        .reshape(gate_weight.shape[0], 2 * ffn_cols)
    )
    down_mat = down_weight.astype(jnp.bfloat16)
    gain_one = norm_gains[0]
    gain_two = norm_gains[1]
    query_use, kv_use, ffn_use, out_use, down_use = fetch_weights(
        query_mat, kv_mat, ffn_mat, out_mat, down_mat
    )
    use_rows = tok_count // row_size
    seq_use = seq_count // row_size
    prefix_use = lax.dynamic_slice_in_dim(prefix, row_index * seq_use, seq_use, 0)
    kv_used = max(1, col_heads // group_width)
    group_here = col_heads // kv_used
    cosine_one, sine_one = rope_tables(SEQUENCE_LENGTH)
    cosine_table = jnp.tile(cosine_one, (seq_use, 1))
    sine_table = jnp.tile(sine_one, (seq_use, 1))

    def spread(values):
        return enter_rows(values)

    def to_tokens(product_fn):
        whole = leave_rows(product_fn(0, use_rows))

        def term(start_row, rows_here):
            return whole

        return sum_tokens(term, tok_rows)

    input_float = tokens.astype(jnp.float32)
    hidden_first, normed_one, factor_one = rms_forward(input_float, gain_one)
    h_one_use = spread(gather_tokens(hidden_first))
    query_sum = matrix_multiply(h_one_use, query_use)
    kv_frame = matrix_multiply(h_one_use, kv_use).reshape(use_rows, 2, frame_width)
    query_round = (
        rope(query_sum.reshape(use_rows, col_heads, HEAD_SIZE), cosine_table, sine_table)
        * ATTN_SCALE
    ).astype(jnp.bfloat16)
    key_round = rope(
        kv_frame[:, 0].reshape(use_rows, kv_used, HEAD_SIZE), cosine_table, sine_table
    ).astype(jnp.bfloat16)
    value_round = kv_frame[:, 1].reshape(use_rows, kv_used, HEAD_SIZE).astype(jnp.bfloat16)
    query_seq = query_round.reshape(seq_use, SEQUENCE_LENGTH, kv_used, group_here, HEAD_SIZE)
    key_seq = key_round.reshape(seq_use, SEQUENCE_LENGTH, kv_used, HEAD_SIZE)
    value_seq = value_round.reshape(seq_use, SEQUENCE_LENGTH, kv_used, HEAD_SIZE)

    def forward_sequence(inputs):
        return attend_sequence(inputs[0], inputs[1], inputs[2], inputs[3], rows_per_block)

    attended, logsum = lax.map(forward_sequence, (query_seq, key_seq, value_seq, prefix_use))
    head_round = attended.reshape(use_rows, col_heads * HEAD_SIZE).astype(jnp.bfloat16)

    def out_term(start_row, rows_here):
        return matrix_multiply(head_round, out_use)

    residual_mid = input_float + RESID * to_tokens(out_term)
    h_two, normed_two, factor_two = rms_forward(residual_mid, gain_two)
    h_two_use = spread(gather_tokens(h_two))
    ffn_part = matrix_multiply(h_two_use, ffn_use).reshape(use_rows, 2, ffn_cols)
    gate_value = ffn_part[:, 0]
    up_value = ffn_part[:, 1]
    hidden = (jax.nn.silu(gate_value) * up_value).astype(jnp.bfloat16)

    def down_term(start_row, rows_here):
        return matrix_multiply(hidden, down_use)

    layer_out = (residual_mid + RESID * to_tokens(down_term)).astype(jnp.bfloat16)
    grad_output = cotangent.astype(jnp.float32)
    grad_mlp = (RESID * grad_output).astype(jnp.bfloat16)
    grad_mlp_use = spread(gather_tokens(grad_mlp))
    down_local = left_product(hidden, grad_mlp_use)
    hidden_part = right_product(grad_mlp_use, down_use)
    sigmoid_gate = jax.nn.sigmoid(gate_value)
    grad_gate = hidden_part * up_value * sigmoid_gate * (1.0 + gate_value * (1.0 - sigmoid_gate))
    grad_up = hidden_part * (gate_value * sigmoid_gate)
    grad_pair = jnp.stack([grad_gate, grad_up], axis=1).astype(jnp.bfloat16)
    pair_flat = grad_pair.reshape(use_rows, 2 * ffn_cols)
    ffn_local = left_product(h_two_use, pair_flat).reshape(-1, 2, ffn_cols)

    def ffn_back_term(start_row, rows_here):
        return right_product(pair_flat, ffn_use)

    grad_mid_part, gain_two_part = rms_backward(
        to_tokens(ffn_back_term), normed_two, factor_two, gain_two
    )
    grad_mid = grad_output + grad_mid_part
    grad_attended = (RESID * grad_mid).astype(jnp.bfloat16)
    grad_attended_use = spread(gather_tokens(grad_attended))
    out_local = left_product(head_round, grad_attended_use)
    head_part = right_product(grad_attended_use, out_use)
    head_grad = head_part
    head_grad = head_grad.astype(jnp.bfloat16).reshape(
        seq_use, SEQUENCE_LENGTH, kv_used, group_here, HEAD_SIZE
    )

    def backward_sequence(inputs):
        return attend_back(
            inputs[0], inputs[1], inputs[2], inputs[3], inputs[4], inputs[5], rows_per_block
        )

    query_back, key_back, value_back = lax.map(
        backward_sequence, (query_seq, key_seq, value_seq, prefix_use, logsum, head_grad)
    )
    query_grad_heads = rope_back(
        query_back.reshape(use_rows, col_heads, HEAD_SIZE) * ATTN_SCALE, cosine_table, sine_table
    )
    query_grad_round = query_grad_heads.reshape(use_rows, col_heads * HEAD_SIZE).astype(
        jnp.bfloat16
    )
    key_grad_heads = rope_back(
        key_back.reshape(use_rows, kv_used, HEAD_SIZE), cosine_table, sine_table
    )
    kv_grad_used = jnp.stack(
        [
            key_grad_heads.reshape(use_rows, kv_used * HEAD_SIZE),
            value_back.reshape(use_rows, kv_used * HEAD_SIZE),
        ],
        axis=1,
    )
    kv_grad = kv_grad_used.astype(jnp.bfloat16)
    kv_flat = kv_grad.reshape(use_rows, 2 * frame_width)
    query_local = left_product(h_one_use, query_grad_round)
    kv_frame_local = left_product(h_one_use, kv_flat).reshape(-1, 2, frame_width)
    kv_local = lax.dynamic_update_slice_in_dim(
        jnp.zeros((kv_frame_local.shape[0], 2, kv_all), jnp.float32),
        kv_frame_local,
        frame_start * HEAD_SIZE,
        2,
    )

    def input_term(start_row, rows_here):
        return right_product(query_grad_round, query_use) + right_product(kv_flat, kv_use)

    grad_in_part, gain_one_part = rms_backward(
        to_tokens(input_term), normed_one, factor_one, gain_one
    )
    input_grad = (grad_mid + grad_in_part).astype(jnp.bfloat16)
    local_grads = reduce_rows(query_local, kv_local, out_local, ffn_local, down_local)
    summed = (
        lax.psum(local_grads[0].astype(jnp.bfloat16), "dp").astype(jnp.float32),
        lax.psum(local_grads[2].astype(jnp.bfloat16), "dp").astype(jnp.float32),
        lax.psum(local_grads[3].astype(jnp.bfloat16), "dp").astype(jnp.float32),
        lax.psum(local_grads[4].astype(jnp.bfloat16), "dp").astype(jnp.float32),
    )
    kv_summed, gains_total = lax.psum(
        (local_grads[1], jnp.stack([gain_one_part, gain_two_part])), ("dp", "col")
    )
    raw_grads = (
        summed[0],
        kv_summed[:, 0],
        kv_summed[:, 1],
        summed[1],
        summed[2][:, 0],
        summed[2][:, 1],
        summed[3],
    )
    masters = (
        query_weight,
        key_projection,
        value_projection,
        out_weight,
        gate_weight,
        up_weight,
        down_weight,
    )
    moments = (
        query_moment,
        key_first_moment,
        value_first_moment,
        out_moment,
        gate_moment,
        up_moment,
        down_moment,
    )
    squares = (
        query_square,
        key_second_moment,
        value_second_moment,
        out_square,
        gate_square,
        up_square,
        down_square,
    )
    copied_sum = jnp.sum(gains_total * gains_total) + jnp.sum(kv_summed * kv_summed)
    square_local = jnp.where(col_index == 0, copied_sum, 0.0)
    for position in (0, 3, 4, 5, 6):
        square_local = square_local + jnp.sum(raw_grads[position] * raw_grads[position])
    total_sum = lax.psum(square_local, ("row", "col"))
    grad_norm = jnp.sqrt(total_sum)
    factor = jnp.minimum(1.0, CLIP / grad_norm)
    clipped = []
    nexts = []
    variances = []
    for position in range(7):
        gradient = raw_grads[position] * factor
        weight_next, variance = adam(
            masters[position], gradient, moments[position], squares[position], DECAY, LEARN
        )
        clipped.append(gradient)
        nexts.append(weight_next)
        variances.append(variance)
    gains_grad = gains_total * factor
    gains_next, gains_variance = adam(
        norm_gains, gains_grad, gains_moment, gains_square, 0.0, GAINS_LEARN
    )
    return (
        layer_out,
        input_grad,
        clipped[0],
        clipped[1],
        clipped[2],
        clipped[3],
        clipped[4],
        clipped[5],
        clipped[6],
        gains_grad,
        nexts[0],
        nexts[1],
        nexts[2],
        nexts[3],
        nexts[4],
        nexts[5],
        nexts[6],
        gains_next,
        variances[0],
        variances[1],
        variances[2],
        variances[3],
        variances[4],
        variances[5],
        variances[6],
        gains_variance,
        grad_norm,
    )


def solution(mesh):
    placed = (
        P(("dp", "col"), "row"),
        P(("dp", "col"), "row"),
        P("dp"),
        P("row", "col"),
        P("row", None),
        P("row", None),
        P("col", "row"),
        P("row", "col"),
        P("row", "col"),
        P("col", "row"),
        P(None, "row"),
        P("row", "col"),
        P("row", None),
        P("row", None),
        P("col", "row"),
        P("row", "col"),
        P("row", "col"),
        P("col", "row"),
        P(None, "row"),
        P("row", "col"),
        P("row", None),
        P("row", None),
        P("col", "row"),
        P("row", "col"),
        P("row", "col"),
        P("col", "row"),
        P(None, "row"),
    )
    return jax.shard_map(
        shards,
        mesh=mesh,
        in_specs=placed,
        out_specs=(
            P(("dp", "col"), "row"),
            P(("dp", "col"), "row"),
            P("row", "col"),
            P("row", None),
            P("row", None),
            P("col", "row"),
            P("row", "col"),
            P("row", "col"),
            P("col", "row"),
            P(None, "row"),
            P("row", "col"),
            P("row", None),
            P("row", None),
            P("col", "row"),
            P("row", "col"),
            P("row", "col"),
            P("col", "row"),
            P(None, "row"),
            P("row", "col"),
            P("row", None),
            P("row", None),
            P("col", "row"),
            P("row", "col"),
            P("row", "col"),
            P("col", "row"),
            P(None, "row"),
            P(),
        ),
        check_vma=False,
    )
```

profile of v0, /device:TPU:1, one launch (start us, length us, event | category | flops | bytes accessed | tf_op | source)
XLA Modules:
  0.0 3744.7 jit_solution(2059251223926982497)
XLA Ops:
  20.0 152.7 %all-gather.10.cloned.1.call-done = bf16[4096,1024]{1,0:T(8,128)(2,1)} async-done(((bf16[1024,1024]{1,0:T(8,128)(2,1)}), bf16[4096,1024]{1,0:T(8,128)(2,1)}) %all-gather.10.cloned.1.call-update) | async-done | bytes 8388624 | tf_op jit(solution)/shard_map/all_gather | solution.py:48
  190.5 46.4 %all-gather.12.cloned.1.call-done = bf16[2048,512]{1,0:T(8,128)(2,1)} async-done(((bf16[1024,512]{1,0:T(8,128)(2,1)}), bf16[2048,512]{1,0:T(8,128)(2,1)}) %all-gather.12.cloned.1.call-update) | async-done | bytes 2097168 | tf_op jit(solution)/shard_map/all_gather | solution.py:62
  240.9 85.8 %all-to-all-done = bf16[2,2048,1024]{2,1,0:T(8,128)(2,1)} async-done(((bf16[2,2048,1024]{2,1,0:T(8,128)(2,1)}), bf16[2,2048,1024]{2,1,0:T(8,128)(2,1)}, u32[]{:S(2)}, u32[]{:S(2)}) %all-to-all-start) | async-done | bytes 8388640 | tf_op jit(solution)/shard_map/all_to_all | solution.py:71
  326.7 16.4 copy.110
  343.0 14.4 reshape.293
  380.9 185.5 %while.50 = (s32[]{:T(128)}, bf16[4,512,2,4,64]{1,4,3,2,0:T(8,128)(2,1)}, f32[4,2,4,512]{3,2,1,0:T(4,128)}, s32[4,512]{1,0:T(4,128)S(1)}, s32[]{:T(128)}, /*inde...) while((s32[]{:T(128)}, ...), condition=%wide.region_5.6_spmd.clone.clone, body=%wide.region_2.5_spmd.clone.clone.sunk | while | flops 2225076224 | bytes 107620464 | solution.py:160
  382.6 14.3 bitcast_reduce_fusion.2
  396.9 14.6 fusion.220
  411.5 15.3 fusion.221
  443.1 14.6 fusion.220
  457.7 15.3 fusion.221
  489.3 14.6 fusion.220
  503.9 15.3 fusion.221
  535.5 14.6 fusion.220
  550.1 15.3 fusion.221
  578.8 94.2 %all_to_all.152 = bf16[2048,2,1024]{0,2,1:T(8,128)(2,1)} all-to-all(bf16[2048,2,1024]{0,2,1:T(8,128)(2,1)S(1)} %bitcast.391), channel_id=1, replica_groups=mesh['dp'=4,'row'=2,'col'=4] {'row'}, dimensions={1} | all-to-all | bytes 16777216 | tf_op jit(solution)/shard_map/all_to_all | solution.py:75
  688.7 140.6 %reduce-scatter.10.cloned.1.call-done = bf16[1024,1024]{1,0:T(8,128)(2,1)} async-done(((bf16[4096,1024]{1,0:T(8,128)(2,1)}), bf16[1024,1024]{1,0:T(8,128)(2,1)}) %reduce-scatter.10.cloned.1.call-update) | async-done | bytes 2097168 | tf_op jit(solution)/shard_map/reduce_scatter | solution.py:52
  862.8 119.4 %all-gather.24.cloned.1.call-done = bf16[4096,1024]{1,0:T(8,128)(2,1)} async-done(((bf16[1024,1024]{1,0:T(8,128)(2,1)}), bf16[4096,1024]{1,0:T(8,128)(2,1)}) %all-gather.24.cloned.1.call-update) | async-done | bytes 8388624 | tf_op jit(solution)/shard_map/all_gather | solution.py:48
  982.3 103.1 %all_to_all.153 = bf16[2,2048,1024]{2,1,0:T(8,128)(2,1)} all-to-all(bf16[2,2048,1024]{2,1,0:T(8,128)(2,1)} %bitcast.385), channel_id=1, replica_groups=mesh['dp'=4,'row'=2,'col'=4] {'row'}, dimensions={0} | all-to-all | bytes 16777216 | tf_op jit(solution)/shard_map/all_to_all | solution.py:71
  1085.3 46.8 %all-gather.18.cloned.1.call-done = bf16[4096,1024]{1,0:T(8,128)(2,1)} async-done(((bf16[1024,1024]{1,0:T(8,128)(2,1)}), bf16[4096,1024]{1,0:T(8,128)(2,1)}) %all-gather.18.cloned.1.call-update) | async-done | bytes 8388624 | tf_op jit(solution)/shard_map/all_gather | solution.py:48
  1160.3 150.4 %all-to-all-done.2 = bf16[2,2048,1024]{2,1,0:T(8,128)(2,1)} async-done(((bf16[2,2048,1024]{2,1,0:T(8,128)(2,1)}), bf16[2,2048,1024]{2,1,0:T(8,128)(2,1)}, u32[]{:S(2)}, u32[]{:S(2)}) %all-to-all-start.2) | async-done | bytes 8388640 | tf_op jit(solution)/shard_map/all_to_all | solution.py:71
  1310.7 16.4 copy.117
  1327.1 14.4 reshape.294
  1341.5 70.4 %all-gather.20.cloned.1.call-done = bf16[2048,4096]{0,1:T(8,128)(2,1)} async-done(((bf16[1024,4096]{0,1:T(8,128)(2,1)}), bf16[2048,4096]{0,1:T(8,128)(2,1)}) %all-gather.20.cloned.1.call-update) | async-done | bytes 16777232 | tf_op jit(solution)/shard_map/all_gather | solution.py:64
  1411.9 43.3 %fusion.171 = f32[2048,2,2048]{0,2,1:T(8,128)} fusion(bf16[2048,2048,1]{1,0,2:T(8,128)(2,1)} %reshape.294, bf16[2,2048,2048]{2,1,0:T(8,128)(2,1)} %bitcast.417), kind=kOutput, calls=%fused_computation.255 | convolution fusion | flops 34359738368 | bytes 58720256 | tf_op jit(solution)/shard_map/dot_general | solution.py:28
  1455.2 59.8 %all-gather.22.cloned.1.call-done = bf16[2048,2048]{1,0:T(8,128)(2,1)} async-done(((bf16[2048,1024]{1,0:T(8,128)(2,1)}), bf16[2048,2048]{1,0:T(8,128)(2,1)}) %all-gather.22.cloned.1.call-update) | async-done | bytes 8388624 | tf_op jit(solution)/shard_map/all_gather | solution.py:66
  1515.0 32.4 fusion.90
  1561.1 43.2 %convolution_convert_fusion.1 = bf16[2048,2048]{0,1:T(8,128)(2,1)} fusion(bf16[2048,4096]{0,1:T(8,128)(2,1)} %bitcast.368, bf16[2048,4096]{0,1:T(8,128)(2,1)} %all-gather.20.cloned.1.call-done), kind=kOutput, calls=%fused_computation.122 | convolution fusion | flops 34363932672 | bytes 41943040 | tf_op jit(solution)/shard_map/dot_general | solution.py:38
  1604.3 102.8 %all_to_all.154 = bf16[2048,2,1024]{0,2,1:T(8,128)(2,1)} all-to-all(bf16[2048,2,1024]{0,2,1:T(8,128)(2,1)} %bitcast.389), channel_id=1, replica_groups=mesh['dp'=4,'row'=2,'col'=4] {'row'}, dimensions={1} | all-to-all | bytes 16777216 | tf_op jit(solution)/shard_map/all_to_all | solution.py:75
  1718.9 145.3 %reduce-scatter.14.cloned.1.call-done = bf16[1024,1024]{1,0:T(8,128)(2,1)} async-done(((bf16[4096,1024]{1,0:T(8,128)(2,1)}), bf16[1024,1024]{1,0:T(8,128)(2,1)}) %reduce-scatter.14.cloned.1.call-update) | async-done | bytes 2097168 | tf_op jit(solution)/shard_map/reduce_scatter | solution.py:52
  1878.3 26.3 fusion.94
  1916.7 42.2 %fusion.61 = bf16[2048,2,2048]{2,0,1:T(8,128)(2,1)} fusion(bf16[2048,2048,1]{0,1,2:T(8,128)(2,1)} %bitcast.388, bf16[2048,1,2048]{0,2,1:T(8,128)(2,1)} %get-tuple-element.462, bf16[2048,1,2048]{0,2,1:T(8,128)(2,1)} %get-tuple-element.461), kind=kOutput, calls=%fused_computation.85 | convolution fusion | flops 34401681408 | bytes 41943040 | tf_op jit(solution)/shard_map/dot_general | solution.py:32
  1958.9 71.5 %all-gather.26.cloned.1.call-done = bf16[4096,1024]{1,0:T(8,128)(2,1)} async-done(((bf16[1024,1024]{1,0:T(8,128)(2,1)}), bf16[4096,1024]{1,0:T(8,128)(2,1)}) %all-gather.26.cloned.1.call-update) | async-done | bytes 8388624 | tf_op jit(solution)/shard_map/all_gather | solution.py:48
  2046.3 173.5 %all-to-all-done.6 = bf16[2,2048,1024]{2,1,0:T(8,128)(2,1)} async-done(((bf16[2,2048,1024]{2,1,0:T(8,128)(2,1)}), bf16[2,2048,1024]{2,1,0:T(8,128)(2,1)}, u32[]{:S(2)}, u32[]{:S(2)}) %all-to-all-start.6) | async-done | bytes 8388640 | tf_op jit(solution)/shard_map/all_to_all | solution.py:71
  2266.3 489.6 %while.51 = (s32[]{:T(128)}, f32[2048,2,64]{0,2,1:T(8,128)S(1)}, f32[2048,2,64]{0,2,1:T(8,128)}, f32[4,512,2,4,64]{1,0,4,3,2:T(4,128)}, bf16[4,512,2,4,64]{1,4,3...) while((s32[]{:T(128)}, f32[2048,2,64]{0,2,1:T(8,128)S(1)}, ...), condition=%wide.region_15.16_spmd.clone.clone, body=%wide.region_13.15_spmd.clone.clone.sunk | while | flops 5472516096 | bytes 352971008 | solution.py:216
  2269.4 14.5 fusion.230
  2283.9 14.6 fusion.235
  2298.5 23.7 fusion.232
  2322.1 27.9 fusion.233
  2367.9 21.1 dynamic_update_slice.41
  2391.9 14.3 fusion.230
  2406.2 14.5 fusion.235
  2420.7 23.6 fusion.232
  2444.3 27.9 fusion.233
  2490.1 21.1 dynamic_update_slice.41
  2514.1 14.3 fusion.230
  2528.4 14.5 fusion.235
  2542.9 23.6 fusion.232
  2566.5 27.9 fusion.233
  2612.3 21.1 dynamic_update_slice.41
  2636.2 14.3 fusion.230
  2650.5 14.5 fusion.235
  2665.1 23.6 fusion.232
  2688.6 27.9 fusion.233
  2734.4 21.1 dynamic_update_slice.41
  2831.5 122.2 %all_to_all.155 = bf16[2048,2,1024]{0,2,1:T(8,128)(2,1)} all-to-all(bf16[2048,2,1024]{0,2,1:T(8,128)(2,1)S(1)} %bitcast.356), channel_id=1, replica_groups=mesh['dp'=4,'row'=2,'col'=4] {'row'}, dimensions={1} | all-to-all | bytes 16777216 | tf_op jit(solution)/shard_map/all_to_all | solution.py:75
  2966.0 26.0 fusion.91
  2992.1 102.7 %all_to_all.156 = bf16[2048,2,1024]{0,2,1:T(8,128)(2,1)} all-to-all(bf16[2048,2,1024]{0,2,1:T(8,128)(2,1)} %bitcast.390), channel_id=1, replica_groups=mesh['dp'=4,'row'=2,'col'=4] {'row'}, dimensions={1} | all-to-all | bytes 16777216 | tf_op jit(solution)/shard_map/all_to_all | solution.py:75
  3106.8 41.9 %all-reduce.5.cloned.1.call-done = (bf16[1024,512]{1,0:T(8,128)(2,1)}, bf16[512,1024]{1,0:T(8,128)(2,1)}, bf16[1024,2,2048]{2,0,1:T(8,128)(2,1)}, bf16[2048,1024]{1,0:T(8,128)(2,1)}) async-done(((bf16[1024,512]{1,0:T(8,128)(2,1)}, bf16[512,1024]{1,0:T(8,128)(2,1)}, bf16[1024,2,2048]{2,0,1:T(8,128)(2,1)}, bf16[2048,1024]{1,0:T(8,128)(2,1)}), (bf16[1024,512]{1,0:T(8,128)(2,1)}, bf16[512,1024]{1,0:T(8,128)(2,1)}, ...) | async-done | bytes 14680080 | tf_op jit(solution)/shard_map/psum | solution.py:427
  3173.5 123.0 %reduce-scatter.16.cloned.1.call-done = bf16[1024,1024]{1,0:T(8,128)(2,1)} async-done(((bf16[4096,1024]{1,0:T(8,128)(2,1)}), bf16[1024,1024]{1,0:T(8,128)(2,1)}) %reduce-scatter.16.cloned.1.call-update) | async-done | bytes 2097168 | tf_op jit(solution)/shard_map/reduce_scatter | solution.py:52
  3299.6 316.2 %all-reduce.6 = (f32[2,1024]{1,0:T(2,128)S(1)}, f32[1024,2,512]{2,0,1:T(8,128)}) all-reduce(f32[2,1024]{1,0:T(2,128)S(1)} %pad_maximum_fusion.6, bf16[1024,2,512]{2,0,1:T(8,128)(2,1)} %reduce-scatter.20.cloned.1.call-done), channel_id=1, replica_groups=mesh['dp'=4,'row'=2,'col'=4] {'dp','col'}, use_global_device_ids=true, to_apply=%region_23.24 | all-reduce | flops 1050624 | bytes 6307840 | tf_op jit(solution)/shard_map/psum | solution.py:432
  3624.9 17.5 psum.87
  3667.6 18.9 fusion.81
  3686.5 41.4 %fusion.75 = (f32[1024,2048]{1,0:T(8,128)}, f32[1024,2048]{1,0:T(8,128)}, f32[1024,2048]{1,0:T(8,128)}, f32[1024,2048]{1,0:T(8,128)}, f32[1024,2048]{1,0:T(8,128)}, /*index=5*/f32[1024,2048]{1,0:T(8,128)}) fusion(f32[1024,2048]{1,0:T(8,128)} %param.39, f32[1024,2048]{1,0:T(8,128)} %param.47, f32[1024,2048]{1,0:T(8,128)} %param.55, f32[]{:T(128)S(6)} %min.3, ...), kind=kLoop, calls=%fused_computation.99 | loop fusion | flops 62914560 | bytes 117440512 | tf_op jit(solution)/shard_map/sub | solution.py:226
  (335 shorter events, 558.6 us)
Async XLA Ops:
  8.0 164.6 %all-gather.10.cloned.1.call-start = ((), (), s32[]{:S(2)}) async-start(), calls=%async_computation.17 | async-start | bytes 10485760 | tf_op jit(solution)/shard_map/all_gather | solution.py:48
  172.7 154.0 %all-to-all-start = ((bf16[2,2048,1024]{2,1,0:T(8,128)(2,1)}), bf16[2,2048,1024]{2,1,0:T(8,128)(2,1)}, u32[]{:S(2)}, u32[]{:S(2)}) async-start(bf16[2,2048,1024]{2,1,0:T(8,128)(2,1)} %bitcast.380), calls=%async_computation | async-start | bytes 16777216 | tf_op jit(solution)/shard_map/all_to_all | solution.py:71
  179.7 57.3 %all-gather.12.cloned.1.call-start = ((), (), s32[]{:S(2)}) async-start(), calls=%async_computation.18 | async-start | bytes 3145728 | tf_op jit(solution)/shard_map/all_gather | solution.py:62
  182.6 174.8 %all-gather.14.cloned.1.call-start = ((), (), s32[]{:S(2)}) async-start(), calls=%async_computation.19 | async-start | bytes 1572864 | tf_op jit(solution)/shard_map/all_gather | solution.py:63
  185.6 386.4 %all-gather.16.cloned.1.call-start = ((), (), s32[]{:S(2)}) async-start(), calls=%async_computation.20 | async-start | bytes 3145728 | tf_op jit(solution)/shard_map/all_gather | solution.py:65
  186.8 642.5 %reduce-scatter.10.cloned.1.call-start = ((), (), s32[]{:S(2)}) async-start(), calls=%async_computation.21 | async-start | bytes 10485760 | tf_op jit(solution)/shard_map/reduce_scatter | solution.py:52
  190.5 190.1 %copy-start.13 = (f32[2048,64]{0,1:T(8,128)}, f32[2048,64]{0,1:T(8,128)S(1)}, u32[]{:S(2)}) copy-start(f32[2048,64]{0,1:T(8,128)S(1)} %get-tuple-element.483) | copy-start | bytes 1572868
  190.5 190.1 %copy-start.16 = (f32[2048,64]{0,1:T(8,128)}, f32[2048,64]{0,1:T(8,128)S(1)}, u32[]{:S(2)}) copy-start(f32[2048,64]{0,1:T(8,128)S(1)} %get-tuple-element.484) | copy-start | bytes 1572868
  684.9 144.4 %copy-start.3 = (bf16[1024,1024]{1,0:T(8,128)(2,1)S(1)}, bf16[1024,1024]{1,0:T(8,128)(2,1)}, u32[]{:S(2)}) copy-start(bf16[1024,1024]{1,0:T(8,128)(2,1)} %param.31) | copy-start | bytes 6291460
  684.9 297.3 %all-gather.24.cloned.1.call-start = ((), (), s32[]{:S(2)}) async-start(), calls=%async_computation.26 | async-start | bytes 10485760 | tf_op jit(solution)/shard_map/all_gather | solution.py:48
  688.6 147.6 %copy-start.43 = (f32[1,1024]{1,0:T(1,128)S(1)}, f32[1,1024]{1,0:T(1,128)}, u32[]{:S(2)}) copy-start(f32[1,1024]{1,0:T(1,128)} %get-tuple-element.486) | copy-start | bytes 12292
  688.6 443.5 %all-gather.18.cloned.1.call-start = ((), (), s32[]{:S(2)}) async-start(), calls=%async_computation.22 | async-start | bytes 10485760 | tf_op jit(solution)/shard_map/all_gather | solution.py:48
  840.0 571.9 %all-gather.20.cloned.1.call-start = ((), (), s32[]{:S(2)}) async-start(), calls=%async_computation.23 | async-start | bytes 25165824 | tf_op jit(solution)/shard_map/all_gather | solution.py:64
  1132.2 178.6 %all-to-all-start.2 = ((bf16[2,2048,1024]{2,1,0:T(8,128)(2,1)}), bf16[2,2048,1024]{2,1,0:T(8,128)(2,1)}, u32[]{:S(2)}, u32[]{:S(2)}) async-start(bf16[2,2048,1024]{2,1,0:T(8,128)(2,1)} %bitcast.383), calls=%async_computation.3 | async-start | bytes 16777216 | tf_op jit(solution)/shard_map/all_to_all | solution.py:71
  1139.1 375.8 %all-gather.22.cloned.1.call-start = ((), (), s32[]{:S(2)}) async-start(), calls=%async_computation.24 | async-start | bytes 12582912 | tf_op jit(solution)/shard_map/all_gather | solution.py:66
  1148.2 716.1 %reduce-scatter.14.cloned.1.call-start = ((), (), s32[]{:S(2)}) async-start(), calls=%async_computation.27 | async-start | bytes 10485760 | tf_op jit(solution)/shard_map/reduce_scatter | solution.py:52
  1718.9 145.4 %copy-start.4 = (bf16[1024,1024]{1,0:T(8,128)(2,1)S(1)}, bf16[1024,1024]{1,0:T(8,128)(2,1)}, u32[]{:S(2)}) copy-start(bf16[1024,1024]{1,0:T(8,128)(2,1)} %param.31) | copy-start | bytes 6291460
  1718.9 145.4 %copy-start.41 = (f32[1024]{0:T(1024)S(1)}, f32[1024]{0:T(1024)}, u32[]{:S(2)}) copy-start(f32[1024]{0:T(1024)} %copy-done.40) | copy-start | bytes 12292
  1718.9 145.4 %copy-start.44 = (f32[1,1024]{1,0:T(1,128)S(1)}, f32[1,1024]{1,0:T(1,128)}, u32[]{:S(2)}) copy-start(f32[1,1024]{1,0:T(1,128)} %get-tuple-element.486) | copy-start | bytes 12292
  1718.9 311.5 %all-gather.26.cloned.1.call-start = ((), (), s32[]{:S(2)}) async-start(), calls=%async_computation.28 | async-start | bytes 10485760 | tf_op jit(solution)/shard_map/all_gather | solution.py:48
  1878.3 920.0 %reduce-scatter.26.cloned.1.call-start = ((), (), s32[]{:S(2)}) async-start(), calls=%async_computation.34 | async-start | bytes 12582912 | tf_op jit(solution)/shard_map/reduce_scatter | solution.py:94
  1904.7 893.6 %reduce-scatter.24.cloned.1.call-start = ((), (), s32[]{:S(2)}) async-start(), calls=%async_computation.33 | async-start | bytes 25165824 | tf_op jit(solution)/shard_map/reduce_scatter | solution.py:91
  2030.4 189.4 %all-to-all-start.6 = ((bf16[2,2048,1024]{2,1,0:T(8,128)(2,1)}), bf16[2,2048,1024]{2,1,0:T(8,128)(2,1)}, u32[]{:S(2)}, u32[]{:S(2)}) async-start(bf16[2,2048,1024]{2,1,0:T(8,128)(2,1)} %bitcast.384), calls=%async_computation.9 | async-start | bytes 16777216 | tf_op jit(solution)/shard_map/all_to_all | solution.py:71
  2037.4 761.0 %reduce-scatter.22.cloned.1.call-start = ((), (), s32[]{:S(2)}) async-start(), calls=%async_computation.32 | async-start | bytes 3145728 | tf_op jit(solution)/shard_map/reduce_scatter | solution.py:88
  2256.0 10.3 copy-start.2
  2256.0 10.3 copy-start.8
  2266.2 541.9 %reduce-scatter.18.cloned.1.call-start = ((), (), s32[]{:S(2)}) async-start(), calls=%async_computation.30 | async-start | bytes 3145728 | tf_op jit(solution)/shard_map/reduce_scatter | solution.py:82
  2269.3 14.5 copy-start.12
  2269.3 14.5 copy-start.38
  2298.5 23.7 copy-start.39
  2350.0 10.7 copy-start
  2391.9 14.3 copy-start.12
  2391.9 14.3 copy-start.38
  2420.7 23.6 copy-start.39
  2472.2 10.7 copy-start
  2514.0 14.3 copy-start.12
  2514.1 14.3 copy-start.38
  2542.9 23.6 copy-start.39
  2594.4 10.7 copy-start
  2636.2 14.3 copy-start.12
  2636.2 14.3 copy-start.38
  2665.1 23.6 copy-start.39
  2716.5 10.7 copy-start
  2770.8 8.9 copy-start.14
  2778.3 328.5 %reduce-scatter.20.cloned.1.call-start = ((), (), s32[]{:S(2)}) async-start(), calls=%async_computation.31 | async-start | bytes 6291456 | tf_op jit(solution)/shard_map/reduce_scatter | solution.py:85
  2798.2 350.5 %all-reduce.5.cloned.1.call-start = ((), (), s32[]{:S(2)}) async-start(), calls=%async_computation.35 | async-start | bytes 29360128 | tf_op jit(solution)/shard_map/psum | solution.py:427
  2808.1 488.4 %reduce-scatter.16.cloned.1.call-start = ((), (), s32[]{:S(2)}) async-start(), calls=%async_computation.29 | async-start | bytes 10485760 | tf_op jit(solution)/shard_map/reduce_scatter | solution.py:52
  2966.0 761.9 %reduce-scatter.12.cloned.1.call-start = ((), (), s32[]{:S(2)}) async-start(), calls=%async_computation.25 | async-start | bytes 10485760 | tf_op jit(solution)/shard_map/reduce_scatter | solution.py:52
  3148.7 12.0 copy-start.22
  3148.7 13.2 copy-start.21
  3148.7 14.3 copy-start.11
  3165.8 130.8 %copy-start.5 = (bf16[1024,1024]{1,0:T(8,128)(2,1)S(1)}, bf16[1024,1024]{1,0:T(8,128)(2,1)}, u32[]{:S(2)}) copy-start(bf16[1024,1024]{1,0:T(8,128)(2,1)} %param.31) | copy-start | bytes 6291460
  3165.8 130.8 %copy-start.48 = (f32[1024]{0:T(1024)S(1)}, f32[1024]{0:T(1024)}, u32[]{:S(2)}) copy-start(f32[1024]{0:T(1024)} %copy-done.47) | copy-start | bytes 12292
  3165.8 130.8 %copy-start.50 = (f32[1,1024]{1,0:T(1,128)S(1)}, f32[1,1024]{1,0:T(1,128)}, u32[]{:S(2)}) copy-start(f32[1,1024]{1,0:T(1,128)} %copy-done.49) | copy-start | bytes 12292
  3173.5 126.1 %copy-start.54 = (f32[1024]{0:T(1024)S(1)}, f32[1024]{0:T(1024)}, u32[]{:S(2)}) copy-start(f32[1024]{0:T(1024)} %get-tuple-element.385) | copy-start | bytes 12292
  3299.6 347.4 %copy-start.53 = (f32[2,1024]{1,0:T(2,128)S(1)}, f32[2,1024]{1,0:T(2,128)}, u32[]{:S(2)}) copy-start(f32[2,1024]{1,0:T(2,128)} %param.41) | copy-start | bytes 24580
  3299.6 347.3 %copy-start.55 = (f32[2,1024]{1,0:T(2,128)S(1)}, f32[2,1024]{1,0:T(2,128)}, u32[]{:S(2)}) copy-start(f32[2,1024]{1,0:T(2,128)} %param.49) | copy-start | bytes 24580
  3299.6 347.3 %copy-start.56 = (f32[2,1024]{1,0:T(2,128)S(1)}, f32[2,1024]{1,0:T(2,128)}, u32[]{:S(2)}) copy-start(f32[2,1024]{1,0:T(2,128)} %param.57) | copy-start | bytes 24580
  3647.6 7.3 copy-start.33
  3647.6 11.4 copy-start.36
  3647.6 11.4 copy-start.37
  3686.5 41.4 %copy-start.42 = (f32[1024]{0:T(1024)S(1)}, f32[1024]{0:T(1024)}, u32[]{:S(2)}) copy-start(f32[1024]{0:T(1024)} %copy-done.40) | copy-start | bytes 12292
  3686.5 41.4 %copy-start.45 = (f32[1,1024]{1,0:T(1,128)S(1)}, f32[1,1024]{1,0:T(1,128)}, u32[]{:S(2)}) copy-start(f32[1,1024]{1,0:T(1,128)} %get-tuple-element.486) | copy-start | bytes 12292
  3686.5 41.4 %copy-start.52 = (f32[1024]{0:T(1024)S(1)}, f32[1024]{0:T(1024)}, u32[]{:S(2)}) copy-start(f32[1024]{0:T(1024)} %copy-done.51) | copy-start | bytes 12292
  (30 other events, 129.9 us)
Sparse Core Ops, SparseCore 0:
  20.1 152.5 all-gather.9
  685.0 144.2 reduce-scatter.9
  831.5 150.7 all-gather.23
  984.3 147.8 all-gather.17
  1134.1 277.7 all-gather.19
  1413.9 101.0 all-gather.21
  1719.0 145.1 reduce-scatter.13
  1878.4 151.9 all-gather.25
Sparse Core Ops, SparseCore 1:
  182.7 54.2 all-gather.11
  238.9 32.5 all-gather.13
  273.5 54.9 all-gather.15
  1904.8 101.1 reduce-scatter.25
  2008.3 278.9 reduce-scatter.23
  2290.1 31.7 reduce-scatter.21
  2778.3 29.7 reduce-scatter.17
  2810.8 78.8 reduce-scatter.19
  2892.6 256.1 all-reduce.4
  3151.8 144.7 reduce-scatter.15
  3298.9 277.4 reduce-scatter.11
where the time goes:
time: 3760 us; the launch traced here: 3740 us
  waiting for transfers between devices  1440 us (38%)
  blocking collectives  874 us (23%)
  matrix products  667 us (18%)
  other arithmetic  378 us (10%)
  local copies, waits for them, and re-layouts  339 us (9%)
    all_to_all x4, blocking collectives, leave_rows(): lax.all_to_all(values.astype(jnp.bfloat16), 'row', split_axis=1, concat_a...  422 us
    all_to_all x3, waiting for transfers between devices, enter_rows(): lax.all_to_all(values, 'row', split_axis=0, concat_axis=1, tiled=True)  410 us
    reduce_scatter x4, waiting for transfers between devices, sum_tokens(): lax.psum_scatter(term(jnp.int32(0), lax.axis_size('col') * tok_rows).asty...  409 us
    all_gather x4, waiting for transfers between devices, gather_tokens(): return lax.all_gather(values, 'col', axis=0, tiled=True)  390 us
    psum x1, blocking collectives, shards(): lax.psum((local_grads[1], jnp.stack([gain_one_part, gain_two_part])), ('d...  316 us
    dot_general x8, matrix products, one_block(): jnp.einsum('qhgd,khd->hgqk', query_block, heads_of_keys, preferred_elemen...  115 us
    convert_element_type x4, other arithmetic, one_block(): grad_scores = (probability * (grad_prob - delta_sum)).astype(jnp.bfloat16)  111 us
    all_to_all x8, local copies, waits for them, and re-layouts, enter_rows(): lax.all_to_all(values, 'row', split_axis=0, concat_axis=1, tiled=True)  106 us
  transfers between devices with their start and end apart: 22, of which 15 were waited for; matrix products, arithmetic and copies ran while one was open for 33% of the time, Pallas kernels for 0%

commit v1 on v0

--- a/solution.py
+++ b/solution.py
@@ -1,6 +1,10 @@
+import functools
+
 import jax
 import jax.numpy as jnp
 from jax import lax
+from jax.experimental import pallas as pl
+from jax.experimental.pallas import tpu as pltpu
 from jax.sharding import PartitionSpec as P
 
 MODEL_WIDTH = 2048
@@ -521,6 +525,783 @@
     )
 
 
+LOW = jnp.bfloat16
+WIDE = jnp.float32
+CHUNK = 512
+LANES = 128
+MASKED = -1e30
+VMEM_BYTES = 48 * 1024 * 1024
+
+
+def swaps_fit(mesh):
+    return dict(mesh.shape) == {"dp": 4, "row": 2, "col": 4}
+
+
+def swap(values, axis, bit):
+    size = lax.axis_size(axis)
+    return lax.ppermute(values, axis, [(place, place ^ bit) for place in range(size)])
+
+
+def swap_core(values):
+    return swap(values, "dp", 1)
+
+
+def swap_y(values):
+    return swap(values, "dp", 2)
+
+
+def swap_x(values):
+    return swap(values, "row", 1)
+
+
+def swap_near(values):
+    return swap(values, "col", 1)
+
+
+def swap_far(values):
+    return swap(values, "col", 2)
+
+
+def swap_corner(values):
+    cols = lax.axis_size("col")
+    pairs = [
+        (row * cols + col, (row ^ 1) * cols + (col ^ 1))
+        for row in range(lax.axis_size("row"))
+        for col in range(cols)
+    ]
+    return lax.ppermute(values, ("row", "col"), pairs)
+
+
+def fold(kept, sent, move):
+    return kept + move(sent.astype(LOW)).astype(WIDE)
+
+
+def in_order(place, own, other, axis):
+    return jnp.concatenate(
+        [jnp.where(place == 0, own, other), jnp.where(place == 0, other, own)], axis=axis
+    )
+
+
+def cut(values, start, size, axis):
+    return lax.dynamic_slice_in_dim(values, start, size, axis)
+
+
+def partner_lanes(values):
+    lane = lax.broadcasted_iota(jnp.int32, values.shape, 1)
+    half = HEAD_SIZE // 2
+    ahead = pltpu.roll(values, values.shape[1] - half, 1)
+    behind = pltpu.roll(values, half, 1)
+    return jnp.where(lane % HEAD_SIZE < half, ahead, behind)
+
+
+def first_lanes(shape):
+    return lax.broadcasted_iota(jnp.int32, shape, 1) < HEAD_SIZE
+
+
+def dot_nt(left_side, right_side):
+    return lax.dot_general(
+        left_side, right_side, (((1,), (1,)), ((), ())), preferred_element_type=WIDE
+    )
+
+
+def dot_tn(left_side, right_side):
+    return lax.dot_general(
+        left_side, right_side, (((0,), (0,)), ((), ())), preferred_element_type=WIDE
+    )
+
+
+def project_kernel(normed_ref, weight_ref, cosine_ref, sine_ref, out_ref):
+    product = jnp.dot(normed_ref[0], weight_ref[...], preferred_element_type=WIDE)
+    cosine = cosine_ref[0]
+    sine = sine_ref[0]
+    for tile in range(3):
+        part = product[:, tile * LANES : (tile + 1) * LANES]
+        turned = part * cosine + partner_lanes(part) * sine
+        if tile < 2:
+            turned = turned * ATTN_SCALE
+        else:
+            turned = jnp.where(first_lanes(part.shape), turned, part)
+        out_ref[0, 0, :, tile * LANES : (tile + 1) * LANES] = turned.astype(LOW)
+
+
+def project(normed_pair, weights, cosine, sine):
+    groups = 4
+    wide = 3 * LANES
+    return pl.pallas_call(
+        project_kernel,
+        grid=(2, groups),
+        in_specs=[
+            pl.BlockSpec((1, CHUNK, MODEL_WIDTH), lambda i, j: (i, 0, 0)),
+            pl.BlockSpec((MODEL_WIDTH, wide), lambda i, j: (0, j)),
+            pl.BlockSpec((1, CHUNK, LANES), lambda i, j: (0, 0, 0)),
+            pl.BlockSpec((1, CHUNK, LANES), lambda i, j: (0, 0, 0)),
+        ],
+        out_specs=pl.BlockSpec((1, 1, CHUNK, wide), lambda i, j: (j, i, 0, 0)),
+        out_shape=jax.ShapeDtypeStruct((groups, 2, CHUNK, wide), LOW),
+        compiler_params=pltpu.CompilerParams(vmem_limit_bytes=VMEM_BYTES),
+        cost_estimate=pl.CostEstimate(
+            flops=2 * 2 * CHUNK * MODEL_WIDTH * groups * wide,
+            bytes_accessed=4 * MODEL_WIDTH * (2 * CHUNK + groups * wide),
+            transcendentals=0,
+        ),
+    )(normed_pair, weights, cosine, sine)
+
+
+def split_heads(tiles, lanes_from):
+    heads = []
+    for head in range(4):
+        tile = tiles[:, (head // 2) * LANES : (head // 2 + 1) * LANES].astype(WIDE)
+        if (head % 2) * HEAD_SIZE != lanes_from:
+            tile = pltpu.roll(tile, HEAD_SIZE, 1)
+        low = first_lanes(tile.shape)
+        heads.append(jnp.where(low if lanes_from == 0 else ~low, tile, 0.0).astype(LOW))
+    return heads
+
+
+def join_heads(heads, lanes_from):
+    tiles = []
+    for pair in range(2):
+        even, odd = heads[2 * pair], heads[2 * pair + 1]
+        if lanes_from == 0:
+            odd = pltpu.roll(odd, HEAD_SIZE, 1)
+        else:
+            even = pltpu.roll(even, HEAD_SIZE, 1)
+        tiles.append(jnp.where(first_lanes(even.shape), even, odd))
+    return tiles
+
+
+def visible_chunks(chunk, prefix):
+    whole = jnp.maximum(chunk, prefix // CHUNK)
+    some = jnp.maximum(chunk + 1, (prefix + CHUNK - 1) // CHUNK)
+    return whole, some
+
+
+def attend_kernel(place_ref, prefix_ref, q_ref, kv_ref, o_ref, lse_ref, heads, top, total, acc):
+    sequence = pl.program_id(0)
+    place = place_ref[0]
+    prefix = prefix_ref[sequence]
+    chunk = pl.program_id(1) ^ place
+    for head, tile in enumerate(split_heads(q_ref[0, 0], 0)):
+        heads[head] = tile
+        top[head] = jnp.full((CHUNK, LANES), MASKED, WIDE)
+        total[head] = jnp.zeros((CHUNK, LANES), WIDE)
+        acc[head] = jnp.zeros((CHUNK, LANES), WIDE)
+
+    def step(masked, other, carry):
+        kv = kv_ref[other ^ place, 0]
+        if masked:
+            row = lax.broadcasted_iota(jnp.int32, (CHUNK, CHUNK), 0) + chunk * CHUNK
+            key = lax.broadcasted_iota(jnp.int32, (CHUNK, CHUNK), 1) + other * CHUNK
+            visible = key <= jnp.maximum(row, prefix - 1)
+        for head in range(4):
+            scores = dot_nt(heads[head], kv)
+            if masked:
+                scores = jnp.where(visible, scores, MASKED)
+            old = top[head]
+            new = jnp.maximum(old, jnp.max(scores, axis=1, keepdims=True))
+            exponent = jnp.exp(scores - new[:, :1])
+            shrink = jnp.exp(old - new)
+            top[head] = new
+            total[head] = total[head] * shrink + jnp.sum(exponent, axis=1, keepdims=True)
+            acc[head] = acc[head] * shrink + jnp.dot(
+                exponent.astype(LOW), kv, preferred_element_type=WIDE
+            )
+        return carry
+
+    whole, some = visible_chunks(chunk, prefix)
+    lax.fori_loop(0, whole, functools.partial(step, False), 0)
+    lax.fori_loop(whole, some, functools.partial(step, True), 0)
+    lane = lax.broadcasted_iota(jnp.int32, (CHUNK, LANES), 1)
+    logs = jnp.zeros((CHUNK, LANES), WIDE)
+    results = []
+    for head in range(4):
+        results.append(acc[head] / total[head])
+        logs = jnp.where(lane == head, top[head] + jnp.log(total[head]), logs)
+    lse_ref[0, 0] = jnp.transpose(logs)[:8]
+    for pair, tile in enumerate(join_heads(results, HEAD_SIZE)):
+        o_ref[0, 0, :, pair * LANES : (pair + 1) * LANES] = tile.astype(LOW)
+
+
+def attend(place, prefixes, packed):
+    units = 2 * 4 * 10
+    return pl.pallas_call(
+        attend_kernel,
+        grid_spec=pltpu.PrefetchScalarGridSpec(
+            num_scalar_prefetch=2,
+            grid=(2, 4),
+            in_specs=[
+                pl.BlockSpec((1, 1, CHUNK, 2 * LANES), lambda i, j, *_: (j, i, 0, 0)),
+                pl.BlockSpec((4, 1, CHUNK, LANES), lambda i, j, *_: (0, i, 0, 2)),
+            ],
+            out_specs=[
+                pl.BlockSpec((1, 1, CHUNK, 2 * LANES), lambda i, j, *_: (j, i, 0, 0)),
+                pl.BlockSpec((1, 1, 8, CHUNK), lambda i, j, *_: (j, i, 0, 0)),
+            ],
+            scratch_shapes=[
+                pltpu.VMEM((4, CHUNK, LANES), LOW),
+                pltpu.VMEM((4, CHUNK, LANES), WIDE),
+                pltpu.VMEM((4, CHUNK, LANES), WIDE),
+                pltpu.VMEM((4, CHUNK, LANES), WIDE),
+            ],
+        ),
+        out_shape=[
+            jax.ShapeDtypeStruct((4, 2, CHUNK, 2 * LANES), LOW),
+            jax.ShapeDtypeStruct((4, 2, 8, CHUNK), WIDE),
+        ],
+        compiler_params=pltpu.CompilerParams(vmem_limit_bytes=VMEM_BYTES),
+        cost_estimate=pl.CostEstimate(
+            flops=units * 4 * CHUNK * CHUNK * 256 * 2 * 2,
+            bytes_accessed=8 * 1024 * 1024,
+            transcendentals=units * 4 * CHUNK * CHUNK,
+        ),
+    )(place, prefixes, packed, packed)
+
+
+def attend_back_kernel(
+    place_ref,
+    prefix_ref,
+    q_ref,
+    kv_ref,
+    o_ref,
+    do_ref,
+    lse_ref,
+    cosine_ref,
+    sine_ref,
+    out_ref,
+    heads,
+    grads,
+    deltas,
+    q_acc,
+    kv_acc,
+):
+    sequence = pl.program_id(0)
+    slot = pl.program_id(1)
+    place = place_ref[0]
+    prefix = prefix_ref[sequence]
+    chunk = slot ^ place
+
+    @pl.when(slot == 0)
+    def _():
+        kv_acc[...] = jnp.zeros_like(kv_acc)
+
+    ones = jnp.ones((8, LANES), WIDE)
+    out_heads = split_heads(o_ref[0, 0], HEAD_SIZE)
+    grad_heads = split_heads(do_ref[0, 0], HEAD_SIZE)
+    for head, tile in enumerate(split_heads(q_ref[0, 0], 0)):
+        heads[head] = tile
+        grads[head] = grad_heads[head]
+        product = out_heads[head].astype(WIDE) * grad_heads[head].astype(WIDE)
+        deltas[head] = lax.dot_general(
+            ones,
+            product,
+            (((1,), (1,)), ((), ())),
+            precision=lax.Precision.HIGHEST,
+            preferred_element_type=WIDE,
+        )
+        q_acc[head] = jnp.zeros((CHUNK, LANES), WIDE)
+
+    def step(masked, other, carry):
+        other_slot = other ^ place
+        kv = kv_ref[other_slot, 0]
+        if masked:
+            key = lax.broadcasted_iota(jnp.int32, (CHUNK, CHUNK), 0) + other * CHUNK
+            row = lax.broadcasted_iota(jnp.int32, (CHUNK, CHUNK), 1) + chunk * CHUNK
+            visible = key <= jnp.maximum(row, prefix - 1)
+        for head in range(4):
+            scores = dot_nt(kv, heads[head])
+            if masked:
+                scores = jnp.where(visible, scores, MASKED)
+            probability = jnp.exp(scores - lse_ref[0, 0, head : head + 1])
+            grad_prob = dot_nt(kv, grads[head])
+            grad_scores = (probability * (grad_prob - deltas[head][:1])).astype(LOW)
+            kv_acc[other_slot] += jnp.dot(
+                grad_scores, heads[head], preferred_element_type=WIDE
+            ) + jnp.dot(probability.astype(LOW), grads[head], preferred_element_type=WIDE)
+            q_acc[head] += dot_tn(grad_scores, kv)
+        return carry
+
+    whole, some = visible_chunks(chunk, prefix)
+    lax.fori_loop(0, whole, functools.partial(step, False), 0)
+    lax.fori_loop(whole, some, functools.partial(step, True), 0)
+    cosine = cosine_ref[slot]
+    sine = sine_ref[slot]
+    for pair, tile in enumerate(join_heads([q_acc[head] for head in range(4)], 0)):
+        tile = tile * ATTN_SCALE
+        turned = tile * cosine + partner_lanes(tile * sine)
+        out_ref[slot, 0, :, pair * LANES : (pair + 1) * LANES] = turned.astype(LOW)
+
+    @pl.when(slot == 3)
+    def _():
+        for other in range(4):
+            tile = kv_acc[other]
+            turned = tile * cosine_ref[other] + partner_lanes(tile * sine_ref[other])
+            turned = jnp.where(first_lanes(tile.shape), turned, tile)
+            out_ref[other, 0, :, 2 * LANES :] = turned.astype(LOW)
+
+
+def attend_grad(place, prefixes, packed, attended, grad_attended, logsum, cosine, sine):
+    units = 2 * 4 * 10
+    return pl.pallas_call(
+        attend_back_kernel,
+        grid_spec=pltpu.PrefetchScalarGridSpec(
+            num_scalar_prefetch=2,
+            grid=(2, 4),
+            in_specs=[
+                pl.BlockSpec((1, 1, CHUNK, 2 * LANES), lambda i, j, *_: (j, i, 0, 0)),
+                pl.BlockSpec((4, 1, CHUNK, LANES), lambda i, j, *_: (0, i, 0, 2)),
+                pl.BlockSpec((1, 1, CHUNK, 2 * LANES), lambda i, j, *_: (j, i, 0, 0)),
+                pl.BlockSpec((1, 1, CHUNK, 2 * LANES), lambda i, j, *_: (j, i, 0, 0)),
+                pl.BlockSpec((1, 1, 8, CHUNK), lambda i, j, *_: (j, i, 0, 0)),
+                pl.BlockSpec((4, CHUNK, LANES), lambda i, j, *_: (0, 0, 0)),
+                pl.BlockSpec((4, CHUNK, LANES), lambda i, j, *_: (0, 0, 0)),
+            ],
+            out_specs=pl.BlockSpec((4, 1, CHUNK, 3 * LANES), lambda i, j, *_: (0, i, 0, 0)),
+            scratch_shapes=[
+                pltpu.VMEM((4, CHUNK, LANES), LOW),
+                pltpu.VMEM((4, CHUNK, LANES), LOW),
+                pltpu.VMEM((4, 8, CHUNK), WIDE),
+                pltpu.VMEM((4, CHUNK, LANES), WIDE),
+                pltpu.VMEM((4, CHUNK, LANES), WIDE),
+            ],
+        ),
+        out_shape=jax.ShapeDtypeStruct((4, 2, CHUNK, 3 * LANES), LOW),
+        compiler_params=pltpu.CompilerParams(vmem_limit_bytes=VMEM_BYTES),
+        cost_estimate=pl.CostEstimate(
+            flops=units * 4 * CHUNK * CHUNK * 256 * 2 * 5,
+            bytes_accessed=16 * 1024 * 1024,
+            transcendentals=units * 4 * CHUNK * CHUNK,
+        ),
+    )(place, prefixes, packed, packed, attended, grad_attended, logsum, cosine, sine)
+
+
+def dp_spot(dp):
+    return dp.reshape(1)
+
+
+def step_kernel(spot_ref, factor_ref, grad_ref, weight_ref, moment_ref, square_ref, *outs):
+    gradient = grad_ref[0].astype(WIDE) * factor_ref[0, 0]
+    following, variance = adam(
+        weight_ref[...], gradient, moment_ref[...], square_ref[...], DECAY, LEARN
+    )
+    outs[0][...] = gradient
+    outs[1][...] = following
+    outs[2][...] = variance
+
+
+def step_weight(spot, factor, pieces, axis, weight, moment, square):
+    count, rows, columns = pieces.shape
+    block_rows = min(rows, (1 << 17) // columns)
+    parts = rows // block_rows
+
+    def piece_at(block, part, spot_ref):
+        code = spot_ref[0]
+        return (block ^ ((code % 2) * 2 + code // 2), part, 0)
+
+    def weight_at(block, part, spot_ref):
+        return (part, block) if axis == 1 else (block * parts + part, 0)
+
+    spec = pl.BlockSpec((block_rows, columns), weight_at)
+    return pl.pallas_call(
+        step_kernel,
+        grid_spec=pltpu.PrefetchScalarGridSpec(
+            num_scalar_prefetch=1,
+            grid=(count, parts),
+            in_specs=[
+                pl.BlockSpec(memory_space=pltpu.SMEM),
+                pl.BlockSpec((1, block_rows, columns), piece_at),
+                spec,
+                spec,
+                spec,
+            ],
+            out_specs=[spec] * 3,
+        ),
+        out_shape=[jax.ShapeDtypeStruct(weight.shape, WIDE)] * 3,
+        compiler_params=pltpu.CompilerParams(vmem_limit_bytes=VMEM_BYTES),
+        cost_estimate=pl.CostEstimate(
+            flops=12 * weight.size, bytes_accessed=26 * weight.size, transcendentals=weight.size
+        ),
+    )(spot, factor, pieces, weight, moment, square)
+
+
+def step_pair_kernel(spot_ref, factor_ref, grad_ref, *refs):
+    core, start = spot_ref[0], spot_ref[1]
+    factor = factor_ref[0, 0]
+    for group in range(4):
+        turned = group ^ start
+        slot = turned // 2 + (turned % 2) * 2
+        first = grad_ref[core * 4 + slot].astype(WIDE) * factor
+        second = grad_ref[(1 - core) * 4 + slot].astype(WIDE) * factor
+        low = first_lanes(first.shape)
+        lanes = pl.ds(group * LANES, LANES)
+        key_grad = jnp.where(low, first, pltpu.roll(second, HEAD_SIZE, 1))
+        value_grad = jnp.where(low, pltpu.roll(first, HEAD_SIZE, 1), second)
+        for gradient, at in ((key_grad, 0), (value_grad, 1)):
+            weight_ref, moment_ref, square_ref = refs[3 * at : 3 * at + 3]
+            following, variance = adam(
+                weight_ref[:, lanes],
+                gradient,
+                moment_ref[:, lanes],
+                square_ref[:, lanes],
+                DECAY,
+                LEARN,
+            )
+            outs = refs[6 + 3 * at : 9 + 3 * at]
+            outs[0][:, lanes] = gradient
+            outs[1][:, lanes] = following
+            outs[2][:, lanes] = variance
+
+
+def step_pair(spot, factor, pieces, key, value):
+    rows, columns = key[0].shape
+    block_rows = 128
+    spec = pl.BlockSpec((block_rows, columns), lambda i, *_: (i, 0))
+    outs = pl.pallas_call(
+        step_pair_kernel,
+        grid_spec=pltpu.PrefetchScalarGridSpec(
+            num_scalar_prefetch=1,
+            grid=(rows // block_rows,),
+            in_specs=[
+                pl.BlockSpec(memory_space=pltpu.SMEM),
+                pl.BlockSpec((8, block_rows, LANES), lambda i, *_: (0, i, 0)),
+            ]
+            + [spec] * 6,
+            out_specs=[spec] * 6,
+        ),
+        out_shape=[jax.ShapeDtypeStruct((rows, columns), WIDE)] * 6,
+        compiler_params=pltpu.CompilerParams(vmem_limit_bytes=VMEM_BYTES),
+        cost_estimate=pl.CostEstimate(
+            flops=24 * rows * columns,
+            bytes_accessed=52 * rows * columns,
+            transcendentals=2 * rows * columns,
+        ),
+    )(spot, factor, pieces, *key, *value)
+    return outs[:3], outs[3:]
+
+
+def slot_tables(place):
+    half = HEAD_SIZE // 2
+    frequency = THETA ** (-(jnp.arange(half, dtype=WIDE) * 2.0 / HEAD_SIZE))
+    chunk = jnp.arange(4, dtype=jnp.int32) ^ place
+    position = (chunk[:, None] * CHUNK + jnp.arange(CHUNK)[None, :]).astype(WIDE)
+    angles = position[:, :, None] * frequency[None, None, :]
+    cosine, sine = jnp.cos(angles), jnp.sin(angles)
+    return (
+        jnp.concatenate([cosine] * 4, axis=2),
+        jnp.concatenate([-sine, sine, -sine, sine], axis=2),
+    )
+
+
+def exchange(pieces):
+    return [
+        pieces[0],
+        swap_x(pieces[1]),
+        swap_near(pieces[2]),
+        swap_corner(pieces[3]),
+    ]
+
+
+def rows_norm(values):
+    factor = lax.rsqrt(
+        jnp.sum(values * values, axis=1, keepdims=True) / MODEL_WIDTH + EPS_NORM
+    )
+    return values * factor, factor
+
+
+def rows_norm_back(gradient, normed, factor, gain_row):
+    weighted = gradient * gain_row
+    inner = jnp.sum(weighted * normed, axis=1, keepdims=True) / MODEL_WIDTH
+    return factor * (weighted - normed * inner), jnp.sum(gradient * normed, axis=0)
+
+
+def swapped_shards(
+    tokens,
+    cotangent,
+    prefix,
+    query_weight,
+    key_projection,
+    value_projection,
+    out_weight,
+    gate_weight,
+    up_weight,
+    down_weight,
+    norm_gains,
+    query_moment,
+    key_first_moment,
+    value_first_moment,
+    out_moment,
+    gate_moment,
+    up_moment,
+    down_moment,
+    gains_moment,
+    query_square,
+    key_second_moment,
+    value_second_moment,
+    out_square,
+    gate_square,
+    up_square,
+    down_square,
+    gains_square,
+):
+    row = lax.axis_index("row")
+    col = lax.axis_index("col")
+    dp = lax.axis_index("dp")
+    core = dp % 2
+    side = dp // 2
+    near = col % 2
+    far = col // 2
+    place = near * 2 + row
+    half_rows = tokens.shape[0] // 2
+    half_width = tokens.shape[1]
+
+    owner = [col ^ (2 * row), col ^ (2 - 2 * row), col ^ (1 + 2 * row), col ^ (3 - 2 * row)]
+
+    def by_owner(block, axis):
+        other = swap_far(block)
+        first = jnp.where(row == 0, block, other)
+        second = jnp.where(row == 0, other, block)
+        pair = jnp.stack([first, second])
+        return jnp.concatenate([pair, swap_near(pair)])
+
+    swapped = [1, 0, 3, 2]
+
+    def reorder(blocks):
+        return jnp.stack([blocks[place_at] for place_at in swapped])
+
+    q_cut = cut(query_weight, core * 2 * LANES + side * LANES, LANES, 1).astype(LOW)
+    q_blocks = by_owner(q_cut, 1)
+    q_own = jnp.stack([q_blocks, swap_y(q_blocks)], axis=1)
+    q_whole = jnp.concatenate(
+        [q_own, swap_x(reorder(q_own))], axis=2
+    )
+
+    def heads_of(matrix):
+        return jnp.stack(
+            [cut(matrix, (at * 2 + core) * HEAD_SIZE, HEAD_SIZE, 1) for at in owner]
+        ).astype(LOW)
+
+    kv_own = jnp.concatenate([heads_of(key_projection), heads_of(value_projection)], axis=2)
+    kv_whole = jnp.concatenate([kv_own, swap_x(reorder(kv_own))], axis=1)
+    in_weights = jnp.stack([q_whole[:, 0], q_whole[:, 1], kv_whole], axis=1)
+    in_weights = in_weights.transpose(2, 0, 1, 3).reshape(MODEL_WIDTH, 4 * 3 * LANES)
+
+    o_cut = cut(out_weight, core * 2 * LANES + side * LANES, LANES, 0).astype(LOW)
+    o_blocks = by_owner(o_cut, 0)
+    o_rows = jnp.concatenate([o_blocks, swap_x(reorder(o_blocks))], axis=2)
+    out_weights = jnp.stack([o_rows, swap_y(o_rows)], axis=1).reshape(
+        4 * 2 * LANES, MODEL_WIDTH
+    )
+
+    units = gate_weight.shape[1] // 2
+
+    def hidden_cut(matrix, axis):
+        return cut(matrix, core * units + side * (units // 2), units // 2, axis).astype(LOW)
+
+    def widen(matrix, unit_axis, x_first):
+        block = hidden_cut(matrix, unit_axis)
+        block = jnp.concatenate([block, swap_far(block)], axis=unit_axis)
+        if x_first:
+            block = jnp.concatenate([block, swap_x(block)], axis=1 - unit_axis)
+            return jnp.concatenate([block, swap_y(block)], axis=unit_axis)
+        block = jnp.concatenate([block, swap_y(block)], axis=unit_axis)
+        return jnp.concatenate([block, swap_x(block)], axis=1 - unit_axis)
+
+    gate_whole = widen(gate_weight, 1, True)
+    up_whole = widen(up_weight, 1, False)
+    down_whole = widen(down_weight, 0, True)
+
+    def enter(values):
+        own = cut(values, row * half_rows, half_rows, 0)
+        sent = cut(values, (1 - row) * half_rows, half_rows, 0)
+        return jnp.concatenate([own, swap_x(sent)], axis=1)
+
+    def leave(values):
+        back = swap_x(values[:, half_width:])
+        return in_order(row, values[:, :half_width], back, 0)
+
+    def pair_core(values):
+        return jnp.concatenate([values, swap_core(values)], axis=0)
+
+    def gather_four(values):
+        both = jnp.concatenate([values, swap_near(values)], axis=0)
+        return jnp.concatenate([both, swap_core(both)], axis=0)
+
+    def sum_four(part):
+        count = part.shape[0] // 4
+        part = fold(part[: 2 * count], part[2 * count :], swap_core)
+        return fold(part[:count], part[count:], swap_near)
+
+    gains = jnp.concatenate([norm_gains, swap_x(norm_gains)], axis=1)
+    prefixes = jnp.stack([prefix[far], swap_core(prefix)[far]])
+    place_array = place.reshape(1)
+    cosine, sine = slot_tables(place)
+
+    x = enter(tokens).astype(WIDE)
+    normed_one, factor_one = rows_norm(x)
+    h_one = pair_core((normed_one * gains[0]).astype(LOW))
+    projected = project(h_one.reshape(2, CHUNK, MODEL_WIDTH), in_weights, cosine, sine)
+    packed = jnp.stack(exchange([projected[slot] for slot in range(4)]))
+    attended, logsum = attend(place_array, prefixes, packed)
+    back = exchange([attended[slot] for slot in range(4)])
+    o_tokens = jnp.concatenate(back, axis=2).reshape(2 * CHUNK, 4 * 2 * LANES)
+    out_part = matrix_multiply(o_tokens, out_weights)
+    residual = x + RESID * fold(out_part[:half_rows], out_part[half_rows:], swap_core)
+
+    normed_two, factor_two = rows_norm(residual)
+    h_two = gather_four((normed_two * gains[1]).astype(LOW))
+    gate_value = matrix_multiply(h_two, gate_whole)
+    up_value = matrix_multiply(h_two, up_whole)
+    hidden = (jax.nn.silu(gate_value) * up_value).astype(LOW)
+    down_part = sum_four(matrix_multiply(hidden, down_whole))
+    layer_out = leave((residual + RESID * down_part).astype(LOW))
+
+    grad_output = enter(cotangent).astype(WIDE)
+    grad_mlp = gather_four((RESID * grad_output).astype(LOW))
+    down_local = left_product(hidden, grad_mlp)
+    hidden_part = right_product(grad_mlp, down_whole)
+    sigmoid_gate = jax.nn.sigmoid(gate_value)
+    grad_gate = (
+        hidden_part * up_value * sigmoid_gate * (1.0 + gate_value * (1.0 - sigmoid_gate))
+    ).astype(LOW)
+    grad_up = (hidden_part * (gate_value * sigmoid_gate)).astype(LOW)
+    h_two_part = right_product(grad_gate, gate_whole) + right_product(grad_up, up_whole)
+    gate_local = left_product(h_two, grad_gate)
+    up_local = left_product(h_two, grad_up)
+    grad_mid_part, gain_two_part = rows_norm_back(
+        sum_four(h_two_part), normed_two, factor_two, gains[1]
+    )
+    grad_mid = grad_output + grad_mid_part
+
+    grad_attended = pair_core((RESID * grad_mid).astype(LOW))
+    head_grad = right_product(grad_attended, out_weights).astype(LOW)
+    head_grad = head_grad.reshape(2, CHUNK, 4, 2 * LANES)
+    out_local = left_product(o_tokens, grad_attended)
+    head_pieces = jnp.stack(exchange([head_grad[:, :, slot] for slot in range(4)]))
+    packed_grad = attend_grad(
+        place_array, prefixes, packed, attended, head_pieces, logsum, cosine, sine
+    )
+    pieces = exchange([packed_grad[slot] for slot in range(4)])
+    in_grads = jnp.concatenate(pieces, axis=2).reshape(2 * CHUNK, 4 * 3 * LANES)
+    in_local = left_product(h_one, in_grads)
+    h_one_part = right_product(in_grads, in_weights)
+    grad_in_part, gain_one_part = rows_norm_back(
+        fold(h_one_part[:half_rows], h_one_part[half_rows:], swap_core),
+        normed_one,
+        factor_one,
+        gains[0],
+    )
+    input_grad = leave((grad_mid + grad_in_part).astype(LOW))
+
+    def halve_hidden(part, unit_axis, x_first):
+        def half(values, axis, which):
+            size = values.shape[axis] // 2
+            return lax.slice_in_dim(values, which * size, (which + 1) * size, axis=axis)
+
+        steps = [(swap_x, 1 - unit_axis), (swap_y, unit_axis)]
+        if not x_first:
+            steps = steps[::-1]
+        for move, axis in steps + [(swap_far, unit_axis)]:
+            part = fold(half(part, axis, 0), half(part, axis, 1), move)
+        return part.astype(LOW)
+
+    def spread(piece):
+        pair = jnp.stack([piece, swap_y(piece)])
+        return jnp.concatenate([pair, swap_core(pair)])
+
+    gate_piece = halve_hidden(gate_local, 1, False)
+    up_piece = halve_hidden(up_local, 1, True)
+    down_piece = halve_hidden(down_local, 0, True)
+
+    wide = 3 * LANES
+
+    def columns(values, order, size):
+        return jnp.concatenate([values[:, at * size : (at + 1) * size] for at in order], axis=1)
+
+    in_part = fold(
+        in_local[:half_width], columns(in_local[half_width:], swapped, wide), swap_x
+    )
+    in_part = fold(in_part[:, : 2 * wide], in_part[:, 2 * wide :], swap_near)
+    in_part = fold(
+        jnp.where(row == 0, in_part[:, :wide], in_part[:, wide:]),
+        jnp.where(row == 0, in_part[:, wide:], in_part[:, :wide]),
+        swap_far,
+    ).astype(LOW)
+    from_side = swap_y(in_part[:, LANES:])
+    query_piece = (
+        in_part[:, :LANES].astype(WIDE) + from_side[:, :LANES].astype(WIDE)
+    ).astype(LOW)
+    kv_piece = (
+        in_part[:, 2 * LANES :].astype(WIDE) + from_side[:, LANES:].astype(WIDE)
+    ).astype(LOW)
+
+    def out_rows(values):
+        size = 2 * LANES
+        return jnp.concatenate([values[at * size : (at + 1) * size] for at in swapped])
+
+    out_part = fold(out_local[:, :half_width], out_rows(out_local[:, half_width:]), swap_x)
+    out_part = fold(out_part[: 4 * LANES], out_part[4 * LANES :], swap_near)
+    out_part = fold(
+        jnp.where(row == 0, out_part[: 2 * LANES], out_part[2 * LANES :]),
+        jnp.where(row == 0, out_part[2 * LANES :], out_part[: 2 * LANES]),
+        swap_far,
+    )
+    out_piece = fold(out_part[:LANES], out_part[LANES:], swap_y).astype(LOW)
+
+    kv_pieces = jnp.stack([kv_piece, swap_far(kv_piece)])
+    kv_pieces = jnp.concatenate([kv_pieces, swap_near(kv_pieces)])
+    kv_pieces = jnp.concatenate([kv_pieces, swap_core(kv_pieces)])
+
+    gain_parts = jnp.stack([gain_one_part, gain_two_part])
+    gain_parts = gain_parts[:, :half_width] + swap_x(gain_parts[:, half_width:])
+    gains_total = lax.psum(gain_parts, ("dp", "col"))
+
+    def squares_of(values):
+        values = values.astype(WIDE)
+        return jnp.sum(values * values)
+
+    square_local = jnp.where((col == 0) & (dp == 0), squares_of(gains_total), 0.0)
+    square_local = square_local + jnp.where(side == 0, squares_of(kv_piece), 0.0)
+    for piece in (query_piece, out_piece, gate_piece, up_piece, down_piece):
+        square_local = square_local + squares_of(piece)
+    grad_norm = jnp.sqrt(lax.psum(square_local, ("dp", "row", "col")))
+    factor = jnp.minimum(1.0, CLIP / grad_norm)
+    factor_cell = factor.reshape(1, 1)
+    spot = dp_spot(dp)
+
+    def step(piece, axis, weight, moment, square):
+        return step_weight(spot, factor_cell, spread(piece), axis, weight, moment, square)
+
+    query_out = step(query_piece, 1, query_weight, query_moment, query_square)
+    out_out = step(out_piece, 0, out_weight, out_moment, out_square)
+    gate_out = step(gate_piece, 1, gate_weight, gate_moment, gate_square)
+    up_out = step(up_piece, 1, up_weight, up_moment, up_square)
+    down_out = step(down_piece, 0, down_weight, down_moment, down_square)
+    kv_spot = jnp.stack([core, col])
+    key_out, value_out = step_pair(
+        kv_spot,
+        factor_cell,
+        kv_pieces,
+        (key_projection, key_first_moment, key_second_moment),
+        (value_projection, value_first_moment, value_second_moment),
+    )
+    results = (query_out, key_out, value_out, out_out, gate_out, up_out, down_out)
+    clipped, nexts, variances = zip(*results)
+    gains_grad = gains_total * factor
+    gains_next, gains_variance = adam(
+        norm_gains, gains_grad, gains_moment, gains_square, 0.0, GAINS_LEARN
+    )
+    return (
+        layer_out,
+        input_grad,
+        *clipped,
+        gains_grad,
+        *nexts,
+        gains_next,
+        *variances,
+        gains_variance,
+        grad_norm,
+    )
+
+
 def solution(mesh):
     placed = (
         P(("dp", "col"), "row"),
@@ -552,7 +1333,7 @@
         P(None, "row"),
     )
     return jax.shard_map(
-        shards,
+        swapped_shards if swaps_fit(mesh) else shards,
         mesh=mesh,
         in_specs=placed,
         out_specs=(

time: 3760 us -> 1620 us (0.43)
  waiting for transfers between devices: 1440 us -> 519 us
  blocking collectives: 874 us -> 68.7 us
  matrix products: 667 us -> 293 us
  Pallas kernels: 0 us -> 256 us
  local copies, waits for them, and re-layouts: 339 us -> 129 us
  other arithmetic: 378 us -> 210 us
  starting transfers between devices: 22.6 us -> 129 us
    all_gather x9 -> x0, waiting for transfers between devices: 567 us -> none  [the longest x4 390 us: gather_tokens(): return lax.all_gather(values, 'col', axis=0, tiled=True)]
    all_to_all x5 -> x0, blocking collectives: 525 us -> none  [the longest x4 422 us: leave_rows(): lax.all_to_all(values.astype(jnp.bfloat16), 'row', split_axis=1, concat_a...]
    ppermute x0 -> x79, waiting for transfers between devices: none -> 519 us  [the longest x75 493 us: swap(): lax.ppermute(values, axis, [(place, place ^ bit) for place in range(size)])]
    reduce_scatter x9 -> x0, waiting for transfers between devices: 419 us -> none  [the longest x4 409 us: sum_tokens(): lax.psum_scatter(term(jnp.int32(0), lax.axis_size('col') * tok_rows).asty...]
    all_to_all x3 -> x0, waiting for transfers between devices: 410 us -> none  [enter_rows(): lax.all_to_all(values, 'row', split_axis=0, concat_axis=1, tiled=True)]
    dot_general x28 -> x0, matrix products: 386 us -> none  [the longest x8 115 us: one_block(): jnp.einsum('qhgd,khd->hgqk', query_block, heads_of_keys, preferred_elemen...]
    psum x6 -> x2, blocking collectives: 349 us -> 68.7 us  [the longest x1 37.3 us: swapped_shards(): grad_norm = jnp.sqrt(lax.psum(square_local, ('dp', 'row', 'col')))]
    pallas_call x0 -> x9, Pallas kernels: none -> 256 us  [the longest x5 87.6 us: step_weight(): pl.pallas_call(step_kernel, grid_spec=pltpu.PrefetchScalarGridSpec(num_sc...]
  transfers between devices with their start and end apart: 22 -> 79, of which waited for: 15 -> 30; matrix products, arithmetic and copies ran while one was open for 33% -> 30% of each run, Pallas kernels for 0% -> 15%
where the time goes in v1:
time: 1620 us; the launch traced here: 1610 us
  waiting for transfers between devices  519 us (32%)
  matrix products  293 us (18%)
  Pallas kernels  256 us (16%)
  other arithmetic  210 us (13%)
  starting transfers between devices  129 us (8%)
  local copies, waits for them, and re-layouts  129 us (8%)
  blocking collectives  68.7 us (4%)
    ppermute x75, waiting for transfers between devices, swap(): lax.ppermute(values, axis, [(place, place ^ bit) for place in range(size)])  493 us
    ppermute x75, starting transfers between devices, swap(): lax.ppermute(values, axis, [(place, place ^ bit) for place in range(size)])  126 us
    dot_general x5, matrix products, right_product(): lax.dot_general(left_side, right_side, (((1,), (1,)), ((), ())), preferre...  107 us
    dot_general x5, matrix products, left_product(): lax.dot_general(left_side, right_side, (((0,), (0,)), ((), ())), preferre...  94.4 us
    dot_general x4, matrix products, matrix_multiply(): return jnp.dot(left_side, right_side, preferred_element_type=jnp.float32)  91.6 us
    pallas_call x5, Pallas kernels, step_weight(): pl.pallas_call(step_kernel, grid_spec=pltpu.PrefetchScalarGridSpec(num_sc...  87.6 us
    pallas_call x1, Pallas kernels, attend_grad(): pl.pallas_call(attend_back_kernel, grid_spec=pltpu.PrefetchScalarGridSpec...  78.5 us
    pallas_call x1, Pallas kernels, attend(): pl.pallas_call(attend_kernel, grid_spec=pltpu.PrefetchScalarGridSpec(num_...  61.8 us
  transfers between devices with their start and end apart: 79, of which 30 were waited for; matrix products, arithmetic and copies ran while one was open for 30% of the time, Pallas kernels for 15%

profile of v1, /device:TPU:1, one launch (start us, length us, event | category | flops | bytes accessed | tf_op | source)
XLA Modules:
  0.0 1613.9 jit_solution(9076740463510412846)
XLA Ops:
  41.0 9.5 collective-permute-done.5
  58.8 14.8 collective-permute-done.6
  100.2 20.0 %collective-permute-done.7 = bf16[4,2,1024,128]{2,3,1,0:T(8,128)(2,1)} collective-permute-done((bf16[4,2,1024,128]{2,3,1,0:T(8,128)(2,1)}, bf16[4,2,1024,128]{2,3,1,0:T(8,128)(2,1)}, u32[]{:S(2)}, u32[]{:S(2)}) %collective-permute-start.7) | collective-permute-done | bytes 2097184 | tf_op jit(solution)/shard_map/ppermute | solution.py:542
  125.1 8.6 copy.67.weight_ref
  134.9 15.4 shard_map.466
  161.2 11.0 collective-permute-done.17
  172.2 11.6 collective-permute-start.22
  188.0 19.1 %collective-permute-done.10 = bf16[2,512,384]{2,1,0:T(8,128)(2,1)S(1)} collective-permute-done((bf16[2,512,384]{2,1,0:T(8,128)(2,1)S(1)}, bf16[2,512,384]{2,1,0:T(8,128)(2,1)S(1)}, u32[]{:S(2)}, u32[]{:S(2)}) %collective-permute-start.10) | collective-permute-done | bytes 786464 | tf_op jit(solution)/shard_map/ppermute | solution.py:542
  207.6 61.8 %shard_map.467 = (bf16[4,2,512,256]{3,2,1,0:T(8,128)(2,1)S(1)}, f32[4,2,8,512]{3,2,1,0:T(8,128)S(1)}) custom-call(s32[1]{0:T(128)} %bitcast.place_ref, s32[2]{0:T(128)S(1)} %pad_add_fusion.prefix_ref, bf16[4,2,512,384]{3,2,1,0:T(8,128)(2,1)S(1)} %pad_maximum_fusion.19.q_ref.kv_ref, bf16[4,2,512,384]{3,2,1,0:T(8,128)(2,1)S(1)} %pad_maximum_fusion.19.q_ref.kv_ref), custom_call_target="tpu_custom_call" | custom-call | flops 85899345920 | bytes 8388608 | tf_op jit(solution)/shard_map/pallas_call | solution.py:727
  284.6 27.6 %collective-permute-done.13 = bf16[2,512,256]{2,1,0:T(8,128)(2,1)S(1)} collective-permute-done((bf16[2,512,256]{2,1,0:T(8,128)(2,1)S(1)}, bf16[2,512,256]{2,1,0:T(8,128)(2,1)S(1)}, u32[]{:S(2)}, u32[]{:S(2)}) %collective-permute-start.13) | collective-permute-done | bytes 524320 | tf_op jit(solution)/shard_map/ppermute | solution.py:542
  313.2 5.9 fusion.40
  320.9 14.3 collective-permute-start.19
  340.6 8.4 pad_maximum_fusion.9
  350.1 9.0 collective-permute-done.35
  367.6 15.2 collective-permute-done.29
  382.8 6.1 pad_maximum_fusion.11
  404.0 36.6 %collective-permute-done.20 = bf16[512,2048]{1,0:T(8,128)(2,1)} collective-permute-done((bf16[512,2048]{1,0:T(8,128)(2,1)S(1)}, bf16[512,2048]{1,0:T(8,128)(2,1)}, u32[]{:S(2)}, u32[]{:S(2)}) %collective-permute-start.20) | collective-permute-done | bytes 2097184 | tf_op jit(solution)/shard_map/ppermute | solution.py:542
  444.7 6.1 collective-permute-start.21
  450.9 25.5 %collective-permute-done.24 = bf16[2048,1024]{1,0:T(8,128)(2,1)} collective-permute-done((bf16[2048,1024]{1,0:T(8,128)(2,1)S(1)}, bf16[2048,1024]{1,0:T(8,128)(2,1)}, u32[]{:S(2)}, u32[]{:S(2)}) %collective-permute-start.24) | collective-permute-done | bytes 4194336 | tf_op jit(solution)/shard_map/ppermute | solution.py:542
  476.4 21.8 %pad_maximum_fusion.46.clone.5 = bf16[2048,2048]{1,0:T(8,128)(2,1)} fusion(bf16[2048,1024]{1,0:T(8,128)(2,1)} %collective-permute-done.24, bf16[1024,1024]{1,0:T(8,128)(2,1)S(1)} %collective-permute-done.23, bf16[1024,512]{1,0:T(8,128)(2,1)S(1)} %collective-permute-done.22, bf16[1024,512]{1,0:T(8,128)(2,1)S(1)} %copy-done.27), kind=kLoop, calls=%fused_computation.17.clone.1.clone.clone.clone.2 | loop fusion | flops 33554432 | bytes 16777216 | tf_op jit(solution)/shard_map/convert_element_type | solution.py:1164
  498.2 68.1 %collective-permute-done.30 = bf16[1024,2048]{1,0:T(8,128)(2,1)} collective-permute-done((bf16[1024,2048]{1,0:T(8,128)(2,1)S(1)}, bf16[1024,2048]{1,0:T(8,128)(2,1)}, u32[]{:S(2)}, u32[]{:S(2)}) %collective-permute-start.30) | collective-permute-done | bytes 4194336 | tf_op jit(solution)/shard_map/ppermute | solution.py:542
  566.3 28.4 %fusion.21 = f32[2048,2048]{1,0:T(8,128)} fusion(bf16[1024,2048]{1,0:T(8,128)(2,1)} %collective-permute-done.36, bf16[512,2048]{1,0:T(8,128)(2,1)} %copy-done.74, bf16[512,2048]{1,0:T(8,128)(2,1)} %copy-done.50, bf16[1024,2048]{1,0:T(8,128)(2,1)} %collective-permute-done.30, bf16[1024,1024]{1,0:T(8,128)(2,1)} %collective-permute-done.29, ...), kind=kOutput, calls=%fused_computation.80 | convolution fusion | flops 17238589440 | bytes 33554432 | tf_op jit(solution)/shard_map/dot_general | solution.py:42
  594.7 26.2 %fusion.32 = f32[2048,2048]{1,0:T(8,128)} fusion(bf16[1024,2048]{1,0:T(8,128)(2,1)} %collective-permute-done.27, bf16[1024,1024]{1,0:T(8,128)(2,1)} %collective-permute-done.26, bf16[1024,512]{1,0:T(8,128)(2,1)} %copy-done.63, bf16[1024,512]{1,0:T(8,128)(2,1)} %dynamic-slice_convert_fusion.1, bf16[1024,2048]{1,0:T(8,128)(2,1)} %collective-permute-done.21, ...), kind=kOutput, calls=%fused_computation.136 | convolution fusion | flops 17238589440 | bytes 33554432 | tf_op jit(solution)/shard_map/dot_general | solution.py:32
  620.9 36.2 %multiply_convert_fusion.1 = (bf16[2048,2048]{1,0:T(8,128)(2,1)}, bf16[2048,2048]{1,0:T(8,128)(2,1)}, bf16[2048,2048]{1,0:T(8,128)(2,1)}) fusion(f32[2048,2048]{1,0:T(8,128)} %fusion.21, f32[2048,2048]{1,0:T(8,128)} %fusion.32, bf16[1024,2048]{1,0:T(8,128)(2,1)} %collective-permute-done.21, bf16[512,2048]{1,0:T(8,128)(2,1)} %collective-permute-done.20, ...), kind=kOutput, calls=%fused_computation.1 | convolution fusion | flops 17267949568 | bytes 75497472 | tf_op jit(solution)/shard_map/dot_general | solution.py:32
  657.1 23.3 %fusion.30 = f32[2048,2048]{1,0:T(8,128)S(1)} fusion(bf16[2048,2048]{1,0:T(8,128)(2,1)} %get-tuple-element.98, bf16[1024,2048]{1,0:T(8,128)(2,1)} %collective-permute-done.30, bf16[1024,1024]{1,0:T(8,128)(2,1)} %collective-permute-done.29, bf16[512,1024]{1,0:T(8,128)(2,1)} %collective-permute-done.28, bf16[512,1024]{1,0:T(8,128)(2,1)} %copy-done.43), kind=kOutput, calls=%fused_computation.134 | convolution fusion | flops 17213423616 | bytes 33554432 | tf_op jit(solution)/shard_map/dot_general | solution.py:32
  680.4 5.9 copy-done.38
  689.0 22.4 %fusion.20 = f32[2048,2048]{1,0:T(8,128)S(1)} fusion(bf16[2048,2048]{1,0:T(8,128)(2,1)} %get-tuple-element.98, bf16[1024,2048]{1,0:T(8,128)(2,1)} %collective-permute-done.36, bf16[512,2048]{1,0:T(8,128)(2,1)} %copy-done.74, bf16[512,2048]{1,0:T(8,128)(2,1)S(1)} %copy-done.51), kind=kOutput, calls=%fused_computation.79 | convolution fusion | flops 17205035008 | bytes 33554432 | tf_op jit(solution)/shard_map/dot_general | solution.py:36
  718.6 27.0 %fusion.31 = f32[2048,2048]{1,0:T(8,128)} fusion(bf16[2048,2048]{1,0:T(8,128)(2,1)} %get-tuple-element.97, bf16[1024,2048]{1,0:T(8,128)(2,1)} %collective-permute-done.27, bf16[1024,1024]{1,0:T(8,128)(2,1)} %collective-permute-done.26, bf16[1024,512]{1,0:T(8,128)(2,1)} %copy-done.63, bf16[1024,512]{1,0:T(8,128)(2,1)S(1)} %copy-done.40), kind=kOutput, calls=%fused_computation.135 | convolution fusion | flops 17213423616 | bytes 33554432 | tf_op jit(solution)/shard_map/dot_general | solution.py:42
  745.6 36.2 %convolution_add_fusion = f32[2048,2048]{1,0:T(8,128)} fusion(f32[2048,2048]{1,0:T(8,128)} %fusion.31, bf16[2048,2048]{1,0:T(8,128)(2,1)} %get-tuple-element.96, bf16[2048,1024]{1,0:T(8,128)(2,1)} %collective-permute-done.24, bf16[1024,1024]{1,0:T(8,128)(2,1)S(1)} %copy-done.56, bf16[1024,512]{1,0:T(8,128)(2,1)S(1)} %copy-done.42, ...), kind=kOutput, calls=%fused_computation.5 | convolution fusion | flops 17217617920 | bytes 50331648 | tf_op jit(solution)/shard_map/dot_general | solution.py:42
  781.8 6.2 slice.610
  788.9 22.6 %fusion.62 = f32[2048,2048]{1,0:T(8,128)S(1)} fusion(bf16[2048,2048]{1,0:T(8,128)(2,1)} %get-tuple-element.96, bf16[1024,2048]{1,0:T(8,128)(2,1)} %collective-permute-done.21, bf16[512,2048]{1,0:T(8,128)(2,1)} %collective-permute-done.20, bf16[512,2048]{1,0:T(8,128)(2,1)S(1)} %copy-done.49), kind=kOutput, calls=%fused_computation.251 | convolution fusion | flops 17205035008 | bytes 33554432 | tf_op jit(solution)/shard_map/dot_general | solution.py:36
  836.3 26.2 %fusion.61 = f32[2048,2048]{1,0:T(8,128)} fusion(bf16[2048,2048]{1,0:T(8,128)(2,1)} %get-tuple-element.97, bf16[1024,2048]{1,0:T(8,128)(2,1)} %collective-permute-done.21, bf16[512,2048]{1,0:T(8,128)(2,1)} %collective-permute-done.20, bf16[512,2048]{1,0:T(8,128)(2,1)S(1)} %copy-done.49), kind=kOutput, calls=%fused_computation.250 | convolution fusion | flops 17205035008 | bytes 33554432 | tf_op jit(solution)/shard_map/dot_general | solution.py:36
  862.4 6.1 slice.608
  869.2 49.7 %collective-permute-done.38 = bf16[512,2048]{1,0:T(8,128)(2,1)} collective-permute-done((bf16[512,2048]{1,0:T(8,128)(2,1)}, bf16[512,2048]{1,0:T(8,128)(2,1)}, u32[]{:S(2)}, u32[]{:S(2)}) %collective-permute-start.38) | collective-permute-done | bytes 2097184 | tf_op jit(solution)/shard_map/ppermute | solution.py:542
  918.9 5.9 multiply_reduce_fusion
  924.8 8.3 multiply_convert_fusion.3
  934.0 5.9 slice_add_fusion
  943.9 5.9 slice_add_fusion.2
  953.9 7.2 collective-permute-done.60
  973.4 7.3 fusion.29
  985.2 8.0 fusion.72
  1002.7 14.5 collective-permute-done.58
  1030.0 78.5 %shard_map.468 = bf16[4,2,512,384]{3,2,1,0:T(8,128)(2,1)} custom-call(s32[1]{0:T(128)} %bitcast.place_ref, s32[2]{0:T(128)S(1)} %copy-done.14, bf16[4,2,512,384]{3,2,1,0:T(8,128)(2,1)} %copy-done.5, bf16[4,2,512,384]{3,2,1,0:T(8,128)(2,1)} %copy-done.5, bf16[4,2,512,256]{3,2,1,0:T(8,128)(2,1)S(1)} %copy-done.8, ...), custom_call_target="tpu_custom_call" | custom-call | flops 214748364800 | bytes 16777216 | tf_op jit(solution)/shard_map/pallas_call | solution.py:844
  1118.6 6.2 collective-permute-start.59
  1127.2 25.0 %collective-permute-done.45 = bf16[2,512,384]{2,1,0:T(8,128)(2,1)S(1)} collective-permute-done((bf16[2,512,384]{2,1,0:T(8,128)(2,1)S(1)}, bf16[2,512,384]{2,1,0:T(8,128)(2,1)S(1)}, u32[]{:S(2)}, u32[]{:S(2)}) %collective-permute-start.45) | collective-permute-done | bytes 786464 | tf_op jit(solution)/shard_map/ppermute | solution.py:572
  1154.0 14.5 collective-permute-done.44
  1168.5 7.4 collective-permute-start.77
  1176.9 13.7 fusion.77
  1196.2 24.1 %collective-permute-done.62 = bf16[1024,512]{1,0:T(8,128)(2,1)S(1)} collective-permute-done((bf16[1024,512]{1,0:T(8,128)(2,1)}, bf16[1024,512]{1,0:T(8,128)(2,1)S(1)}, u32[]{:S(2)}, u32[]{:S(2)}) %collective-permute-start.62) | collective-permute-done | bytes 1048608 | tf_op jit(solution)/shard_map/ppermute | solution.py:542
  1225.9 9.6 fusion.78
  1248.7 12.0 collective-permute-done.49
  1266.9 8.4 fusion.35
  1275.7 30.0 %collective-permute-done.53 = bf16[1024,1024]{1,0:T(8,128)(2,1)} collective-permute-done((bf16[1024,1024]{1,0:T(8,128)(2,1)}, bf16[1024,1024]{1,0:T(8,128)(2,1)}, u32[]{:S(2)}, u32[]{:S(2)}) %collective-permute-start.53) | collective-permute-done | bytes 2097184 | tf_op jit(solution)/shard_map/ppermute | solution.py:542
  1326.6 22.9 %collective-permute-done.54 = bf16[512,1024]{1,0:T(8,128)(2,1)S(1)} collective-permute-done((bf16[512,1024]{1,0:T(8,128)(2,1)S(1)}, bf16[512,1024]{1,0:T(8,128)(2,1)S(1)}, u32[]{:S(2)}, u32[]{:S(2)}) %collective-permute-start.54) | collective-permute-done | bytes 1048608 | tf_op jit(solution)/shard_map/ppermute | solution.py:542
  1350.4 19.8 %collective-permute-done.51 = bf16[1024,384]{1,0:T(8,128)(2,1)S(1)} collective-permute-done((bf16[1024,384]{1,0:T(8,128)(2,1)S(1)}, bf16[1024,384]{1,0:T(8,128)(2,1)S(1)}, u32[]{:S(2)}, u32[]{:S(2)}) %collective-permute-start.51) | collective-permute-done | bytes 786464 | tf_op jit(solution)/shard_map/ppermute | solution.py:542
  1373.5 7.9 collective-permute-done.55
  1391.1 6.7 collective-permute-done.68
  1400.5 12.1 collective-permute-done.48
  1412.6 31.4 %psum.14 = f32[2,1024]{1,0:T(2,128)S(1)} all-reduce(f32[2,1024]{1,0:T(2,128)S(1)} %fusion.46), channel_id=1, replica_groups=mesh['dp'=4,'row'=2,'col'=4] {'dp','col'}, use_global_device_ids=true, to_apply=%region_6.7 | all-reduce | flops 2048 | bytes 16384 | tf_op jit(solution)/shard_map/psum | solution.py:1255
  1467.5 37.3 %psum.15 = f32[]{:T(128)} all-reduce(f32[]{:T(128)S(6)} %add.306), channel_id=1, replica_groups=mesh['dp'=4,'row'=2,'col'=4] {'dp','row','col'}, use_global_device_ids=true, to_apply=%region_14.15 | all-reduce | flops 1 | bytes 8 | tf_op jit(solution)/shard_map/psum | solution.py:1265
  1514.6 25.3 %shard_map.474 = (f32[2048,1024]{1,0:T(8,128)}, f32[2048,1024]{1,0:T(8,128)}, f32[2048,1024]{1,0:T(8,128)}) custom-call(s32[1]{0:T(128)} %bitcast.54.spot_ref, f32[1,1]{1,0:T(1,128)} %bitcast.57.factor_ref, bf16[4,512,1024]{2,1,0:T(8,128)(2,1)S(1)} %copy-done.1, f32[2048,1024]{1,0:T(8,128)} %weight_ref.9, f32[2048,1024]{1,0:T(8,128)} %moment_ref.9, ...), custom_call_target="tpu_custom_call" | custom-call | flops 25165824 | bytes 54525952 | tf_op jit(solution)/shard_map/pallas_call | solution.py:904
  1540.0 25.3 %shard_map.473 = (f32[1024,2048]{1,0:T(8,128)}, f32[1024,2048]{1,0:T(8,128)}, f32[1024,2048]{1,0:T(8,128)}) custom-call(s32[1]{0:T(128)} %bitcast.54.spot_ref, f32[1,1]{1,0:T(1,128)} %bitcast.57.factor_ref, bf16[4,1024,512]{2,1,0:T(8,128)(2,1)S(1)} %copy-done.2, f32[1024,2048]{1,0:T(8,128)} %weight_ref.8, f32[1024,2048]{1,0:T(8,128)} %moment_ref.8, ...), custom_call_target="tpu_custom_call" | custom-call | flops 25165824 | bytes 54525952 | tf_op jit(solution)/shard_map/pallas_call | solution.py:904
  1565.4 25.5 %shard_map.472 = (f32[1024,2048]{1,0:T(8,128)}, f32[1024,2048]{1,0:T(8,128)}, f32[1024,2048]{1,0:T(8,128)}) custom-call(s32[1]{0:T(128)} %bitcast.54.spot_ref, f32[1,1]{1,0:T(1,128)} %bitcast.57.factor_ref, bf16[4,1024,512]{2,1,0:T(8,128)(2,1)S(1)} %copy-done, f32[1024,2048]{1,0:T(8,128)} %weight_ref.7, f32[1024,2048]{1,0:T(8,128)} %moment_ref.7, ...), custom_call_target="tpu_custom_call" | custom-call | flops 25165824 | bytes 54525952 | tf_op jit(solution)/shard_map/pallas_call | solution.py:904
  1600.1 12.4 shard_map.470
  (510 shorter events, 353.3 us)
Async XLA Ops:
  0.7 151.4 %collective-permute-start.1 = (s32[2]{0:T(128)}, s32[2]{0:T(128)}, u32[]{:S(2)}, u32[]{:S(2)}) collective-permute-start(s32[2]{0:T(128)} %param.29), channel_id=1, source_target_pairs={{0,8},{8,0},{16,24},{24,16},{1,9},{9,1},{17,25},{25,17},{2,10},{10... | collective-permute-start | bytes 32 | tf_op jit(solution)/shard_map/ppermute | solution.py:542
  0.8 39.0 %collective-permute-start.2 = (f32[2,1024]{1,0:T(2,128)}, f32[2,1024]{1,0:T(2,128)S(1)}, u32[]{:S(2)}, u32[]{:S(2)}) collective-permute-start(f32[2,1024]{1,0:T(2,128)} %param.37), channel_id=1, source_target_pairs={{0,4},{4,0},{1,5},{5,1},{2,6},{6,2},{3,7},{7,3},{8,12},{12,8},{9,1... | collective-permute-start | bytes 24584 | tf_op jit(solution)/shard_map/ppermute | solution.py:542
  5.2 70.7 %collective-permute-start.15 = (bf16[128,1024]{1,0:T(8,128)(2,1)}, bf16[128,1024]{1,0:T(8,128)(2,1)}, u32[]{:S(2)}, u32[]{:S(2)}) collective-permute-start(bf16[128,1024]{1,0:T(8,128)(2,1)} %dynamic-slice_convert_fusion.3), channel_id=1, source_target_pairs={{0,2},{1,3},{2,0},{3,1},{4,6},{5,7},{6,4},{7,5},{8,10},{9,11},{10,... | collective-permute-start | bytes 786440 | tf_op jit(solution)/shard_map/ppermute | solution.py:542
  12.4 39.4 %collective-permute-start = (bf16[512,1024]{1,0:T(8,128)(2,1)}, bf16[512,1024]{1,0:T(8,128)(2,1)}, u32[]{:S(2)}, u32[]{:S(2)}) collective-permute-start(bf16[512,1024]{1,0:T(8,128)(2,1)} %get-tuple-element.142), channel_id=1, source_target_pairs={{0,4},{4,0},{1,5},{5,1},{2,6},{6,2},{3,7},{7,3},{8,12},{12,8},{9,1... | collective-permute-start | bytes 3145736 | tf_op jit(solution)/shard_map/ppermute | solution.py:542
  39.8 52.8 %collective-permute-start.8 = (bf16[4,1024,128]{1,2,0:T(8,128)(2,1)}, bf16[4,1024,128]{1,2,0:T(8,128)(2,1)}, u32[]{:S(2)}, u32[]{:S(2)}) collective-permute-start(bf16[4,1024,128]{1,2,0:T(8,128)(2,1)} %pad_maximum_fusion.48), channel_id=1, source_target_pairs={{0,4},{4,0},{1,5},{5,1},{2,6},{6,2},{3,7},{7,3},{8,12},{12,8},{9,1... | collective-permute-start | bytes 3145736 | tf_op jit(solution)/shard_map/ppermute | solution.py:542
  56.6 38.6 %collective-permute-start.3 = (bf16[512,2048]{1,0:T(8,128)(2,1)}, bf16[512,2048]{1,0:T(8,128)(2,1)}, u32[]{:S(2)}, u32[]{:S(2)}) collective-permute-start(bf16[512,2048]{1,0:T(8,128)(2,1)} %fusion.6), channel_id=1, source_target_pairs={{0,8},{8,0},{16,24},{24,16},{1,9},{9,1},{17,25},{25,17},{2,10},{10... | collective-permute-start | bytes 6291464 | tf_op jit(solution)/shard_map/ppermute | solution.py:542
  75.4 44.8 %collective-permute-start.7 = (bf16[4,2,1024,128]{2,3,1,0:T(8,128)(2,1)}, bf16[4,2,1024,128]{2,3,1,0:T(8,128)(2,1)}, u32[]{:S(2)}, u32[]{:S(2)}) collective-permute-start(bf16[4,2,1024,128]{2,3,1,0:T(8,128)(2,1)} %fusion.25), channel_id=1, source_target_pairs={{0,4},{4,0},{1,5},{5,1},{2,6},{6,2},{3,7},{7,3},{8,12},{12,8},{9,1... | collective-permute-start | bytes 6291464 | tf_op jit(solution)/shard_map/ppermute | solution.py:542
  89.2 68.5 %collective-permute-start.34 = (bf16[512,1024]{1,0:T(8,128)(2,1)}, bf16[512,1024]{1,0:T(8,128)(2,1)}, u32[]{:S(2)}, u32[]{:S(2)}) collective-permute-start(bf16[512,1024]{1,0:T(8,128)(2,1)} %get-tuple-element.125), channel_id=1, source_target_pairs={{0,4},{4,0},{1,5},{5,1},{2,6},{6,2},{3,7},{7,3},{8,12},{12,8},{9,1... | collective-permute-start | bytes 3145736 | tf_op jit(solution)/shard_map/ppermute | solution.py:542
  92.7 79.5 %collective-permute-start.17 = (bf16[4,128,1024]{2,1,0:T(8,128)(2,1)}, bf16[4,128,1024]{2,1,0:T(8,128)(2,1)}, u32[]{:S(2)}, u32[]{:S(2)}) collective-permute-start(bf16[4,128,1024]{2,1,0:T(8,128)(2,1)} %pad_maximum_fusion.51), channel_id=1, source_target_pairs={{0,4},{4,0},{1,5},{5,1},{2,6},{6,2},{3,7},{7,3},{8,12},{12,8},{9,1... | collective-permute-start | bytes 3145736 | tf_op jit(solution)/shard_map/ppermute | solution.py:542
  150.6 37.0 %collective-permute-start.11 = (bf16[2,512,384]{2,1,0:T(8,128)(2,1)S(1)}, bf16[2,512,384]{2,1,0:T(8,128)(2,1)S(1)}, u32[]{:S(2)}, u32[]{:S(2)}) collective-permute-start(bf16[2,512,384]{2,1,0:T(8,128)(2,1)S(1)} %get-tuple-element.117), channel_id=1, source_target_pairs={{0,5},{1,4},{2,7},{3,6},{4,1},{5,0},{6,3},{7,2},{8,13},{9,12},{10,... | collective-permute-start | bytes 2359304 | tf_op jit(solution)/shard_map/ppermute | solution.py:572
  151.9 55.1 %collective-permute-start.10 = (bf16[2,512,384]{2,1,0:T(8,128)(2,1)S(1)}, bf16[2,512,384]{2,1,0:T(8,128)(2,1)S(1)}, u32[]{:S(2)}, u32[]{:S(2)}) collective-permute-start(bf16[2,512,384]{2,1,0:T(8,128)(2,1)S(1)} %get-tuple-element.118), channel_id=1, source_target_pairs={{0,1},{1,0},{2,3},{3,2},{4,5},{5,4},{6,7},{7,6},{8,9},{9,8},{10,11... | collective-permute-start | bytes 2359304 | tf_op jit(solution)/shard_map/ppermute | solution.py:542
  152.1 55.0 %collective-permute-start.9 = (bf16[2,512,384]{2,1,0:T(8,128)(2,1)S(1)}, bf16[2,512,384]{2,1,0:T(8,128)(2,1)S(1)}, u32[]{:S(2)}, u32[]{:S(2)}) collective-permute-start(bf16[2,512,384]{2,1,0:T(8,128)(2,1)S(1)} %get-tuple-element.119), channel_id=1, source_target_pairs={{0,4},{4,0},{1,5},{5,1},{2,6},{6,2},{3,7},{7,3},{8,12},{12,8},{9,1... | collective-permute-start | bytes 2359304 | tf_op jit(solution)/shard_map/ppermute | solution.py:542
  157.7 115.8 %collective-permute-start.28 = (bf16[512,1024]{1,0:T(8,128)(2,1)S(1)}, bf16[512,1024]{1,0:T(8,128)(2,1)}, u32[]{:S(2)}, u32[]{:S(2)}) collective-permute-start(bf16[512,1024]{1,0:T(8,128)(2,1)S(1)} %dynamic-slice_convert_fusion), channel_id=1, source_target_pairs={{0,2},{1,3},{2,0},{3,1},{4,6},{5,7},{6,4},{7,5},{8,10},{9,11},{10,... | collective-permute-start | bytes 3145736 | tf_op jit(solution)/shard_map/ppermute | solution.py:542
  172.2 101.1 %collective-permute-start.22 = (bf16[1024,512]{1,0:T(8,128)(2,1)S(1)}, bf16[1024,512]{1,0:T(8,128)(2,1)S(1)}, u32[]{:S(2)}, u32[]{:S(2)}) collective-permute-start(bf16[1024,512]{1,0:T(8,128)(2,1)S(1)} %copy-done.27), channel_id=1, source_target_pairs={{0,2},{1,3},{2,0},{3,1},{4,6},{5,7},{6,4},{7,5},{8,10},{9,11},{10,... | collective-permute-start | bytes 3145736 | tf_op jit(solution)/shard_map/ppermute | solution.py:542
  187.7 92.5 %collective-permute-start.18 = (bf16[4,128,2048]{2,1,0:T(8,128)(2,1)}, bf16[4,128,2048]{2,1,0:T(8,128)(2,1)}, u32[]{:S(2)}, u32[]{:S(2)}) collective-permute-start(bf16[4,128,2048]{2,1,0:T(8,128)(2,1)} %get-tuple-element.144), channel_id=1, source_target_pairs={{0,16},{8,24},{16,0},{24,8},{1,17},{9,25},{17,1},{25,9},{2,18},{10... | collective-permute-start | bytes 6291464 | tf_op jit(solution)/shard_map/ppermute | solution.py:542
  271.1 41.1 %collective-permute-start.13 = (bf16[2,512,256]{2,1,0:T(8,128)(2,1)S(1)}, bf16[2,512,256]{2,1,0:T(8,128)(2,1)S(1)}, u32[]{:S(2)}, u32[]{:S(2)}) collective-permute-start(bf16[2,512,256]{2,1,0:T(8,128)(2,1)S(1)} %get-tuple-element.128), channel_id=1, source_target_pairs={{0,1},{1,0},{2,3},{3,2},{4,5},{5,4},{6,7},{7,6},{8,9},{9,8},{10,11... | collective-permute-start | bytes 1572872 | tf_op jit(solution)/shard_map/ppermute | solution.py:542
  273.3 38.9 %collective-permute-start.12 = (bf16[2,512,256]{2,1,0:T(8,128)(2,1)S(1)}, bf16[2,512,256]{2,1,0:T(8,128)(2,1)S(1)}, u32[]{:S(2)}, u32[]{:S(2)}) collective-permute-start(bf16[2,512,256]{2,1,0:T(8,128)(2,1)S(1)} %get-tuple-element.129), channel_id=1, source_target_pairs={{0,4},{4,0},{1,5},{5,1},{2,6},{6,2},{3,7},{7,3},{8,12},{12,8},{9,1... | collective-permute-start | bytes 1572872 | tf_op jit(solution)/shard_map/ppermute | solution.py:542
  273.6 61.6 %collective-permute-start.25 = (bf16[1024,512]{1,0:T(8,128)(2,1)S(1)}, bf16[1024,512]{1,0:T(8,128)(2,1)S(1)}, u32[]{:S(2)}, u32[]{:S(2)}) collective-permute-start(bf16[1024,512]{1,0:T(8,128)(2,1)S(1)} %copy-done.39), channel_id=1, source_target_pairs={{0,2},{1,3},{2,0},{3,1},{4,6},{5,7},{6,4},{7,5},{8,10},{9,11},{10,... | collective-permute-start | bytes 3145736 | tf_op jit(solution)/shard_map/ppermute | solution.py:542
  280.1 60.5 %collective-permute-start.23 = (bf16[1024,1024]{1,0:T(8,128)(2,1)S(1)}, bf16[1024,1024]{1,0:T(8,128)(2,1)S(1)}, u32[]{:S(2)}, u32[]{:S(2)}) collective-permute-start(bf16[1024,1024]{1,0:T(8,128)(2,1)S(1)} %pad_maximum_fusion.27), channel_id=1, source_target_pairs={{0,4},{4,0},{1,5},{5,1},{2,6},{6,2},{3,7},{7,3},{8,12},{12,8},{9,1... | collective-permute-start | bytes 6291464 | tf_op jit(solution)/shard_map/ppermute | solution.py:542
  283.1 75.9 %collective-permute-start.35 = (bf16[512,2048]{1,0:T(8,128)(2,1)S(1)}, bf16[512,2048]{1,0:T(8,128)(2,1)S(1)}, u32[]{:S(2)}, u32[]{:S(2)}) collective-permute-start(bf16[512,2048]{1,0:T(8,128)(2,1)S(1)} %fusion.5), channel_id=1, source_target_pairs={{0,1},{1,0},{2,3},{3,2},{4,5},{5,4},{6,7},{7,6},{8,9},{9,8},{10,11... | collective-permute-start | bytes 6291464 | tf_op jit(solution)/shard_map/ppermute | solution.py:542
  312.2 70.6 %collective-permute-start.29 = (bf16[1024,1024]{1,0:T(8,128)(2,1)S(1)}, bf16[1024,1024]{1,0:T(8,128)(2,1)}, u32[]{:S(2)}, u32[]{:S(2)}) collective-permute-start(bf16[1024,1024]{1,0:T(8,128)(2,1)S(1)} %pad_maximum_fusion.29), channel_id=1, source_target_pairs={{0,4},{4,0},{1,5},{5,1},{2,6},{6,2},{3,7},{7,3},{8,12},{12,8},{9,1... | collective-permute-start | bytes 6291464 | tf_op jit(solution)/shard_map/ppermute | solution.py:542
  320.9 71.8 %collective-permute-start.19 = (bf16[512,2048]{1,0:T(8,128)(2,1)}, bf16[512,2048]{1,0:T(8,128)(2,1)}, u32[]{:S(2)}, u32[]{:S(2)}) collective-permute-start(bf16[512,2048]{1,0:T(8,128)(2,1)} %slice.618), channel_id=1, source_target_pairs={{0,8},{8,0},{16,24},{24,16},{1,9},{9,1},{17,25},{25,17},{2,10},{10... | collective-permute-start | bytes 6291464 | tf_op jit(solution)/shard_map/ppermute | solution.py:542
  336.9 63.1 %collective-permute-start.26 = (bf16[1024,1024]{1,0:T(8,128)(2,1)}, bf16[1024,1024]{1,0:T(8,128)(2,1)}, u32[]{:S(2)}, u32[]{:S(2)}) collective-permute-start(bf16[1024,1024]{1,0:T(8,128)(2,1)} %pad_maximum_fusion.28), channel_id=1, source_target_pairs={{0,16},{8,24},{16,0},{24,8},{1,17},{9,25},{17,1},{25,9},{2,18},{10... | collective-permute-start | bytes 6291464 | tf_op jit(solution)/shard_map/ppermute | solution.py:542
  349.0 127.4 %collective-permute-start.24 = (bf16[2048,1024]{1,0:T(8,128)(2,1)S(1)}, bf16[2048,1024]{1,0:T(8,128)(2,1)}, u32[]{:S(2)}, u32[]{:S(2)}) collective-permute-start(bf16[2048,1024]{1,0:T(8,128)(2,1)S(1)} %pad_maximum_fusion.9), channel_id=1, source_target_pairs={{0,16},{8,24},{16,0},{24,8},{1,17},{9,25},{17,1},{25,9},{2,18},{10... | collective-permute-start | bytes 12582920 | tf_op jit(solution)/shard_map/ppermute | solution.py:542
  361.7 136.4 %collective-permute-start.36 = (bf16[1024,2048]{1,0:T(8,128)(2,1)}, bf16[1024,2048]{1,0:T(8,128)(2,1)}, u32[]{:S(2)}, u32[]{:S(2)}) collective-permute-start(bf16[1024,2048]{1,0:T(8,128)(2,1)} %pad_maximum_fusion.12), channel_id=1, source_target_pairs={{0,8},{8,0},{16,24},{24,16},{1,9},{9,1},{17,25},{25,17},{2,10},{10... | collective-permute-start | bytes 12582920 | tf_op jit(solution)/shard_map/ppermute | solution.py:542
  388.9 177.4 %collective-permute-start.30 = (bf16[1024,2048]{1,0:T(8,128)(2,1)S(1)}, bf16[1024,2048]{1,0:T(8,128)(2,1)}, u32[]{:S(2)}, u32[]{:S(2)}) collective-permute-start(bf16[1024,2048]{1,0:T(8,128)(2,1)S(1)} %pad_maximum_fusion.11), channel_id=1, source_target_pairs={{0,16},{8,24},{16,0},{24,8},{1,17},{9,25},{17,1},{25,9},{2,18},{10... | collective-permute-start | bytes 12582920 | tf_op jit(solution)/shard_map/ppermute | solution.py:542
  397.4 43.2 %collective-permute-start.20 = (bf16[512,2048]{1,0:T(8,128)(2,1)S(1)}, bf16[512,2048]{1,0:T(8,128)(2,1)}, u32[]{:S(2)}, u32[]{:S(2)}) collective-permute-start(bf16[512,2048]{1,0:T(8,128)(2,1)S(1)} %multiply_convert_fusion.4), channel_id=1, source_target_pairs={{0,1},{1,0},{2,3},{3,2},{4,5},{5,4},{6,7},{7,6},{8,9},{9,8},{10,11... | collective-permute-start | bytes 6291464 | tf_op jit(solution)/shard_map/ppermute | solution.py:542
  403.5 191.2 %collective-permute-start.27 = (bf16[1024,2048]{1,0:T(8,128)(2,1)}, bf16[1024,2048]{1,0:T(8,128)(2,1)}, u32[]{:S(2)}, u32[]{:S(2)}) collective-permute-start(bf16[1024,2048]{1,0:T(8,128)(2,1)} %pad_maximum_fusion.10), channel_id=1, source_target_pairs={{0,4},{4,0},{1,5},{5,1},{2,6},{6,2},{3,7},{7,3},{8,12},{12,8},{9,1... | collective-permute-start | bytes 12582920 | tf_op jit(solution)/shard_map/ppermute | solution.py:542
  444.7 149.9 %collective-permute-start.21 = (bf16[1024,2048]{1,0:T(8,128)(2,1)}, bf16[1024,2048]{1,0:T(8,128)(2,1)}, u32[]{:S(2)}, u32[]{:S(2)}) collective-permute-start(bf16[1024,2048]{1,0:T(8,128)(2,1)} %pad_maximum_fusion.8), channel_id=1, source_target_pairs={{0,8},{8,0},{16,24},{24,16},{1,9},{9,1},{17,25},{25,17},{2,10},{10... | collective-permute-start | bytes 12582920 | tf_op jit(solution)/shard_map/ppermute | solution.py:542
  714.1 219.9 %collective-permute-start.63 = (bf16[2048,1024]{1,0:T(8,128)(2,1)}, bf16[2048,1024]{1,0:T(8,128)(2,1)}, u32[]{:S(2)}, u32[]{:S(2)}) collective-permute-start(bf16[2048,1024]{1,0:T(8,128)(2,1)} %slice.607), channel_id=1, source_target_pairs={{0,4},{4,0},{1,5},{5,1},{2,6},{6,2},{3,7},{7,3},{8,12},{12,8},{9,1... | collective-permute-start | bytes 12582920 | tf_op jit(solution)/shard_map/ppermute | solution.py:542
  714.7 103.9 %collective-permute-start.31 = (bf16[1024,2048]{1,0:T(8,128)(2,1)}, bf16[1024,2048]{1,0:T(8,128)(2,1)}, u32[]{:S(2)}, u32[]{:S(2)}) collective-permute-start(bf16[1024,2048]{1,0:T(8,128)(2,1)} %slice.611), channel_id=1, source_target_pairs={{0,8},{8,0},{16,24},{24,16},{1,9},{9,1},{17,25},{25,17},{2,10},{10... | collective-permute-start | bytes 12582920 | tf_op jit(solution)/shard_map/ppermute | solution.py:542
  788.0 40.6 %collective-permute-start.37 = (bf16[1024,2048]{1,0:T(8,128)(2,1)}, bf16[1024,2048]{1,0:T(8,128)(2,1)}, u32[]{:S(2)}, u32[]{:S(2)}) collective-permute-start(bf16[1024,2048]{1,0:T(8,128)(2,1)} %slice.610), channel_id=1, source_target_pairs={{0,8},{8,0},{16,24},{24,16},{1,9},{9,1},{17,25},{25,17},{2,10},{10... | collective-permute-start | bytes 12582920 | tf_op jit(solution)/shard_map/ppermute | solution.py:542
  814.6 129.3 %collective-permute-start.57 = (bf16[2048,1024]{1,0:T(8,128)(2,1)}, bf16[2048,1024]{1,0:T(8,128)(2,1)}, u32[]{:S(2)}, u32[]{:S(2)}) collective-permute-start(bf16[2048,1024]{1,0:T(8,128)(2,1)} %slice.609), channel_id=1, source_target_pairs={{0,16},{8,24},{16,0},{24,8},{1,17},{9,25},{17,1},{25,9},{2,18},{10... | collective-permute-start | bytes 12582920 | tf_op jit(solution)/shard_map/ppermute | solution.py:542
  826.4 98.4 %collective-permute-start.32 = (bf16[512,2048]{1,0:T(8,128)(2,1)}, bf16[512,2048]{1,0:T(8,128)(2,1)}, u32[]{:S(2)}, u32[]{:S(2)}) collective-permute-start(bf16[512,2048]{1,0:T(8,128)(2,1)} %slice.617), channel_id=1, source_target_pairs={{0,1},{1,0},{2,3},{3,2},{4,5},{5,4},{6,7},{7,6},{8,9},{9,8},{10,11... | collective-permute-start | bytes 6291464 | tf_op jit(solution)/shard_map/ppermute | solution.py:542
  836.3 82.6 %collective-permute-start.38 = (bf16[512,2048]{1,0:T(8,128)(2,1)}, bf16[512,2048]{1,0:T(8,128)(2,1)}, u32[]{:S(2)}, u32[]{:S(2)}) collective-permute-start(bf16[512,2048]{1,0:T(8,128)(2,1)} %slice.616), channel_id=1, source_target_pairs={{0,1},{1,0},{2,3},{3,2},{4,5},{5,4},{6,7},{7,6},{8,9},{9,8},{10,11... | collective-permute-start | bytes 6291464 | tf_op jit(solution)/shard_map/ppermute | solution.py:542
  868.5 92.5 %collective-permute-start.60 = (bf16[1024,2048]{1,0:T(8,128)(2,1)}, bf16[1024,2048]{1,0:T(8,128)(2,1)}, u32[]{:S(2)}, u32[]{:S(2)}) collective-permute-start(bf16[1024,2048]{1,0:T(8,128)(2,1)} %slice.608), channel_id=1, source_target_pairs={{0,4},{4,0},{1,5},{5,1},{2,6},{6,2},{3,7},{7,3},{8,12},{12,8},{9,1... | collective-permute-start | bytes 12582920 | tf_op jit(solution)/shard_map/ppermute | solution.py:542
  933.1 40.3 %collective-permute-start.39 = (bf16[512,2048]{1,0:T(8,128)(2,1)S(1)}, bf16[512,2048]{1,0:T(8,128)(2,1)}, u32[]{:S(2)}, u32[]{:S(2)}) collective-permute-start(bf16[512,2048]{1,0:T(8,128)(2,1)S(1)} %get-tuple-element.92), channel_id=1, source_target_pairs={{0,8},{8,0},{16,24},{24,16},{1,9},{9,1},{17,25},{25,17},{2,10},{10... | collective-permute-start | bytes 6291464 | tf_op jit(solution)/shard_map/ppermute | solution.py:542
  941.8 52.5 %collective-permute-start.64 = (bf16[1024,1024]{1,0:T(8,128)(2,1)}, bf16[1024,1024]{1,0:T(8,128)(2,1)}, u32[]{:S(2)}, u32[]{:S(2)}) collective-permute-start(bf16[1024,1024]{1,0:T(8,128)(2,1)} %slice.612), channel_id=1, source_target_pairs={{0,16},{8,24},{16,0},{24,8},{1,17},{9,25},{17,1},{25,9},{2,18},{10... | collective-permute-start | bytes 6291464 | tf_op jit(solution)/shard_map/ppermute | solution.py:542
  951.7 65.5 %collective-permute-start.58 = (bf16[1024,1024]{1,0:T(8,128)(2,1)}, bf16[1024,1024]{1,0:T(8,128)(2,1)}, u32[]{:S(2)}, u32[]{:S(2)}) collective-permute-start(bf16[1024,1024]{1,0:T(8,128)(2,1)} %slice.614), channel_id=1, source_target_pairs={{0,4},{4,0},{1,5},{5,1},{2,6},{6,2},{3,7},{7,3},{8,12},{12,8},{9,1... | collective-permute-start | bytes 6291464 | tf_op jit(solution)/shard_map/ppermute | solution.py:542
  971.9 140.7 %collective-permute-start.61 = (bf16[1024,1024]{1,0:T(8,128)(2,1)}, bf16[1024,1024]{1,0:T(8,128)(2,1)}, u32[]{:S(2)}, u32[]{:S(2)}) collective-permute-start(bf16[1024,1024]{1,0:T(8,128)(2,1)} %slice.613), channel_id=1, source_target_pairs={{0,16},{8,24},{16,0},{24,8},{1,17},{9,25},{17,1},{25,9},{2,18},{10... | collective-permute-start | bytes 6291464 | tf_op jit(solution)/shard_map/ppermute | solution.py:542
  993.6 34.9 %collective-permute-start.40 = (bf16[2,512,256]{2,1,0:T(8,128)(2,1)S(1)}, bf16[2,512,256]{2,1,0:T(8,128)(2,1)S(1)}, u32[]{:S(2)}, u32[]{:S(2)}) collective-permute-start(bf16[2,512,256]{2,1,0:T(8,128)(2,1)S(1)} %bitcast.183), channel_id=1, source_target_pairs={{0,4},{4,0},{1,5},{5,1},{2,6},{6,2},{3,7},{7,3},{8,12},{12,8},{9,1... | collective-permute-start | bytes 1572872 | tf_op jit(solution)/shard_map/ppermute | solution.py:542
  1017.2 101.4 %collective-permute-start.65 = (bf16[512,1024]{1,0:T(8,128)(2,1)}, bf16[512,1024]{1,0:T(8,128)(2,1)}, u32[]{:S(2)}, u32[]{:S(2)}) collective-permute-start(bf16[512,1024]{1,0:T(8,128)(2,1)} %slice.620), channel_id=1, source_target_pairs={{0,2},{1,3},{2,0},{3,1},{4,6},{5,7},{6,4},{7,5},{8,10},{9,11},{10,... | collective-permute-start | bytes 3145736 | tf_op jit(solution)/shard_map/ppermute | solution.py:542
  1022.8 200.1 %collective-permute-start.33 = (bf16[512,1024]{1,0:T(8,128)(2,1)}, bf16[512,1024]{1,0:T(8,128)(2,1)}, u32[]{:S(2)}, u32[]{:S(2)}) collective-permute-start(bf16[512,1024]{1,0:T(8,128)(2,1)} %slice.426), channel_id=1, source_target_pairs={{0,4},{4,0},{1,5},{5,1},{2,6},{6,2},{3,7},{7,3},{8,12},{12,8},{9,1... | collective-permute-start | bytes 3145736 | tf_op jit(solution)/shard_map/ppermute | solution.py:542
  1110.7 41.4 %collective-permute-start.45 = (bf16[2,512,384]{2,1,0:T(8,128)(2,1)S(1)}, bf16[2,512,384]{2,1,0:T(8,128)(2,1)S(1)}, u32[]{:S(2)}, u32[]{:S(2)}) collective-permute-start(bf16[2,512,384]{2,1,0:T(8,128)(2,1)S(1)} %get-tuple-element.111), channel_id=1, source_target_pairs={{0,5},{1,4},{2,7},{3,6},{4,1},{5,0},{6,3},{7,2},{8,13},{9,12},{10,... | collective-permute-start | bytes 2359304 | tf_op jit(solution)/shard_map/ppermute | solution.py:572
  1110.8 57.7 %collective-permute-start.44 = (bf16[2,512,384]{2,1,0:T(8,128)(2,1)S(1)}, bf16[2,512,384]{2,1,0:T(8,128)(2,1)S(1)}, u32[]{:S(2)}, u32[]{:S(2)}) collective-permute-start(bf16[2,512,384]{2,1,0:T(8,128)(2,1)S(1)} %get-tuple-element.112), channel_id=1, source_target_pairs={{0,1},{1,0},{2,3},{3,2},{4,5},{5,4},{6,7},{7,6},{8,9},{9,8},{10,11... | collective-permute-start | bytes 2359304 | tf_op jit(solution)/shard_map/ppermute | solution.py:542
  1112.6 63.4 %collective-permute-start.43 = (bf16[2,512,384]{2,1,0:T(8,128)(2,1)S(1)}, bf16[2,512,384]{2,1,0:T(8,128)(2,1)S(1)}, u32[]{:S(2)}, u32[]{:S(2)}) collective-permute-start(bf16[2,512,384]{2,1,0:T(8,128)(2,1)S(1)} %get-tuple-element.113), channel_id=1, source_target_pairs={{0,4},{4,0},{1,5},{5,1},{2,6},{6,2},{3,7},{7,3},{8,12},{12,8},{9,1... | collective-permute-start | bytes 2359304 | tf_op jit(solution)/shard_map/ppermute | solution.py:542
  1118.6 75.6 %collective-permute-start.59 = (bf16[1024,512]{1,0:T(8,128)(2,1)S(1)}, bf16[1024,512]{1,0:T(8,128)(2,1)S(1)}, u32[]{:S(2)}, u32[]{:S(2)}) collective-permute-start(bf16[1024,512]{1,0:T(8,128)(2,1)S(1)} %copy-done.86), channel_id=1, source_target_pairs={{0,2},{1,3},{2,0},{3,1},{4,6},{5,7},{6,4},{7,5},{8,10},{9,11},{10,... | collective-permute-start | bytes 3145736 | tf_op jit(solution)/shard_map/ppermute | solution.py:542
  1152.2 68.2 %collective-permute-start.62 = (bf16[1024,512]{1,0:T(8,128)(2,1)}, bf16[1024,512]{1,0:T(8,128)(2,1)S(1)}, u32[]{:S(2)}, u32[]{:S(2)}) collective-permute-start(bf16[1024,512]{1,0:T(8,128)(2,1)} %slice.621), channel_id=1, source_target_pairs={{0,2},{1,3},{2,0},{3,1},{4,6},{5,7},{6,4},{7,5},{8,10},{9,11},{10,... | collective-permute-start | bytes 3145736 | tf_op jit(solution)/shard_map/ppermute | solution.py:542
  1168.5 69.2 %collective-permute-start.77 = (bf16[512,1024]{1,0:T(8,128)(2,1)S(1)}, bf16[512,1024]{1,0:T(8,128)(2,1)S(1)}, u32[]{:S(2)}, u32[]{:S(2)}) collective-permute-start(bf16[512,1024]{1,0:T(8,128)(2,1)S(1)} %get-tuple-element.81), channel_id=1, source_target_pairs={{0,16},{8,24},{16,0},{24,8},{1,17},{9,25},{17,1},{25,9},{2,18},{10... | collective-permute-start | bytes 3145736 | tf_op jit(solution)/shard_map/ppermute | solution.py:542
  1193.3 67.5 %collective-permute-start.49 = (bf16[1024,1536]{1,0:T(8,128)(2,1)S(1)}, bf16[1024,1536]{1,0:T(8,128)(2,1)}, u32[]{:S(2)}, u32[]{:S(2)}) collective-permute-start(bf16[1024,1536]{1,0:T(8,128)(2,1)S(1)} %pad_maximum_fusion.21), channel_id=1, source_target_pairs={{0,4},{4,0},{1,5},{5,1},{2,6},{6,2},{3,7},{7,3},{8,12},{12,8},{9,1... | collective-permute-start | bytes 9437192 | tf_op jit(solution)/shard_map/ppermute | solution.py:542
  1196.2 44.3 %collective-permute-start.73 = (bf16[1024,512]{1,0:T(8,128)(2,1)S(1)}, bf16[1024,512]{1,0:T(8,128)(2,1)S(1)}, u32[]{:S(2)}, u32[]{:S(2)}) collective-permute-start(bf16[1024,512]{1,0:T(8,128)(2,1)S(1)} %get-tuple-element.85), channel_id=1, source_target_pairs={{0,16},{8,24},{16,0},{24,8},{1,17},{9,25},{17,1},{25,9},{2,18},{10... | collective-permute-start | bytes 3145736 | tf_op jit(solution)/shard_map/ppermute | solution.py:542
  1237.1 68.5 %collective-permute-start.53 = (bf16[1024,1024]{1,0:T(8,128)(2,1)}, bf16[1024,1024]{1,0:T(8,128)(2,1)}, u32[]{:S(2)}, u32[]{:S(2)}) collective-permute-start(bf16[1024,1024]{1,0:T(8,128)(2,1)} %pad_maximum_fusion.34), channel_id=1, source_target_pairs={{0,4},{4,0},{1,5},{5,1},{2,6},{6,2},{3,7},{7,3},{8,12},{12,8},{9,1... | collective-permute-start | bytes 6291464 | tf_op jit(solution)/shard_map/ppermute | solution.py:542
  1239.4 73.3 %collective-permute-start.78 = (bf16[2,512,1024]{2,1,0:T(8,128)(2,1)}, bf16[2,512,1024]{2,1,0:T(8,128)(2,1)}, u32[]{:S(2)}, u32[]{:S(2)}) collective-permute-start(bf16[2,512,1024]{2,1,0:T(8,128)(2,1)} %pad_maximum_fusion.38), channel_id=1, source_target_pairs={{0,8},{8,0},{16,24},{24,16},{1,9},{9,1},{17,25},{25,17},{2,10},{10... | collective-permute-start | bytes 6291464 | tf_op jit(solution)/shard_map/ppermute | solution.py:542
  1242.1 74.3 %collective-permute-start.74 = (bf16[2,1024,512]{2,1,0:T(8,128)(2,1)}, bf16[2,1024,512]{2,1,0:T(8,128)(2,1)}, u32[]{:S(2)}, u32[]{:S(2)}) collective-permute-start(bf16[2,1024,512]{2,1,0:T(8,128)(2,1)} %pad_maximum_fusion.36), channel_id=1, source_target_pairs={{0,8},{8,0},{16,24},{24,16},{1,9},{9,1},{17,25},{25,17},{2,10},{10... | collective-permute-start | bytes 6291464 | tf_op jit(solution)/shard_map/ppermute | solution.py:542
  1247.5 75.7 %collective-permute-start.76 = (bf16[2,1024,512]{2,1,0:T(8,128)(2,1)}, bf16[2,1024,512]{2,1,0:T(8,128)(2,1)}, u32[]{:S(2)}, u32[]{:S(2)}) collective-permute-start(bf16[2,1024,512]{2,1,0:T(8,128)(2,1)} %pad_maximum_fusion.37), channel_id=1, source_target_pairs={{0,8},{8,0},{16,24},{24,16},{1,9},{9,1},{17,25},{25,17},{2,10},{10... | collective-permute-start | bytes 6291464 | tf_op jit(solution)/shard_map/ppermute | solution.py:542
  1266.9 53.0 %collective-permute-start.50 = (bf16[1024,768]{1,0:T(8,128)(2,1)}, bf16[1024,768]{1,0:T(8,128)(2,1)}, u32[]{:S(2)}, u32[]{:S(2)}) collective-permute-start(bf16[1024,768]{1,0:T(8,128)(2,1)} %slice.619), channel_id=1, source_target_pairs={{0,1},{1,0},{2,3},{3,2},{4,5},{5,4},{6,7},{7,6},{8,9},{9,8},{10,11... | collective-permute-start | bytes 4718600 | tf_op jit(solution)/shard_map/ppermute | solution.py:542
  1305.7 65.0 %collective-permute-start.46 = (bf16[512,2048]{1,0:T(8,128)(2,1)S(1)}, bf16[512,2048]{1,0:T(8,128)(2,1)S(1)}, u32[]{:S(2)}, u32[]{:S(2)}) collective-permute-start(bf16[512,2048]{1,0:T(8,128)(2,1)S(1)} %slice.615), channel_id=1, source_target_pairs={{0,8},{8,0},{16,24},{24,16},{1,9},{9,1},{17,25},{25,17},{2,10},{10... | collective-permute-start | bytes 6291464 | tf_op jit(solution)/shard_map/ppermute | solution.py:542
  1312.7 36.8 %collective-permute-start.54 = (bf16[512,1024]{1,0:T(8,128)(2,1)S(1)}, bf16[512,1024]{1,0:T(8,128)(2,1)S(1)}, u32[]{:S(2)}, u32[]{:S(2)}) collective-permute-start(bf16[512,1024]{1,0:T(8,128)(2,1)S(1)} %slice.623), channel_id=1, source_target_pairs={{0,1},{1,0},{2,3},{3,2},{4,5},{5,4},{6,7},{7,6},{8,9},{9,8},{10,11... | collective-permute-start | bytes 3145736 | tf_op jit(solution)/shard_map/ppermute | solution.py:542
  1322.0 48.3 %collective-permute-start.51 = (bf16[1024,384]{1,0:T(8,128)(2,1)S(1)}, bf16[1024,384]{1,0:T(8,128)(2,1)S(1)}, u32[]{:S(2)}, u32[]{:S(2)}) collective-permute-start(bf16[1024,384]{1,0:T(8,128)(2,1)S(1)} %select_convert_fusion), channel_id=1, source_target_pairs={{0,2},{1,3},{2,0},{3,1},{4,6},{5,7},{6,4},{7,5},{8,10},{9,11},{10,... | collective-permute-start | bytes 2359304 | tf_op jit(solution)/shard_map/ppermute | solution.py:542
  1389.5 63.4 %collective-permute-start.47 = (bf16[512,1024]{1,0:T(8,128)(2,1)}, bf16[512,1024]{1,0:T(8,128)(2,1)}, u32[]{:S(2)}, u32[]{:S(2)}) collective-permute-start(bf16[512,1024]{1,0:T(8,128)(2,1)} %slice.442), channel_id=1, source_target_pairs={{0,4},{4,0},{1,5},{5,1},{2,6},{6,2},{3,7},{7,3},{8,12},{12,8},{9,1... | collective-permute-start | bytes 3145736 | tf_op jit(solution)/shard_map/ppermute | solution.py:542
  1398.7 51.7 %collective-permute-start.69 = (bf16[2,1024,128]{2,1,0:T(8,128)(2,1)}, bf16[2,1024,128]{2,1,0:T(8,128)(2,1)}, u32[]{:S(2)}, u32[]{:S(2)}) collective-permute-start(bf16[2,1024,128]{2,1,0:T(8,128)(2,1)} %pad_maximum_fusion.60), channel_id=1, source_target_pairs={{0,1},{1,0},{2,3},{3,2},{4,5},{5,4},{6,7},{7,6},{8,9},{9,8},{10,11... | collective-permute-start | bytes 1572872 | tf_op jit(solution)/shard_map/ppermute | solution.py:542
  1400.1 45.2 %collective-permute-start.71 = (bf16[128,1024]{1,0:T(8,128)(2,1)}, bf16[128,1024]{1,0:T(8,128)(2,1)S(1)}, u32[]{:S(2)}, u32[]{:S(2)}) collective-permute-start(bf16[128,1024]{1,0:T(8,128)(2,1)} %get-tuple-element.87), channel_id=1, source_target_pairs={{0,16},{8,24},{16,0},{24,8},{1,17},{9,25},{17,1},{25,9},{2,18},{10... | collective-permute-start | bytes 786440 | tf_op jit(solution)/shard_map/ppermute | solution.py:542
  1452.6 145.9 %collective-permute-start.70 = (bf16[4,1024,128]{2,1,0:T(8,128)(2,1)}, bf16[4,1024,128]{2,1,0:T(8,128)(2,1)}, u32[]{:S(2)}, u32[]{:S(2)}) collective-permute-start(bf16[4,1024,128]{2,1,0:T(8,128)(2,1)} %pad_maximum_fusion.53), channel_id=1, source_target_pairs={{0,8},{8,0},{16,24},{24,16},{1,9},{9,1},{17,25},{25,17},{2,10},{10... | collective-permute-start | bytes 3145736 | tf_op jit(solution)/shard_map/ppermute | solution.py:542
  1459.9 131.6 %collective-permute-start.67 = (bf16[2,1024,128]{2,1,0:T(8,128)(2,1)}, bf16[2,1024,128]{2,1,0:T(8,128)(2,1)}, u32[]{:S(2)}, u32[]{:S(2)}) collective-permute-start(bf16[2,1024,128]{2,1,0:T(8,128)(2,1)} %pad_maximum_fusion.59), channel_id=1, source_target_pairs={{0,8},{8,0},{16,24},{24,16},{1,9},{9,1},{17,25},{25,17},{2,10},{10... | collective-permute-start | bytes 1572872 | tf_op jit(solution)/shard_map/ppermute | solution.py:542
  (136 other events, 3361.2 us)

commit v2 on v1

--- a/solution.py
+++ b/solution.py
@@ -572,6 +572,10 @@
     return lax.ppermute(values, ("row", "col"), pairs)
 
 
+def after(value, *others):
+    return lax.optimization_barrier((value,) + others)[0]
+
+
 def fold(kept, sent, move):
     return kept + move(sent.astype(LOW)).astype(WIDE)
 
@@ -610,8 +614,210 @@
     )
 
 
-def project_kernel(normed_ref, weight_ref, cosine_ref, sine_ref, out_ref):
-    product = jnp.dot(normed_ref[0], weight_ref[...], preferred_element_type=WIDE)
+WIDE_BLOCK = 512
+COST_SHARE = 1
+
+
+def one_buffer(shape, index_map):
+    return pl.BlockSpec(shape, index_map, pipeline_mode=pl.Buffered(1))
+
+
+def cost(flops, read, written):
+    return pl.CostEstimate(
+        flops=int(flops * COST_SHARE),
+        bytes_accessed=int(2 * (read + written) * COST_SHARE),
+        transcendentals=0,
+    )
+
+
+def mm(left_side, right_side):
+    return jnp.dot(left_side, right_side, preferred_element_type=WIDE)
+
+
+def both(refs, axis):
+    return jnp.concatenate([ref[...] for ref in refs], axis=axis)
+
+
+def flat(*blocks):
+    return [array for block in blocks for array in block]
+
+
+def both_of(refs, which, axis):
+    return jnp.concatenate([ref[which] for ref in refs], axis=axis)
+
+
+def hidden_kernel(normed_ref, *refs):
+    hidden_ref, gate_ref, up_ref = refs[4:]
+    half = normed_ref.shape[1] // 2
+    left, right = normed_ref[:, :half], normed_ref[:, half:]
+    gate = mm(left, both_of(refs[0:2], 0, 1)) + mm(right, both_of(refs[2:4], 0, 1))
+    up = mm(left, both_of(refs[0:2], 1, 1)) + mm(right, both_of(refs[2:4], 1, 1))
+    hidden_ref[...] = (gate * jax.nn.sigmoid(gate) * up).astype(LOW)
+    gate_ref[...] = gate.astype(LOW)
+    up_ref[...] = up.astype(LOW)
+
+
+def hidden_units(normed, pairs):
+    tokens, width = normed.shape
+    weights = flat(*pairs)
+    units = 2 * weights[0].shape[2]
+    block = WIDE_BLOCK
+    weight = one_buffer(weights[0].shape, lambda i: (0, 0, 0))
+    out = pl.BlockSpec((block, units), lambda i: (i, 0))
+    return pl.pallas_call(
+        hidden_kernel,
+        grid=(tokens // block,),
+        in_specs=[pl.BlockSpec((block, width), lambda i: (i, 0))] + [weight] * 4,
+        out_specs=[out] * 3,
+        out_shape=[jax.ShapeDtypeStruct((tokens, units), LOW)] * 3,
+        compiler_params=pltpu.CompilerParams(vmem_limit_bytes=VMEM_BYTES),
+        cost_estimate=cost(
+            4 * tokens * width * units, tokens * width + 2 * width * units, 3 * tokens * units
+        ),
+    )(normed, *weights)
+
+
+def down_kernel(h0, h1, *refs):
+    weights, outs = refs[:8], refs[8:]
+    half = weights[0].shape[1]
+    for at, out_ref in enumerate(outs):
+
+        @pl.when(pl.program_id(0) == at)
+        def _(out_ref=out_ref):
+            for side in range(2):
+                total = mm(h0[...], both(weights[2 * side : 2 * side + 2], 0))
+                total = total + mm(h1[...], both(weights[4 + 2 * side : 6 + 2 * side], 0))
+                out_ref[:, side * half : (side + 1) * half] = total.astype(LOW)
+
+
+def down_units(hidden, down):
+    tokens, units = hidden[0].shape
+    weights = flat(*down[0], *down[1])
+    half = weights[0].shape[1]
+    block = WIDE_BLOCK
+    weight = one_buffer(weights[0].shape, lambda i: (0, 0))
+    left = pl.BlockSpec((block, units), lambda i: (i, 0))
+    return pl.pallas_call(
+        down_kernel,
+        grid=(tokens // block,),
+        in_specs=[left] * 2 + [weight] * 8,
+        out_specs=[one_buffer((block, 2 * half), lambda i: (0, 0))] * (tokens // block),
+        out_shape=[jax.ShapeDtypeStruct((block, 2 * half), LOW)] * (tokens // block),
+        compiler_params=pltpu.CompilerParams(vmem_limit_bytes=VMEM_BYTES),
+        cost_estimate=cost(
+            8 * tokens * units * half, 2 * tokens * units + 4 * units * half, 2 * tokens * half
+        ),
+    )(*hidden, *weights)
+
+
+def hidden_back_kernel(grad_ref, d0, d1, d2, d3, gate_ref, up_ref, grad_gate_ref, grad_up_ref):
+    half = d0.shape[1]
+    part = dot_nt(grad_ref[:, :half], both((d0, d1), 0))
+    part = part + dot_nt(grad_ref[:, half:], both((d2, d3), 0))
+    gate = gate_ref[...].astype(WIDE)
+    up = up_ref[...].astype(WIDE)
+    sigmoid = jax.nn.sigmoid(gate)
+    grad_gate_ref[...] = (part * up * sigmoid * (1.0 + gate * (1.0 - sigmoid))).astype(LOW)
+    grad_up_ref[...] = (part * (gate * sigmoid)).astype(LOW)
+
+
+def hidden_back(grads, down, gate, up):
+    tokens, width = grads.shape
+    weights = flat(*down)
+    units = 2 * weights[0].shape[0]
+    block = WIDE_BLOCK
+    weight = one_buffer(weights[0].shape, lambda i: (0, 0))
+    row = pl.BlockSpec((block, units), lambda i: (i, 0))
+    return pl.pallas_call(
+        hidden_back_kernel,
+        grid=(tokens // block,),
+        in_specs=[pl.BlockSpec((block, width), lambda i: (i, 0))] + [weight] * 4 + [row] * 2,
+        out_specs=[row] * 2,
+        out_shape=[jax.ShapeDtypeStruct((tokens, units), LOW)] * 2,
+        compiler_params=pltpu.CompilerParams(vmem_limit_bytes=VMEM_BYTES),
+        cost_estimate=cost(
+            2 * tokens * width * units,
+            tokens * width + width * units + 2 * tokens * units,
+            2 * tokens * units,
+        ),
+    )(grads, *weights, gate, up)
+
+
+def normed_back_kernel(a0, a1, b0, b1, *refs):
+    weights, outs = refs[:8], refs[8:]
+    half = weights[0].shape[1]
+    for at, out_ref in enumerate(outs):
+
+        @pl.when(pl.program_id(0) == at)
+        def _(out_ref=out_ref):
+            for side in range(2):
+                total = jnp.zeros((a0.shape[0], half), WIDE)
+                for which, lefts in enumerate(((a0, b0), (a1, b1))):
+                    start = 4 * which + 2 * side
+                    for kind, left in enumerate(lefts):
+                        right = both_of(weights[start : start + 2], kind, 1)
+                        total = total + dot_nt(left[...], right)
+                out_ref[:, side * half : (side + 1) * half] = total.astype(LOW)
+
+
+def normed_back(grad_gate, grad_up, pairs):
+    tokens, units = grad_gate[0].shape
+    weights = flat(*pairs[0], *pairs[1])
+    half = weights[0].shape[1]
+    block = WIDE_BLOCK
+    weight = one_buffer(weights[0].shape, lambda i: (0, 0, 0))
+    left = pl.BlockSpec((block, units), lambda i: (i, 0))
+    return pl.pallas_call(
+        normed_back_kernel,
+        grid=(tokens // block,),
+        in_specs=[left] * 4 + [weight] * 8,
+        out_specs=[one_buffer((block, 2 * half), lambda i: (0, 0))] * (tokens // block),
+        out_shape=[jax.ShapeDtypeStruct((block, 2 * half), LOW)] * (tokens // block),
+        compiler_params=pltpu.CompilerParams(vmem_limit_bytes=VMEM_BYTES),
+        cost_estimate=cost(
+            16 * tokens * units * half, 4 * tokens * units + 8 * units * half, 2 * tokens * half
+        ),
+    )(*grad_gate, *grad_up, *weights)
+
+
+def weight_grad(lefts, place, rights, columns):
+    count, tokens, parts = len(rights), lefts[0].shape[0], len(lefts)
+    span = rights[0][0].shape[1]
+    block = WIDE_BLOCK
+
+    def kernel(*refs):
+        left_refs, out_ref = refs[:parts], refs[-1]
+        for at in range(count):
+            right_refs = refs[parts * (at + 1) : parts * (at + 2)]
+            total = dot_tn(left_refs[0][...], right_refs[0][...])
+            for left_ref, right_ref in zip(left_refs[1:], right_refs[1:]):
+                total = total + dot_tn(left_ref[...], right_ref[...])
+            out_ref[:, at * span : (at + 1) * span] = total.astype(LOW)
+
+    start = place * columns // block
+    return pl.pallas_call(
+        kernel,
+        grid=(columns // block,),
+        in_specs=[pl.BlockSpec((tokens, block), lambda i: (0, i + start))] * parts
+        + [one_buffer((tokens, span), lambda i: (0, 0))] * (count * parts),
+        out_specs=pl.BlockSpec((block, count * span), lambda i: (i, 0)),
+        out_shape=jax.ShapeDtypeStruct((columns, count * span), LOW),
+        compiler_params=pltpu.CompilerParams(vmem_limit_bytes=VMEM_BYTES),
+        cost_estimate=cost(
+            2 * count * parts * tokens * columns * span,
+            parts * tokens * (columns + count * span),
+            count * columns * span,
+        ),
+    )(*lefts, *[value for right in rights for value in right])
+
+
+def project_kernel(
+    normed_ref, own_ref, kv_ref, first_ref, second_ref, kv_other_ref, cosine_ref, sine_ref, out_ref
+):
+    half = own_ref.shape[1]
+    near_rows = jnp.concatenate([own_ref[0], kv_ref[0]], axis=1)
+    other_rows = jnp.concatenate([first_ref[0], second_ref[0], kv_other_ref[0]], axis=1)
+    product = mm(normed_ref[0, :, :half], near_rows) + mm(normed_ref[0, :, half:], other_rows)
     cosine = cosine_ref[0]
     sine = sine_ref[0]
     for tile in range(3):
@@ -624,27 +830,64 @@
         out_ref[0, 0, :, tile * LANES : (tile + 1) * LANES] = turned.astype(LOW)
 
 
-def project(normed_pair, weights, cosine, sine):
+def piece_specs(pieces):
+    return [pl.BlockSpec((1,) + piece.shape[1:], lambda j, i: (j, 0, 0)) for piece in pieces]
+
+
+def project(normed, pieces, cosine, sine):
+    groups = 4
+    wide = 3 * LANES
+    table = pl.BlockSpec((1, CHUNK, LANES), lambda j, i: (0, 0, 0))
+    return pl.pallas_call(
+        project_kernel,
+        grid=(groups, 2),
+        in_specs=[pl.BlockSpec((1, CHUNK, MODEL_WIDTH), lambda j, i: (i, 0, 0))]
+        + piece_specs(pieces)
+        + [table, table],
+        out_specs=pl.BlockSpec((1, 1, CHUNK, wide), lambda j, i: (j, i, 0, 0)),
+        out_shape=jax.ShapeDtypeStruct((groups, 2, CHUNK, wide), LOW),
+        compiler_params=pltpu.CompilerParams(vmem_limit_bytes=VMEM_BYTES),
+        cost_estimate=cost(
+            2 * CHUNK * MODEL_WIDTH * groups * wide, MODEL_WIDTH * (CHUNK + groups * wide), 0
+        ),
+    )(normed, *pieces, cosine, sine)
+
+
+def project_back_kernel(
+    grad_ref, own_ref, kv_ref, first_ref, second_ref, kv_other_ref, out_ref, acc
+):
+    group, tokens = pl.program_id(0), pl.program_id(1)
+    half = own_ref.shape[1]
+
+    @pl.when(group == 0)
+    def _():
+        acc[tokens] = jnp.zeros(acc.shape[1:], WIDE)
+
+    near_rows = jnp.concatenate([own_ref[0], kv_ref[0]], axis=1)
+    other_rows = jnp.concatenate([first_ref[0], second_ref[0], kv_other_ref[0]], axis=1)
+    acc[tokens, :, :half] += dot_nt(grad_ref[0], near_rows)
+    acc[tokens, :, half:] += dot_nt(grad_ref[0], other_rows)
+
+    @pl.when(group == pl.num_programs(0) - 1)
+    def _():
+        out_ref[tokens] = acc[tokens].astype(LOW)
+
+
+def project_back(grads, pieces):
     groups = 4
     wide = 3 * LANES
     return pl.pallas_call(
-        project_kernel,
-        grid=(2, groups),
-        in_specs=[
-            pl.BlockSpec((1, CHUNK, MODEL_WIDTH), lambda i, j: (i, 0, 0)),
-            pl.BlockSpec((MODEL_WIDTH, wide), lambda i, j: (0, j)),
-            pl.BlockSpec((1, CHUNK, LANES), lambda i, j: (0, 0, 0)),
-            pl.BlockSpec((1, CHUNK, LANES), lambda i, j: (0, 0, 0)),
-        ],
-        out_specs=pl.BlockSpec((1, 1, CHUNK, wide), lambda i, j: (j, i, 0, 0)),
-        out_shape=jax.ShapeDtypeStruct((groups, 2, CHUNK, wide), LOW),
+        project_back_kernel,
+        grid=(groups, 2),
+        in_specs=[pl.BlockSpec((1, CHUNK, wide), lambda j, i: (i, 0, j))] + piece_specs(pieces),
+        out_specs=pl.BlockSpec((2, CHUNK, MODEL_WIDTH), lambda j, i: (0, 0, 0)),
+        out_shape=jax.ShapeDtypeStruct((2, CHUNK, MODEL_WIDTH), LOW),
+        scratch_shapes=[pltpu.VMEM((2, CHUNK, MODEL_WIDTH), WIDE)],
         compiler_params=pltpu.CompilerParams(vmem_limit_bytes=VMEM_BYTES),
-        cost_estimate=pl.CostEstimate(
-            flops=2 * 2 * CHUNK * MODEL_WIDTH * groups * wide,
-            bytes_accessed=4 * MODEL_WIDTH * (2 * CHUNK + groups * wide),
-            transcendentals=0,
+        cost_estimate=cost(
+            2 * CHUNK * MODEL_WIDTH * groups * wide, MODEL_WIDTH * (CHUNK + groups * wide), 0
         ),
-    )(normed_pair, weights, cosine, sine)
+    )(grads, *pieces)
 
 
 def split_heads(tiles, lanes_from):
@@ -676,10 +919,10 @@
     return whole, some
 
 
-def attend_kernel(place_ref, prefix_ref, q_ref, kv_ref, o_ref, lse_ref, heads, top, total, acc):
-    sequence = pl.program_id(0)
+def attend_kernel(place_ref, q_ref, kv_ref, *rest):
+    o_ref, lse_ref, heads, top, total, acc = rest[-6:]
     place = place_ref[0]
-    prefix = prefix_ref[sequence]
+    prefix = place_ref[1 + pl.program_id(0)]
     chunk = pl.program_id(1) ^ place
     for head, tile in enumerate(split_heads(q_ref[0, 0], 0)):
         heads[head] = tile
@@ -722,17 +965,18 @@
         o_ref[0, 0, :, pair * LANES : (pair + 1) * LANES] = tile.astype(LOW)
 
 
-def attend(place, prefixes, packed):
+def attend(spot, packed, holds=()):
     units = 2 * 4 * 10
     return pl.pallas_call(
         attend_kernel,
         grid_spec=pltpu.PrefetchScalarGridSpec(
-            num_scalar_prefetch=2,
+            num_scalar_prefetch=1,
             grid=(2, 4),
             in_specs=[
                 pl.BlockSpec((1, 1, CHUNK, 2 * LANES), lambda i, j, *_: (j, i, 0, 0)),
                 pl.BlockSpec((4, 1, CHUNK, LANES), lambda i, j, *_: (0, i, 0, 2)),
-            ],
+            ]
+            + [pl.BlockSpec(memory_space=pl.ANY)] * len(holds),
             out_specs=[
                 pl.BlockSpec((1, 1, CHUNK, 2 * LANES), lambda i, j, *_: (j, i, 0, 0)),
                 pl.BlockSpec((1, 1, 8, CHUNK), lambda i, j, *_: (j, i, 0, 0)),
@@ -750,34 +994,20 @@
         ],
         compiler_params=pltpu.CompilerParams(vmem_limit_bytes=VMEM_BYTES),
         cost_estimate=pl.CostEstimate(
-            flops=units * 4 * CHUNK * CHUNK * 256 * 2 * 2,
-            bytes_accessed=8 * 1024 * 1024,
-            transcendentals=units * 4 * CHUNK * CHUNK,
+            flops=int(units * 4 * CHUNK * CHUNK * 256 * 2 * 2 * COST_SHARE),
+            bytes_accessed=1024 * 1024,
+            transcendentals=0,
         ),
-    )(place, prefixes, packed, packed)
+    )(spot, packed, packed, *holds)
 
 
 def attend_back_kernel(
-    place_ref,
-    prefix_ref,
-    q_ref,
-    kv_ref,
-    o_ref,
-    do_ref,
-    lse_ref,
-    cosine_ref,
-    sine_ref,
-    out_ref,
-    heads,
-    grads,
-    deltas,
-    q_acc,
-    kv_acc,
+    sequence, place_ref, q_ref, kv_ref, o_ref, do_ref, lse_ref, cosine_ref, sine_ref, *rest
 ):
-    sequence = pl.program_id(0)
-    slot = pl.program_id(1)
+    out_ref, heads, grads, deltas, q_acc, kv_acc = rest[-6:]
+    slot = pl.program_id(0)
     place = place_ref[0]
-    prefix = prefix_ref[sequence]
+    prefix = place_ref[1 + sequence]
     chunk = slot ^ place
 
     @pl.when(slot == 0)
@@ -828,7 +1058,7 @@
     for pair, tile in enumerate(join_heads([q_acc[head] for head in range(4)], 0)):
         tile = tile * ATTN_SCALE
         turned = tile * cosine + partner_lanes(tile * sine)
-        out_ref[slot, 0, :, pair * LANES : (pair + 1) * LANES] = turned.astype(LOW)
+        out_ref[slot, :, pair * LANES : (pair + 1) * LANES] = turned.astype(LOW)
 
     @pl.when(slot == 3)
     def _():
@@ -836,26 +1066,29 @@
             tile = kv_acc[other]
             turned = tile * cosine_ref[other] + partner_lanes(tile * sine_ref[other])
             turned = jnp.where(first_lanes(tile.shape), turned, tile)
-            out_ref[other, 0, :, 2 * LANES :] = turned.astype(LOW)
-
-
-def attend_grad(place, prefixes, packed, attended, grad_attended, logsum, cosine, sine):
-    units = 2 * 4 * 10
+            out_ref[other, :, 2 * LANES :] = turned.astype(LOW)
+
+
+def attend_grad(sequence, spot, packed, attended, grad_attended, logsum, cosine, sine, holds=()):
+    units = 4 * 10
+    tile = pl.BlockSpec((1, 1, CHUNK, 2 * LANES), lambda j, *_: (j, sequence, 0, 0))
+    table = pl.BlockSpec((4, CHUNK, LANES), lambda j, *_: (0, 0, 0))
     return pl.pallas_call(
-        attend_back_kernel,
+        functools.partial(attend_back_kernel, sequence),
         grid_spec=pltpu.PrefetchScalarGridSpec(
-            num_scalar_prefetch=2,
-            grid=(2, 4),
+            num_scalar_prefetch=1,
+            grid=(4,),
             in_specs=[
-                pl.BlockSpec((1, 1, CHUNK, 2 * LANES), lambda i, j, *_: (j, i, 0, 0)),
-                pl.BlockSpec((4, 1, CHUNK, LANES), lambda i, j, *_: (0, i, 0, 2)),
-                pl.BlockSpec((1, 1, CHUNK, 2 * LANES), lambda i, j, *_: (j, i, 0, 0)),
-                pl.BlockSpec((1, 1, CHUNK, 2 * LANES), lambda i, j, *_: (j, i, 0, 0)),
-                pl.BlockSpec((1, 1, 8, CHUNK), lambda i, j, *_: (j, i, 0, 0)),
-                pl.BlockSpec((4, CHUNK, LANES), lambda i, j, *_: (0, 0, 0)),
-                pl.BlockSpec((4, CHUNK, LANES), lambda i, j, *_: (0, 0, 0)),
-            ],
-            out_specs=pl.BlockSpec((4, 1, CHUNK, 3 * LANES), lambda i, j, *_: (0, i, 0, 0)),
+                tile,
+                pl.BlockSpec((4, 1, CHUNK, LANES), lambda j, *_: (0, sequence, 0, 2)),
+                tile,
+                tile,
+                pl.BlockSpec((1, 1, 8, CHUNK), lambda j, *_: (j, sequence, 0, 0)),
+                table,
+                table,
+            ]
+            + [pl.BlockSpec(memory_space=pl.ANY)] * len(holds),
+            out_specs=pl.BlockSpec((4, CHUNK, 3 * LANES), lambda j, *_: (0, 0, 0)),
             scratch_shapes=[
                 pltpu.VMEM((4, CHUNK, LANES), LOW),
                 pltpu.VMEM((4, CHUNK, LANES), LOW),
@@ -864,14 +1097,14 @@
                 pltpu.VMEM((4, CHUNK, LANES), WIDE),
             ],
         ),
-        out_shape=jax.ShapeDtypeStruct((4, 2, CHUNK, 3 * LANES), LOW),
+        out_shape=jax.ShapeDtypeStruct((4, CHUNK, 3 * LANES), LOW),
         compiler_params=pltpu.CompilerParams(vmem_limit_bytes=VMEM_BYTES),
         cost_estimate=pl.CostEstimate(
-            flops=units * 4 * CHUNK * CHUNK * 256 * 2 * 5,
-            bytes_accessed=16 * 1024 * 1024,
-            transcendentals=units * 4 * CHUNK * CHUNK,
+            flops=int(units * 4 * CHUNK * CHUNK * 256 * 2 * 5 * COST_SHARE),
+            bytes_accessed=1024 * 1024,
+            transcendentals=0,
         ),
-    )(place, prefixes, packed, packed, attended, grad_attended, logsum, cosine, sine)
+    )(spot, packed, packed, attended, grad_attended, logsum, cosine, sine, *holds)
 
 
 def dp_spot(dp):
@@ -890,7 +1123,7 @@
 
 def step_weight(spot, factor, pieces, axis, weight, moment, square):
     count, rows, columns = pieces.shape
-    block_rows = min(rows, (1 << 17) // columns)
+    block_rows = min(rows, (1 << 19) // columns)
     parts = rows // block_rows
 
     def piece_at(block, part, spot_ref):
@@ -1053,26 +1286,40 @@
     half_rows = tokens.shape[0] // 2
     half_width = tokens.shape[1]
 
+    swapped = [1, 0, 3, 2]
+    wide = 3 * LANES
     owner = [col ^ (2 * row), col ^ (2 - 2 * row), col ^ (1 + 2 * row), col ^ (3 - 2 * row)]
-
-    def by_owner(block, axis):
-        other = swap_far(block)
-        first = jnp.where(row == 0, block, other)
-        second = jnp.where(row == 0, other, block)
-        pair = jnp.stack([first, second])
-        return jnp.concatenate([pair, swap_near(pair)])
-
-    swapped = [1, 0, 3, 2]
 
     def reorder(blocks):
         return jnp.stack([blocks[place_at] for place_at in swapped])
 
-    q_cut = cut(query_weight, core * 2 * LANES + side * LANES, LANES, 1).astype(LOW)
-    q_blocks = by_owner(q_cut, 1)
-    q_own = jnp.stack([q_blocks, swap_y(q_blocks)], axis=1)
-    q_whole = jnp.concatenate(
-        [q_own, swap_x(reorder(q_own))], axis=2
-    )
+    def ordered_halves(matrix, axis):
+        start = core * 2 * LANES
+        return jnp.concatenate(
+            [
+                cut(matrix, start + side * LANES, LANES, axis),
+                cut(matrix, start + (1 - side) * LANES, LANES, axis),
+            ],
+            axis=axis,
+        ).astype(LOW)
+
+    def halves_of(values):
+        own = cut(values, row * half_rows, half_rows, 0)
+        return own, cut(values, (1 - row) * half_rows, half_rows, 0)
+
+    def leave(values, others):
+        back = after(swap_x(after(values[:, half_width:], others[0])), others[1])
+        return in_order(row, values[:, :half_width], back, 0)
+
+    def add_low(kept, got):
+        return (kept.astype(WIDE) + got.astype(WIDE)).astype(LOW)
+
+    own_rows, other_rows = halves_of(tokens)
+    got_rows = swap_x(other_rows)
+    gains = jnp.concatenate([norm_gains, swap_x(norm_gains)], axis=1)
+    prefixes = [prefix[far], swap_core(prefix)[far]]
+    spot = jnp.stack([place, *prefixes])
+    cosine, sine = slot_tables(place)
 
     def heads_of(matrix):
         return jnp.stack(
@@ -1080,189 +1327,380 @@
         ).astype(LOW)
 
     kv_own = jnp.concatenate([heads_of(key_projection), heads_of(value_projection)], axis=2)
-    kv_whole = jnp.concatenate([kv_own, swap_x(reorder(kv_own))], axis=1)
-    in_weights = jnp.stack([q_whole[:, 0], q_whole[:, 1], kv_whole], axis=1)
-    in_weights = in_weights.transpose(2, 0, 1, 3).reshape(MODEL_WIDTH, 4 * 3 * LANES)
-
-    o_cut = cut(out_weight, core * 2 * LANES + side * LANES, LANES, 0).astype(LOW)
-    o_blocks = by_owner(o_cut, 0)
-    o_rows = jnp.concatenate([o_blocks, swap_x(reorder(o_blocks))], axis=2)
-    out_weights = jnp.stack([o_rows, swap_y(o_rows)], axis=1).reshape(
-        4 * 2 * LANES, MODEL_WIDTH
-    )
+    kv_other = swap_x(reorder(kv_own))
+
+    def far_pair(block, other):
+        return jnp.stack([jnp.where(row == 0, block, other), jnp.where(row == 0, other, block)])
 
     units = gate_weight.shape[1] // 2
 
-    def hidden_cut(matrix, axis):
-        return cut(matrix, core * units + side * (units // 2), units // 2, axis).astype(LOW)
-
-    def widen(matrix, unit_axis, x_first):
-        block = hidden_cut(matrix, unit_axis)
-        block = jnp.concatenate([block, swap_far(block)], axis=unit_axis)
-        if x_first:
-            block = jnp.concatenate([block, swap_x(block)], axis=1 - unit_axis)
-            return jnp.concatenate([block, swap_y(block)], axis=unit_axis)
-        block = jnp.concatenate([block, swap_y(block)], axis=unit_axis)
-        return jnp.concatenate([block, swap_x(block)], axis=1 - unit_axis)
-
-    gate_whole = widen(gate_weight, 1, True)
-    up_whole = widen(up_weight, 1, False)
-    down_whole = widen(down_weight, 0, True)
-
-    def enter(values):
-        own = cut(values, row * half_rows, half_rows, 0)
-        sent = cut(values, (1 - row) * half_rows, half_rows, 0)
-        return jnp.concatenate([own, swap_x(sent)], axis=1)
-
-    def leave(values):
-        back = swap_x(values[:, half_width:])
-        return in_order(row, values[:, :half_width], back, 0)
-
-    def pair_core(values):
-        return jnp.concatenate([values, swap_core(values)], axis=0)
-
-    def gather_four(values):
-        both = jnp.concatenate([values, swap_near(values)], axis=0)
-        return jnp.concatenate([both, swap_core(both)], axis=0)
-
-    def sum_four(part):
-        count = part.shape[0] // 4
-        part = fold(part[: 2 * count], part[2 * count :], swap_core)
-        return fold(part[:count], part[count:], swap_near)
-
-    gains = jnp.concatenate([norm_gains, swap_x(norm_gains)], axis=1)
-    prefixes = jnp.stack([prefix[far], swap_core(prefix)[far]])
-    place_array = place.reshape(1)
-    cosine, sine = slot_tables(place)
-
-    x = enter(tokens).astype(WIDE)
+    def hidden_low(matrix, axis, which):
+        start = core * units + (side if which == 0 else 1 - side) * (units // 2)
+        return cut(matrix, start, units // 2, axis).astype(LOW)
+
+    pair_own = [
+        jnp.stack([hidden_low(gate_weight, 1, which), hidden_low(up_weight, 1, which)])
+        for which in range(2)
+    ]
+    down_own = [hidden_low(down_weight, 0, which) for which in range(2)]
+    q_low, o_low = ordered_halves(query_weight, 1), ordered_halves(out_weight, 0)
+
+    q_far = swap_far(q_low)
+    q_pair = after(far_pair(q_low, q_far), kv_other)
+    q_near = swap_near(q_pair)
+    q_pair_x = swap_x(jnp.stack([q_pair[1, :, :LANES], q_pair[0, :, :LANES]]))
+    q_near_x = swap_near(after(q_pair_x, q_near))
+    q_pair_y = swap_y(q_pair_x)
+    pair_x = swap_x(after(pair_own[0], q_pair_x))
+    q_near_y = swap_y(after(q_near_x, q_pair_y))
+    o_far = swap_far(after(o_low, q_near_x))
+    pair_far = swap_far(after(pair_own[0], o_far))
+    o_pair = far_pair(o_low, o_far)
+    o_near = swap_near(o_pair)
+
+    in_pieces = (
+        jnp.concatenate([q_pair, q_near]),
+        kv_own,
+        jnp.concatenate([q_pair_x, q_near_x]),
+        jnp.concatenate([q_pair_y, q_near_y]),
+        kv_other,
+    )
+
+    def exchange(pieces):
+        return [
+            pieces[0],
+            swap_x(pieces[1]),
+            swap_near(pieces[2]),
+            swap_corner(pieces[3]),
+        ]
+
+    def tokens_of(pieces):
+        return jnp.concatenate(exchange([pieces[slot] for slot in range(4)]), axis=1)
+
+    def slots_of(values):
+        size = values.shape[1] // 4
+        return jnp.stack(exchange([values[:, at * size : (at + 1) * size] for at in range(4)]))
+
+    x = jnp.concatenate([own_rows, after(got_rows, q_pair_x)], axis=1).astype(WIDE)
     normed_one, factor_one = rows_norm(x)
-    h_one = pair_core((normed_one * gains[0]).astype(LOW))
-    projected = project(h_one.reshape(2, CHUNK, MODEL_WIDTH), in_weights, cosine, sine)
+    h_own = (normed_one * gains[0]).astype(LOW)
+    h_one = [h_own, swap_core(h_own)]
+    h_pair = after(jnp.stack(h_one), pair_x)
+    projected = project(h_pair, in_pieces, cosine, sine)
+    pair_x_y = swap_y(after(pair_x, projected))
     packed = jnp.stack(exchange([projected[slot] for slot in range(4)]))
-    attended, logsum = attend(place_array, prefixes, packed)
-    back = exchange([attended[slot] for slot in range(4)])
-    o_tokens = jnp.concatenate(back, axis=2).reshape(2 * CHUNK, 4 * 2 * LANES)
-    out_part = matrix_multiply(o_tokens, out_weights)
-    residual = x + RESID * fold(out_part[:half_rows], out_part[half_rows:], swap_core)
-
-    normed_two, factor_two = rows_norm(residual)
-    h_two = gather_four((normed_two * gains[1]).astype(LOW))
-    gate_value = matrix_multiply(h_two, gate_whole)
-    up_value = matrix_multiply(h_two, up_whole)
-    hidden = (jax.nn.silu(gate_value) * up_value).astype(LOW)
-    down_part = sum_four(matrix_multiply(hidden, down_whole))
-    layer_out = leave((residual + RESID * down_part).astype(LOW))
-
-    grad_output = enter(cotangent).astype(WIDE)
-    grad_mlp = gather_four((RESID * grad_output).astype(LOW))
-    down_local = left_product(hidden, grad_mlp)
-    hidden_part = right_product(grad_mlp, down_whole)
-    sigmoid_gate = jax.nn.sigmoid(gate_value)
-    grad_gate = (
-        hidden_part * up_value * sigmoid_gate * (1.0 + gate_value * (1.0 - sigmoid_gate))
-    ).astype(LOW)
-    grad_up = (hidden_part * (gate_value * sigmoid_gate)).astype(LOW)
-    h_two_part = right_product(grad_gate, gate_whole) + right_product(grad_up, up_whole)
-    gate_local = left_product(h_two, grad_gate)
-    up_local = left_product(h_two, grad_up)
-    grad_mid_part, gain_two_part = rows_norm_back(
-        sum_four(h_two_part), normed_two, factor_two, gains[1]
-    )
-    grad_mid = grad_output + grad_mid_part
-
-    grad_attended = pair_core((RESID * grad_mid).astype(LOW))
-    head_grad = right_product(grad_attended, out_weights).astype(LOW)
-    head_grad = head_grad.reshape(2, CHUNK, 4, 2 * LANES)
-    out_local = left_product(o_tokens, grad_attended)
-    head_pieces = jnp.stack(exchange([head_grad[:, :, slot] for slot in range(4)]))
-    packed_grad = attend_grad(
-        place_array, prefixes, packed, attended, head_pieces, logsum, cosine, sine
-    )
-    pieces = exchange([packed_grad[slot] for slot in range(4)])
-    in_grads = jnp.concatenate(pieces, axis=2).reshape(2 * CHUNK, 4 * 3 * LANES)
-    in_local = left_product(h_one, in_grads)
-    h_one_part = right_product(in_grads, in_weights)
-    grad_in_part, gain_one_part = rows_norm_back(
-        fold(h_one_part[:half_rows], h_one_part[half_rows:], swap_core),
-        normed_one,
-        factor_one,
-        gains[0],
-    )
-    input_grad = leave((grad_mid + grad_in_part).astype(LOW))
-
-    def halve_hidden(part, unit_axis, x_first):
-        def half(values, axis, which):
-            size = values.shape[axis] // 2
-            return lax.slice_in_dim(values, which * size, (which + 1) * size, axis=axis)
-
-        steps = [(swap_x, 1 - unit_axis), (swap_y, unit_axis)]
-        if not x_first:
-            steps = steps[::-1]
-        for move, axis in steps + [(swap_far, unit_axis)]:
-            part = fold(half(part, axis, 0), half(part, axis, 1), move)
-        return part.astype(LOW)
-
-    def spread(piece):
-        pair = jnp.stack([piece, swap_y(piece)])
-        return jnp.concatenate([pair, swap_core(pair)])
-
-    gate_piece = halve_hidden(gate_local, 1, False)
-    up_piece = halve_hidden(up_local, 1, True)
-    down_piece = halve_hidden(down_local, 0, True)
-
-    wide = 3 * LANES
-
+    packed = after(packed, pair_far, pair_x_y, o_near)
+    pair_far_x = swap_x(after(pair_far, packed))
+    pair_far_y = swap_y(after(pair_far, packed))
+    o_own = jnp.concatenate([o_pair, o_near])
+    o_first = swap_x(after(reorder(o_own[:, :LANES]), packed))
+    down_far = swap_far(after(down_own[0], packed))
+    attended, logsum = attend(spot, packed)
+    attended = after(attended, pair_far_x, pair_far_y, o_first, down_far)
+    o_second = swap_y(after(o_first, attended))
+    o_back = jnp.concatenate(exchange([attended[slot] for slot in range(4)]), axis=2)
+    pair_far_xy = swap_y(after(pair_far_x, o_second))
+    o_tokens = [o_back[0], o_back[1]]
+    out_weights = jnp.concatenate(
+        [o_own, jnp.concatenate([o_first, o_second], axis=1)], axis=2
+    ).reshape(4 * 2 * LANES, MODEL_WIDTH)
+    out_part = matrix_multiply(o_back.reshape(2 * CHUNK, 4 * 2 * LANES), out_weights)
+    residual = x + RESID * fold(out_part[:CHUNK], out_part[CHUNK:], swap_core)
+    pairs = (
+        ((pair_own[0], pair_far), (pair_x, pair_far_x)),
+        ((pair_own[1], pair_far_y), (pair_x_y, pair_far_xy)),
+    )
+
+    own_grad, other_grad = halves_of(cotangent)
+    got_grad = swap_x(after(other_grad, o_back))
     def columns(values, order, size):
         return jnp.concatenate([values[:, at * size : (at + 1) * size] for at in order], axis=1)
 
-    in_part = fold(
-        in_local[:half_width], columns(in_local[half_width:], swapped, wide), swap_x
-    )
-    in_part = fold(in_part[:, : 2 * wide], in_part[:, 2 * wide :], swap_near)
-    in_part = fold(
-        jnp.where(row == 0, in_part[:, :wide], in_part[:, wide:]),
-        jnp.where(row == 0, in_part[:, wide:], in_part[:, :wide]),
-        swap_far,
-    ).astype(LOW)
-    from_side = swap_y(in_part[:, LANES:])
-    query_piece = (
-        in_part[:, :LANES].astype(WIDE) + from_side[:, :LANES].astype(WIDE)
-    ).astype(LOW)
-    kv_piece = (
-        in_part[:, 2 * LANES :].astype(WIDE) + from_side[:, LANES:].astype(WIDE)
-    ).astype(LOW)
-
-    def out_rows(values):
-        size = 2 * LANES
-        return jnp.concatenate([values[at * size : (at + 1) * size] for at in swapped])
-
-    out_part = fold(out_local[:, :half_width], out_rows(out_local[:, half_width:]), swap_x)
-    out_part = fold(out_part[: 4 * LANES], out_part[4 * LANES :], swap_near)
-    out_part = fold(
-        jnp.where(row == 0, out_part[: 2 * LANES], out_part[2 * LANES :]),
-        jnp.where(row == 0, out_part[2 * LANES :], out_part[: 2 * LANES]),
-        swap_far,
-    )
-    out_piece = fold(out_part[:LANES], out_part[LANES:], swap_y).astype(LOW)
+    def rows(values, order, size):
+        return jnp.concatenate([values[at * size : (at + 1) * size] for at in order])
+
+    def beyond_of(parts):
+        return add_low(parts[0], swap_core(parts[1]))
+
+    def sum_four(parts):
+        beyond = swap_near(parts[1])
+
+        def finish(*others):
+            own = parts[0][0].astype(WIDE) + swap_core(parts[0][1]).astype(WIDE)
+            return own + after(beyond, *others).astype(WIDE)
+
+        return finish
+
+    normed_two, factor_two = rows_norm(residual)
+    h_own = (normed_two * gains[1]).astype(LOW)
+    h_near = swap_near(h_own)
+    h_two = [jnp.concatenate([h_own, swap_core(h_own)]), None]
+    down_pair = jnp.stack([down_own[0], down_far])
+    down_pair_x = swap_x(after(down_pair, o_back))
+    down_far_y = swap_y(after(down_far, pair_far_xy))
+    down_pair_xy = swap_y(after(down_pair_x, down_far_y))
+    down = (
+        ((down_own[0], down_far), (down_pair_x[0], down_pair_x[1])),
+        ((down_own[1], down_far_y), (down_pair_xy[0], down_pair_xy[1])),
+    )
+
+    hidden, gate_values, up_values = [[], []], [[], []], [[], []]
+    for half in range(2):
+        if half == 1:
+            h_near, got_grad = after(h_near, hidden[0][0]), after(got_grad, hidden[0][0])
+            grad_output = jnp.concatenate([own_grad, got_grad], axis=1).astype(WIDE)
+            grad_own = (RESID * grad_output).astype(LOW)
+            grad_near = swap_near(after(grad_own, h_near))
+            h_two[1] = jnp.concatenate([h_near, swap_core(h_near)])
+        for which in range(2):
+            one, two, three = hidden_units(h_two[half], pairs[which])
+            hidden[which].append(one)
+            gate_values[which].append(two)
+            up_values[which].append(three)
+
+    grad_near = after(grad_near, hidden[0][1])
+    grad_mlp = [
+        jnp.concatenate([grad_own, swap_core(grad_own)]),
+        jnp.concatenate([grad_near, swap_core(grad_near)]),
+    ]
+    down_sent, down_kept = [
+        weight_grad(hidden[which], 0, [grad_mlp], units) for which in (1, 0)
+    ]
+    part_rows = units // 2
+    down_y = swap_y(down_sent[:part_rows])
+    down_x = swap_x(
+        jnp.concatenate([down_kept[part_rows:, half_width:], down_sent[part_rows:, half_width:]])
+    )
+    down_first = down_kept[:part_rows]
+    down_second = jnp.concatenate(
+        [down_kept[part_rows:, :half_width], down_sent[part_rows:, :half_width]]
+    )
+    down_pair_xy = after(down_pair_xy, down_kept)
+    down = (
+        ((down_own[0], down_far), (down_pair_x[0], down_pair_x[1])),
+        ((down_own[1], down_far_y), (down_pair_xy[0], down_pair_xy[1])),
+    )
+
+
+    grad_gate, grad_up = [[None, None], [None, None]], [[None, None], [None, None]]
+    for half in (1, 0):
+        grads_here = after(grad_mlp[half], down_sent, down_kept)
+        for which in range(2):
+            grad_gate[which][half], grad_up[which][half] = hidden_back(
+                grads_here, down[which], gate_values[which][half], up_values[which][half]
+            )
+    up_sent = weight_grad(h_two, 1, grad_up, half_width)
+    gate_sent = weight_grad(h_two, 0, grad_gate[1:], MODEL_WIDTH)
+    h_two_parts = [None, None]
+
+    def back_of(half, *others):
+        grads = [[after(kind[which][half], *others) for which in range(2)]
+                 for kind in (grad_gate, grad_up)]
+        return normed_back(*grads, pairs)
+
+    h_two_parts[1] = back_of(1, up_sent, gate_sent)
+    h_two_beyond = beyond_of(h_two_parts[1])
+    down_y, down_x = after(down_y, *h_two_parts[1]), after(down_x, *h_two_parts[1])
+    down_first = [
+        add_low(down_first[:, at * half_width : (at + 1) * half_width],
+                down_y[:, at * half_width : (at + 1) * half_width])
+        for at in range(2)
+    ]
+    down_second = [
+        add_low(down_second[at * part_rows : (at + 1) * part_rows],
+                down_x[at * part_rows : (at + 1) * part_rows])
+        for at in range(2)
+    ]
+    h_two_parts[0] = back_of(0, h_two_beyond, *down_first, *down_second)
+    h_two_sum = sum_four((h_two_parts[0], h_two_beyond))
+    hidden_late = [[after(value, *h_two_parts[0]) for value in values] for values in hidden]
+    down_parts = [
+        down_units([hidden_late[0][half], hidden_late[1][half]], down) for half in (1, 0)
+    ][::-1]
+    up_kept = weight_grad([after(value, *h_two_parts[0]) for value in h_two], 0, grad_up, half_width)
+    up_sum_x = swap_x(up_sent)
+    gate_sum_y = swap_y(after(gate_sent, down_y))
+    down_first_x, down_second_y = swap_x(down_first[1]), swap_y(down_second[1])
+
+    grad_mid_part, gain_two_part = rows_norm_back(
+        h_two_sum(up_kept, *down_parts[0], *down_parts[1]), normed_two, factor_two, gains[1]
+    )
+    grad_mid = grad_output + grad_mid_part
+
+    grad_attended = [(RESID * grad_mid).astype(LOW)]
+    gate_kept = weight_grad(
+        [after(value, grad_attended[0]) for value in h_two], 0, grad_gate[:1], MODEL_WIDTH
+    )
+    layer_sum = sum_four((down_parts[0], beyond_of(down_parts[1])))
+    grad_attended.append(swap_core(grad_attended[0]))
+    head_grad = right_product(jnp.concatenate(grad_attended), out_weights).astype(LOW)
+    head_grad = head_grad.reshape(2, CHUNK, 4 * 2 * LANES)
+    head_grad = jnp.stack(
+        exchange([head_grad[:, :, at * 2 * LANES : (at + 1) * 2 * LANES] for at in range(4)])
+    )
+    out_local = [
+        weight_grad(o_tokens, 0, [[values[:, half * half_width : (half + 1) * half_width]
+                                   for values in grad_attended]], 4 * 2 * LANES)
+        for half in range(2)
+    ]
+    out_near = swap_near(jnp.concatenate([values[4 * LANES :] for values in out_local], axis=1))
+    down_first_x, down_second_y, up_sum_x, gate_sum_y = (
+        after(value, gate_kept)
+        for value in (down_first_x, down_second_y, up_sum_x, gate_sum_y)
+    )
+    down_part = add_low(down_first[0], down_first_x)
+    down_far_sum = swap_far(add_low(down_second[0], down_second_y))
+    size = up_kept.shape[1] // 2
+    up_kept = [
+        add_low(up_kept[:, at * size : (at + 1) * size], up_sum_x[:, at * size : (at + 1) * size])
+        for at in range(2)
+    ]
+    gate_kept = [
+        add_low(
+            gate_kept[at * half_width : (at + 1) * half_width],
+            gate_sum_y[at * half_width : (at + 1) * half_width],
+        )
+        for at in range(2)
+    ]
+    gate_sum_x = swap_x(gate_kept[1])
+    up_sum_y = swap_y(up_kept[1])
+    def sequence_grad(sequence, *others):
+        return attend_grad(
+            sequence,
+            spot,
+            packed,
+            attended,
+            after(head_grad, *others),
+            logsum,
+            cosine,
+            sine,
+        )
+
+    packed_first = sequence_grad(0, down_part, *up_kept, *gate_kept)
+    up_sum_y, gate_sum_x, down_far_sum, out_near = (
+        after(value, packed_first) for value in (up_sum_y, gate_sum_x, down_far_sum, out_near)
+    )
+    gate_part = add_low(gate_kept[0], gate_sum_x)
+    up_part = add_low(up_kept[0], up_sum_y)
+    gate_far_sum = swap_far(gate_part[:, units // 2 :])
+    in_first = tokens_of(packed_first)
+    packed_second = sequence_grad(1, gate_part, up_part)
+    gate_far_sum, in_first = after(gate_far_sum, packed_second), after(in_first, packed_second)
+    up_far_sum = swap_far(after(up_part[:, units // 2 :], gate_far_sum))
+    layer_part = (residual + RESID * layer_sum(packed_second)).astype(LOW)
+    in_back = jnp.stack([in_first, tokens_of(after(packed_second, gate_far_sum))])
+    down_piece = add_low(down_part, down_far_sum)
+    gate_piece = add_low(gate_part[:, : units // 2], gate_far_sum)
+    up_piece = add_low(up_part[:, : units // 2], up_far_sum)
+    in_grads = [in_back[0], in_back[1]]
+    out_kept = add_low(
+        jnp.concatenate([values[: 4 * LANES] for values in out_local], axis=1), out_near
+    )
+    out_kept = add_low(
+        out_kept[:, :half_width],
+        swap_x(after(rows(out_kept[:, half_width:], [1, 0], 2 * LANES), in_back)),
+    )
+    in_local = [weight_grad(h_one, half, [in_grads], half_width) for half in (1, 0)][::-1]
+    h_one_parts = project_back(after(in_back, up_far_sum), in_pieces)
+    grad_in_part, gain_one_part = rows_norm_back(
+        h_one_parts[0].astype(WIDE) + swap_core(h_one_parts[1]).astype(WIDE), normed_one, factor_one, gains[0]
+    )
+    input_part = (grad_mid + grad_in_part).astype(LOW)
+
+    def spread(piece):
+        pair = jnp.stack([piece, after(swap_y(piece), h_one_parts)])
+        return jnp.concatenate([pair, swap_core(pair)])
+
+
+    pair = 2 * LANES
+    first_cut, second_cut = half_width * 3 // 8, half_width * 5 // 8
+
+    def keep_side(values, got):
+        size = values.shape[1] // wide
+        kept = jnp.concatenate(
+            [
+                jnp.concatenate(
+                    [
+                        values[:, at * wide : at * wide + LANES],
+                        values[:, at * wide + pair : (at + 1) * wide],
+                    ],
+                    axis=1,
+                )
+                for at in range(size)
+            ],
+            axis=1,
+        )
+        return add_low(kept, got)
+
+    def for_side(values):
+        size = values.shape[1] // wide
+        return jnp.concatenate(
+            [values[:, at * wide + LANES : (at + 1) * wide] for at in range(size)], axis=1
+        )
+
+    def rows_of(start, stop):
+        return [values[start:stop] for values in in_local]
+
+    def near_halves(values):
+        size = values.shape[1] // 2
+        return values[:, :size], values[:, size:]
+
+    part = rows_of(0, first_cut)
+    part = add_low(part[0], swap_x(columns(part[1], swapped, wide)))
+    part = keep_side(part, swap_y(for_side(part)))
+    kept, sent = near_halves(part)
+    ways = [add_low(kept, swap_near(sent))]
+
+    part = jnp.concatenate(rows_of(first_cut, second_cut))
+    part = keep_side(part, swap_y(for_side(part)))
+    kept, sent = near_halves(part)
+    part = add_low(kept, swap_near(sent))
+    size = second_cut - first_cut
+    ways.append(add_low(part[:size], swap_x(columns(part[size:], [1, 0], pair))))
+
+    part = jnp.concatenate(rows_of(second_cut, half_width))
+    kept, sent = near_halves(part)
+    part = add_low(kept, swap_near(sent))
+    size = half_width - second_cut
+    part = add_low(part[:size], swap_x(columns(part[size:], [1, 0], wide)))
+    ways.append(keep_side(part, swap_y(for_side(part))))
+
+    in_part = jnp.concatenate(ways)
+    in_part = add_low(
+        jnp.where(row == 0, in_part[:, :pair], in_part[:, pair:]),
+        swap_far(jnp.where(row == 0, in_part[:, pair:], in_part[:, :pair])),
+    )
+    query_piece = in_part[:, :LANES]
+    kv_piece = in_part[:, LANES:]
+
+    out_part = add_low(
+        jnp.where(row == 0, out_kept[:pair], out_kept[pair:]),
+        swap_far(jnp.where(row == 0, out_kept[pair:], out_kept[:pair])),
+    )
+    out_piece = add_low(out_part[:LANES], swap_y(out_part[LANES:]))
+
+    gain_sums = jnp.stack([gain_one_part, gain_two_part]).reshape(2, 2, 8, half_width // 8)
+    gain_sums = gain_sums[:, 0] + swap_x(gain_sums[:, 1])
+    for move in (swap_y, swap_core, swap_near, swap_far):
+        gain_sums = gain_sums + move(gain_sums)
+    gains_total = gain_sums.reshape(2, half_width)
 
     kv_pieces = jnp.stack([kv_piece, swap_far(kv_piece)])
     kv_pieces = jnp.concatenate([kv_pieces, swap_near(kv_pieces)])
     kv_pieces = jnp.concatenate([kv_pieces, swap_core(kv_pieces)])
 
-    gain_parts = jnp.stack([gain_one_part, gain_two_part])
-    gain_parts = gain_parts[:, :half_width] + swap_x(gain_parts[:, half_width:])
-    gains_total = lax.psum(gain_parts, ("dp", "col"))
-
     def squares_of(values):
         values = values.astype(WIDE)
         return jnp.sum(values * values)
 
-    square_local = jnp.where((col == 0) & (dp == 0), squares_of(gains_total), 0.0)
-    square_local = square_local + jnp.where(side == 0, squares_of(kv_piece), 0.0)
+    square_local = jnp.where(side == 0, squares_of(kv_piece), 0.0)
+    square_local = square_local + jnp.where((col == 0) & (dp == 0), squares_of(gains_total), 0.0)
     for piece in (query_piece, out_piece, gate_piece, up_piece, down_piece):
         square_local = square_local + squares_of(piece)
-    grad_norm = jnp.sqrt(lax.psum(square_local, ("dp", "row", "col")))
+    square_local = jnp.full((8, LANES), square_local, WIDE)
+    for move in (swap_y, swap_core):
+        square_local = square_local + move(square_local)
+    grad_norm = jnp.sqrt(lax.psum(square_local[0, 0], ("row", "col")))
     factor = jnp.minimum(1.0, CLIP / grad_norm)
     factor_cell = factor.reshape(1, 1)
     spot = dp_spot(dp)
@@ -1275,6 +1713,8 @@
     gate_out = step(gate_piece, 1, gate_weight, gate_moment, gate_square)
     up_out = step(up_piece, 1, up_weight, up_moment, up_square)
     down_out = step(down_piece, 0, down_weight, down_moment, down_square)
+    layer_out = leave(layer_part, (in_part, up_out[0]))
+    input_grad = leave(input_part, (in_part, up_out[0]))
     kv_spot = jnp.stack([core, col])
     key_out, value_out = step_pair(
         kv_spot,

time: 1620 us -> 1330 us (0.82)
  matrix products: 293 us -> 10.9 us
  Pallas kernels: 256 us -> 538 us
  waiting for transfers between devices: 519 us -> 346 us
  blocking collectives: 68.7 us -> 16.7 us
  other arithmetic: 210 us -> 166 us
  local copies, waits for them, and re-layouts: 129 us -> 96.1 us
    pallas_call x2 -> x26, Pallas kernels: 93.9 us -> 388 us  [the longest x10 99.2 us: weight_grad(): pl.pallas_call(kernel, grid=(columns // block,), in_specs=[pl.BlockSpec((...]
    ppermute x75 -> x98, waiting for transfers between devices: 493 us -> 316 us  [swap(): lax.ppermute(values, axis, [(place, place ^ bit) for place in range(size)])]
    dot_general x5 -> x1, matrix products: 107 us -> 6.37 us  [right_product(): lax.dot_general(left_side, right_side, (((1,), (1,)), ((), ())), preferre...]
    dot_general x5 -> x0, matrix products: 94.4 us -> none  [left_product(): lax.dot_general(left_side, right_side, (((0,), (0,)), ((), ())), preferre...]
    dot_general x4 -> x1, matrix products: 91.6 us -> 4.5 us  [matrix_multiply(): return jnp.dot(left_side, right_side, preferred_element_type=jnp.float32)]
    psum x2 -> x1, blocking collectives: 68.7 us -> 16.7 us  [swapped_shards(): grad_norm = jnp.sqrt(lax.psum(square_local[0, 0], ('row', 'col')))]
    add x14 -> x6, other arithmetic: 50.5 us -> 0.02 us  [the longest x3 0.01 us: swapped_shards(): gain_sums = gain_sums + move(gain_sums)]
    convert_element_type x9 -> x30, other arithmetic: 38.5 us -> 68.6 us  [the longest x23 46.7 us: add_low(): return (kept.astype(WIDE) + got.astype(WIDE)).astype(LOW)]
  transfers between devices with their start and end apart: 79 -> 103, of which waited for: 30 -> 31; matrix products, arithmetic and copies ran while one was open for 30% -> 18% of each run, Pallas kernels for 15% -> 35%
where the time goes in v2:
time: 1330 us
  Pallas kernels  538 us (40%)
  waiting for transfers between devices  346 us (26%)
  other arithmetic  166 us (12%)
  starting transfers between devices  144 us (11%)
  local copies, waits for them, and re-layouts  96.1 us (7%)
  blocking collectives  16.7 us (1%)
    ppermute x98, waiting for transfers between devices, swap(): lax.ppermute(values, axis, [(place, place ^ bit) for place in range(size)])  316 us
    ppermute x98, starting transfers between devices, swap(): lax.ppermute(values, axis, [(place, place ^ bit) for place in range(size)])  136 us
    pallas_call x10, Pallas kernels, weight_grad(): pl.pallas_call(kernel, grid=(columns // block,), in_specs=[pl.BlockSpec((...  99.2 us
    pallas_call x2, Pallas kernels, attend_grad(): pl.pallas_call(functools.partial(attend_back_kernel, sequence), grid_spec...  82 us
    pallas_call x5, Pallas kernels, step_weight(): pl.pallas_call(step_kernel, grid_spec=pltpu.PrefetchScalarGridSpec(num_sc...  72.1 us
    pallas_call x1, Pallas kernels, attend(): pl.pallas_call(attend_kernel, grid_spec=pltpu.PrefetchScalarGridSpec(num_...  64.8 us
    pallas_call x4, Pallas kernels, hidden_units(): pl.pallas_call(hidden_kernel, grid=(tokens // block,), in_specs=[pl.Block...  56.5 us
    pallas_call x2, Pallas kernels, normed_back(): pl.pallas_call(normed_back_kernel, grid=(tokens // block,), in_specs=[lef...  53.6 us
  transfers between devices with their start and end apart: 103, of which 31 were waited for; matrix products, arithmetic and copies ran while one was open for 18% of the time, Pallas kernels for 35%

profile of v2, /device:TPU:1, one launch (start us, length us, event | category | flops | bytes accessed | tf_op | source)
XLA Modules:
  0.0 1326.3 jit_solution(17570499065479761131)
XLA Ops:
  15.6 5.8 fusion.39
  37.0 20.2 %collective-permute-done = bf16[512,1024]{1,0:T(8,128)(2,1)} collective-permute-done((bf16[512,1024]{1,0:T(8,128)(2,1)}, bf16[512,1024]{1,0:T(8,128)(2,1)}, u32[]{:S(2)}, u32[]{:S(2)}) %collective-permute-start) | collective-permute-done | bytes 1048608 | tf_op jit(solution)/shard_map/ppermute | solution.py:542
  57.2 11.1 collective-permute-done.3
  80.0 7.7 collective-permute-done.9
  93.2 19.4 %collective-permute-done.15 = bf16[256,1024]{1,0:T(8,128)(2,1)S(1)} collective-permute-done((bf16[256,1024]{1,0:T(8,128)(2,1)S(1)}, bf16[256,1024]{1,0:T(8,128)(2,1)S(1)}, u32[]{:S(2)}, u32[]{:S(2)}) %collective-permute-start.15) | collective-permute-done | bytes 524320 | tf_op jit(solution)/shard_map/ppermute | solution.py:542
  118.1 7.2 collective-permute-done.7.refs_2_
  125.3 16.0 %shard_map.466 = bf16[4,2,512,384]{3,2,1,0:T(8,128)(2,1)} custom-call(bf16[2,512,2048]{2,1,0:T(8,128)(2,1)} %pad_maximum_fusion.normed_ref, bf16[4,1024,256]{2,1,0:T(8,128)(2,1)} %copy-done.62, bf16[4,1024,128]{2,1,0:T(8,128)(2,1)S(1)} %maximum_maximum_fusion.1.kv_ref, bf16[4,1024,128]{2,1,0:T(8,128)(2,1)S(1)} %constant_dynamic-update-slice_fusion.4.first_ref, ...), custom_call_target="tpu_custom_call" | custom-call | flops 3221225472 | bytes 8388608 | tf_op jit(solution)/shard_map/pallas_call | solution.py:841
  149.2 9.6 collective-permute-done.18
  165.8 30.4 %collective-permute-done.14 = bf16[2,512,384]{2,1,0:T(8,128)(2,1)} collective-permute-done((bf16[2,512,384]{2,1,0:T(8,128)(2,1)}, bf16[2,512,384]{2,1,0:T(8,128)(2,1)}, u32[]{:S(2)}, u32[]{:S(2)}) %collective-permute-start.14) | collective-permute-done | bytes 786464 | tf_op jit(solution)/shard_map/ppermute | solution.py:572
  196.2 19.5 %collective-permute-done.13 = bf16[2,512,384]{2,1,0:T(8,128)(2,1)} collective-permute-done((bf16[2,512,384]{2,1,0:T(8,128)(2,1)}, bf16[2,512,384]{2,1,0:T(8,128)(2,1)}, u32[]{:S(2)}, u32[]{:S(2)}) %collective-permute-start.13) | collective-permute-done | bytes 786464 | tf_op jit(solution)/shard_map/ppermute | solution.py:542
  221.9 64.8 %shard_map.467 = (bf16[4,2,512,256]{3,2,1,0:T(8,128)(2,1)S(1)}, f32[4,2,8,512]{3,2,1,0:T(8,128)S(1)}) custom-call(s32[3]{0:T(128)S(1)} %pad_add_fusion.place_ref, bf16[4,2,512,384]{3,2,1,0:T(8,128)(2,1)S(1)} %pad_maximum_fusion.6.q_ref.kv_ref, bf16[4,2,512,384]{3,2,1,0:T(8,128)(2,1)S(1)} %pad_maximum_fusion.6.q_ref.kv_ref), custom_call_target="tpu_custom_call" | custom-call | flops 85899345920 | bytes 1048576 | tf_op jit(solution)/shard_map/pallas_call | solution.py:970
  292.9 18.4 %collective-permute-done.26 = bf16[4,128,1024]{2,1,0:T(8,128)(2,1)S(1)} collective-permute-done((bf16[4,128,1024]{2,1,0:T(8,128)(2,1)S(1)}, bf16[4,128,1024]{2,1,0:T(8,128)(2,1)S(1)}, u32[]{:S(2)}, u32[]{:S(2)}) %collective-permute-start.26) | collective-permute-done | bytes 1048608 | tf_op jit(solution)/shard_map/ppermute | solution.py:542
  342.1 14.1 %shard_map.468 = (bf16[1024,1024]{1,0:T(8,128)(2,1)S(1)}, bf16[1024,1024]{1,0:T(8,128)(2,1)S(1)}, bf16[1024,1024]{1,0:T(8,128)(2,1)}) custom-call(bf16[1024,2048]{1,0:T(8,128)(2,1)} %pad_maximum_fusion.1.normed_ref.refs_0_, bf16[2,1024,512]{2,1,0:T(8,128)(2,1)} %pad_maximum_fusion.9.refs_0_, bf16[2,1024,512]{2,1,0:T(8,128)(2,1)} %collective-permute-done.16.refs_1_, ...), custom_call_target="tpu_custom_call" | custom-call | flops 8589934592 | bytes 18874368 | tf_op jit(solution)/shard_map/pallas_call | solution.py:667
  356.2 21.8 %collective-permute-done.32 = bf16[512,2048]{1,0:T(8,128)(2,1)} collective-permute-done((bf16[512,2048]{1,0:T(8,128)(2,1)S(1)}, bf16[512,2048]{1,0:T(8,128)(2,1)}, u32[]{:S(2)}, u32[]{:S(2)}) %collective-permute-start.32) | collective-permute-done | bytes 2097184 | tf_op jit(solution)/shard_map/ppermute | solution.py:542
  388.4 18.7 %collective-permute-done.36 = bf16[2,512,1024]{2,1,0:T(8,128)(2,1)} collective-permute-done((bf16[2,512,1024]{2,1,0:T(8,128)(2,1)}, bf16[2,512,1024]{2,1,0:T(8,128)(2,1)}, u32[]{:S(2)}, u32[]{:S(2)}) %collective-permute-start.36) | collective-permute-done | bytes 2097184 | tf_op jit(solution)/shard_map/ppermute | solution.py:542
  415.9 14.3 %shard_map.471 = (bf16[1024,1024]{1,0:T(8,128)(2,1)S(1)}, bf16[1024,1024]{1,0:T(8,128)(2,1)S(1)}, bf16[1024,1024]{1,0:T(8,128)(2,1)}) custom-call(bf16[1024,2048]{1,0:T(8,128)(2,1)} %constant_dynamic-update-slice_fusion.8.normed_ref.refs_1_, bf16[2,1024,512]{2,1,0:T(8,128)(2,1)} %pad_maximum_fusion.9.refs_0_, ...), custom_call_target="tpu_custom_call" | custom-call | flops 8589934592 | bytes 18874368 | tf_op jit(solution)/shard_map/pallas_call | solution.py:667
  434.1 14.1 %shard_map.469 = (bf16[1024,1024]{1,0:T(8,128)(2,1)S(1)}, bf16[1024,1024]{1,0:T(8,128)(2,1)S(1)}, bf16[1024,1024]{1,0:T(8,128)(2,1)}) custom-call(bf16[1024,2048]{1,0:T(8,128)(2,1)} %pad_maximum_fusion.1.normed_ref.refs_0_, bf16[2,1024,512]{2,1,0:T(8,128)(2,1)} %pad_maximum_fusion.12.refs_0_.refs_4_, bf16[2,1024,512]{2,1,0:T(8,128)(2,1)} %copy-done.130, ...), custom_call_target="tpu_custom_call" | custom-call | flops 8589934592 | bytes 18874368 | tf_op jit(solution)/shard_map/pallas_call | solution.py:667
  455.6 14.1 %shard_map.470 = (bf16[1024,1024]{1,0:T(8,128)(2,1)S(1)}, bf16[1024,1024]{1,0:T(8,128)(2,1)S(1)}, bf16[1024,1024]{1,0:T(8,128)(2,1)}) custom-call(bf16[1024,2048]{1,0:T(8,128)(2,1)} %constant_dynamic-update-slice_fusion.8.normed_ref.refs_1_, bf16[2,1024,512]{2,1,0:T(8,128)(2,1)} %pad_maximum_fusion.12.refs_0_.refs_4_, bf16[2,1024,512]{2,1,0:T(8,128)(2,1)} %copy-done.130, ...), custom_call_target="tpu_custom_call" | custom-call | flops 8589934592 | bytes 18874368 | tf_op jit(solution)/shard_map/pallas_call | solution.py:667
  478.3 14.0 %shard_map.473 = bf16[1024,2048]{1,0:T(8,128)(2,1)} custom-call(bf16[1024,1024]{1,0:T(8,128)(2,1)S(1)} %get-tuple-element.213.refs_0_.h0, bf16[1024,1024]{1,0:T(8,128)(2,1)S(1)} %copy-done.51, bf16[1024,2048]{1,0:T(8,128)(2,1)} %pad_maximum_fusion.2.refs_2_.grad_ref, bf16[1024,2048]{1,0:T(8,128)(2,1)} %constant_dynamic-update-slice_fusion.10.refs_3_.grad_ref), custom_call_target="tpu_custom_call" | custom-call | flops 8589934592 | bytes 16777216 | tf_op jit(solution)/shard_map/pallas_call | solution.py:798
  496.3 14.4 %shard_map.472 = bf16[1024,2048]{1,0:T(8,128)(2,1)} custom-call(bf16[1024,1024]{1,0:T(8,128)(2,1)S(1)} %copy-done.49, bf16[1024,1024]{1,0:T(8,128)(2,1)S(1)} %copy-done.53, bf16[1024,2048]{1,0:T(8,128)(2,1)} %pad_maximum_fusion.2.refs_2_.grad_ref, bf16[1024,2048]{1,0:T(8,128)(2,1)} %constant_dynamic-update-slice_fusion.10.refs_3_.grad_ref), custom_call_target="tpu_custom_call" | custom-call | flops 8589934592 | bytes 16777216 | tf_op jit(solution)/shard_map/pallas_call | solution.py:798
  516.9 10.1 shard_map.477
  527.1 9.5 shard_map.476
  538.2 12.1 shard_map.479
  550.3 9.5 shard_map.475
  559.9 9.5 shard_map.474
  571.0 13.4 %shard_map.478 = bf16[1024,2048]{1,0:T(8,128)(2,1)} custom-call(bf16[1024,2048]{1,0:T(8,128)(2,1)} %pad_maximum_fusion.1.normed_ref.refs_0_, bf16[1024,2048]{1,0:T(8,128)(2,1)} %constant_dynamic-update-slice_fusion.8.normed_ref.refs_1_, bf16[1024,1024]{1,0:T(8,128)(2,1)S(1)} %copy-done.41, bf16[1024,1024]{1,0:T(8,128)(2,1)S(1)} %copy-done.38, ...), custom_call_target="tpu_custom_call" | custom-call | flops 8589934592 | bytes 16777216 | tf_op jit(solution)/shard_map/pallas_call | solution.py:798
  586.3 26.6 %shard_map.480 = (bf16[512,2048]{1,0:T(8,128)(2,1)S(1)}, bf16[512,2048]{1,0:T(8,128)(2,1)}) custom-call(bf16[1024,1024]{1,0:T(8,128)(2,1)} %get-tuple-element.199.a0.refs_3_, bf16[1024,1024]{1,0:T(8,128)(2,1)} %get-tuple-element.200.refs_3_.a1, bf16[1024,1024]{1,0:T(8,128)(2,1)} %get-tuple-element.201.refs_3_.b0, ...), custom_call_target="tpu_custom_call" | custom-call | flops 17179869184 | bytes 29360128 | tf_op jit(solution)/shard_map/pallas_call | solution.py:770
  618.2 14.6 %collective-permute-done.41 = bf16[1024,1024]{1,0:T(8,128)(2,1)} collective-permute-done((bf16[1024,1024]{1,0:T(8,128)(2,1)}, bf16[1024,1024]{1,0:T(8,128)(2,1)}, u32[]{:S(2)}, u32[]{:S(2)}) %collective-permute-start.41) | collective-permute-done | bytes 2097184 | tf_op jit(solution)/shard_map/ppermute | solution.py:542
  646.3 27.0 %shard_map.481 = (bf16[512,2048]{1,0:T(8,128)(2,1)S(1)}, bf16[512,2048]{1,0:T(8,128)(2,1)}) custom-call(bf16[1024,1024]{1,0:T(8,128)(2,1)} %get-tuple-element.207.a0.refs_2_, bf16[1024,1024]{1,0:T(8,128)(2,1)} %get-tuple-element.208.refs_2_.a1, bf16[1024,1024]{1,0:T(8,128)(2,1)} %get-tuple-element.209.refs_2_.b0, ...), custom_call_target="tpu_custom_call" | custom-call | flops 17179869184 | bytes 29360128 | tf_op jit(solution)/shard_map/pallas_call | solution.py:770
  678.5 13.4 %shard_map.484 = bf16[1024,2048]{1,0:T(8,128)(2,1)} custom-call(bf16[1024,2048]{1,0:T(8,128)(2,1)} %pad_maximum_fusion.1.normed_ref.refs_0_, bf16[1024,2048]{1,0:T(8,128)(2,1)} %constant_dynamic-update-slice_fusion.8.normed_ref.refs_1_, bf16[1024,1024]{1,0:T(8,128)(2,1)S(1)} %copy-done.42, bf16[1024,1024]{1,0:T(8,128)(2,1)S(1)} %copy-done.39, ...), custom_call_target="tpu_custom_call" | custom-call | flops 8589934592 | bytes 16777216 | tf_op jit(solution)/shard_map/pallas_call | solution.py:798
  691.9 13.5 %shard_map.483 = (bf16[512,2048]{1,0:T(8,128)(2,1)}, bf16[512,2048]{1,0:T(8,128)(2,1)}) custom-call(bf16[1024,1024]{1,0:T(8,128)(2,1)} %copy-done.50, bf16[1024,1024]{1,0:T(8,128)(2,1)} %copy-done.52, bf16[512,1024]{1,0:T(8,128)(2,1)S(1)} %get-tuple-element.164.d0.refs_0_, bf16[512,1024]{1,0:T(8,128)(2,1)S(1)} %copy-done.25, ...), custom_call_target="tpu_custom_call" | custom-call | flops 8589934592 | bytes 16777216 | tf_op jit(solution)/shard_map/pallas_call | solution.py:700
  705.5 13.9 %shard_map.482 = (bf16[512,2048]{1,0:T(8,128)(2,1)}, bf16[512,2048]{1,0:T(8,128)(2,1)}) custom-call(bf16[1024,1024]{1,0:T(8,128)(2,1)} %copy-done.47, bf16[1024,1024]{1,0:T(8,128)(2,1)} %copy-done.48, bf16[512,1024]{1,0:T(8,128)(2,1)S(1)} %get-tuple-element.164.d0.refs_0_, bf16[512,1024]{1,0:T(8,128)(2,1)S(1)} %copy-done.25, ...), custom_call_target="tpu_custom_call" | custom-call | flops 8589934592 | bytes 16777216 | tf_op jit(solution)/shard_map/pallas_call | solution.py:700
  728.7 5.7 multiply_convert_fusion
  734.4 12.0 shard_map.485
  758.0 5.0 add_convert_fusion.4
  763.1 6.4 fusion.29
  787.3 51.1 %collective-permute-done.51 = bf16[2048,1024]{1,0:T(8,128)(2,1)} collective-permute-done((bf16[2048,1024]{1,0:T(8,128)(2,1)}, bf16[2048,1024]{1,0:T(8,128)(2,1)}, u32[]{:S(2)}, u32[]{:S(2)}) %collective-permute-start.51) | collective-permute-done | bytes 4194336 | tf_op jit(solution)/shard_map/ppermute | solution.py:542
  838.8 4.8 add_convert_fusion.7
  849.0 39.5 %shard_map.486 = bf16[4,512,384]{2,1,0:T(8,128)(2,1)S(1)} custom-call(s32[3]{0:T(128)S(1)} %copy-done.33, bf16[4,2,512,384]{3,2,1,0:T(8,128)(2,1)} %copy-done.13, bf16[4,2,512,384]{3,2,1,0:T(8,128)(2,1)} %copy-done.13, bf16[4,2,512,256]{3,2,1,0:T(8,128)(2,1)S(1)} %copy-done.17, bf16[4,2,512,256]{3,2,1,0:T(8,128)(2,1)} %pad_maximum_fusion.15.do_ref, ...), custom_call_target="tpu_custom_call" | custom-call | flops 107374182400 | bytes 1048576 | tf_op jit(solution)/shard_map/pallas_call | solution.py:1076
  899.4 6.1 collective-permute-start.42
  907.6 5.6 collective-permute-start.101
  921.4 42.5 %shard_map.487 = bf16[4,512,384]{2,1,0:T(8,128)(2,1)S(1)} custom-call(s32[3]{0:T(128)S(1)} %copy-done.33, bf16[4,2,512,384]{3,2,1,0:T(8,128)(2,1)} %copy-done.13, bf16[4,2,512,384]{3,2,1,0:T(8,128)(2,1)} %copy-done.13, bf16[4,2,512,256]{3,2,1,0:T(8,128)(2,1)S(1)} %copy-done.17, bf16[4,2,512,256]{3,2,1,0:T(8,128)(2,1)} %pad_maximum_fusion.15.do_ref, ...), custom_call_target="tpu_custom_call" | custom-call | flops 107374182400 | bytes 1048576 | tf_op jit(solution)/shard_map/pallas_call | solution.py:1076
  963.9 8.2 collective-permute-done.44
  972.3 4.8 collective-permute-start.62
  977.6 5.0 add_convert_fusion.1
  986.2 5.8 collective-permute-start.99
  997.8 6.4 shard_map.489
  1010.0 6.0 shard_map.488
  1020.3 11.0 collective-permute-start.66
  1033.5 14.8 %shard_map.490 = bf16[2,512,2048]{2,1,0:T(8,128)(2,1)} custom-call(bf16[2,512,1536]{2,1,0:T(8,128)(2,1)} %pad_maximum_fusion.7.grad_ref, bf16[4,1024,256]{2,1,0:T(8,128)(2,1)} %copy-done.62, bf16[4,1024,128]{2,1,0:T(8,128)(2,1)S(1)} %maximum_maximum_fusion.1.kv_ref, bf16[4,1024,128]{2,1,0:T(8,128)(2,1)S(1)} %copy-done.5, ...), custom_call_target="tpu_custom_call" | custom-call | flops 3221225472 | bytes 8388608 | tf_op jit(solution)/shard_map/pallas_call | solution.py:879
  1067.5 6.5 collective-permute-done.63
  1080.3 18.9 %collective-permute-done.83 = bf16[256,1024]{1,0:T(8,128)(2,1)S(1)} collective-permute-done((bf16[256,1024]{1,0:T(8,128)(2,1)S(1)}, bf16[256,1024]{1,0:T(8,128)(2,1)S(1)}, u32[]{:S(2)}, u32[]{:S(2)}) %collective-permute-start.83) | collective-permute-done | bytes 524320 | tf_op jit(solution)/shard_map/ppermute | solution.py:542
  1104.9 8.3 collective-permute-done.70
  1115.4 9.3 collective-permute-done.84
  1127.4 11.1 collective-permute-done.97
  1167.1 9.1 collective-permute-done.80
  1195.4 16.7 %psum.7 = f32[]{:T(128)} all-reduce(f32[]{:T(128)} %bitcast.67), channel_id=1, replica_groups=mesh['dp'=4,'row'=2,'col'=4] {'row','col'}, use_global_device_ids=true, to_apply=%region_12.13 | all-reduce | flops 1 | bytes 8 | tf_op jit(solution)/shard_map/psum | solution.py:1703
  1214.4 5.8 shard_map.496
  1220.2 20.1 %shard_map.498 = (f32[2048,1024]{1,0:T(8,128)}, f32[2048,1024]{1,0:T(8,128)}, f32[2048,1024]{1,0:T(8,128)}) custom-call(s32[1]{0:T(128)} %bitcast.56.spot_ref, f32[1,1]{1,0:T(1,128)} %bitcast.68.factor_ref, bf16[4,512,1024]{2,1,0:T(8,128)(2,1)S(1)} %copy-done, f32[2048,1024]{1,0:T(8,128)} %weight_ref.9, f32[2048,1024]{1,0:T(8,128)} %moment_ref.9, ...), custom_call_target="tpu_custom_call" | custom-call | flops 25165824 | bytes 54525952 | tf_op jit(solution)/shard_map/pallas_call | solution.py:1137
  1240.4 20.1 %shard_map.497 = (f32[1024,2048]{1,0:T(8,128)}, f32[1024,2048]{1,0:T(8,128)}, f32[1024,2048]{1,0:T(8,128)}) custom-call(s32[1]{0:T(128)} %bitcast.56.spot_ref, f32[1,1]{1,0:T(1,128)} %bitcast.68.factor_ref, bf16[4,1024,512]{2,1,0:T(8,128)(2,1)S(1)} %copy-done.1, f32[1024,2048]{1,0:T(8,128)} %weight_ref.8, f32[1024,2048]{1,0:T(8,128)} %moment_ref.8, ...), custom_call_target="tpu_custom_call" | custom-call | flops 25165824 | bytes 54525952 | tf_op jit(solution)/shard_map/pallas_call | solution.py:1137
  1271.6 5.4 collective-permute-start.96
  1278.1 6.0 shard_map.494
  1285.9 20.2 %shard_map.493 = (f32[1024,2048]{1,0:T(8,128)}, f32[1024,2048]{1,0:T(8,128)}, f32[1024,2048]{1,0:T(8,128)}) custom-call(s32[1]{0:T(128)} %bitcast.56.spot_ref, f32[1,1]{1,0:T(1,128)} %bitcast.68.factor_ref, bf16[4,1024,512]{2,1,0:T(8,128)(2,1)S(1)} %pad_maximum_fusion.3.grad_ref, f32[1024,2048]{1,0:T(8,128)} %weight_ref.5, f32[1024,2048]{1,0:T(8,128)} %moment_ref.5, ...), custom_call_target="tpu_custom_call" | custom-call | flops 25165824 | bytes 54525952 | tf_op jit(solution)/shard_map/pallas_call | solution.py:1137
  1312.6 12.4 shard_map.495
  (631 shorter events, 377.5 us)
Async XLA Ops:
  0.7 35.0 %collective-permute-start.5 = (f32[2,1024]{1,0:T(2,128)}, f32[2,1024]{1,0:T(2,128)S(1)}, u32[]{:S(2)}, u32[]{:S(2)}) collective-permute-start(f32[2,1024]{1,0:T(2,128)} %param.37), channel_id=1, source_target_pairs={{0,4},{4,0},{1,5},{5,1},{2,6},{6,2},{3,7},{7,3},{8,12},{12,8},{9,1... | collective-permute-start | bytes 24584 | tf_op jit(solution)/shard_map/ppermute | solution.py:542
  4.9 28.7 %collective-permute-start.1 = (bf16[1024,256]{1,0:T(8,128)(2,1)}, bf16[1024,256]{1,0:T(8,128)(2,1)}, u32[]{:S(2)}, u32[]{:S(2)}) collective-permute-start(bf16[1024,256]{1,0:T(8,128)(2,1)} %pad_maximum_fusion.40), channel_id=1, source_target_pairs={{0,2},{1,3},{2,0},{3,1},{4,6},{5,7},{6,4},{7,5},{8,10},{9,11},{10,... | collective-permute-start | bytes 1572872 | tf_op jit(solution)/shard_map/ppermute | solution.py:542
  14.4 42.8 %collective-permute-start = (bf16[512,1024]{1,0:T(8,128)(2,1)}, bf16[512,1024]{1,0:T(8,128)(2,1)}, u32[]{:S(2)}, u32[]{:S(2)}) collective-permute-start(bf16[512,1024]{1,0:T(8,128)(2,1)} %get-tuple-element.351), channel_id=1, source_target_pairs={{0,4},{4,0},{1,5},{5,1},{2,6},{6,2},{3,7},{7,3},{8,12},{12,8},{9,1... | collective-permute-start | bytes 3145736 | tf_op jit(solution)/shard_map/ppermute | solution.py:542
  35.2 33.2 %collective-permute-start.3 = (bf16[2,1024,128]{2,1,0:T(8,128)(2,1)S(1)}, bf16[2,1024,128]{2,1,0:T(8,128)(2,1)S(1)}, u32[]{:S(2)}, u32[]{:S(2)}) collective-permute-start(bf16[2,1024,128]{2,1,0:T(8,128)(2,1)S(1)} %pad_maximum_fusion.41), channel_id=1, source_target_pairs={{0,4},{4,0},{1,5},{5,1},{2,6},{6,2},{3,7},{7,3},{8,12},{12,8},{9,1... | collective-permute-start | bytes 1572872 | tf_op jit(solution)/shard_map/ppermute | solution.py:542
  35.7 38.4 %collective-permute-start.8 = (bf16[2,1024,256]{2,1,0:T(8,128)(2,1)S(1)}, bf16[2,1024,256]{2,1,0:T(8,128)(2,1)S(1)}, u32[]{:S(2)}, u32[]{:S(2)}) collective-permute-start(bf16[2,1024,256]{2,1,0:T(8,128)(2,1)S(1)} %pad_maximum_fusion.27), channel_id=1, source_target_pairs={{0,1},{1,0},{2,3},{3,2},{4,5},{5,4},{6,7},{7,6},{8,9},{9,8},{10,11... | collective-permute-start | bytes 3145736 | tf_op jit(solution)/shard_map/ppermute | solution.py:542
  71.8 43.6 %collective-permute-start.6 = (bf16[512,2048]{1,0:T(8,128)(2,1)S(1)}, bf16[512,2048]{1,0:T(8,128)(2,1)S(1)}, u32[]{:S(2)}, u32[]{:S(2)}) collective-permute-start(bf16[512,2048]{1,0:T(8,128)(2,1)S(1)} %fusion.5.refs_0_), channel_id=1, source_target_pairs={{0,8},{8,0},{16,24},{24,16},{1,9},{9,1},{17,25},{25,17},{2,10},{10... | collective-permute-start | bytes 6291464 | tf_op jit(solution)/shard_map/ppermute | solution.py:542
  78.2 47.2 %collective-permute-start.7 = (bf16[2,1024,512]{2,1,0:T(8,128)(2,1)}, bf16[2,1024,512]{2,1,0:T(8,128)(2,1)}, u32[]{:S(2)}, u32[]{:S(2)}) collective-permute-start(bf16[2,1024,512]{2,1,0:T(8,128)(2,1)} %pad_maximum_fusion.9.refs_0_), channel_id=1, source_target_pairs={{0,4},{4,0},{1,5},{5,1},{2,6},{6,2},{3,7},{7,3},{8,12},{12,8},{9,1... | collective-permute-start | bytes 6291464 | tf_op jit(solution)/shard_map/ppermute | solution.py:542
  113.0 45.9 %collective-permute-start.18 = (bf16[2,256,1024]{2,1,0:T(8,128)(2,1)S(1)}, bf16[2,256,1024]{2,1,0:T(8,128)(2,1)}, u32[]{:S(2)}, u32[]{:S(2)}) collective-permute-start(bf16[2,256,1024]{2,1,0:T(8,128)(2,1)S(1)} %pad_maximum_fusion.31), channel_id=1, source_target_pairs={{0,1},{1,0},{2,3},{3,2},{4,5},{5,4},{6,7},{7,6},{8,9},{9,8},{10,11... | collective-permute-start | bytes 3145736 | tf_op jit(solution)/shard_map/ppermute | solution.py:542
  113.1 104.5 %collective-permute-start.16 = (bf16[2,1024,512]{2,1,0:T(8,128)(2,1)}, bf16[2,1024,512]{2,1,0:T(8,128)(2,1)}, u32[]{:S(2)}, u32[]{:S(2)}) collective-permute-start(bf16[2,1024,512]{2,1,0:T(8,128)(2,1)} %pad_maximum_fusion.9.refs_0_), channel_id=1, source_target_pairs={{0,2},{1,3},{2,0},{3,1},{4,6},{5,7},{6,4},{7,5},{8,10},{9,11},{10,... | collective-permute-start | bytes 6291464 | tf_op jit(solution)/shard_map/ppermute | solution.py:542
  141.4 76.2 %collective-permute-start.17 = (bf16[2,1024,512]{2,1,0:T(8,128)(2,1)}, bf16[2,1024,512]{2,1,0:T(8,128)(2,1)}, u32[]{:S(2)}, u32[]{:S(2)}) collective-permute-start(bf16[2,1024,512]{2,1,0:T(8,128)(2,1)} %collective-permute-done.7.refs_2_), channel_id=1, source_target_pairs={{0,16},{8,24},{16,0},{24,8},{1,17},{9,25},{17,1},{25,9},{2,18},{10... | collective-permute-start | bytes 6291464 | tf_op jit(solution)/shard_map/ppermute | solution.py:542
  147.6 48.6 %collective-permute-start.14 = (bf16[2,512,384]{2,1,0:T(8,128)(2,1)}, bf16[2,512,384]{2,1,0:T(8,128)(2,1)}, u32[]{:S(2)}, u32[]{:S(2)}) collective-permute-start(bf16[2,512,384]{2,1,0:T(8,128)(2,1)} %get-tuple-element.320), channel_id=1, source_target_pairs={{0,5},{1,4},{2,7},{3,6},{4,1},{5,0},{6,3},{7,2},{8,13},{9,12},{10,... | collective-permute-start | bytes 2359304 | tf_op jit(solution)/shard_map/ppermute | solution.py:572
  147.9 67.7 %collective-permute-start.13 = (bf16[2,512,384]{2,1,0:T(8,128)(2,1)}, bf16[2,512,384]{2,1,0:T(8,128)(2,1)}, u32[]{:S(2)}, u32[]{:S(2)}) collective-permute-start(bf16[2,512,384]{2,1,0:T(8,128)(2,1)} %get-tuple-element.321), channel_id=1, source_target_pairs={{0,1},{1,0},{2,3},{3,2},{4,5},{5,4},{6,7},{7,6},{8,9},{9,8},{10,11... | collective-permute-start | bytes 2359304 | tf_op jit(solution)/shard_map/ppermute | solution.py:542
  158.9 56.8 %collective-permute-start.12 = (bf16[2,512,384]{2,1,0:T(8,128)(2,1)}, bf16[2,512,384]{2,1,0:T(8,128)(2,1)}, u32[]{:S(2)}, u32[]{:S(2)}) collective-permute-start(bf16[2,512,384]{2,1,0:T(8,128)(2,1)} %get-tuple-element.322), channel_id=1, source_target_pairs={{0,4},{4,0},{1,5},{5,1},{2,6},{6,2},{3,7},{7,3},{8,12},{12,8},{9,1... | collective-permute-start | bytes 2359304 | tf_op jit(solution)/shard_map/ppermute | solution.py:542
  217.6 69.2 %collective-permute-start.20 = (bf16[2,1024,512]{2,1,0:T(8,128)(2,1)}, bf16[2,1024,512]{2,1,0:T(8,128)(2,1)S(1)}, u32[]{:S(2)}, u32[]{:S(2)}) collective-permute-start(bf16[2,1024,512]{2,1,0:T(8,128)(2,1)} %collective-permute-done.16.refs_1_), channel_id=1, source_target_pairs={{0,16},{8,24},{16,0},{24,8},{1,17},{9,25},{17,1},{25,9},{2,18},{10... | collective-permute-start | bytes 6291464 | tf_op jit(solution)/shard_map/ppermute | solution.py:542
  218.9 67.9 %collective-permute-start.19 = (bf16[2,1024,512]{2,1,0:T(8,128)(2,1)}, bf16[2,1024,512]{2,1,0:T(8,128)(2,1)}, u32[]{:S(2)}, u32[]{:S(2)}) collective-permute-start(bf16[2,1024,512]{2,1,0:T(8,128)(2,1)} %collective-permute-done.16.refs_1_), channel_id=1, source_target_pairs={{0,4},{4,0},{1,5},{5,1},{2,6},{6,2},{3,7},{7,3},{8,12},{12,8},{9,1... | collective-permute-start | bytes 6291464 | tf_op jit(solution)/shard_map/ppermute | solution.py:542
  219.3 67.5 %collective-permute-start.21 = (bf16[4,128,1024]{2,1,0:T(8,128)(2,1)S(1)}, bf16[4,128,1024]{2,1,0:T(8,128)(2,1)S(1)}, u32[]{:S(2)}, u32[]{:S(2)}) collective-permute-start(bf16[4,128,1024]{2,1,0:T(8,128)(2,1)S(1)} %pad_maximum_fusion.32), channel_id=1, source_target_pairs={{0,4},{4,0},{1,5},{5,1},{2,6},{6,2},{3,7},{7,3},{8,12},{12,8},{9,1... | collective-permute-start | bytes 3145736 | tf_op jit(solution)/shard_map/ppermute | solution.py:542
  220.3 66.4 %collective-permute-start.22 = (bf16[512,1024]{1,0:T(8,128)(2,1)S(1)}, bf16[512,1024]{1,0:T(8,128)(2,1)S(1)}, u32[]{:S(2)}, u32[]{:S(2)}) collective-permute-start(bf16[512,1024]{1,0:T(8,128)(2,1)S(1)} %get-tuple-element.164.d0.refs_0_), channel_id=1, source_target_pairs={{0,2},{1,3},{2,0},{3,1},{4,6},{5,7},{6,4},{7,5},{8,10},{9,11},{10,... | collective-permute-start | bytes 3145736 | tf_op jit(solution)/shard_map/ppermute | solution.py:542
  330.8 47.2 %collective-permute-start.32 = (bf16[512,2048]{1,0:T(8,128)(2,1)S(1)}, bf16[512,2048]{1,0:T(8,128)(2,1)}, u32[]{:S(2)}, u32[]{:S(2)}) collective-permute-start(bf16[512,2048]{1,0:T(8,128)(2,1)S(1)} %multiply_convert_fusion.1), channel_id=1, source_target_pairs={{0,1},{1,0},{2,3},{3,2},{4,5},{5,4},{6,7},{7,6},{8,9},{9,8},{10,11... | collective-permute-start | bytes 6291464 | tf_op jit(solution)/shard_map/ppermute | solution.py:542
  332.9 47.2 %collective-permute-start.31 = (bf16[2,1024,512]{2,1,0:T(8,128)(2,1)}, bf16[2,1024,512]{2,1,0:T(8,128)(2,1)}, u32[]{:S(2)}, u32[]{:S(2)}) collective-permute-start(bf16[2,1024,512]{2,1,0:T(8,128)(2,1)} %collective-permute-done.19.refs_3_), channel_id=1, source_target_pairs={{0,16},{8,24},{16,0},{24,8},{1,17},{9,25},{17,1},{25,9},{2,18},{10... | collective-permute-start | bytes 6291464 | tf_op jit(solution)/shard_map/ppermute | solution.py:542
  338.0 43.5 %collective-permute-start.29 = (bf16[512,1024]{1,0:T(8,128)(2,1)S(1)}, bf16[512,1024]{1,0:T(8,128)(2,1)S(1)}, u32[]{:S(2)}, u32[]{:S(2)}) collective-permute-start(bf16[512,1024]{1,0:T(8,128)(2,1)S(1)} %get-tuple-element.168), channel_id=1, source_target_pairs={{0,4},{4,0},{1,5},{5,1},{2,6},{6,2},{3,7},{7,3},{8,12},{12,8},{9,1... | collective-permute-start | bytes 3145736 | tf_op jit(solution)/shard_map/ppermute | solution.py:542
  338.4 68.7 %collective-permute-start.36 = (bf16[2,512,1024]{2,1,0:T(8,128)(2,1)}, bf16[2,512,1024]{2,1,0:T(8,128)(2,1)}, u32[]{:S(2)}, u32[]{:S(2)}) collective-permute-start(bf16[2,512,1024]{2,1,0:T(8,128)(2,1)} %pad_maximum_fusion.13), channel_id=1, source_target_pairs={{0,4},{4,0},{1,5},{5,1},{2,6},{6,2},{3,7},{7,3},{8,12},{12,8},{9,1... | collective-permute-start | bytes 6291464 | tf_op jit(solution)/shard_map/ppermute | solution.py:542
  378.0 36.3 %collective-permute-start.33 = (bf16[512,2048]{1,0:T(8,128)(2,1)}, bf16[512,2048]{1,0:T(8,128)(2,1)S(1)}, u32[]{:S(2)}, u32[]{:S(2)}) collective-permute-start(bf16[512,2048]{1,0:T(8,128)(2,1)} %collective-permute-done.32), channel_id=1, source_target_pairs={{0,8},{8,0},{16,24},{24,16},{1,9},{9,1},{17,25},{25,17},{2,10},{10... | collective-permute-start | bytes 6291464 | tf_op jit(solution)/shard_map/ppermute | solution.py:542
  380.1 28.8 %collective-permute-start.37 = (bf16[512,1024]{1,0:T(8,128)(2,1)S(1)}, bf16[512,1024]{1,0:T(8,128)(2,1)S(1)}, u32[]{:S(2)}, u32[]{:S(2)}) collective-permute-start(bf16[512,1024]{1,0:T(8,128)(2,1)S(1)} %collective-permute-done.22.d1.refs_1_), channel_id=1, source_target_pairs={{0,16},{8,24},{16,0},{24,8},{1,17},{9,25},{17,1},{25,9},{2,18},{10... | collective-permute-start | bytes 3145736 | tf_op jit(solution)/shard_map/ppermute | solution.py:542
  385.7 47.1 %collective-permute-start.34 = (bf16[512,2048]{1,0:T(8,128)(2,1)}, bf16[512,2048]{1,0:T(8,128)(2,1)}, u32[]{:S(2)}, u32[]{:S(2)}) collective-permute-start(bf16[512,2048]{1,0:T(8,128)(2,1)} %fusion.4), channel_id=1, source_target_pairs={{0,1},{1,0},{2,3},{3,2},{4,5},{5,4},{6,7},{7,6},{8,9},{9,8},{10,11... | collective-permute-start | bytes 6291464 | tf_op jit(solution)/shard_map/ppermute | solution.py:542
  408.9 106.3 %collective-permute-start.38 = (bf16[2,512,1024]{2,1,0:T(8,128)(2,1)}, bf16[2,512,1024]{2,1,0:T(8,128)(2,1)}, u32[]{:S(2)}, u32[]{:S(2)}) collective-permute-start(bf16[2,512,1024]{2,1,0:T(8,128)(2,1)} %collective-permute-done.36), channel_id=1, source_target_pairs={{0,16},{8,24},{16,0},{24,8},{1,17},{9,25},{17,1},{25,9},{2,18},{10... | collective-permute-start | bytes 6291464 | tf_op jit(solution)/shard_map/ppermute | solution.py:542
  409.8 41.0 %collective-permute-start.30 = (bf16[512,2048]{1,0:T(8,128)(2,1)}, bf16[512,2048]{1,0:T(8,128)(2,1)}, u32[]{:S(2)}, u32[]{:S(2)}) collective-permute-start(bf16[512,2048]{1,0:T(8,128)(2,1)} %fusion.4), channel_id=1, source_target_pairs={{0,8},{8,0},{16,24},{24,16},{1,9},{9,1},{17,25},{25,17},{2,10},{10... | collective-permute-start | bytes 6291464 | tf_op jit(solution)/shard_map/ppermute | solution.py:542
  432.9 42.1 %collective-permute-start.35 = (bf16[512,2048]{1,0:T(8,128)(2,1)}, bf16[512,2048]{1,0:T(8,128)(2,1)}, u32[]{:S(2)}, u32[]{:S(2)}) collective-permute-start(bf16[512,2048]{1,0:T(8,128)(2,1)} %collective-permute-done.34), channel_id=1, source_target_pairs={{0,8},{8,0},{16,24},{24,16},{1,9},{9,1},{17,25},{25,17},{2,10},{10... | collective-permute-start | bytes 6291464 | tf_op jit(solution)/shard_map/ppermute | solution.py:542
  584.4 48.4 %collective-permute-start.40 = (bf16[512,2048]{1,0:T(8,128)(2,1)}, bf16[512,2048]{1,0:T(8,128)(2,1)}, u32[]{:S(2)}, u32[]{:S(2)}) collective-permute-start(bf16[512,2048]{1,0:T(8,128)(2,1)} %slice.606), channel_id=1, source_target_pairs={{0,16},{8,24},{16,0},{24,8},{1,17},{9,25},{17,1},{25,9},{2,18},{10... | collective-permute-start | bytes 6291464 | tf_op jit(solution)/shard_map/ppermute | solution.py:542
  585.9 46.9 %collective-permute-start.41 = (bf16[1024,1024]{1,0:T(8,128)(2,1)}, bf16[1024,1024]{1,0:T(8,128)(2,1)}, u32[]{:S(2)}, u32[]{:S(2)}) collective-permute-start(bf16[1024,1024]{1,0:T(8,128)(2,1)} %pad_maximum_fusion.14), channel_id=1, source_target_pairs={{0,4},{4,0},{1,5},{5,1},{2,6},{6,2},{3,7},{7,3},{8,12},{12,8},{9,1... | collective-permute-start | bytes 6291464 | tf_op jit(solution)/shard_map/ppermute | solution.py:542
  614.2 28.4 %collective-permute-start.39 = (bf16[512,2048]{1,0:T(8,128)(2,1)}, bf16[512,2048]{1,0:T(8,128)(2,1)}, u32[]{:S(2)}, u32[]{:S(2)}) collective-permute-start(bf16[512,2048]{1,0:T(8,128)(2,1)} %get-tuple-element.204), channel_id=1, source_target_pairs={{0,8},{8,0},{16,24},{24,16},{1,9},{9,1},{17,25},{25,17},{2,10},{10... | collective-permute-start | bytes 6291464 | tf_op jit(solution)/shard_map/ppermute | solution.py:542
  617.1 140.9 %collective-permute-start.54 = (bf16[1024,2048]{1,0:T(8,128)(2,1)}, bf16[1024,2048]{1,0:T(8,128)(2,1)}, u32[]{:S(2)}, u32[]{:S(2)}) collective-permute-start(bf16[1024,2048]{1,0:T(8,128)(2,1)} %shard_map.478), channel_id=1, source_target_pairs={{0,4},{4,0},{1,5},{5,1},{2,6},{6,2},{3,7},{7,3},{8,12},{12,8},{9,1... | collective-permute-start | bytes 12582920 | tf_op jit(solution)/shard_map/ppermute | solution.py:542
  637.4 112.9 %collective-permute-start.53 = (bf16[512,1024]{1,0:T(8,128)(2,1)}, bf16[512,1024]{1,0:T(8,128)(2,1)}, u32[]{:S(2)}, u32[]{:S(2)}) collective-permute-start(bf16[512,1024]{1,0:T(8,128)(2,1)} %get-tuple-element.308), channel_id=1, source_target_pairs={{0,4},{4,0},{1,5},{5,1},{2,6},{6,2},{3,7},{7,3},{8,12},{12,8},{9,1... | collective-permute-start | bytes 3145736 | tf_op jit(solution)/shard_map/ppermute | solution.py:542
  640.9 105.5 %collective-permute-start.85 = (bf16[512,1024]{1,0:T(8,128)(2,1)}, bf16[512,1024]{1,0:T(8,128)(2,1)}, u32[]{:S(2)}, u32[]{:S(2)}) collective-permute-start(bf16[512,1024]{1,0:T(8,128)(2,1)} %add_convert_fusion.19), channel_id=1, source_target_pairs={{0,16},{8,24},{16,0},{24,8},{1,17},{9,25},{17,1},{25,9},{2,18},{10... | collective-permute-start | bytes 3145736 | tf_op jit(solution)/shard_map/ppermute | solution.py:542
  673.4 50.7 %collective-permute-start.45 = (bf16[512,2048]{1,0:T(8,128)(2,1)}, bf16[512,2048]{1,0:T(8,128)(2,1)}, u32[]{:S(2)}, u32[]{:S(2)}) collective-permute-start(bf16[512,2048]{1,0:T(8,128)(2,1)} %get-tuple-element.212), channel_id=1, source_target_pairs={{0,8},{8,0},{16,24},{24,16},{1,9},{9,1},{17,25},{25,17},{2,10},{10... | collective-permute-start | bytes 6291464 | tf_op jit(solution)/shard_map/ppermute | solution.py:542
  675.7 47.5 %collective-permute-start.46 = (bf16[512,2048]{1,0:T(8,128)(2,1)}, bf16[512,2048]{1,0:T(8,128)(2,1)}, u32[]{:S(2)}, u32[]{:S(2)}) collective-permute-start(bf16[512,2048]{1,0:T(8,128)(2,1)} %add_convert_fusion.9), channel_id=1, source_target_pairs={{0,1},{1,0},{2,3},{3,2},{4,5},{5,4},{6,7},{7,6},{8,9},{9,8},{10,11... | collective-permute-start | bytes 6291464 | tf_op jit(solution)/shard_map/ppermute | solution.py:542
  723.2 30.8 %collective-permute-start.43 = (bf16[512,2048]{1,0:T(8,128)(2,1)}, bf16[512,2048]{1,0:T(8,128)(2,1)}, u32[]{:S(2)}, u32[]{:S(2)}) collective-permute-start(bf16[512,2048]{1,0:T(8,128)(2,1)} %get-tuple-element.220), channel_id=1, source_target_pairs={{0,8},{8,0},{16,24},{24,16},{1,9},{9,1},{17,25},{25,17},{2,10},{10... | collective-permute-start | bytes 6291464 | tf_op jit(solution)/shard_map/ppermute | solution.py:542
  734.3 28.7 %collective-permute-start.47 = (bf16[512,2048]{1,0:T(8,128)(2,1)S(1)}, bf16[512,2048]{1,0:T(8,128)(2,1)}, u32[]{:S(2)}, u32[]{:S(2)}) collective-permute-start(bf16[512,2048]{1,0:T(8,128)(2,1)S(1)} %get-tuple-element.294), channel_id=1, source_target_pairs={{0,8},{8,0},{16,24},{24,16},{1,9},{9,1},{17,25},{25,17},{2,10},{10... | collective-permute-start | bytes 6291464 | tf_op jit(solution)/shard_map/ppermute | solution.py:542
  746.4 92.0 %collective-permute-start.51 = (bf16[2048,1024]{1,0:T(8,128)(2,1)}, bf16[2048,1024]{1,0:T(8,128)(2,1)}, u32[]{:S(2)}, u32[]{:S(2)}) collective-permute-start(bf16[2048,1024]{1,0:T(8,128)(2,1)} %shard_map.479), channel_id=1, source_target_pairs={{0,16},{8,24},{16,0},{24,8},{1,17},{9,25},{17,1},{25,9},{2,18},{10... | collective-permute-start | bytes 12582920 | tf_op jit(solution)/shard_map/ppermute | solution.py:542
  750.3 140.0 %collective-permute-start.86 = (bf16[512,1024]{1,0:T(8,128)(2,1)}, bf16[512,1024]{1,0:T(8,128)(2,1)}, u32[]{:S(2)}, u32[]{:S(2)}) collective-permute-start(bf16[512,1024]{1,0:T(8,128)(2,1)} %add_convert_fusion.13), channel_id=1, source_target_pairs={{0,2},{1,3},{2,0},{3,1},{4,6},{5,7},{6,4},{7,5},{8,10},{9,11},{10,... | collective-permute-start | bytes 3145736 | tf_op jit(solution)/shard_map/ppermute | solution.py:542
  770.6 73.0 %collective-permute-start.50 = (bf16[2,512,256]{2,1,0:T(8,128)(2,1)}, bf16[2,512,256]{2,1,0:T(8,128)(2,1)}, u32[]{:S(2)}, u32[]{:S(2)}) collective-permute-start(bf16[2,512,256]{2,1,0:T(8,128)(2,1)} %get-tuple-element.336), channel_id=1, source_target_pairs={{0,5},{1,4},{2,7},{3,6},{4,1},{5,0},{6,3},{7,2},{8,13},{9,12},{10,... | collective-permute-start | bytes 1572872 | tf_op jit(solution)/shard_map/ppermute | solution.py:572
  771.9 72.9 %collective-permute-start.49 = (bf16[2,512,256]{2,1,0:T(8,128)(2,1)}, bf16[2,512,256]{2,1,0:T(8,128)(2,1)}, u32[]{:S(2)}, u32[]{:S(2)}) collective-permute-start(bf16[2,512,256]{2,1,0:T(8,128)(2,1)} %get-tuple-element.337), channel_id=1, source_target_pairs={{0,1},{1,0},{2,3},{3,2},{4,5},{5,4},{6,7},{7,6},{8,9},{9,8},{10,11... | collective-permute-start | bytes 1572872 | tf_op jit(solution)/shard_map/ppermute | solution.py:542
  772.9 73.0 %collective-permute-start.48 = (bf16[2,512,256]{2,1,0:T(8,128)(2,1)}, bf16[2,512,256]{2,1,0:T(8,128)(2,1)}, u32[]{:S(2)}, u32[]{:S(2)}) collective-permute-start(bf16[2,512,256]{2,1,0:T(8,128)(2,1)} %get-tuple-element.338), channel_id=1, source_target_pairs={{0,4},{4,0},{1,5},{5,1},{2,6},{6,2},{3,7},{7,3},{8,12},{12,8},{9,1... | collective-permute-start | bytes 1572872 | tf_op jit(solution)/shard_map/ppermute | solution.py:542
  838.4 50.7 %collective-permute-start.55 = (bf16[1024,1024]{1,0:T(8,128)(2,1)}, bf16[1024,1024]{1,0:T(8,128)(2,1)S(1)}, u32[]{:S(2)}, u32[]{:S(2)}) collective-permute-start(bf16[1024,1024]{1,0:T(8,128)(2,1)} %get-tuple-element.300), channel_id=1, source_target_pairs={{0,16},{8,24},{16,0},{24,8},{1,17},{9,25},{17,1},{25,9},{2,18},{10... | collective-permute-start | bytes 6291464 | tf_op jit(solution)/shard_map/ppermute | solution.py:542
  843.6 69.8 %collective-permute-start.81 = (bf16[512,2048]{1,0:T(8,128)(2,1)}, bf16[512,2048]{1,0:T(8,128)(2,1)}, u32[]{:S(2)}, u32[]{:S(2)}) collective-permute-start(bf16[512,2048]{1,0:T(8,128)(2,1)} %pad_maximum_fusion.16), channel_id=1, source_target_pairs={{0,1},{1,0},{2,3},{3,2},{4,5},{5,4},{6,7},{7,6},{8,9},{9,8},{10,11... | collective-permute-start | bytes 6291464 | tf_op jit(solution)/shard_map/ppermute | solution.py:542
  844.8 72.6 %collective-permute-start.52 = (bf16[1024,1024]{1,0:T(8,128)(2,1)}, bf16[1024,1024]{1,0:T(8,128)(2,1)}, u32[]{:S(2)}, u32[]{:S(2)}) collective-permute-start(bf16[1024,1024]{1,0:T(8,128)(2,1)} %get-tuple-element.299), channel_id=1, source_target_pairs={{0,4},{4,0},{1,5},{5,1},{2,6},{6,2},{3,7},{7,3},{8,12},{12,8},{9,1... | collective-permute-start | bytes 6291464 | tf_op jit(solution)/shard_map/ppermute | solution.py:542
  899.4 78.1 %collective-permute-start.42 = (bf16[512,2048]{1,0:T(8,128)(2,1)}, bf16[512,2048]{1,0:T(8,128)(2,1)}, u32[]{:S(2)}, u32[]{:S(2)}) collective-permute-start(bf16[512,2048]{1,0:T(8,128)(2,1)} %get-tuple-element.216), channel_id=1, source_target_pairs={{0,8},{8,0},{16,24},{24,16},{1,9},{9,1},{17,25},{25,17},{2,10},{10... | collective-permute-start | bytes 6291464 | tf_op jit(solution)/shard_map/ppermute | solution.py:542
  905.5 66.6 %collective-permute-start.44 = (bf16[512,2048]{1,0:T(8,128)(2,1)}, bf16[512,2048]{1,0:T(8,128)(2,1)}, u32[]{:S(2)}, u32[]{:S(2)}) collective-permute-start(bf16[512,2048]{1,0:T(8,128)(2,1)} %add_convert_fusion.8), channel_id=1, source_target_pairs={{0,1},{1,0},{2,3},{3,2},{4,5},{5,4},{6,7},{7,6},{8,9},{9,8},{10,11... | collective-permute-start | bytes 6291464 | tf_op jit(solution)/shard_map/ppermute | solution.py:542
  907.6 140.7 %collective-permute-start.101 = (bf16[512,1024]{1,0:T(8,128)(2,1)}, bf16[512,1024]{1,0:T(8,128)(2,1)}, u32[]{:S(2)}, u32[]{:S(2)}) collective-permute-start(bf16[512,1024]{1,0:T(8,128)(2,1)} %get-tuple-element.285), channel_id=1, source_target_pairs={{0,16},{8,24},{16,0},{24,8},{1,17},{9,25},{17,1},{25,9},{2,18},{10... | collective-permute-start | bytes 3145736 | tf_op jit(solution)/shard_map/ppermute | solution.py:542
  921.1 51.0 %collective-permute-start.59 = (bf16[1024,512]{1,0:T(8,128)(2,1)S(1)}, bf16[1024,512]{1,0:T(8,128)(2,1)S(1)}, u32[]{:S(2)}, u32[]{:S(2)}) collective-permute-start(bf16[1024,512]{1,0:T(8,128)(2,1)S(1)} %slice.626), channel_id=1, source_target_pairs={{0,2},{1,3},{2,0},{3,1},{4,6},{5,7},{6,4},{7,5},{8,10},{9,11},{10,... | collective-permute-start | bytes 3145736 | tf_op jit(solution)/shard_map/ppermute | solution.py:542
  983.7 49.8 %collective-permute-start.74 = (bf16[1024,512]{1,0:T(8,128)(2,1)}, bf16[1024,512]{1,0:T(8,128)(2,1)}, u32[]{:S(2)}, u32[]{:S(2)}) collective-permute-start(bf16[1024,512]{1,0:T(8,128)(2,1)} %slice.679), channel_id=1, source_target_pairs={{0,2},{1,3},{2,0},{3,1},{4,6},{5,7},{6,4},{7,5},{8,10},{9,11},{10,... | collective-permute-start | bytes 3145736 | tf_op jit(solution)/shard_map/ppermute | solution.py:542
  986.2 64.6 %collective-permute-start.99 = (bf16[1024,512]{1,0:T(8,128)(2,1)S(1)}, bf16[1024,512]{1,0:T(8,128)(2,1)}, u32[]{:S(2)}, u32[]{:S(2)}) collective-permute-start(bf16[1024,512]{1,0:T(8,128)(2,1)S(1)} %get-tuple-element.289), channel_id=1, source_target_pairs={{0,16},{8,24},{16,0},{24,8},{1,17},{9,25},{17,1},{25,9},{2,18},{10... | collective-permute-start | bytes 3145736 | tf_op jit(solution)/shard_map/ppermute | solution.py:542
  1008.7 56.9 %collective-permute-start.82 = (bf16[512,1024]{1,0:T(8,128)(2,1)}, bf16[512,1024]{1,0:T(8,128)(2,1)}, u32[]{:S(2)}, u32[]{:S(2)}) collective-permute-start(bf16[512,1024]{1,0:T(8,128)(2,1)} %pad_maximum_fusion.34), channel_id=1, source_target_pairs={{0,4},{4,0},{1,5},{5,1},{2,6},{6,2},{3,7},{7,3},{8,12},{12,8},{9,1... | collective-permute-start | bytes 3145736 | tf_op jit(solution)/shard_map/ppermute | solution.py:542
  1020.3 40.6 %collective-permute-start.66 = (bf16[512,1024]{1,0:T(8,128)(2,1)S(1)}, bf16[512,1024]{1,0:T(8,128)(2,1)}, u32[]{:S(2)}, u32[]{:S(2)}) collective-permute-start(bf16[512,1024]{1,0:T(8,128)(2,1)S(1)} %fusion.38), channel_id=1, source_target_pairs={{0,16},{8,24},{16,0},{24,8},{1,17},{9,25},{17,1},{25,9},{2,18},{10... | collective-permute-start | bytes 3145736 | tf_op jit(solution)/shard_map/ppermute | solution.py:542
  1033.5 44.5 %collective-permute-start.69 = (bf16[768,768]{1,0:T(8,128)(2,1)}, bf16[768,768]{1,0:T(8,128)(2,1)}, u32[]{:S(2)}, u32[]{:S(2)}) collective-permute-start(bf16[768,768]{1,0:T(8,128)(2,1)} %pad_maximum_fusion.25), channel_id=1, source_target_pairs={{0,1},{1,0},{2,3},{3,2},{4,5},{5,4},{6,7},{7,6},{8,9},{9,8},{10,11... | collective-permute-start | bytes 3538952 | tf_op jit(solution)/shard_map/ppermute | solution.py:542
  1050.9 52.4 %collective-permute-start.89 = (bf16[1024,512]{1,0:T(8,128)(2,1)S(1)}, bf16[1024,512]{1,0:T(8,128)(2,1)S(1)}, u32[]{:S(2)}, u32[]{:S(2)}) collective-permute-start(bf16[1024,512]{1,0:T(8,128)(2,1)S(1)} %get-tuple-element.287), channel_id=1, source_target_pairs={{0,16},{8,24},{16,0},{24,8},{1,17},{9,25},{17,1},{25,9},{2,18},{10... | collective-permute-start | bytes 3145736 | tf_op jit(solution)/shard_map/ppermute | solution.py:542
  1060.9 82.0 %collective-permute-start.75 = (bf16[512,2048]{1,0:T(8,128)(2,1)S(1)}, bf16[512,2048]{1,0:T(8,128)(2,1)S(1)}, u32[]{:S(2)}, u32[]{:S(2)}) collective-permute-start(bf16[512,2048]{1,0:T(8,128)(2,1)S(1)} %slice_bitcast_fusion), channel_id=1, source_target_pairs={{0,8},{8,0},{16,24},{24,16},{1,9},{9,1},{17,25},{25,17},{2,10},{10... | collective-permute-start | bytes 6291464 | tf_op jit(solution)/shard_map/ppermute | solution.py:542
  1065.6 98.1 %collective-permute-start.102 = (bf16[2,512,1024]{2,1,0:T(8,128)(2,1)S(1)}, bf16[2,512,1024]{2,1,0:T(8,128)(2,1)S(1)}, u32[]{:S(2)}, u32[]{:S(2)}) collective-permute-start(bf16[2,512,1024]{2,1,0:T(8,128)(2,1)S(1)} %pad_maximum_fusion.22), channel_id=1, source_target_pairs={{0,8},{8,0},{16,24},{24,16},{1,9},{9,1},{17,25},{25,17},{2,10},{10... | collective-permute-start | bytes 6291464 | tf_op jit(solution)/shard_map/ppermute | solution.py:542
  1138.5 50.3 %collective-permute-start.100 = (bf16[2,1024,512]{2,1,0:T(8,128)(2,1)}, bf16[2,1024,512]{2,1,0:T(8,128)(2,1)}, u32[]{:S(2)}, u32[]{:S(2)}) collective-permute-start(bf16[2,1024,512]{2,1,0:T(8,128)(2,1)} %pad_maximum_fusion.21), channel_id=1, source_target_pairs={{0,8},{8,0},{16,24},{24,16},{1,9},{9,1},{17,25},{25,17},{2,10},{10... | collective-permute-start | bytes 6291464 | tf_op jit(solution)/shard_map/ppermute | solution.py:542
  1141.9 142.2 %collective-permute-start.90 = (bf16[2,1024,512]{2,1,0:T(8,128)(2,1)}, bf16[2,1024,512]{2,1,0:T(8,128)(2,1)}, u32[]{:S(2)}, u32[]{:S(2)}) collective-permute-start(bf16[2,1024,512]{2,1,0:T(8,128)(2,1)} %pad_maximum_fusion.17), channel_id=1, source_target_pairs={{0,8},{8,0},{16,24},{24,16},{1,9},{9,1},{17,25},{25,17},{2,10},{10... | collective-permute-start | bytes 6291464 | tf_op jit(solution)/shard_map/ppermute | solution.py:542
  1187.4 73.1 %collective-permute-start.92 = (bf16[1024,128]{1,0:T(8,128)(2,1)}, bf16[1024,128]{1,0:T(8,128)(2,1)}, u32[]{:S(2)}, u32[]{:S(2)}) collective-permute-start(bf16[1024,128]{1,0:T(8,128)(2,1)} %get-tuple-element.404), channel_id=1, source_target_pairs={{0,16},{8,24},{16,0},{24,8},{1,17},{9,25},{17,1},{25,9},{2,18},{10... | collective-permute-start | bytes 786440 | tf_op jit(solution)/shard_map/ppermute | solution.py:542
  1187.7 72.8 %collective-permute-start.94 = (bf16[1024,128]{1,0:T(8,128)(2,1)}, bf16[1024,128]{1,0:T(8,128)(2,1)}, u32[]{:S(2)}, u32[]{:S(2)}) collective-permute-start(bf16[1024,128]{1,0:T(8,128)(2,1)} %get-tuple-element.405), channel_id=1, source_target_pairs={{0,2},{1,3},{2,0},{3,1},{4,6},{5,7},{6,4},{7,5},{8,10},{9,11},{10,... | collective-permute-start | bytes 786440 | tf_op jit(solution)/shard_map/ppermute | solution.py:542
  1193.4 112.7 %collective-permute-start.73 = (bf16[512,1024]{1,0:T(8,128)(2,1)}, bf16[512,1024]{1,0:T(8,128)(2,1)}, u32[]{:S(2)}, u32[]{:S(2)}) collective-permute-start(bf16[512,1024]{1,0:T(8,128)(2,1)} %slice.621), channel_id=1, source_target_pairs={{0,4},{4,0},{1,5},{5,1},{2,6},{6,2},{3,7},{7,3},{8,12},{12,8},{9,1... | collective-permute-start | bytes 3145736 | tf_op jit(solution)/shard_map/ppermute | solution.py:542
  1193.7 112.4 %collective-permute-start.91 = (bf16[512,1024]{1,0:T(8,128)(2,1)}, bf16[512,1024]{1,0:T(8,128)(2,1)}, u32[]{:S(2)}, u32[]{:S(2)}) collective-permute-start(bf16[512,1024]{1,0:T(8,128)(2,1)} %slice.705), channel_id=1, source_target_pairs={{0,4},{4,0},{1,5},{5,1},{2,6},{6,2},{3,7},{7,3},{8,12},{12,8},{9,1... | collective-permute-start | bytes 3145736 | tf_op jit(solution)/shard_map/ppermute | solution.py:542
  1271.6 39.3 %collective-permute-start.96 = (bf16[4,1024,128]{2,1,0:T(8,128)(2,1)S(1)}, bf16[4,1024,128]{2,1,0:T(8,128)(2,1)S(1)}, u32[]{:S(2)}, u32[]{:S(2)}) collective-permute-start(bf16[4,1024,128]{2,1,0:T(8,128)(2,1)S(1)} %pad_maximum_fusion.36), channel_id=1, source_target_pairs={{0,8},{8,0},{16,24},{24,16},{1,9},{9,1},{17,25},{25,17},{2,10},{10... | collective-permute-start | bytes 3145736 | tf_op jit(solution)/shard_map/ppermute | solution.py:542
  (171 other events, 3536.5 us)

commit v3 on v2

--- a/solution.py
+++ b/solution.py
@@ -1385,7 +1385,7 @@
     normed_one, factor_one = rows_norm(x)
     h_own = (normed_one * gains[0]).astype(LOW)
     h_one = [h_own, swap_core(h_own)]
-    h_pair = after(jnp.stack(h_one), pair_x)
+    h_pair = jnp.stack(h_one)
     projected = project(h_pair, in_pieces, cosine, sine)
     pair_x_y = swap_y(after(pair_x, projected))
     packed = jnp.stack(exchange([projected[slot] for slot in range(4)]))
@@ -1519,7 +1519,7 @@
     ][::-1]
     up_kept = weight_grad([after(value, *h_two_parts[0]) for value in h_two], 0, grad_up, half_width)
     up_sum_x = swap_x(up_sent)
-    gate_sum_y = swap_y(after(gate_sent, down_y))
+    gate_got_y = swap_y(after(gate_sent[:, :part_rows], down_y))
     down_first_x, down_second_y = swap_x(down_first[1]), swap_y(down_second[1])
 
     grad_mid_part, gain_two_part = rows_norm_back(
@@ -1530,6 +1530,9 @@
     grad_attended = [(RESID * grad_mid).astype(LOW)]
     gate_kept = weight_grad(
         [after(value, grad_attended[0]) for value in h_two], 0, grad_gate[:1], MODEL_WIDTH
+    )
+    gate_got_x = swap_x(
+        jnp.concatenate([gate_kept[half_width:, part_rows:], gate_sent[half_width:, part_rows:]])
     )
     layer_sum = sum_four((down_parts[0], beyond_of(down_parts[1])))
     grad_attended.append(swap_core(grad_attended[0]))
@@ -1544,10 +1547,10 @@
         for half in range(2)
     ]
     out_near = swap_near(jnp.concatenate([values[4 * LANES :] for values in out_local], axis=1))
-    down_first_x, down_second_y, up_sum_x, gate_sum_y = (
-        after(value, gate_kept)
-        for value in (down_first_x, down_second_y, up_sum_x, gate_sum_y)
-    )
+    down_first_x, down_second_y, up_sum_x = (
+        after(value, gate_kept) for value in (down_first_x, down_second_y, up_sum_x)
+    )
+    gate_got_y, gate_got_x = after(gate_got_y, *out_local), after(gate_got_x, *out_local)
     down_part = add_low(down_first[0], down_first_x)
     down_far_sum = swap_far(add_low(down_second[0], down_second_y))
     size = up_kept.shape[1] // 2
@@ -1555,15 +1558,12 @@
         add_low(up_kept[:, at * size : (at + 1) * size], up_sum_x[:, at * size : (at + 1) * size])
         for at in range(2)
     ]
-    gate_kept = [
-        add_low(
-            gate_kept[at * half_width : (at + 1) * half_width],
-            gate_sum_y[at * half_width : (at + 1) * half_width],
-        )
-        for at in range(2)
-    ]
-    gate_sum_x = swap_x(gate_kept[1])
+    gate_first = add_low(gate_kept[:half_width, :part_rows], gate_got_y[:half_width])
+    gate_second = add_low(gate_kept[:half_width, part_rows:], gate_got_x[:half_width])
+    gate_first_x = swap_x(add_low(gate_kept[half_width:, :part_rows], gate_got_y[half_width:]))
+    gate_second_y = swap_y(add_low(gate_sent[:half_width, part_rows:], gate_got_x[half_width:]))
     up_sum_y = swap_y(up_kept[1])
+
     def sequence_grad(sequence, *others):
         return attend_grad(
             sequence,
@@ -1576,21 +1576,24 @@
             sine,
         )
 
-    packed_first = sequence_grad(0, down_part, *up_kept, *gate_kept)
-    up_sum_y, gate_sum_x, down_far_sum, out_near = (
-        after(value, packed_first) for value in (up_sum_y, gate_sum_x, down_far_sum, out_near)
-    )
-    gate_part = add_low(gate_kept[0], gate_sum_x)
+    packed_first = sequence_grad(0, down_part, *up_kept, gate_first, gate_second)
+    gate_first_x, gate_second_y, down_far_sum, out_near = (
+        after(value, packed_first)
+        for value in (gate_first_x, gate_second_y, down_far_sum, out_near)
+    )
+    gate_first = add_low(gate_first, gate_first_x)
+    gate_far_sum = swap_far(add_low(gate_second, gate_second_y))
+    in_first = tokens_of(packed_first)
+    packed_second = sequence_grad(1, gate_first)
+    gate_far_sum, in_first, up_sum_y = (
+        after(value, packed_second) for value in (gate_far_sum, in_first, up_sum_y)
+    )
     up_part = add_low(up_kept[0], up_sum_y)
-    gate_far_sum = swap_far(gate_part[:, units // 2 :])
-    in_first = tokens_of(packed_first)
-    packed_second = sequence_grad(1, gate_part, up_part)
-    gate_far_sum, in_first = after(gate_far_sum, packed_second), after(in_first, packed_second)
     up_far_sum = swap_far(after(up_part[:, units // 2 :], gate_far_sum))
     layer_part = (residual + RESID * layer_sum(packed_second)).astype(LOW)
-    in_back = jnp.stack([in_first, tokens_of(after(packed_second, gate_far_sum))])
+    in_back = jnp.stack([in_first, tokens_of(after(packed_second, gate_far_sum, up_part))])
     down_piece = add_low(down_part, down_far_sum)
-    gate_piece = add_low(gate_part[:, : units // 2], gate_far_sum)
+    gate_piece = add_low(gate_first, gate_far_sum)
     up_piece = add_low(up_part[:, : units // 2], up_far_sum)
     in_grads = [in_back[0], in_back[1]]
     out_kept = add_low(

time: 1330 us -> 1370 us (1.030)
  waiting for transfers between devices: 346 us -> 407 us
  starting transfers between devices: 144 us -> 117 us
    ppermute x98 -> x100, waiting for transfers between devices: 316 us -> 363 us  [swap(): lax.ppermute(values, axis, [(place, place ^ bit) for place in range(size)])]
    ppermute x98 -> x100, starting transfers between devices: 136 us -> 112 us  [swap(): lax.ppermute(values, axis, [(place, place ^ bit) for place in range(size)])]
    ppermute x5, waiting for transfers between devices: 30.4 us -> 44.4 us  [swap_corner(): return lax.ppermute(values, ('row', 'col'), pairs)]
    unnamed x274 -> x254, local copies, waits for them, and re-layouts: 35.3 us -> 31.6 us
    convert_element_type x23 -> x25, other arithmetic: 46.7 us -> 49.9 us  [add_low(): return (kept.astype(WIDE) + got.astype(WIDE)).astype(LOW)]
  transfers between devices with their start and end apart: 103 -> 105, of which waited for: 31 -> 40; matrix products, arithmetic and copies ran while one was open for 18% -> 17% of each run, Pallas kernels for 35% -> 34%
where the time goes in v3:
time: 1370 us; the launch traced here: 1360 us
  Pallas kernels  543 us (40%)
  waiting for transfers between devices  407 us (30%)
  other arithmetic  162 us (12%)
  starting transfers between devices  117 us (9%)
  local copies, waits for them, and re-layouts  94.1 us (7%)
  blocking collectives  17.2 us (1%)
    ppermute x100, waiting for transfers between devices, swap(): lax.ppermute(values, axis, [(place, place ^ bit) for place in range(size)])  363 us
    ppermute x100, starting transfers between devices, swap(): lax.ppermute(values, axis, [(place, place ^ bit) for place in range(size)])  112 us
    pallas_call x10, Pallas kernels, weight_grad(): pl.pallas_call(kernel, grid=(columns // block,), in_specs=[pl.BlockSpec((...  98.3 us
    pallas_call x2, Pallas kernels, attend_grad(): pl.pallas_call(functools.partial(attend_back_kernel, sequence), grid_spec...  85.4 us
    pallas_call x5, Pallas kernels, step_weight(): pl.pallas_call(step_kernel, grid_spec=pltpu.PrefetchScalarGridSpec(num_sc...  72 us
    pallas_call x1, Pallas kernels, attend(): pl.pallas_call(attend_kernel, grid_spec=pltpu.PrefetchScalarGridSpec(num_...  67.1 us
    pallas_call x4, Pallas kernels, hidden_units(): pl.pallas_call(hidden_kernel, grid=(tokens // block,), in_specs=[pl.Block...  56.7 us
    pallas_call x2, Pallas kernels, normed_back(): pl.pallas_call(normed_back_kernel, grid=(tokens // block,), in_specs=[lef...  53.5 us
  transfers between devices with their start and end apart: 105, of which 40 were waited for; matrix products, arithmetic and copies ran while one was open for 17% of the time, Pallas kernels for 34%

profile of v3, /device:TPU:1, one launch (start us, length us, event | category | flops | bytes accessed | tf_op | source)
XLA Modules:
  0.0 1362.5 jit_solution(1471035185463615562)
XLA Ops:
  36.7 20.5 %collective-permute-done = bf16[512,1024]{1,0:T(8,128)(2,1)} collective-permute-done((bf16[512,1024]{1,0:T(8,128)(2,1)}, bf16[512,1024]{1,0:T(8,128)(2,1)}, u32[]{:S(2)}, u32[]{:S(2)}) %collective-permute-start) | collective-permute-done | bytes 1048608 | tf_op jit(solution)/shard_map/ppermute | solution.py:542
  57.2 11.1 collective-permute-done.3
  82.2 5.5 collective-permute-done.8
  95.4 17.2 %collective-permute-done.14 = bf16[256,1024]{1,0:T(8,128)(2,1)S(1)} collective-permute-done((bf16[256,1024]{1,0:T(8,128)(2,1)S(1)}, bf16[256,1024]{1,0:T(8,128)(2,1)S(1)}, u32[]{:S(2)}, u32[]{:S(2)}) %collective-permute-start.14) | collective-permute-done | bytes 524320 | tf_op jit(solution)/shard_map/ppermute | solution.py:542
  118.5 16.0 %shard_map.466 = bf16[4,2,512,384]{3,2,1,0:T(8,128)(2,1)} custom-call(bf16[2,512,2048]{2,1,0:T(8,128)(2,1)} %pad_maximum_fusion.normed_ref, bf16[4,1024,256]{2,1,0:T(8,128)(2,1)} %copy-done.62, bf16[4,1024,128]{2,1,0:T(8,128)(2,1)S(1)} %maximum_maximum_fusion.1.kv_ref, bf16[4,1024,128]{2,1,0:T(8,128)(2,1)S(1)} %constant_dynamic-update-slice_fusion.4.first_ref, ...), custom_call_target="tpu_custom_call" | custom-call | flops 3221225472 | bytes 8388608 | tf_op jit(solution)/shard_map/pallas_call | solution.py:841
  142.3 16.7 %collective-permute-done.18 = bf16[2,256,1024]{2,1,0:T(8,128)(2,1)} collective-permute-done((bf16[2,256,1024]{2,1,0:T(8,128)(2,1)S(1)}, bf16[2,256,1024]{2,1,0:T(8,128)(2,1)}, u32[]{:S(2)}, u32[]{:S(2)}) %collective-permute-start.18) | collective-permute-done | bytes 1048608 | tf_op jit(solution)/shard_map/ppermute | solution.py:542
  165.9 30.5 %collective-permute-done.13 = bf16[2,512,384]{2,1,0:T(8,128)(2,1)} collective-permute-done((bf16[2,512,384]{2,1,0:T(8,128)(2,1)}, bf16[2,512,384]{2,1,0:T(8,128)(2,1)}, u32[]{:S(2)}, u32[]{:S(2)}) %collective-permute-start.13) | collective-permute-done | bytes 786464 | tf_op jit(solution)/shard_map/ppermute | solution.py:572
  196.4 19.5 %collective-permute-done.12 = bf16[2,512,384]{2,1,0:T(8,128)(2,1)} collective-permute-done((bf16[2,512,384]{2,1,0:T(8,128)(2,1)}, bf16[2,512,384]{2,1,0:T(8,128)(2,1)}, u32[]{:S(2)}, u32[]{:S(2)}) %collective-permute-start.12) | collective-permute-done | bytes 786464 | tf_op jit(solution)/shard_map/ppermute | solution.py:542
  222.1 67.1 %shard_map.467 = (bf16[4,2,512,256]{3,2,1,0:T(8,128)(2,1)S(1)}, f32[4,2,8,512]{3,2,1,0:T(8,128)S(1)}) custom-call(s32[3]{0:T(128)S(1)} %pad_add_fusion.place_ref, bf16[4,2,512,384]{3,2,1,0:T(8,128)(2,1)S(1)} %pad_maximum_fusion.6.q_ref.kv_ref, bf16[4,2,512,384]{3,2,1,0:T(8,128)(2,1)S(1)} %pad_maximum_fusion.6.q_ref.kv_ref), custom_call_target="tpu_custom_call" | custom-call | flops 85899345920 | bytes 1048576 | tf_op jit(solution)/shard_map/pallas_call | solution.py:970
  293.9 19.2 %collective-permute-done.26 = bf16[4,128,1024]{2,1,0:T(8,128)(2,1)S(1)} collective-permute-done((bf16[4,128,1024]{2,1,0:T(8,128)(2,1)S(1)}, bf16[4,128,1024]{2,1,0:T(8,128)(2,1)S(1)}, u32[]{:S(2)}, u32[]{:S(2)}) %collective-permute-start.26) | collective-permute-done | bytes 1048608 | tf_op jit(solution)/shard_map/ppermute | solution.py:542
  340.5 14.1 %shard_map.468 = (bf16[1024,1024]{1,0:T(8,128)(2,1)S(1)}, bf16[1024,1024]{1,0:T(8,128)(2,1)S(1)}, bf16[1024,1024]{1,0:T(8,128)(2,1)}) custom-call(bf16[1024,2048]{1,0:T(8,128)(2,1)} %pad_maximum_fusion.1.normed_ref.refs_0_, bf16[2,1024,512]{2,1,0:T(8,128)(2,1)} %pad_maximum_fusion.9.refs_0_, bf16[2,1024,512]{2,1,0:T(8,128)(2,1)} %collective-permute-done.15.refs_1_, ...), custom_call_target="tpu_custom_call" | custom-call | flops 8589934592 | bytes 18874368 | tf_op jit(solution)/shard_map/pallas_call | solution.py:667
  354.6 24.4 %collective-permute-done.32 = bf16[512,2048]{1,0:T(8,128)(2,1)} collective-permute-done((bf16[512,2048]{1,0:T(8,128)(2,1)S(1)}, bf16[512,2048]{1,0:T(8,128)(2,1)}, u32[]{:S(2)}, u32[]{:S(2)}) %collective-permute-start.32) | collective-permute-done | bytes 2097184 | tf_op jit(solution)/shard_map/ppermute | solution.py:542
  385.9 19.8 %collective-permute-done.36 = bf16[2,512,1024]{2,1,0:T(8,128)(2,1)} collective-permute-done((bf16[2,512,1024]{2,1,0:T(8,128)(2,1)S(1)}, bf16[2,512,1024]{2,1,0:T(8,128)(2,1)}, u32[]{:S(2)}, u32[]{:S(2)}) %collective-permute-start.36) | collective-permute-done | bytes 2097184 | tf_op jit(solution)/shard_map/ppermute | solution.py:542
  415.0 14.5 %shard_map.471 = (bf16[1024,1024]{1,0:T(8,128)(2,1)S(1)}, bf16[1024,1024]{1,0:T(8,128)(2,1)S(1)}, bf16[1024,1024]{1,0:T(8,128)(2,1)}) custom-call(bf16[1024,2048]{1,0:T(8,128)(2,1)} %constant_dynamic-update-slice_fusion.8.normed_ref.refs_1_, bf16[2,1024,512]{2,1,0:T(8,128)(2,1)} %pad_maximum_fusion.9.refs_0_, ...), custom_call_target="tpu_custom_call" | custom-call | flops 8589934592 | bytes 18874368 | tf_op jit(solution)/shard_map/pallas_call | solution.py:667
  431.9 14.1 %shard_map.469 = (bf16[1024,1024]{1,0:T(8,128)(2,1)S(1)}, bf16[1024,1024]{1,0:T(8,128)(2,1)S(1)}, bf16[1024,1024]{1,0:T(8,128)(2,1)}) custom-call(bf16[1024,2048]{1,0:T(8,128)(2,1)} %pad_maximum_fusion.1.normed_ref.refs_0_, bf16[2,1024,512]{2,1,0:T(8,128)(2,1)} %pad_maximum_fusion.12.refs_0_.refs_4_, bf16[2,1024,512]{2,1,0:T(8,128)(2,1)} %copy-done.120, ...), custom_call_target="tpu_custom_call" | custom-call | flops 8589934592 | bytes 18874368 | tf_op jit(solution)/shard_map/pallas_call | solution.py:667
  447.3 5.6 pad_maximum_fusion.2.refs_2_.grad_ref
  452.9 14.1 %shard_map.470 = (bf16[1024,1024]{1,0:T(8,128)(2,1)S(1)}, bf16[1024,1024]{1,0:T(8,128)(2,1)S(1)}, bf16[1024,1024]{1,0:T(8,128)(2,1)}) custom-call(bf16[1024,2048]{1,0:T(8,128)(2,1)} %constant_dynamic-update-slice_fusion.8.normed_ref.refs_1_, bf16[2,1024,512]{2,1,0:T(8,128)(2,1)} %pad_maximum_fusion.12.refs_0_.refs_4_, bf16[2,1024,512]{2,1,0:T(8,128)(2,1)} %copy-done.120, ...), custom_call_target="tpu_custom_call" | custom-call | flops 8589934592 | bytes 18874368 | tf_op jit(solution)/shard_map/pallas_call | solution.py:667
  475.5 14.0 %shard_map.473 = bf16[1024,2048]{1,0:T(8,128)(2,1)} custom-call(bf16[1024,1024]{1,0:T(8,128)(2,1)S(1)} %get-tuple-element.213.refs_0_.h0, bf16[1024,1024]{1,0:T(8,128)(2,1)S(1)} %copy-done.50, bf16[1024,2048]{1,0:T(8,128)(2,1)} %pad_maximum_fusion.2.refs_2_.grad_ref, bf16[1024,2048]{1,0:T(8,128)(2,1)} %constant_dynamic-update-slice_fusion.10.refs_3_.grad_ref), custom_call_target="tpu_custom_call" | custom-call | flops 8589934592 | bytes 16777216 | tf_op jit(solution)/shard_map/pallas_call | solution.py:798
  491.4 14.2 %shard_map.472 = bf16[1024,2048]{1,0:T(8,128)(2,1)} custom-call(bf16[1024,1024]{1,0:T(8,128)(2,1)S(1)} %get-tuple-element.214.refs_0_.h1, bf16[1024,1024]{1,0:T(8,128)(2,1)S(1)} %copy-done.52, bf16[1024,2048]{1,0:T(8,128)(2,1)} %pad_maximum_fusion.2.refs_2_.grad_ref, bf16[1024,2048]{1,0:T(8,128)(2,1)} %constant_dynamic-update-slice_fusion.10.refs_3_.grad_ref), custom_call_target="tpu_custom_call" | custom-call | flops 8589934592 | bytes 16777216 | tf_op jit(solution)/shard_map/pallas_call | solution.py:798
  511.8 10.1 shard_map.477
  521.9 9.5 shard_map.476
  533.0 12.0 shard_map.479
  545.0 9.5 shard_map.475
  554.6 9.5 shard_map.474
  565.7 13.3 shard_map.478
  581.8 26.8 %shard_map.480 = (bf16[512,2048]{1,0:T(8,128)(2,1)S(1)}, bf16[512,2048]{1,0:T(8,128)(2,1)}) custom-call(bf16[1024,1024]{1,0:T(8,128)(2,1)} %get-tuple-element.199.a0.refs_3_, bf16[1024,1024]{1,0:T(8,128)(2,1)} %get-tuple-element.200.refs_3_.a1, bf16[1024,1024]{1,0:T(8,128)(2,1)} %get-tuple-element.201.refs_3_.b0, ...), custom_call_target="tpu_custom_call" | custom-call | flops 17179869184 | bytes 29360128 | tf_op jit(solution)/shard_map/pallas_call | solution.py:770
  617.1 11.6 collective-permute-done.41
  641.1 26.7 %shard_map.481 = (bf16[512,2048]{1,0:T(8,128)(2,1)S(1)}, bf16[512,2048]{1,0:T(8,128)(2,1)}) custom-call(bf16[1024,1024]{1,0:T(8,128)(2,1)} %get-tuple-element.207.a0.refs_2_, bf16[1024,1024]{1,0:T(8,128)(2,1)} %get-tuple-element.208.refs_2_.a1, bf16[1024,1024]{1,0:T(8,128)(2,1)} %get-tuple-element.209.refs_2_.b0, ...), custom_call_target="tpu_custom_call" | custom-call | flops 17179869184 | bytes 29360128 | tf_op jit(solution)/shard_map/pallas_call | solution.py:770
  672.3 13.5 shard_map.484
  685.8 13.6 shard_map.483
  699.4 14.2 %shard_map.482 = (bf16[512,2048]{1,0:T(8,128)(2,1)}, bf16[512,2048]{1,0:T(8,128)(2,1)}) custom-call(bf16[1024,1024]{1,0:T(8,128)(2,1)} %copy-done.47, bf16[1024,1024]{1,0:T(8,128)(2,1)} %copy-done.48, bf16[512,1024]{1,0:T(8,128)(2,1)S(1)} %get-tuple-element.164.d0.refs_0_, bf16[512,1024]{1,0:T(8,128)(2,1)S(1)} %copy-done.25, ...), custom_call_target="tpu_custom_call" | custom-call | flops 8589934592 | bytes 16777216 | tf_op jit(solution)/shard_map/pallas_call | solution.py:700
  723.1 5.5 multiply_convert_fusion
  728.6 12.2 shard_map.485
  754.8 4.8 add_convert_fusion.3
  768.7 22.1 %collective-permute-done.55 = bf16[2048,512]{1,0:T(8,128)(2,1)} collective-permute-done((bf16[2048,512]{1,0:T(8,128)(2,1)}, bf16[2048,512]{1,0:T(8,128)(2,1)}, u32[]{:S(2)}, u32[]{:S(2)}) %collective-permute-start.55) | collective-permute-done | bytes 2097184 | tf_op jit(solution)/shard_map/ppermute | solution.py:542
  790.8 7.4 fusion.29
  811.8 7.0 collective-permute-done.50
  818.8 11.1 collective-permute-done.49
  834.7 42.4 %shard_map.488 = bf16[4,512,384]{2,1,0:T(8,128)(2,1)S(1)} custom-call(s32[3]{0:T(128)S(1)} %copy-done.33, bf16[4,2,512,384]{3,2,1,0:T(8,128)(2,1)} %copy-done.15, bf16[4,2,512,384]{3,2,1,0:T(8,128)(2,1)} %copy-done.15, bf16[4,2,512,256]{3,2,1,0:T(8,128)(2,1)S(1)} %copy-done.19, bf16[4,2,512,256]{3,2,1,0:T(8,128)(2,1)} %pad_maximum_fusion.15.do_ref, ...), custom_call_target="tpu_custom_call" | custom-call | flops 107374182400 | bytes 1048576 | tf_op jit(solution)/shard_map/pallas_call | solution.py:1076
  889.1 7.6 collective-permute-done.57
  902.0 43.0 %shard_map.489 = bf16[4,512,384]{2,1,0:T(8,128)(2,1)S(1)} custom-call(s32[3]{0:T(128)S(1)} %copy-done.33, bf16[4,2,512,384]{3,2,1,0:T(8,128)(2,1)} %copy-done.15, bf16[4,2,512,384]{3,2,1,0:T(8,128)(2,1)} %copy-done.15, bf16[4,2,512,256]{3,2,1,0:T(8,128)(2,1)S(1)} %copy-done.19, bf16[4,2,512,256]{3,2,1,0:T(8,128)(2,1)} %pad_maximum_fusion.15.do_ref, ...), custom_call_target="tpu_custom_call" | custom-call | flops 107374182400 | bytes 1048576 | tf_op jit(solution)/shard_map/pallas_call | solution.py:1076
  945.0 19.0 %collective-permute-done.59 = bf16[1024,512]{1,0:T(8,128)(2,1)} collective-permute-done((bf16[1024,512]{1,0:T(8,128)(2,1)}, bf16[1024,512]{1,0:T(8,128)(2,1)}, u32[]{:S(2)}, u32[]{:S(2)}) %collective-permute-start.59) | collective-permute-done | bytes 1048608 | tf_op jit(solution)/shard_map/ppermute | solution.py:542
  964.8 4.6 add_convert_fusion.2
  981.2 14.4 %collective-permute-done.83 = bf16[512,2048]{1,0:T(8,128)(2,1)} collective-permute-done((bf16[512,2048]{1,0:T(8,128)(2,1)}, bf16[512,2048]{1,0:T(8,128)(2,1)}, u32[]{:S(2)}, u32[]{:S(2)}) %collective-permute-start.83) | collective-permute-done | bytes 2097184 | tf_op jit(solution)/shard_map/ppermute | solution.py:542
  998.1 23.1 %collective-permute-done.60 = bf16[1024,512]{1,0:T(8,128)(2,1)S(1)} collective-permute-done((bf16[1024,512]{1,0:T(8,128)(2,1)S(1)}, bf16[1024,512]{1,0:T(8,128)(2,1)S(1)}, u32[]{:S(2)}, u32[]{:S(2)}) %collective-permute-start.60) | collective-permute-done | bytes 1048608 | tf_op jit(solution)/shard_map/ppermute | solution.py:542
  1033.0 13.7 %collective-permute-done.63 = bf16[512,384]{1,0:T(8,128)(2,1)S(1)} collective-permute-done((bf16[512,384]{1,0:T(8,128)(2,1)S(1)}, bf16[512,384]{1,0:T(8,128)(2,1)S(1)}, u32[]{:S(2)}, u32[]{:S(2)}) %collective-permute-start.63) | collective-permute-done | bytes 393248 | tf_op jit(solution)/shard_map/ppermute | solution.py:542
  1048.8 5.9 shard_map.491
  1059.9 5.9 shard_map.490
  1075.4 14.9 %shard_map.492 = bf16[2,512,2048]{2,1,0:T(8,128)(2,1)} custom-call(bf16[2,512,1536]{2,1,0:T(8,128)(2,1)} %pad_maximum_fusion.7.grad_ref, bf16[4,1024,256]{2,1,0:T(8,128)(2,1)} %copy-done.62, bf16[4,1024,128]{2,1,0:T(8,128)(2,1)S(1)} %maximum_maximum_fusion.1.kv_ref, bf16[4,1024,128]{2,1,0:T(8,128)(2,1)S(1)} %copy-done.5, ...), custom_call_target="tpu_custom_call" | custom-call | flops 3221225472 | bytes 8388608 | tf_op jit(solution)/shard_map/pallas_call | solution.py:879
  1099.1 6.8 collective-permute-start.77
  1118.8 18.3 %collective-permute-done.85 = bf16[256,1024]{1,0:T(8,128)(2,1)S(1)} collective-permute-done((bf16[256,1024]{1,0:T(8,128)(2,1)S(1)}, bf16[256,1024]{1,0:T(8,128)(2,1)S(1)}, u32[]{:S(2)}, u32[]{:S(2)}) %collective-permute-start.85) | collective-permute-done | bytes 524320 | tf_op jit(solution)/shard_map/ppermute | solution.py:542
  1140.7 9.1 collective-permute-done.72
  1150.3 7.0 collective-permute-done.86
  1160.0 10.5 collective-permute-done.99
  1170.5 6.5 collective-permute-start.102
  1202.2 9.3 collective-permute-done.82
  1230.7 17.2 %psum.7 = f32[]{:T(128)} all-reduce(f32[]{:T(128)} %bitcast.67), channel_id=1, replica_groups=mesh['dp'=4,'row'=2,'col'=4] {'row','col'}, use_global_device_ids=true, to_apply=%region_12.13 | all-reduce | flops 1 | bytes 8 | tf_op jit(solution)/shard_map/psum | solution.py:1706
  1250.2 5.8 shard_map.496
  1256.0 20.1 %shard_map.498 = (f32[2048,1024]{1,0:T(8,128)}, f32[2048,1024]{1,0:T(8,128)}, f32[2048,1024]{1,0:T(8,128)}) custom-call(s32[1]{0:T(128)} %bitcast.58.spot_ref, f32[1,1]{1,0:T(1,128)} %bitcast.68.factor_ref, bf16[4,512,1024]{2,1,0:T(8,128)(2,1)S(1)} %copy-done, f32[2048,1024]{1,0:T(8,128)} %weight_ref.9, f32[2048,1024]{1,0:T(8,128)} %moment_ref.9, ...), custom_call_target="tpu_custom_call" | custom-call | flops 25165824 | bytes 54525952 | tf_op jit(solution)/shard_map/pallas_call | solution.py:1137
  1276.1 20.0 %shard_map.497 = (f32[1024,2048]{1,0:T(8,128)}, f32[1024,2048]{1,0:T(8,128)}, f32[1024,2048]{1,0:T(8,128)}) custom-call(s32[1]{0:T(128)} %bitcast.58.spot_ref, f32[1,1]{1,0:T(1,128)} %bitcast.68.factor_ref, bf16[4,1024,512]{2,1,0:T(8,128)(2,1)S(1)} %copy-done.1, f32[1024,2048]{1,0:T(8,128)} %weight_ref.8, f32[1024,2048]{1,0:T(8,128)} %moment_ref.8, ...), custom_call_target="tpu_custom_call" | custom-call | flops 25165824 | bytes 54525952 | tf_op jit(solution)/shard_map/pallas_call | solution.py:1137
  1307.1 5.6 collective-permute-start.98
  1313.8 5.9 shard_map.494
  1321.6 20.1 %shard_map.493 = (f32[1024,2048]{1,0:T(8,128)}, f32[1024,2048]{1,0:T(8,128)}, f32[1024,2048]{1,0:T(8,128)}) custom-call(s32[1]{0:T(128)} %bitcast.58.spot_ref, f32[1,1]{1,0:T(1,128)} %bitcast.68.factor_ref, bf16[4,1024,512]{2,1,0:T(8,128)(2,1)S(1)} %pad_maximum_fusion.3.grad_ref, f32[1024,2048]{1,0:T(8,128)} %weight_ref.5, f32[1024,2048]{1,0:T(8,128)} %moment_ref.5, ...), custom_call_target="tpu_custom_call" | custom-call | flops 25165824 | bytes 54525952 | tf_op jit(solution)/shard_map/pallas_call | solution.py:1137
  1348.5 12.4 shard_map.495
  (620 shorter events, 385.8 us)
Async XLA Ops:
  0.7 34.6 %collective-permute-start.5 = (f32[2,1024]{1,0:T(2,128)}, f32[2,1024]{1,0:T(2,128)S(1)}, u32[]{:S(2)}, u32[]{:S(2)}) collective-permute-start(f32[2,1024]{1,0:T(2,128)} %param.37), channel_id=1, source_target_pairs={{0,4},{4,0},{1,5},{5,1},{2,6},{6,2},{3,7},{7,3},{8,12},{12,8},{9,1... | collective-permute-start | bytes 24584 | tf_op jit(solution)/shard_map/ppermute | solution.py:542
  4.9 25.2 %collective-permute-start.1 = (bf16[1024,256]{1,0:T(8,128)(2,1)}, bf16[1024,256]{1,0:T(8,128)(2,1)}, u32[]{:S(2)}, u32[]{:S(2)}) collective-permute-start(bf16[1024,256]{1,0:T(8,128)(2,1)} %pad_maximum_fusion.41), channel_id=1, source_target_pairs={{0,2},{1,3},{2,0},{3,1},{4,6},{5,7},{6,4},{7,5},{8,10},{9,11},{10,... | collective-permute-start | bytes 1572872 | tf_op jit(solution)/shard_map/ppermute | solution.py:542
  14.1 43.1 %collective-permute-start = (bf16[512,1024]{1,0:T(8,128)(2,1)}, bf16[512,1024]{1,0:T(8,128)(2,1)}, u32[]{:S(2)}, u32[]{:S(2)}) collective-permute-start(bf16[512,1024]{1,0:T(8,128)(2,1)} %get-tuple-element.354), channel_id=1, source_target_pairs={{0,4},{4,0},{1,5},{5,1},{2,6},{6,2},{3,7},{7,3},{8,12},{12,8},{9,1... | collective-permute-start | bytes 3145736 | tf_op jit(solution)/shard_map/ppermute | solution.py:542
  34.7 33.6 %collective-permute-start.3 = (bf16[2,1024,128]{2,1,0:T(8,128)(2,1)S(1)}, bf16[2,1024,128]{2,1,0:T(8,128)(2,1)S(1)}, u32[]{:S(2)}, u32[]{:S(2)}) collective-permute-start(bf16[2,1024,128]{2,1,0:T(8,128)(2,1)S(1)} %pad_maximum_fusion.42), channel_id=1, source_target_pairs={{0,4},{4,0},{1,5},{5,1},{2,6},{6,2},{3,7},{7,3},{8,12},{12,8},{9,1... | collective-permute-start | bytes 1572872 | tf_op jit(solution)/shard_map/ppermute | solution.py:542
  35.3 38.7 %collective-permute-start.7 = (bf16[2,1024,256]{2,1,0:T(8,128)(2,1)S(1)}, bf16[2,1024,256]{2,1,0:T(8,128)(2,1)S(1)}, u32[]{:S(2)}, u32[]{:S(2)}) collective-permute-start(bf16[2,1024,256]{2,1,0:T(8,128)(2,1)S(1)} %pad_maximum_fusion.28), channel_id=1, source_target_pairs={{0,1},{1,0},{2,3},{3,2},{4,5},{5,4},{6,7},{7,6},{8,9},{9,8},{10,11... | collective-permute-start | bytes 3145736 | tf_op jit(solution)/shard_map/ppermute | solution.py:542
  71.8 43.8 %collective-permute-start.6 = (bf16[512,2048]{1,0:T(8,128)(2,1)S(1)}, bf16[512,2048]{1,0:T(8,128)(2,1)S(1)}, u32[]{:S(2)}, u32[]{:S(2)}) collective-permute-start(bf16[512,2048]{1,0:T(8,128)(2,1)S(1)} %fusion.5.refs_0_), channel_id=1, source_target_pairs={{0,8},{8,0},{16,24},{24,16},{1,9},{9,1},{17,25},{25,17},{2,10},{10... | collective-permute-start | bytes 6291464 | tf_op jit(solution)/shard_map/ppermute | solution.py:542
  80.5 54.1 %collective-permute-start.16 = (bf16[2,1024,512]{2,1,0:T(8,128)(2,1)}, bf16[2,1024,512]{2,1,0:T(8,128)(2,1)}, u32[]{:S(2)}, u32[]{:S(2)}) collective-permute-start(bf16[2,1024,512]{2,1,0:T(8,128)(2,1)} %pad_maximum_fusion.9.refs_0_), channel_id=1, source_target_pairs={{0,4},{4,0},{1,5},{5,1},{2,6},{6,2},{3,7},{7,3},{8,12},{12,8},{9,1... | collective-permute-start | bytes 6291464 | tf_op jit(solution)/shard_map/ppermute | solution.py:542
  113.2 45.9 %collective-permute-start.18 = (bf16[2,256,1024]{2,1,0:T(8,128)(2,1)S(1)}, bf16[2,256,1024]{2,1,0:T(8,128)(2,1)}, u32[]{:S(2)}, u32[]{:S(2)}) collective-permute-start(bf16[2,256,1024]{2,1,0:T(8,128)(2,1)S(1)} %pad_maximum_fusion.32), channel_id=1, source_target_pairs={{0,1},{1,0},{2,3},{3,2},{4,5},{5,4},{6,7},{7,6},{8,9},{9,8},{10,11... | collective-permute-start | bytes 3145736 | tf_op jit(solution)/shard_map/ppermute | solution.py:542
  113.2 104.5 %collective-permute-start.15 = (bf16[2,1024,512]{2,1,0:T(8,128)(2,1)}, bf16[2,1024,512]{2,1,0:T(8,128)(2,1)}, u32[]{:S(2)}, u32[]{:S(2)}) collective-permute-start(bf16[2,1024,512]{2,1,0:T(8,128)(2,1)} %pad_maximum_fusion.9.refs_0_), channel_id=1, source_target_pairs={{0,2},{1,3},{2,0},{3,1},{4,6},{5,7},{6,4},{7,5},{8,10},{9,11},{10,... | collective-permute-start | bytes 6291464 | tf_op jit(solution)/shard_map/ppermute | solution.py:542
  134.5 83.2 %collective-permute-start.17 = (bf16[2,1024,512]{2,1,0:T(8,128)(2,1)}, bf16[2,1024,512]{2,1,0:T(8,128)(2,1)}, u32[]{:S(2)}, u32[]{:S(2)}) collective-permute-start(bf16[2,1024,512]{2,1,0:T(8,128)(2,1)} %collective-permute-done.16.refs_2_), channel_id=1, source_target_pairs={{0,16},{8,24},{16,0},{24,8},{1,17},{9,25},{17,1},{25,9},{2,18},{10... | collective-permute-start | bytes 6291464 | tf_op jit(solution)/shard_map/ppermute | solution.py:542
  140.7 55.7 %collective-permute-start.13 = (bf16[2,512,384]{2,1,0:T(8,128)(2,1)}, bf16[2,512,384]{2,1,0:T(8,128)(2,1)}, u32[]{:S(2)}, u32[]{:S(2)}) collective-permute-start(bf16[2,512,384]{2,1,0:T(8,128)(2,1)} %get-tuple-element.323), channel_id=1, source_target_pairs={{0,5},{1,4},{2,7},{3,6},{4,1},{5,0},{6,3},{7,2},{8,13},{9,12},{10,... | collective-permute-start | bytes 2359304 | tf_op jit(solution)/shard_map/ppermute | solution.py:572
  140.8 75.1 %collective-permute-start.12 = (bf16[2,512,384]{2,1,0:T(8,128)(2,1)}, bf16[2,512,384]{2,1,0:T(8,128)(2,1)}, u32[]{:S(2)}, u32[]{:S(2)}) collective-permute-start(bf16[2,512,384]{2,1,0:T(8,128)(2,1)} %get-tuple-element.324), channel_id=1, source_target_pairs={{0,1},{1,0},{2,3},{3,2},{4,5},{5,4},{6,7},{7,6},{8,9},{9,8},{10,11... | collective-permute-start | bytes 2359304 | tf_op jit(solution)/shard_map/ppermute | solution.py:542
  159.0 56.8 %collective-permute-start.11 = (bf16[2,512,384]{2,1,0:T(8,128)(2,1)}, bf16[2,512,384]{2,1,0:T(8,128)(2,1)}, u32[]{:S(2)}, u32[]{:S(2)}) collective-permute-start(bf16[2,512,384]{2,1,0:T(8,128)(2,1)} %get-tuple-element.325), channel_id=1, source_target_pairs={{0,4},{4,0},{1,5},{5,1},{2,6},{6,2},{3,7},{7,3},{8,12},{12,8},{9,1... | collective-permute-start | bytes 2359304 | tf_op jit(solution)/shard_map/ppermute | solution.py:542
  217.7 71.5 %collective-permute-start.20 = (bf16[2,1024,512]{2,1,0:T(8,128)(2,1)}, bf16[2,1024,512]{2,1,0:T(8,128)(2,1)S(1)}, u32[]{:S(2)}, u32[]{:S(2)}) collective-permute-start(bf16[2,1024,512]{2,1,0:T(8,128)(2,1)} %collective-permute-done.15.refs_1_), channel_id=1, source_target_pairs={{0,16},{8,24},{16,0},{24,8},{1,17},{9,25},{17,1},{25,9},{2,18},{10... | collective-permute-start | bytes 6291464 | tf_op jit(solution)/shard_map/ppermute | solution.py:542
  219.0 70.2 %collective-permute-start.19 = (bf16[2,1024,512]{2,1,0:T(8,128)(2,1)}, bf16[2,1024,512]{2,1,0:T(8,128)(2,1)}, u32[]{:S(2)}, u32[]{:S(2)}) collective-permute-start(bf16[2,1024,512]{2,1,0:T(8,128)(2,1)} %collective-permute-done.15.refs_1_), channel_id=1, source_target_pairs={{0,4},{4,0},{1,5},{5,1},{2,6},{6,2},{3,7},{7,3},{8,12},{12,8},{9,1... | collective-permute-start | bytes 6291464 | tf_op jit(solution)/shard_map/ppermute | solution.py:542
  219.5 69.7 %collective-permute-start.21 = (bf16[4,128,1024]{2,1,0:T(8,128)(2,1)S(1)}, bf16[4,128,1024]{2,1,0:T(8,128)(2,1)S(1)}, u32[]{:S(2)}, u32[]{:S(2)}) collective-permute-start(bf16[4,128,1024]{2,1,0:T(8,128)(2,1)S(1)} %pad_maximum_fusion.33), channel_id=1, source_target_pairs={{0,4},{4,0},{1,5},{5,1},{2,6},{6,2},{3,7},{7,3},{8,12},{12,8},{9,1... | collective-permute-start | bytes 3145736 | tf_op jit(solution)/shard_map/ppermute | solution.py:542
  220.5 68.7 %collective-permute-start.22 = (bf16[512,1024]{1,0:T(8,128)(2,1)S(1)}, bf16[512,1024]{1,0:T(8,128)(2,1)S(1)}, u32[]{:S(2)}, u32[]{:S(2)}) collective-permute-start(bf16[512,1024]{1,0:T(8,128)(2,1)S(1)} %get-tuple-element.164.d0.refs_0_), channel_id=1, source_target_pairs={{0,2},{1,3},{2,0},{3,1},{4,6},{5,7},{6,4},{7,5},{8,10},{9,11},{10,... | collective-permute-start | bytes 3145736 | tf_op jit(solution)/shard_map/ppermute | solution.py:542
  331.8 47.2 %collective-permute-start.32 = (bf16[512,2048]{1,0:T(8,128)(2,1)S(1)}, bf16[512,2048]{1,0:T(8,128)(2,1)}, u32[]{:S(2)}, u32[]{:S(2)}) collective-permute-start(bf16[512,2048]{1,0:T(8,128)(2,1)S(1)} %multiply_convert_fusion.1), channel_id=1, source_target_pairs={{0,1},{1,0},{2,3},{3,2},{4,5},{5,4},{6,7},{7,6},{8,9},{9,8},{10,11... | collective-permute-start | bytes 6291464 | tf_op jit(solution)/shard_map/ppermute | solution.py:542
  334.1 47.1 %collective-permute-start.31 = (bf16[2,1024,512]{2,1,0:T(8,128)(2,1)}, bf16[2,1024,512]{2,1,0:T(8,128)(2,1)}, u32[]{:S(2)}, u32[]{:S(2)}) collective-permute-start(bf16[2,1024,512]{2,1,0:T(8,128)(2,1)} %collective-permute-done.19.refs_3_), channel_id=1, source_target_pairs={{0,16},{8,24},{16,0},{24,8},{1,17},{9,25},{17,1},{25,9},{2,18},{10... | collective-permute-start | bytes 6291464 | tf_op jit(solution)/shard_map/ppermute | solution.py:542
  336.4 45.3 %collective-permute-start.29 = (bf16[512,1024]{1,0:T(8,128)(2,1)}, bf16[512,1024]{1,0:T(8,128)(2,1)S(1)}, u32[]{:S(2)}, u32[]{:S(2)}) collective-permute-start(bf16[512,1024]{1,0:T(8,128)(2,1)} %get-tuple-element.168), channel_id=1, source_target_pairs={{0,4},{4,0},{1,5},{5,1},{2,6},{6,2},{3,7},{7,3},{8,12},{12,8},{9,1... | collective-permute-start | bytes 3145736 | tf_op jit(solution)/shard_map/ppermute | solution.py:542
  336.8 68.8 %collective-permute-start.36 = (bf16[2,512,1024]{2,1,0:T(8,128)(2,1)S(1)}, bf16[2,512,1024]{2,1,0:T(8,128)(2,1)}, u32[]{:S(2)}, u32[]{:S(2)}) collective-permute-start(bf16[2,512,1024]{2,1,0:T(8,128)(2,1)S(1)} %pad_maximum_fusion.13), channel_id=1, source_target_pairs={{0,4},{4,0},{1,5},{5,1},{2,6},{6,2},{3,7},{7,3},{8,12},{12,8},{9,1... | collective-permute-start | bytes 6291464 | tf_op jit(solution)/shard_map/ppermute | solution.py:542
  379.0 34.5 %collective-permute-start.33 = (bf16[512,2048]{1,0:T(8,128)(2,1)}, bf16[512,2048]{1,0:T(8,128)(2,1)S(1)}, u32[]{:S(2)}, u32[]{:S(2)}) collective-permute-start(bf16[512,2048]{1,0:T(8,128)(2,1)} %collective-permute-done.32), channel_id=1, source_target_pairs={{0,8},{8,0},{16,24},{24,16},{1,9},{9,1},{17,25},{25,17},{2,10},{10... | collective-permute-start | bytes 6291464 | tf_op jit(solution)/shard_map/ppermute | solution.py:542
  381.2 26.3 %collective-permute-start.37 = (bf16[512,1024]{1,0:T(8,128)(2,1)S(1)}, bf16[512,1024]{1,0:T(8,128)(2,1)S(1)}, u32[]{:S(2)}, u32[]{:S(2)}) collective-permute-start(bf16[512,1024]{1,0:T(8,128)(2,1)S(1)} %collective-permute-done.22.d1.refs_1_), channel_id=1, source_target_pairs={{0,16},{8,24},{16,0},{24,8},{1,17},{9,25},{17,1},{25,9},{2,18},{10... | collective-permute-start | bytes 3145736 | tf_op jit(solution)/shard_map/ppermute | solution.py:542
  383.5 47.3 %collective-permute-start.34 = (bf16[512,2048]{1,0:T(8,128)(2,1)}, bf16[512,2048]{1,0:T(8,128)(2,1)}, u32[]{:S(2)}, u32[]{:S(2)}) collective-permute-start(bf16[512,2048]{1,0:T(8,128)(2,1)} %fusion.4), channel_id=1, source_target_pairs={{0,1},{1,0},{2,3},{3,2},{4,5},{5,4},{6,7},{7,6},{8,9},{9,8},{10,11... | collective-permute-start | bytes 6291464 | tf_op jit(solution)/shard_map/ppermute | solution.py:542
  407.4 102.6 %collective-permute-start.38 = (bf16[2,512,1024]{2,1,0:T(8,128)(2,1)}, bf16[2,512,1024]{2,1,0:T(8,128)(2,1)}, u32[]{:S(2)}, u32[]{:S(2)}) collective-permute-start(bf16[2,512,1024]{2,1,0:T(8,128)(2,1)} %collective-permute-done.36), channel_id=1, source_target_pairs={{0,16},{8,24},{16,0},{24,8},{1,17},{9,25},{17,1},{25,9},{2,18},{10... | collective-permute-start | bytes 6291464 | tf_op jit(solution)/shard_map/ppermute | solution.py:542
  408.4 38.9 %collective-permute-start.30 = (bf16[512,2048]{1,0:T(8,128)(2,1)}, bf16[512,2048]{1,0:T(8,128)(2,1)}, u32[]{:S(2)}, u32[]{:S(2)}) collective-permute-start(bf16[512,2048]{1,0:T(8,128)(2,1)} %fusion.4), channel_id=1, source_target_pairs={{0,8},{8,0},{16,24},{24,16},{1,9},{9,1},{17,25},{25,17},{2,10},{10... | collective-permute-start | bytes 6291464 | tf_op jit(solution)/shard_map/ppermute | solution.py:542
  430.8 41.4 %collective-permute-start.35 = (bf16[512,2048]{1,0:T(8,128)(2,1)}, bf16[512,2048]{1,0:T(8,128)(2,1)}, u32[]{:S(2)}, u32[]{:S(2)}) collective-permute-start(bf16[512,2048]{1,0:T(8,128)(2,1)} %collective-permute-done.34), channel_id=1, source_target_pairs={{0,8},{8,0},{16,24},{24,16},{1,9},{9,1},{17,25},{25,17},{2,10},{10... | collective-permute-start | bytes 6291464 | tf_op jit(solution)/shard_map/ppermute | solution.py:542
  579.0 49.7 %collective-permute-start.40 = (bf16[512,2048]{1,0:T(8,128)(2,1)}, bf16[512,2048]{1,0:T(8,128)(2,1)}, u32[]{:S(2)}, u32[]{:S(2)}) collective-permute-start(bf16[512,2048]{1,0:T(8,128)(2,1)} %slice.626), channel_id=1, source_target_pairs={{0,16},{8,24},{16,0},{24,8},{1,17},{9,25},{17,1},{25,9},{2,18},{10... | collective-permute-start | bytes 6291464 | tf_op jit(solution)/shard_map/ppermute | solution.py:542
  581.4 47.3 %collective-permute-start.41 = (bf16[1024,1024]{1,0:T(8,128)(2,1)}, bf16[1024,1024]{1,0:T(8,128)(2,1)}, u32[]{:S(2)}, u32[]{:S(2)}) collective-permute-start(bf16[1024,1024]{1,0:T(8,128)(2,1)} %pad_maximum_fusion.14), channel_id=1, source_target_pairs={{0,4},{4,0},{1,5},{5,1},{2,6},{6,2},{3,7},{7,3},{8,12},{12,8},{9,1... | collective-permute-start | bytes 6291464 | tf_op jit(solution)/shard_map/ppermute | solution.py:542
  609.9 27.4 %collective-permute-start.39 = (bf16[512,2048]{1,0:T(8,128)(2,1)}, bf16[512,2048]{1,0:T(8,128)(2,1)}, u32[]{:S(2)}, u32[]{:S(2)}) collective-permute-start(bf16[512,2048]{1,0:T(8,128)(2,1)} %get-tuple-element.204), channel_id=1, source_target_pairs={{0,8},{8,0},{16,24},{24,16},{1,9},{9,1},{17,25},{25,17},{2,10},{10... | collective-permute-start | bytes 6291464 | tf_op jit(solution)/shard_map/ppermute | solution.py:542
  616.0 138.7 %collective-permute-start.54 = (bf16[1024,2048]{1,0:T(8,128)(2,1)}, bf16[1024,2048]{1,0:T(8,128)(2,1)}, u32[]{:S(2)}, u32[]{:S(2)}) collective-permute-start(bf16[1024,2048]{1,0:T(8,128)(2,1)} %shard_map.478), channel_id=1, source_target_pairs={{0,4},{4,0},{1,5},{5,1},{2,6},{6,2},{3,7},{7,3},{8,12},{12,8},{9,1... | collective-permute-start | bytes 12582920 | tf_op jit(solution)/shard_map/ppermute | solution.py:542
  633.2 110.6 %collective-permute-start.53 = (bf16[512,1024]{1,0:T(8,128)(2,1)}, bf16[512,1024]{1,0:T(8,128)(2,1)}, u32[]{:S(2)}, u32[]{:S(2)}) collective-permute-start(bf16[512,1024]{1,0:T(8,128)(2,1)} %get-tuple-element.310), channel_id=1, source_target_pairs={{0,4},{4,0},{1,5},{5,1},{2,6},{6,2},{3,7},{7,3},{8,12},{12,8},{9,1... | collective-permute-start | bytes 3145736 | tf_op jit(solution)/shard_map/ppermute | solution.py:542
  636.7 110.1 %collective-permute-start.87 = (bf16[512,1024]{1,0:T(8,128)(2,1)}, bf16[512,1024]{1,0:T(8,128)(2,1)}, u32[]{:S(2)}, u32[]{:S(2)}) collective-permute-start(bf16[512,1024]{1,0:T(8,128)(2,1)} %add_convert_fusion.22), channel_id=1, source_target_pairs={{0,16},{8,24},{16,0},{24,8},{1,17},{9,25},{17,1},{25,9},{2,18},{10... | collective-permute-start | bytes 3145736 | tf_op jit(solution)/shard_map/ppermute | solution.py:542
  667.8 50.6 %collective-permute-start.45 = (bf16[512,2048]{1,0:T(8,128)(2,1)}, bf16[512,2048]{1,0:T(8,128)(2,1)}, u32[]{:S(2)}, u32[]{:S(2)}) collective-permute-start(bf16[512,2048]{1,0:T(8,128)(2,1)} %get-tuple-element.212), channel_id=1, source_target_pairs={{0,8},{8,0},{16,24},{24,16},{1,9},{9,1},{17,25},{25,17},{2,10},{10... | collective-permute-start | bytes 6291464 | tf_op jit(solution)/shard_map/ppermute | solution.py:542
  670.0 47.5 %collective-permute-start.46 = (bf16[512,2048]{1,0:T(8,128)(2,1)}, bf16[512,2048]{1,0:T(8,128)(2,1)}, u32[]{:S(2)}, u32[]{:S(2)}) collective-permute-start(bf16[512,2048]{1,0:T(8,128)(2,1)} %add_convert_fusion.6), channel_id=1, source_target_pairs={{0,1},{1,0},{2,3},{3,2},{4,5},{5,4},{6,7},{7,6},{8,9},{9,8},{10,11... | collective-permute-start | bytes 6291464 | tf_op jit(solution)/shard_map/ppermute | solution.py:542
  717.6 32.8 %collective-permute-start.43 = (bf16[512,2048]{1,0:T(8,128)(2,1)}, bf16[512,2048]{1,0:T(8,128)(2,1)}, u32[]{:S(2)}, u32[]{:S(2)}) collective-permute-start(bf16[512,2048]{1,0:T(8,128)(2,1)} %get-tuple-element.220), channel_id=1, source_target_pairs={{0,8},{8,0},{16,24},{24,16},{1,9},{9,1},{17,25},{25,17},{2,10},{10... | collective-permute-start | bytes 6291464 | tf_op jit(solution)/shard_map/ppermute | solution.py:542
  728.6 31.0 %collective-permute-start.47 = (bf16[512,2048]{1,0:T(8,128)(2,1)S(1)}, bf16[512,2048]{1,0:T(8,128)(2,1)}, u32[]{:S(2)}, u32[]{:S(2)}) collective-permute-start(bf16[512,2048]{1,0:T(8,128)(2,1)S(1)} %get-tuple-element.296), channel_id=1, source_target_pairs={{0,8},{8,0},{16,24},{24,16},{1,9},{9,1},{17,25},{25,17},{2,10},{10... | collective-permute-start | bytes 6291464 | tf_op jit(solution)/shard_map/ppermute | solution.py:542
  743.8 47.0 %collective-permute-start.55 = (bf16[2048,512]{1,0:T(8,128)(2,1)}, bf16[2048,512]{1,0:T(8,128)(2,1)}, u32[]{:S(2)}, u32[]{:S(2)}) collective-permute-start(bf16[2048,512]{1,0:T(8,128)(2,1)} %pad_maximum_fusion.16), channel_id=1, source_target_pairs={{0,4},{4,0},{1,5},{5,1},{2,6},{6,2},{3,7},{7,3},{8,12},{12,8},{9,1... | collective-permute-start | bytes 6291464 | tf_op jit(solution)/shard_map/ppermute | solution.py:542
  746.8 54.6 %collective-permute-start.51 = (bf16[2048,512]{1,0:T(8,128)(2,1)}, bf16[2048,512]{1,0:T(8,128)(2,1)}, u32[]{:S(2)}, u32[]{:S(2)}) collective-permute-start(bf16[2048,512]{1,0:T(8,128)(2,1)} %slice.637), channel_id=1, source_target_pairs={{0,16},{8,24},{16,0},{24,8},{1,17},{9,25},{17,1},{25,9},{2,18},{10... | collective-permute-start | bytes 6291464 | tf_op jit(solution)/shard_map/ppermute | solution.py:542
  750.4 131.2 %collective-permute-start.88 = (bf16[512,1024]{1,0:T(8,128)(2,1)}, bf16[512,1024]{1,0:T(8,128)(2,1)}, u32[]{:S(2)}, u32[]{:S(2)}) collective-permute-start(bf16[512,1024]{1,0:T(8,128)(2,1)} %add_convert_fusion.10), channel_id=1, source_target_pairs={{0,2},{1,3},{2,0},{3,1},{4,6},{5,7},{6,4},{7,5},{8,10},{9,11},{10,... | collective-permute-start | bytes 3145736 | tf_op jit(solution)/shard_map/ppermute | solution.py:542
  808.4 90.3 %collective-permute-start.52 = (bf16[1024,512]{1,0:T(8,128)(2,1)}, bf16[1024,512]{1,0:T(8,128)(2,1)}, u32[]{:S(2)}, u32[]{:S(2)}) collective-permute-start(bf16[1024,512]{1,0:T(8,128)(2,1)} %get-tuple-element.309), channel_id=1, source_target_pairs={{0,4},{4,0},{1,5},{5,1},{2,6},{6,2},{3,7},{7,3},{8,12},{12,8},{9,1... | collective-permute-start | bytes 3145736 | tf_op jit(solution)/shard_map/ppermute | solution.py:542
  881.5 83.2 %collective-permute-start.42 = (bf16[512,2048]{1,0:T(8,128)(2,1)}, bf16[512,2048]{1,0:T(8,128)(2,1)}, u32[]{:S(2)}, u32[]{:S(2)}) collective-permute-start(bf16[512,2048]{1,0:T(8,128)(2,1)} %get-tuple-element.216), channel_id=1, source_target_pairs={{0,8},{8,0},{16,24},{24,16},{1,9},{9,1},{17,25},{25,17},{2,10},{10... | collective-permute-start | bytes 6291464 | tf_op jit(solution)/shard_map/ppermute | solution.py:542
  888.4 76.4 %collective-permute-start.44 = (bf16[512,2048]{1,0:T(8,128)(2,1)S(1)}, bf16[512,2048]{1,0:T(8,128)(2,1)}, u32[]{:S(2)}, u32[]{:S(2)}) collective-permute-start(bf16[512,2048]{1,0:T(8,128)(2,1)S(1)} %copy-done.101), channel_id=1, source_target_pairs={{0,1},{1,0},{2,3},{3,2},{4,5},{5,4},{6,7},{7,6},{8,9},{9,8},{10,11... | collective-permute-start | bytes 6291464 | tf_op jit(solution)/shard_map/ppermute | solution.py:542
  896.7 80.9 %collective-permute-start.61 = (bf16[1024,1024]{1,0:T(8,128)(2,1)}, bf16[1024,1024]{1,0:T(8,128)(2,1)}, u32[]{:S(2)}, u32[]{:S(2)}) collective-permute-start(bf16[1024,1024]{1,0:T(8,128)(2,1)} %get-tuple-element.300), channel_id=1, source_target_pairs={{0,16},{8,24},{16,0},{24,8},{1,17},{9,25},{17,1},{25,9},{2,18},{10... | collective-permute-start | bytes 6291464 | tf_op jit(solution)/shard_map/ppermute | solution.py:542
  897.7 66.3 %collective-permute-start.59 = (bf16[1024,512]{1,0:T(8,128)(2,1)}, bf16[1024,512]{1,0:T(8,128)(2,1)}, u32[]{:S(2)}, u32[]{:S(2)}) collective-permute-start(bf16[1024,512]{1,0:T(8,128)(2,1)} %add_convert_fusion.16), channel_id=1, source_target_pairs={{0,16},{8,24},{16,0},{24,8},{1,17},{9,25},{17,1},{25,9},{2,18},{10... | collective-permute-start | bytes 3145736 | tf_op jit(solution)/shard_map/ppermute | solution.py:542
  898.7 96.9 %collective-permute-start.83 = (bf16[512,2048]{1,0:T(8,128)(2,1)}, bf16[512,2048]{1,0:T(8,128)(2,1)}, u32[]{:S(2)}, u32[]{:S(2)}) collective-permute-start(bf16[512,2048]{1,0:T(8,128)(2,1)} %pad_maximum_fusion.17), channel_id=1, source_target_pairs={{0,1},{1,0},{2,3},{3,2},{4,5},{5,4},{6,7},{7,6},{8,9},{9,8},{10,11... | collective-permute-start | bytes 6291464 | tf_op jit(solution)/shard_map/ppermute | solution.py:542
  964.1 126.2 %collective-permute-start.103 = (bf16[512,1024]{1,0:T(8,128)(2,1)S(1)}, bf16[512,1024]{1,0:T(8,128)(2,1)}, u32[]{:S(2)}, u32[]{:S(2)}) collective-permute-start(bf16[512,1024]{1,0:T(8,128)(2,1)S(1)} %get-tuple-element.287), channel_id=1, source_target_pairs={{0,16},{8,24},{16,0},{24,8},{1,17},{9,25},{17,1},{25,9},{2,18},{10... | collective-permute-start | bytes 3145736 | tf_op jit(solution)/shard_map/ppermute | solution.py:542
  973.1 48.2 %collective-permute-start.60 = (bf16[1024,512]{1,0:T(8,128)(2,1)S(1)}, bf16[1024,512]{1,0:T(8,128)(2,1)S(1)}, u32[]{:S(2)}, u32[]{:S(2)}) collective-permute-start(bf16[1024,512]{1,0:T(8,128)(2,1)S(1)} %add_convert_fusion.15), channel_id=1, source_target_pairs={{0,2},{1,3},{2,0},{3,1},{4,6},{5,7},{6,4},{7,5},{8,10},{9,11},{10,... | collective-permute-start | bytes 3145736 | tf_op jit(solution)/shard_map/ppermute | solution.py:542
  1026.3 66.4 %collective-permute-start.101 = (bf16[1024,512]{1,0:T(8,128)(2,1)S(1)}, bf16[1024,512]{1,0:T(8,128)(2,1)}, u32[]{:S(2)}, u32[]{:S(2)}) collective-permute-start(bf16[1024,512]{1,0:T(8,128)(2,1)S(1)} %get-tuple-element.291), channel_id=1, source_target_pairs={{0,16},{8,24},{16,0},{24,8},{1,17},{9,25},{17,1},{25,9},{2,18},{10... | collective-permute-start | bytes 3145736 | tf_op jit(solution)/shard_map/ppermute | solution.py:542
  1030.2 43.2 %collective-permute-start.76 = (bf16[1024,512]{1,0:T(8,128)(2,1)}, bf16[1024,512]{1,0:T(8,128)(2,1)}, u32[]{:S(2)}, u32[]{:S(2)}) collective-permute-start(bf16[1024,512]{1,0:T(8,128)(2,1)} %slice.709), channel_id=1, source_target_pairs={{0,2},{1,3},{2,0},{3,1},{4,6},{5,7},{6,4},{7,5},{8,10},{9,11},{10,... | collective-permute-start | bytes 3145736 | tf_op jit(solution)/shard_map/ppermute | solution.py:542
  1059.3 48.2 %collective-permute-start.84 = (bf16[512,1024]{1,0:T(8,128)(2,1)}, bf16[512,1024]{1,0:T(8,128)(2,1)}, u32[]{:S(2)}, u32[]{:S(2)}) collective-permute-start(bf16[512,1024]{1,0:T(8,128)(2,1)} %pad_maximum_fusion.35), channel_id=1, source_target_pairs={{0,4},{4,0},{1,5},{5,1},{2,6},{6,2},{3,7},{7,3},{8,12},{12,8},{9,1... | collective-permute-start | bytes 3145736 | tf_op jit(solution)/shard_map/ppermute | solution.py:542
  1071.1 28.0 %collective-permute-start.68 = (bf16[512,1024]{1,0:T(8,128)(2,1)}, bf16[512,1024]{1,0:T(8,128)(2,1)}, u32[]{:S(2)}, u32[]{:S(2)}) collective-permute-start(bf16[512,1024]{1,0:T(8,128)(2,1)} %fusion.38), channel_id=1, source_target_pairs={{0,16},{8,24},{16,0},{24,8},{1,17},{9,25},{17,1},{25,9},{2,18},{10... | collective-permute-start | bytes 3145736 | tf_op jit(solution)/shard_map/ppermute | solution.py:542
  1073.4 43.2 %collective-permute-start.71 = (bf16[768,768]{1,0:T(8,128)(2,1)}, bf16[768,768]{1,0:T(8,128)(2,1)}, u32[]{:S(2)}, u32[]{:S(2)}) collective-permute-start(bf16[768,768]{1,0:T(8,128)(2,1)} %pad_maximum_fusion.26), channel_id=1, source_target_pairs={{0,1},{1,0},{2,3},{3,2},{4,5},{5,4},{6,7},{7,6},{8,9},{9,8},{10,11... | collective-permute-start | bytes 3538952 | tf_op jit(solution)/shard_map/ppermute | solution.py:542
  1092.8 45.1 %collective-permute-start.91 = (bf16[1024,512]{1,0:T(8,128)(2,1)S(1)}, bf16[1024,512]{1,0:T(8,128)(2,1)S(1)}, u32[]{:S(2)}, u32[]{:S(2)}) collective-permute-start(bf16[1024,512]{1,0:T(8,128)(2,1)S(1)} %get-tuple-element.289), channel_id=1, source_target_pairs={{0,16},{8,24},{16,0},{24,8},{1,17},{9,25},{17,1},{25,9},{2,18},{10... | collective-permute-start | bytes 3145736 | tf_op jit(solution)/shard_map/ppermute | solution.py:542
  1099.1 79.0 %collective-permute-start.77 = (bf16[512,2048]{1,0:T(8,128)(2,1)S(1)}, bf16[512,2048]{1,0:T(8,128)(2,1)S(1)}, u32[]{:S(2)}, u32[]{:S(2)}) collective-permute-start(bf16[512,2048]{1,0:T(8,128)(2,1)S(1)} %slice_bitcast_fusion), channel_id=1, source_target_pairs={{0,8},{8,0},{16,24},{24,16},{1,9},{9,1},{17,25},{25,17},{2,10},{10... | collective-permute-start | bytes 6291464 | tf_op jit(solution)/shard_map/ppermute | solution.py:542
  1107.6 91.4 %collective-permute-start.104 = (bf16[2,512,1024]{2,1,0:T(8,128)(2,1)S(1)}, bf16[2,512,1024]{2,1,0:T(8,128)(2,1)S(1)}, u32[]{:S(2)}, u32[]{:S(2)}) collective-permute-start(bf16[2,512,1024]{2,1,0:T(8,128)(2,1)S(1)} %pad_maximum_fusion.23), channel_id=1, source_target_pairs={{0,8},{8,0},{16,24},{24,16},{1,9},{9,1},{17,25},{25,17},{2,10},{10... | collective-permute-start | bytes 6291464 | tf_op jit(solution)/shard_map/ppermute | solution.py:542
  1170.5 53.6 %collective-permute-start.102 = (bf16[2,1024,512]{2,1,0:T(8,128)(2,1)}, bf16[2,1024,512]{2,1,0:T(8,128)(2,1)}, u32[]{:S(2)}, u32[]{:S(2)}) collective-permute-start(bf16[2,1024,512]{2,1,0:T(8,128)(2,1)} %pad_maximum_fusion.22), channel_id=1, source_target_pairs={{0,8},{8,0},{16,24},{24,16},{1,9},{9,1},{17,25},{25,17},{2,10},{10... | collective-permute-start | bytes 6291464 | tf_op jit(solution)/shard_map/ppermute | solution.py:542
  1177.0 142.7 %collective-permute-start.92 = (bf16[2,1024,512]{2,1,0:T(8,128)(2,1)}, bf16[2,1024,512]{2,1,0:T(8,128)(2,1)}, u32[]{:S(2)}, u32[]{:S(2)}) collective-permute-start(bf16[2,1024,512]{2,1,0:T(8,128)(2,1)} %pad_maximum_fusion.18), channel_id=1, source_target_pairs={{0,8},{8,0},{16,24},{24,16},{1,9},{9,1},{17,25},{25,17},{2,10},{10... | collective-permute-start | bytes 6291464 | tf_op jit(solution)/shard_map/ppermute | solution.py:542
  1185.1 27.7 %collective-permute-start.74 = (bf16[1024,256]{1,0:T(8,128)(2,1)}, bf16[1024,256]{1,0:T(8,128)(2,1)}, u32[]{:S(2)}, u32[]{:S(2)}) collective-permute-start(bf16[1024,256]{1,0:T(8,128)(2,1)} %broadcast_select_fusion.5), channel_id=1, source_target_pairs={{0,2},{1,3},{2,0},{3,1},{4,6},{5,7},{6,4},{7,5},{8,10},{9,11},{10,... | collective-permute-start | bytes 1572872 | tf_op jit(solution)/shard_map/ppermute | solution.py:542
  1221.7 74.5 %collective-permute-start.94 = (bf16[1024,128]{1,0:T(8,128)(2,1)}, bf16[1024,128]{1,0:T(8,128)(2,1)}, u32[]{:S(2)}, u32[]{:S(2)}) collective-permute-start(bf16[1024,128]{1,0:T(8,128)(2,1)} %get-tuple-element.407), channel_id=1, source_target_pairs={{0,16},{8,24},{16,0},{24,8},{1,17},{9,25},{17,1},{25,9},{2,18},{10... | collective-permute-start | bytes 786440 | tf_op jit(solution)/shard_map/ppermute | solution.py:542
  1222.9 73.2 %collective-permute-start.96 = (bf16[1024,128]{1,0:T(8,128)(2,1)}, bf16[1024,128]{1,0:T(8,128)(2,1)}, u32[]{:S(2)}, u32[]{:S(2)}) collective-permute-start(bf16[1024,128]{1,0:T(8,128)(2,1)} %get-tuple-element.408), channel_id=1, source_target_pairs={{0,2},{1,3},{2,0},{3,1},{4,6},{5,7},{6,4},{7,5},{8,10},{9,11},{10,... | collective-permute-start | bytes 786440 | tf_op jit(solution)/shard_map/ppermute | solution.py:542
  1228.6 113.1 %collective-permute-start.75 = (bf16[512,1024]{1,0:T(8,128)(2,1)}, bf16[512,1024]{1,0:T(8,128)(2,1)}, u32[]{:S(2)}, u32[]{:S(2)}) collective-permute-start(bf16[512,1024]{1,0:T(8,128)(2,1)} %slice.651), channel_id=1, source_target_pairs={{0,4},{4,0},{1,5},{5,1},{2,6},{6,2},{3,7},{7,3},{8,12},{12,8},{9,1... | collective-permute-start | bytes 3145736 | tf_op jit(solution)/shard_map/ppermute | solution.py:542
  1230.1 111.6 %collective-permute-start.93 = (bf16[512,1024]{1,0:T(8,128)(2,1)}, bf16[512,1024]{1,0:T(8,128)(2,1)}, u32[]{:S(2)}, u32[]{:S(2)}) collective-permute-start(bf16[512,1024]{1,0:T(8,128)(2,1)} %slice.728), channel_id=1, source_target_pairs={{0,4},{4,0},{1,5},{5,1},{2,6},{6,2},{3,7},{7,3},{8,12},{12,8},{9,1... | collective-permute-start | bytes 3145736 | tf_op jit(solution)/shard_map/ppermute | solution.py:542
  1307.1 39.4 %collective-permute-start.98 = (bf16[4,1024,128]{2,1,0:T(8,128)(2,1)S(1)}, bf16[4,1024,128]{2,1,0:T(8,128)(2,1)}, u32[]{:S(2)}, u32[]{:S(2)}) collective-permute-start(bf16[4,1024,128]{2,1,0:T(8,128)(2,1)S(1)} %pad_maximum_fusion.37), channel_id=1, source_target_pairs={{0,8},{8,0},{16,24},{24,16},{1,9},{9,1},{17,25},{25,17},{2,10},{10... | collective-permute-start | bytes 3145736 | tf_op jit(solution)/shard_map/ppermute | solution.py:542
  (163 other events, 3204.8 us)

commit v4 on v3

--- a/solution.py
+++ b/solution.py
@@ -1562,7 +1562,6 @@
     gate_second = add_low(gate_kept[:half_width, part_rows:], gate_got_x[:half_width])
     gate_first_x = swap_x(add_low(gate_kept[half_width:, :part_rows], gate_got_y[half_width:]))
     gate_second_y = swap_y(add_low(gate_sent[:half_width, part_rows:], gate_got_x[half_width:]))
-    up_sum_y = swap_y(up_kept[1])
 
     def sequence_grad(sequence, *others):
         return attend_grad(
@@ -1582,9 +1581,11 @@
         for value in (gate_first_x, gate_second_y, down_far_sum, out_near)
     )
     gate_first = add_low(gate_first, gate_first_x)
-    gate_far_sum = swap_far(add_low(gate_second, gate_second_y))
+    gate_second = add_low(gate_second, gate_second_y)
+    gate_far_sum = swap_far(gate_second)
+    up_sum_y = swap_y(after(up_kept[1], gate_second_y))
     in_first = tokens_of(packed_first)
-    packed_second = sequence_grad(1, gate_first)
+    packed_second = sequence_grad(1, gate_first, gate_second)
     gate_far_sum, in_first, up_sum_y = (
         after(value, packed_second) for value in (gate_far_sum, in_first, up_sum_y)
     )

time: 1370 us -> 1370 us (level)
    unnamed x254 -> x252, local copies, waits for them, and re-layouts: 31.6 us -> 32.1 us
  transfers between devices with their start and end apart: 105 -> 105, of which waited for: 40 -> 39; matrix products, arithmetic and copies ran while one was open for 17% -> 17% of each run, Pallas kernels for 34% -> 34%
where the time goes in v4:
time: 1370 us; the launch traced here: 1360 us
  Pallas kernels  542 us (40%)
  waiting for transfers between devices  410 us (30%)
  other arithmetic  163 us (12%)
  starting transfers between devices  110 us (8%)
  local copies, waits for them, and re-layouts  94.6 us (7%)
  blocking collectives  17.8 us (1%)
    ppermute x100, waiting for transfers between devices, swap(): lax.ppermute(values, axis, [(place, place ^ bit) for place in range(size)])  366 us
    ppermute x100, starting transfers between devices, swap(): lax.ppermute(values, axis, [(place, place ^ bit) for place in range(size)])  105 us
    pallas_call x10, Pallas kernels, weight_grad(): pl.pallas_call(kernel, grid=(columns // block,), in_specs=[pl.BlockSpec((...  98.3 us
    pallas_call x2, Pallas kernels, attend_grad(): pl.pallas_call(functools.partial(attend_back_kernel, sequence), grid_spec...  85.3 us
    pallas_call x5, Pallas kernels, step_weight(): pl.pallas_call(step_kernel, grid_spec=pltpu.PrefetchScalarGridSpec(num_sc...  72 us
    pallas_call x1, Pallas kernels, attend(): pl.pallas_call(attend_kernel, grid_spec=pltpu.PrefetchScalarGridSpec(num_...  67 us
    pallas_call x4, Pallas kernels, hidden_units(): pl.pallas_call(hidden_kernel, grid=(tokens // block,), in_specs=[pl.Block...  56.7 us
    pallas_call x2, Pallas kernels, normed_back(): pl.pallas_call(normed_back_kernel, grid=(tokens // block,), in_specs=[lef...  53.5 us
  transfers between devices with their start and end apart: 105, of which 39 were waited for; matrix products, arithmetic and copies ran while one was open for 17% of the time, Pallas kernels for 34%

profile of v4, /device:TPU:1, one launch (start us, length us, event | category | flops | bytes accessed | tf_op | source)
XLA Modules:
  0.0 1359.0 jit_solution(10124343159659811588)
XLA Ops:
  36.7 20.5 %collective-permute-done = bf16[512,1024]{1,0:T(8,128)(2,1)} collective-permute-done((bf16[512,1024]{1,0:T(8,128)(2,1)}, bf16[512,1024]{1,0:T(8,128)(2,1)}, u32[]{:S(2)}, u32[]{:S(2)}) %collective-permute-start) | collective-permute-done | bytes 1048608 | tf_op jit(solution)/shard_map/ppermute | solution.py:542
  57.2 11.1 collective-permute-done.3
  82.2 5.5 collective-permute-done.8
  95.4 17.2 %collective-permute-done.14 = bf16[256,1024]{1,0:T(8,128)(2,1)S(1)} collective-permute-done((bf16[256,1024]{1,0:T(8,128)(2,1)S(1)}, bf16[256,1024]{1,0:T(8,128)(2,1)S(1)}, u32[]{:S(2)}, u32[]{:S(2)}) %collective-permute-start.14) | collective-permute-done | bytes 524320 | tf_op jit(solution)/shard_map/ppermute | solution.py:542
  118.5 16.0 %shard_map.466 = bf16[4,2,512,384]{3,2,1,0:T(8,128)(2,1)} custom-call(bf16[2,512,2048]{2,1,0:T(8,128)(2,1)} %pad_maximum_fusion.normed_ref, bf16[4,1024,256]{2,1,0:T(8,128)(2,1)} %copy-done.62, bf16[4,1024,128]{2,1,0:T(8,128)(2,1)S(1)} %maximum_maximum_fusion.1.kv_ref, bf16[4,1024,128]{2,1,0:T(8,128)(2,1)S(1)} %constant_dynamic-update-slice_fusion.4.first_ref, ...), custom_call_target="tpu_custom_call" | custom-call | flops 3221225472 | bytes 8388608 | tf_op jit(solution)/shard_map/pallas_call | solution.py:841
  142.3 16.7 %collective-permute-done.18 = bf16[2,256,1024]{2,1,0:T(8,128)(2,1)} collective-permute-done((bf16[2,256,1024]{2,1,0:T(8,128)(2,1)S(1)}, bf16[2,256,1024]{2,1,0:T(8,128)(2,1)}, u32[]{:S(2)}, u32[]{:S(2)}) %collective-permute-start.18) | collective-permute-done | bytes 1048608 | tf_op jit(solution)/shard_map/ppermute | solution.py:542
  165.9 30.5 %collective-permute-done.13 = bf16[2,512,384]{2,1,0:T(8,128)(2,1)} collective-permute-done((bf16[2,512,384]{2,1,0:T(8,128)(2,1)}, bf16[2,512,384]{2,1,0:T(8,128)(2,1)}, u32[]{:S(2)}, u32[]{:S(2)}) %collective-permute-start.13) | collective-permute-done | bytes 786464 | tf_op jit(solution)/shard_map/ppermute | solution.py:572
  196.4 19.5 %collective-permute-done.12 = bf16[2,512,384]{2,1,0:T(8,128)(2,1)} collective-permute-done((bf16[2,512,384]{2,1,0:T(8,128)(2,1)}, bf16[2,512,384]{2,1,0:T(8,128)(2,1)}, u32[]{:S(2)}, u32[]{:S(2)}) %collective-permute-start.12) | collective-permute-done | bytes 786464 | tf_op jit(solution)/shard_map/ppermute | solution.py:542
  222.1 67.0 %shard_map.467 = (bf16[4,2,512,256]{3,2,1,0:T(8,128)(2,1)S(1)}, f32[4,2,8,512]{3,2,1,0:T(8,128)S(1)}) custom-call(s32[3]{0:T(128)S(1)} %pad_add_fusion.place_ref, bf16[4,2,512,384]{3,2,1,0:T(8,128)(2,1)S(1)} %pad_maximum_fusion.6.q_ref.kv_ref, bf16[4,2,512,384]{3,2,1,0:T(8,128)(2,1)S(1)} %pad_maximum_fusion.6.q_ref.kv_ref), custom_call_target="tpu_custom_call" | custom-call | flops 85899345920 | bytes 1048576 | tf_op jit(solution)/shard_map/pallas_call | solution.py:970
  293.8 19.2 %collective-permute-done.26 = bf16[4,128,1024]{2,1,0:T(8,128)(2,1)S(1)} collective-permute-done((bf16[4,128,1024]{2,1,0:T(8,128)(2,1)S(1)}, bf16[4,128,1024]{2,1,0:T(8,128)(2,1)S(1)}, u32[]{:S(2)}, u32[]{:S(2)}) %collective-permute-start.26) | collective-permute-done | bytes 1048608 | tf_op jit(solution)/shard_map/ppermute | solution.py:542
  340.5 14.1 %shard_map.468 = (bf16[1024,1024]{1,0:T(8,128)(2,1)S(1)}, bf16[1024,1024]{1,0:T(8,128)(2,1)S(1)}, bf16[1024,1024]{1,0:T(8,128)(2,1)}) custom-call(bf16[1024,2048]{1,0:T(8,128)(2,1)} %pad_maximum_fusion.1.normed_ref.refs_0_, bf16[2,1024,512]{2,1,0:T(8,128)(2,1)} %pad_maximum_fusion.9.refs_0_, bf16[2,1024,512]{2,1,0:T(8,128)(2,1)} %collective-permute-done.15.refs_1_, ...), custom_call_target="tpu_custom_call" | custom-call | flops 8589934592 | bytes 18874368 | tf_op jit(solution)/shard_map/pallas_call | solution.py:667
  354.5 24.4 %collective-permute-done.32 = bf16[512,2048]{1,0:T(8,128)(2,1)} collective-permute-done((bf16[512,2048]{1,0:T(8,128)(2,1)S(1)}, bf16[512,2048]{1,0:T(8,128)(2,1)}, u32[]{:S(2)}, u32[]{:S(2)}) %collective-permute-start.32) | collective-permute-done | bytes 2097184 | tf_op jit(solution)/shard_map/ppermute | solution.py:542
  385.8 19.8 %collective-permute-done.36 = bf16[2,512,1024]{2,1,0:T(8,128)(2,1)} collective-permute-done((bf16[2,512,1024]{2,1,0:T(8,128)(2,1)S(1)}, bf16[2,512,1024]{2,1,0:T(8,128)(2,1)}, u32[]{:S(2)}, u32[]{:S(2)}) %collective-permute-start.36) | collective-permute-done | bytes 2097184 | tf_op jit(solution)/shard_map/ppermute | solution.py:542
  415.0 14.5 %shard_map.471 = (bf16[1024,1024]{1,0:T(8,128)(2,1)S(1)}, bf16[1024,1024]{1,0:T(8,128)(2,1)S(1)}, bf16[1024,1024]{1,0:T(8,128)(2,1)}) custom-call(bf16[1024,2048]{1,0:T(8,128)(2,1)} %constant_dynamic-update-slice_fusion.8.normed_ref.refs_1_, bf16[2,1024,512]{2,1,0:T(8,128)(2,1)} %pad_maximum_fusion.9.refs_0_, ...), custom_call_target="tpu_custom_call" | custom-call | flops 8589934592 | bytes 18874368 | tf_op jit(solution)/shard_map/pallas_call | solution.py:667
  431.8 14.1 %shard_map.469 = (bf16[1024,1024]{1,0:T(8,128)(2,1)S(1)}, bf16[1024,1024]{1,0:T(8,128)(2,1)S(1)}, bf16[1024,1024]{1,0:T(8,128)(2,1)}) custom-call(bf16[1024,2048]{1,0:T(8,128)(2,1)} %pad_maximum_fusion.1.normed_ref.refs_0_, bf16[2,1024,512]{2,1,0:T(8,128)(2,1)} %pad_maximum_fusion.12.refs_0_.refs_4_, bf16[2,1024,512]{2,1,0:T(8,128)(2,1)} %copy-done.119, ...), custom_call_target="tpu_custom_call" | custom-call | flops 8589934592 | bytes 18874368 | tf_op jit(solution)/shard_map/pallas_call | solution.py:667
  447.2 5.6 pad_maximum_fusion.2.refs_2_.grad_ref
  452.8 14.1 %shard_map.470 = (bf16[1024,1024]{1,0:T(8,128)(2,1)S(1)}, bf16[1024,1024]{1,0:T(8,128)(2,1)S(1)}, bf16[1024,1024]{1,0:T(8,128)(2,1)}) custom-call(bf16[1024,2048]{1,0:T(8,128)(2,1)} %constant_dynamic-update-slice_fusion.8.normed_ref.refs_1_, bf16[2,1024,512]{2,1,0:T(8,128)(2,1)} %pad_maximum_fusion.12.refs_0_.refs_4_, bf16[2,1024,512]{2,1,0:T(8,128)(2,1)} %copy-done.119, ...), custom_call_target="tpu_custom_call" | custom-call | flops 8589934592 | bytes 18874368 | tf_op jit(solution)/shard_map/pallas_call | solution.py:667
  475.5 14.0 %shard_map.473 = bf16[1024,2048]{1,0:T(8,128)(2,1)} custom-call(bf16[1024,1024]{1,0:T(8,128)(2,1)S(1)} %get-tuple-element.214.refs_0_.h0, bf16[1024,1024]{1,0:T(8,128)(2,1)S(1)} %copy-done.50, bf16[1024,2048]{1,0:T(8,128)(2,1)} %pad_maximum_fusion.2.refs_2_.grad_ref, bf16[1024,2048]{1,0:T(8,128)(2,1)} %constant_dynamic-update-slice_fusion.10.refs_3_.grad_ref), custom_call_target="tpu_custom_call" | custom-call | flops 8589934592 | bytes 16777216 | tf_op jit(solution)/shard_map/pallas_call | solution.py:798
  491.4 14.2 %shard_map.472 = bf16[1024,2048]{1,0:T(8,128)(2,1)} custom-call(bf16[1024,1024]{1,0:T(8,128)(2,1)S(1)} %get-tuple-element.215.refs_0_.h1, bf16[1024,1024]{1,0:T(8,128)(2,1)S(1)} %copy-done.52, bf16[1024,2048]{1,0:T(8,128)(2,1)} %pad_maximum_fusion.2.refs_2_.grad_ref, bf16[1024,2048]{1,0:T(8,128)(2,1)} %constant_dynamic-update-slice_fusion.10.refs_3_.grad_ref), custom_call_target="tpu_custom_call" | custom-call | flops 8589934592 | bytes 16777216 | tf_op jit(solution)/shard_map/pallas_call | solution.py:798
  511.7 10.1 shard_map.477
  521.8 9.5 shard_map.476
  533.0 12.0 shard_map.479
  545.0 9.5 shard_map.475
  554.5 9.5 shard_map.474
  565.6 13.3 shard_map.478
  581.7 26.8 %shard_map.480 = (bf16[512,2048]{1,0:T(8,128)(2,1)S(1)}, bf16[512,2048]{1,0:T(8,128)(2,1)}) custom-call(bf16[1024,1024]{1,0:T(8,128)(2,1)} %get-tuple-element.200.a0.refs_3_, bf16[1024,1024]{1,0:T(8,128)(2,1)} %get-tuple-element.201.refs_3_.a1, bf16[1024,1024]{1,0:T(8,128)(2,1)} %get-tuple-element.202.refs_3_.b0, ...), custom_call_target="tpu_custom_call" | custom-call | flops 17179869184 | bytes 29360128 | tf_op jit(solution)/shard_map/pallas_call | solution.py:770
  617.0 11.6 collective-permute-done.41
  628.6 4.6 add_convert_fusion.24
  641.1 26.7 %shard_map.481 = (bf16[512,2048]{1,0:T(8,128)(2,1)S(1)}, bf16[512,2048]{1,0:T(8,128)(2,1)}) custom-call(bf16[1024,1024]{1,0:T(8,128)(2,1)} %get-tuple-element.208.a0.refs_2_, bf16[1024,1024]{1,0:T(8,128)(2,1)} %get-tuple-element.209.refs_2_.a1, bf16[1024,1024]{1,0:T(8,128)(2,1)} %get-tuple-element.210.refs_2_.b0, ...), custom_call_target="tpu_custom_call" | custom-call | flops 17179869184 | bytes 29360128 | tf_op jit(solution)/shard_map/pallas_call | solution.py:770
  672.3 13.5 shard_map.484
  685.8 13.6 shard_map.483
  699.4 14.2 %shard_map.482 = (bf16[512,2048]{1,0:T(8,128)(2,1)}, bf16[512,2048]{1,0:T(8,128)(2,1)}) custom-call(bf16[1024,1024]{1,0:T(8,128)(2,1)} %copy-done.47, bf16[1024,1024]{1,0:T(8,128)(2,1)} %copy-done.48, bf16[512,1024]{1,0:T(8,128)(2,1)S(1)} %get-tuple-element.165.d0.refs_0_, bf16[512,1024]{1,0:T(8,128)(2,1)S(1)} %copy-done.25, ...), custom_call_target="tpu_custom_call" | custom-call | flops 8589934592 | bytes 16777216 | tf_op jit(solution)/shard_map/pallas_call | solution.py:700
  718.4 4.6 multiply_reduce_fusion
  723.0 5.5 multiply_convert_fusion
  728.6 12.2 shard_map.485
  754.3 4.8 add_convert_fusion.3
  768.3 22.5 %collective-permute-done.55 = bf16[2048,512]{1,0:T(8,128)(2,1)} collective-permute-done((bf16[2048,512]{1,0:T(8,128)(2,1)}, bf16[2048,512]{1,0:T(8,128)(2,1)}, u32[]{:S(2)}, u32[]{:S(2)}) %collective-permute-start.55) | collective-permute-done | bytes 2097184 | tf_op jit(solution)/shard_map/ppermute | solution.py:542
  790.8 7.4 fusion.29
  811.4 7.0 collective-permute-done.50
  819.3 10.3 collective-permute-done.49
  834.5 42.3 %shard_map.488 = bf16[4,512,384]{2,1,0:T(8,128)(2,1)S(1)} custom-call(s32[3]{0:T(128)S(1)} %copy-done.33, bf16[4,2,512,384]{3,2,1,0:T(8,128)(2,1)} %copy-done.15, bf16[4,2,512,384]{3,2,1,0:T(8,128)(2,1)} %copy-done.15, bf16[4,2,512,256]{3,2,1,0:T(8,128)(2,1)S(1)} %copy-done.19, bf16[4,2,512,256]{3,2,1,0:T(8,128)(2,1)} %pad_maximum_fusion.15.do_ref, ...), custom_call_target="tpu_custom_call" | custom-call | flops 107374182400 | bytes 1048576 | tf_op jit(solution)/shard_map/pallas_call | solution.py:1076
  890.5 5.9 collective-permute-done.58
  904.8 43.0 %shard_map.489 = bf16[4,512,384]{2,1,0:T(8,128)(2,1)S(1)} custom-call(s32[3]{0:T(128)S(1)} %copy-done.33, bf16[4,2,512,384]{3,2,1,0:T(8,128)(2,1)} %copy-done.15, bf16[4,2,512,384]{3,2,1,0:T(8,128)(2,1)} %copy-done.15, bf16[4,2,512,256]{3,2,1,0:T(8,128)(2,1)S(1)} %copy-done.19, bf16[4,2,512,256]{3,2,1,0:T(8,128)(2,1)} %pad_maximum_fusion.15.do_ref, ...), custom_call_target="tpu_custom_call" | custom-call | flops 107374182400 | bytes 1048576 | tf_op jit(solution)/shard_map/pallas_call | solution.py:1076
  947.9 4.6 add_convert_fusion.2
  953.6 56.0 %collective-permute-done.83 = bf16[512,2048]{1,0:T(8,128)(2,1)} collective-permute-done((bf16[512,2048]{1,0:T(8,128)(2,1)}, bf16[512,2048]{1,0:T(8,128)(2,1)}, u32[]{:S(2)}, u32[]{:S(2)}) %collective-permute-start.83) | collective-permute-done | bytes 2097184 | tf_op jit(solution)/shard_map/ppermute | solution.py:542
  1025.8 12.1 collective-permute-done.63
  1040.0 5.9 shard_map.491
  1052.1 5.9 shard_map.490
  1070.2 14.9 %shard_map.492 = bf16[2,512,2048]{2,1,0:T(8,128)(2,1)} custom-call(bf16[2,512,1536]{2,1,0:T(8,128)(2,1)} %pad_maximum_fusion.7.grad_ref, bf16[4,1024,256]{2,1,0:T(8,128)(2,1)} %copy-done.62, bf16[4,1024,128]{2,1,0:T(8,128)(2,1)S(1)} %maximum_maximum_fusion.1.kv_ref, bf16[4,1024,128]{2,1,0:T(8,128)(2,1)S(1)} %copy-done.5, ...), custom_call_target="tpu_custom_call" | custom-call | flops 3221225472 | bytes 8388608 | tf_op jit(solution)/shard_map/pallas_call | solution.py:879
  1094.8 5.7 collective-permute-start.77
  1113.5 19.4 %collective-permute-done.85 = bf16[256,1024]{1,0:T(8,128)(2,1)S(1)} collective-permute-done((bf16[256,1024]{1,0:T(8,128)(2,1)S(1)}, bf16[256,1024]{1,0:T(8,128)(2,1)S(1)}, u32[]{:S(2)}, u32[]{:S(2)}) %collective-permute-start.85) | collective-permute-done | bytes 524320 | tf_op jit(solution)/shard_map/ppermute | solution.py:542
  1136.7 9.5 collective-permute-done.72
  1146.8 8.6 collective-permute-done.86
  1158.5 10.4 collective-permute-done.99
  1198.5 8.9 collective-permute-done.82
  1226.6 17.8 %psum.7 = f32[]{:T(128)} all-reduce(f32[]{:T(128)} %bitcast.67), channel_id=1, replica_groups=mesh['dp'=4,'row'=2,'col'=4] {'row','col'}, use_global_device_ids=true, to_apply=%region_12.13 | all-reduce | flops 1 | bytes 8 | tf_op jit(solution)/shard_map/psum | solution.py:1707
  1246.7 5.8 shard_map.496
  1252.5 20.1 %shard_map.498 = (f32[2048,1024]{1,0:T(8,128)}, f32[2048,1024]{1,0:T(8,128)}, f32[2048,1024]{1,0:T(8,128)}) custom-call(s32[1]{0:T(128)} %bitcast.58.spot_ref, f32[1,1]{1,0:T(1,128)} %bitcast.68.factor_ref, bf16[4,512,1024]{2,1,0:T(8,128)(2,1)S(1)} %copy-done, f32[2048,1024]{1,0:T(8,128)} %weight_ref.9, f32[2048,1024]{1,0:T(8,128)} %moment_ref.9, ...), custom_call_target="tpu_custom_call" | custom-call | flops 25165824 | bytes 54525952 | tf_op jit(solution)/shard_map/pallas_call | solution.py:1137
  1272.6 20.0 %shard_map.497 = (f32[1024,2048]{1,0:T(8,128)}, f32[1024,2048]{1,0:T(8,128)}, f32[1024,2048]{1,0:T(8,128)}) custom-call(s32[1]{0:T(128)} %bitcast.58.spot_ref, f32[1,1]{1,0:T(1,128)} %bitcast.68.factor_ref, bf16[4,1024,512]{2,1,0:T(8,128)(2,1)S(1)} %copy-done.1, f32[1024,2048]{1,0:T(8,128)} %weight_ref.8, f32[1024,2048]{1,0:T(8,128)} %moment_ref.8, ...), custom_call_target="tpu_custom_call" | custom-call | flops 25165824 | bytes 54525952 | tf_op jit(solution)/shard_map/pallas_call | solution.py:1137
  1294.8 4.6 collective-permute-start.95
  1303.8 5.5 collective-permute-start.98
  1310.3 5.9 shard_map.494
  1318.1 20.1 %shard_map.493 = (f32[1024,2048]{1,0:T(8,128)}, f32[1024,2048]{1,0:T(8,128)}, f32[1024,2048]{1,0:T(8,128)}) custom-call(s32[1]{0:T(128)} %bitcast.58.spot_ref, f32[1,1]{1,0:T(1,128)} %bitcast.68.factor_ref, bf16[4,1024,512]{2,1,0:T(8,128)(2,1)S(1)} %pad_maximum_fusion.3.grad_ref, f32[1024,2048]{1,0:T(8,128)} %weight_ref.5, f32[1024,2048]{1,0:T(8,128)} %moment_ref.5, ...), custom_call_target="tpu_custom_call" | custom-call | flops 25165824 | bytes 54525952 | tf_op jit(solution)/shard_map/pallas_call | solution.py:1137
  1345.1 12.4 shard_map.495
  (618 shorter events, 377.2 us)
Async XLA Ops:
  0.7 34.6 %collective-permute-start.5 = (f32[2,1024]{1,0:T(2,128)}, f32[2,1024]{1,0:T(2,128)S(1)}, u32[]{:S(2)}, u32[]{:S(2)}) collective-permute-start(f32[2,1024]{1,0:T(2,128)} %param.37), channel_id=1, source_target_pairs={{0,4},{4,0},{1,5},{5,1},{2,6},{6,2},{3,7},{7,3},{8,12},{12,8},{9,1... | collective-permute-start | bytes 24584 | tf_op jit(solution)/shard_map/ppermute | solution.py:542
  4.9 25.2 %collective-permute-start.1 = (bf16[1024,256]{1,0:T(8,128)(2,1)}, bf16[1024,256]{1,0:T(8,128)(2,1)}, u32[]{:S(2)}, u32[]{:S(2)}) collective-permute-start(bf16[1024,256]{1,0:T(8,128)(2,1)} %pad_maximum_fusion.41), channel_id=1, source_target_pairs={{0,2},{1,3},{2,0},{3,1},{4,6},{5,7},{6,4},{7,5},{8,10},{9,11},{10,... | collective-permute-start | bytes 1572872 | tf_op jit(solution)/shard_map/ppermute | solution.py:542
  14.1 43.1 %collective-permute-start = (bf16[512,1024]{1,0:T(8,128)(2,1)}, bf16[512,1024]{1,0:T(8,128)(2,1)}, u32[]{:S(2)}, u32[]{:S(2)}) collective-permute-start(bf16[512,1024]{1,0:T(8,128)(2,1)} %get-tuple-element.356), channel_id=1, source_target_pairs={{0,4},{4,0},{1,5},{5,1},{2,6},{6,2},{3,7},{7,3},{8,12},{12,8},{9,1... | collective-permute-start | bytes 3145736 | tf_op jit(solution)/shard_map/ppermute | solution.py:542
  34.7 33.6 %collective-permute-start.3 = (bf16[2,1024,128]{2,1,0:T(8,128)(2,1)S(1)}, bf16[2,1024,128]{2,1,0:T(8,128)(2,1)S(1)}, u32[]{:S(2)}, u32[]{:S(2)}) collective-permute-start(bf16[2,1024,128]{2,1,0:T(8,128)(2,1)S(1)} %pad_maximum_fusion.42), channel_id=1, source_target_pairs={{0,4},{4,0},{1,5},{5,1},{2,6},{6,2},{3,7},{7,3},{8,12},{12,8},{9,1... | collective-permute-start | bytes 1572872 | tf_op jit(solution)/shard_map/ppermute | solution.py:542
  35.3 38.7 %collective-permute-start.7 = (bf16[2,1024,256]{2,1,0:T(8,128)(2,1)S(1)}, bf16[2,1024,256]{2,1,0:T(8,128)(2,1)S(1)}, u32[]{:S(2)}, u32[]{:S(2)}) collective-permute-start(bf16[2,1024,256]{2,1,0:T(8,128)(2,1)S(1)} %pad_maximum_fusion.28), channel_id=1, source_target_pairs={{0,1},{1,0},{2,3},{3,2},{4,5},{5,4},{6,7},{7,6},{8,9},{9,8},{10,11... | collective-permute-start | bytes 3145736 | tf_op jit(solution)/shard_map/ppermute | solution.py:542
  71.8 43.8 %collective-permute-start.6 = (bf16[512,2048]{1,0:T(8,128)(2,1)S(1)}, bf16[512,2048]{1,0:T(8,128)(2,1)S(1)}, u32[]{:S(2)}, u32[]{:S(2)}) collective-permute-start(bf16[512,2048]{1,0:T(8,128)(2,1)S(1)} %fusion.5.refs_0_), channel_id=1, source_target_pairs={{0,8},{8,0},{16,24},{24,16},{1,9},{9,1},{17,25},{25,17},{2,10},{10... | collective-permute-start | bytes 6291464 | tf_op jit(solution)/shard_map/ppermute | solution.py:542
  80.5 54.1 %collective-permute-start.16 = (bf16[2,1024,512]{2,1,0:T(8,128)(2,1)}, bf16[2,1024,512]{2,1,0:T(8,128)(2,1)}, u32[]{:S(2)}, u32[]{:S(2)}) collective-permute-start(bf16[2,1024,512]{2,1,0:T(8,128)(2,1)} %pad_maximum_fusion.9.refs_0_), channel_id=1, source_target_pairs={{0,4},{4,0},{1,5},{5,1},{2,6},{6,2},{3,7},{7,3},{8,12},{12,8},{9,1... | collective-permute-start | bytes 6291464 | tf_op jit(solution)/shard_map/ppermute | solution.py:542
  113.2 45.9 %collective-permute-start.18 = (bf16[2,256,1024]{2,1,0:T(8,128)(2,1)S(1)}, bf16[2,256,1024]{2,1,0:T(8,128)(2,1)}, u32[]{:S(2)}, u32[]{:S(2)}) collective-permute-start(bf16[2,256,1024]{2,1,0:T(8,128)(2,1)S(1)} %pad_maximum_fusion.32), channel_id=1, source_target_pairs={{0,1},{1,0},{2,3},{3,2},{4,5},{5,4},{6,7},{7,6},{8,9},{9,8},{10,11... | collective-permute-start | bytes 3145736 | tf_op jit(solution)/shard_map/ppermute | solution.py:542
  113.2 104.5 %collective-permute-start.15 = (bf16[2,1024,512]{2,1,0:T(8,128)(2,1)}, bf16[2,1024,512]{2,1,0:T(8,128)(2,1)}, u32[]{:S(2)}, u32[]{:S(2)}) collective-permute-start(bf16[2,1024,512]{2,1,0:T(8,128)(2,1)} %pad_maximum_fusion.9.refs_0_), channel_id=1, source_target_pairs={{0,2},{1,3},{2,0},{3,1},{4,6},{5,7},{6,4},{7,5},{8,10},{9,11},{10,... | collective-permute-start | bytes 6291464 | tf_op jit(solution)/shard_map/ppermute | solution.py:542
  134.5 83.2 %collective-permute-start.17 = (bf16[2,1024,512]{2,1,0:T(8,128)(2,1)}, bf16[2,1024,512]{2,1,0:T(8,128)(2,1)}, u32[]{:S(2)}, u32[]{:S(2)}) collective-permute-start(bf16[2,1024,512]{2,1,0:T(8,128)(2,1)} %collective-permute-done.16.refs_2_), channel_id=1, source_target_pairs={{0,16},{8,24},{16,0},{24,8},{1,17},{9,25},{17,1},{25,9},{2,18},{10... | collective-permute-start | bytes 6291464 | tf_op jit(solution)/shard_map/ppermute | solution.py:542
  140.7 55.7 %collective-permute-start.13 = (bf16[2,512,384]{2,1,0:T(8,128)(2,1)}, bf16[2,512,384]{2,1,0:T(8,128)(2,1)}, u32[]{:S(2)}, u32[]{:S(2)}) collective-permute-start(bf16[2,512,384]{2,1,0:T(8,128)(2,1)} %get-tuple-element.325), channel_id=1, source_target_pairs={{0,5},{1,4},{2,7},{3,6},{4,1},{5,0},{6,3},{7,2},{8,13},{9,12},{10,... | collective-permute-start | bytes 2359304 | tf_op jit(solution)/shard_map/ppermute | solution.py:572
  140.8 75.1 %collective-permute-start.12 = (bf16[2,512,384]{2,1,0:T(8,128)(2,1)}, bf16[2,512,384]{2,1,0:T(8,128)(2,1)}, u32[]{:S(2)}, u32[]{:S(2)}) collective-permute-start(bf16[2,512,384]{2,1,0:T(8,128)(2,1)} %get-tuple-element.326), channel_id=1, source_target_pairs={{0,1},{1,0},{2,3},{3,2},{4,5},{5,4},{6,7},{7,6},{8,9},{9,8},{10,11... | collective-permute-start | bytes 2359304 | tf_op jit(solution)/shard_map/ppermute | solution.py:542
  159.0 56.8 %collective-permute-start.11 = (bf16[2,512,384]{2,1,0:T(8,128)(2,1)}, bf16[2,512,384]{2,1,0:T(8,128)(2,1)}, u32[]{:S(2)}, u32[]{:S(2)}) collective-permute-start(bf16[2,512,384]{2,1,0:T(8,128)(2,1)} %get-tuple-element.327), channel_id=1, source_target_pairs={{0,4},{4,0},{1,5},{5,1},{2,6},{6,2},{3,7},{7,3},{8,12},{12,8},{9,1... | collective-permute-start | bytes 2359304 | tf_op jit(solution)/shard_map/ppermute | solution.py:542
  217.7 71.4 %collective-permute-start.20 = (bf16[2,1024,512]{2,1,0:T(8,128)(2,1)}, bf16[2,1024,512]{2,1,0:T(8,128)(2,1)S(1)}, u32[]{:S(2)}, u32[]{:S(2)}) collective-permute-start(bf16[2,1024,512]{2,1,0:T(8,128)(2,1)} %collective-permute-done.15.refs_1_), channel_id=1, source_target_pairs={{0,16},{8,24},{16,0},{24,8},{1,17},{9,25},{17,1},{25,9},{2,18},{10... | collective-permute-start | bytes 6291464 | tf_op jit(solution)/shard_map/ppermute | solution.py:542
  219.0 70.1 %collective-permute-start.19 = (bf16[2,1024,512]{2,1,0:T(8,128)(2,1)}, bf16[2,1024,512]{2,1,0:T(8,128)(2,1)}, u32[]{:S(2)}, u32[]{:S(2)}) collective-permute-start(bf16[2,1024,512]{2,1,0:T(8,128)(2,1)} %collective-permute-done.15.refs_1_), channel_id=1, source_target_pairs={{0,4},{4,0},{1,5},{5,1},{2,6},{6,2},{3,7},{7,3},{8,12},{12,8},{9,1... | collective-permute-start | bytes 6291464 | tf_op jit(solution)/shard_map/ppermute | solution.py:542
  219.5 69.7 %collective-permute-start.21 = (bf16[4,128,1024]{2,1,0:T(8,128)(2,1)S(1)}, bf16[4,128,1024]{2,1,0:T(8,128)(2,1)S(1)}, u32[]{:S(2)}, u32[]{:S(2)}) collective-permute-start(bf16[4,128,1024]{2,1,0:T(8,128)(2,1)S(1)} %pad_maximum_fusion.33), channel_id=1, source_target_pairs={{0,4},{4,0},{1,5},{5,1},{2,6},{6,2},{3,7},{7,3},{8,12},{12,8},{9,1... | collective-permute-start | bytes 3145736 | tf_op jit(solution)/shard_map/ppermute | solution.py:542
  220.5 68.6 %collective-permute-start.22 = (bf16[512,1024]{1,0:T(8,128)(2,1)S(1)}, bf16[512,1024]{1,0:T(8,128)(2,1)S(1)}, u32[]{:S(2)}, u32[]{:S(2)}) collective-permute-start(bf16[512,1024]{1,0:T(8,128)(2,1)S(1)} %get-tuple-element.165.d0.refs_0_), channel_id=1, source_target_pairs={{0,2},{1,3},{2,0},{3,1},{4,6},{5,7},{6,4},{7,5},{8,10},{9,11},{10,... | collective-permute-start | bytes 3145736 | tf_op jit(solution)/shard_map/ppermute | solution.py:542
  331.7 47.2 %collective-permute-start.32 = (bf16[512,2048]{1,0:T(8,128)(2,1)S(1)}, bf16[512,2048]{1,0:T(8,128)(2,1)}, u32[]{:S(2)}, u32[]{:S(2)}) collective-permute-start(bf16[512,2048]{1,0:T(8,128)(2,1)S(1)} %multiply_convert_fusion.1), channel_id=1, source_target_pairs={{0,1},{1,0},{2,3},{3,2},{4,5},{5,4},{6,7},{7,6},{8,9},{9,8},{10,11... | collective-permute-start | bytes 6291464 | tf_op jit(solution)/shard_map/ppermute | solution.py:542
  334.0 47.1 %collective-permute-start.31 = (bf16[2,1024,512]{2,1,0:T(8,128)(2,1)}, bf16[2,1024,512]{2,1,0:T(8,128)(2,1)}, u32[]{:S(2)}, u32[]{:S(2)}) collective-permute-start(bf16[2,1024,512]{2,1,0:T(8,128)(2,1)} %collective-permute-done.19.refs_3_), channel_id=1, source_target_pairs={{0,16},{8,24},{16,0},{24,8},{1,17},{9,25},{17,1},{25,9},{2,18},{10... | collective-permute-start | bytes 6291464 | tf_op jit(solution)/shard_map/ppermute | solution.py:542
  336.4 45.3 %collective-permute-start.29 = (bf16[512,1024]{1,0:T(8,128)(2,1)}, bf16[512,1024]{1,0:T(8,128)(2,1)S(1)}, u32[]{:S(2)}, u32[]{:S(2)}) collective-permute-start(bf16[512,1024]{1,0:T(8,128)(2,1)} %get-tuple-element.169), channel_id=1, source_target_pairs={{0,4},{4,0},{1,5},{5,1},{2,6},{6,2},{3,7},{7,3},{8,12},{12,8},{9,1... | collective-permute-start | bytes 3145736 | tf_op jit(solution)/shard_map/ppermute | solution.py:542
  336.8 68.8 %collective-permute-start.36 = (bf16[2,512,1024]{2,1,0:T(8,128)(2,1)S(1)}, bf16[2,512,1024]{2,1,0:T(8,128)(2,1)}, u32[]{:S(2)}, u32[]{:S(2)}) collective-permute-start(bf16[2,512,1024]{2,1,0:T(8,128)(2,1)S(1)} %pad_maximum_fusion.13), channel_id=1, source_target_pairs={{0,4},{4,0},{1,5},{5,1},{2,6},{6,2},{3,7},{7,3},{8,12},{12,8},{9,1... | collective-permute-start | bytes 6291464 | tf_op jit(solution)/shard_map/ppermute | solution.py:542
  378.9 34.5 %collective-permute-start.33 = (bf16[512,2048]{1,0:T(8,128)(2,1)}, bf16[512,2048]{1,0:T(8,128)(2,1)S(1)}, u32[]{:S(2)}, u32[]{:S(2)}) collective-permute-start(bf16[512,2048]{1,0:T(8,128)(2,1)} %collective-permute-done.32), channel_id=1, source_target_pairs={{0,8},{8,0},{16,24},{24,16},{1,9},{9,1},{17,25},{25,17},{2,10},{10... | collective-permute-start | bytes 6291464 | tf_op jit(solution)/shard_map/ppermute | solution.py:542
  381.1 26.3 %collective-permute-start.37 = (bf16[512,1024]{1,0:T(8,128)(2,1)S(1)}, bf16[512,1024]{1,0:T(8,128)(2,1)S(1)}, u32[]{:S(2)}, u32[]{:S(2)}) collective-permute-start(bf16[512,1024]{1,0:T(8,128)(2,1)S(1)} %collective-permute-done.22.d1.refs_1_), channel_id=1, source_target_pairs={{0,16},{8,24},{16,0},{24,8},{1,17},{9,25},{17,1},{25,9},{2,18},{10... | collective-permute-start | bytes 3145736 | tf_op jit(solution)/shard_map/ppermute | solution.py:542
  383.5 47.3 %collective-permute-start.34 = (bf16[512,2048]{1,0:T(8,128)(2,1)}, bf16[512,2048]{1,0:T(8,128)(2,1)}, u32[]{:S(2)}, u32[]{:S(2)}) collective-permute-start(bf16[512,2048]{1,0:T(8,128)(2,1)} %fusion.4), channel_id=1, source_target_pairs={{0,1},{1,0},{2,3},{3,2},{4,5},{5,4},{6,7},{7,6},{8,9},{9,8},{10,11... | collective-permute-start | bytes 6291464 | tf_op jit(solution)/shard_map/ppermute | solution.py:542
  407.4 102.6 %collective-permute-start.38 = (bf16[2,512,1024]{2,1,0:T(8,128)(2,1)}, bf16[2,512,1024]{2,1,0:T(8,128)(2,1)}, u32[]{:S(2)}, u32[]{:S(2)}) collective-permute-start(bf16[2,512,1024]{2,1,0:T(8,128)(2,1)} %collective-permute-done.36), channel_id=1, source_target_pairs={{0,16},{8,24},{16,0},{24,8},{1,17},{9,25},{17,1},{25,9},{2,18},{10... | collective-permute-start | bytes 6291464 | tf_op jit(solution)/shard_map/ppermute | solution.py:542
  408.4 38.9 %collective-permute-start.30 = (bf16[512,2048]{1,0:T(8,128)(2,1)}, bf16[512,2048]{1,0:T(8,128)(2,1)}, u32[]{:S(2)}, u32[]{:S(2)}) collective-permute-start(bf16[512,2048]{1,0:T(8,128)(2,1)} %fusion.4), channel_id=1, source_target_pairs={{0,8},{8,0},{16,24},{24,16},{1,9},{9,1},{17,25},{25,17},{2,10},{10... | collective-permute-start | bytes 6291464 | tf_op jit(solution)/shard_map/ppermute | solution.py:542
  430.8 41.4 %collective-permute-start.35 = (bf16[512,2048]{1,0:T(8,128)(2,1)}, bf16[512,2048]{1,0:T(8,128)(2,1)}, u32[]{:S(2)}, u32[]{:S(2)}) collective-permute-start(bf16[512,2048]{1,0:T(8,128)(2,1)} %collective-permute-done.34), channel_id=1, source_target_pairs={{0,8},{8,0},{16,24},{24,16},{1,9},{9,1},{17,25},{25,17},{2,10},{10... | collective-permute-start | bytes 6291464 | tf_op jit(solution)/shard_map/ppermute | solution.py:542
  578.9 49.7 %collective-permute-start.40 = (bf16[512,2048]{1,0:T(8,128)(2,1)}, bf16[512,2048]{1,0:T(8,128)(2,1)}, u32[]{:S(2)}, u32[]{:S(2)}) collective-permute-start(bf16[512,2048]{1,0:T(8,128)(2,1)} %slice.626), channel_id=1, source_target_pairs={{0,16},{8,24},{16,0},{24,8},{1,17},{9,25},{17,1},{25,9},{2,18},{10... | collective-permute-start | bytes 6291464 | tf_op jit(solution)/shard_map/ppermute | solution.py:542
  581.3 47.3 %collective-permute-start.41 = (bf16[1024,1024]{1,0:T(8,128)(2,1)}, bf16[1024,1024]{1,0:T(8,128)(2,1)}, u32[]{:S(2)}, u32[]{:S(2)}) collective-permute-start(bf16[1024,1024]{1,0:T(8,128)(2,1)} %pad_maximum_fusion.14), channel_id=1, source_target_pairs={{0,4},{4,0},{1,5},{5,1},{2,6},{6,2},{3,7},{7,3},{8,12},{12,8},{9,1... | collective-permute-start | bytes 6291464 | tf_op jit(solution)/shard_map/ppermute | solution.py:542
  609.9 27.4 %collective-permute-start.39 = (bf16[512,2048]{1,0:T(8,128)(2,1)}, bf16[512,2048]{1,0:T(8,128)(2,1)}, u32[]{:S(2)}, u32[]{:S(2)}) collective-permute-start(bf16[512,2048]{1,0:T(8,128)(2,1)} %get-tuple-element.205), channel_id=1, source_target_pairs={{0,8},{8,0},{16,24},{24,16},{1,9},{9,1},{17,25},{25,17},{2,10},{10... | collective-permute-start | bytes 6291464 | tf_op jit(solution)/shard_map/ppermute | solution.py:542
  616.0 138.3 %collective-permute-start.54 = (bf16[1024,2048]{1,0:T(8,128)(2,1)}, bf16[1024,2048]{1,0:T(8,128)(2,1)}, u32[]{:S(2)}, u32[]{:S(2)}) collective-permute-start(bf16[1024,2048]{1,0:T(8,128)(2,1)} %shard_map.478), channel_id=1, source_target_pairs={{0,4},{4,0},{1,5},{5,1},{2,6},{6,2},{3,7},{7,3},{8,12},{12,8},{9,1... | collective-permute-start | bytes 12582920 | tf_op jit(solution)/shard_map/ppermute | solution.py:542
  633.1 110.6 %collective-permute-start.53 = (bf16[512,1024]{1,0:T(8,128)(2,1)}, bf16[512,1024]{1,0:T(8,128)(2,1)}, u32[]{:S(2)}, u32[]{:S(2)}) collective-permute-start(bf16[512,1024]{1,0:T(8,128)(2,1)} %get-tuple-element.312), channel_id=1, source_target_pairs={{0,4},{4,0},{1,5},{5,1},{2,6},{6,2},{3,7},{7,3},{8,12},{12,8},{9,1... | collective-permute-start | bytes 3145736 | tf_op jit(solution)/shard_map/ppermute | solution.py:542
  636.7 110.1 %collective-permute-start.87 = (bf16[512,1024]{1,0:T(8,128)(2,1)}, bf16[512,1024]{1,0:T(8,128)(2,1)}, u32[]{:S(2)}, u32[]{:S(2)}) collective-permute-start(bf16[512,1024]{1,0:T(8,128)(2,1)} %add_convert_fusion.22), channel_id=1, source_target_pairs={{0,16},{8,24},{16,0},{24,8},{1,17},{9,25},{17,1},{25,9},{2,18},{10... | collective-permute-start | bytes 3145736 | tf_op jit(solution)/shard_map/ppermute | solution.py:542
  667.8 50.6 %collective-permute-start.45 = (bf16[512,2048]{1,0:T(8,128)(2,1)}, bf16[512,2048]{1,0:T(8,128)(2,1)}, u32[]{:S(2)}, u32[]{:S(2)}) collective-permute-start(bf16[512,2048]{1,0:T(8,128)(2,1)} %get-tuple-element.213), channel_id=1, source_target_pairs={{0,8},{8,0},{16,24},{24,16},{1,9},{9,1},{17,25},{25,17},{2,10},{10... | collective-permute-start | bytes 6291464 | tf_op jit(solution)/shard_map/ppermute | solution.py:542
  670.0 47.5 %collective-permute-start.46 = (bf16[512,2048]{1,0:T(8,128)(2,1)}, bf16[512,2048]{1,0:T(8,128)(2,1)}, u32[]{:S(2)}, u32[]{:S(2)}) collective-permute-start(bf16[512,2048]{1,0:T(8,128)(2,1)} %add_convert_fusion.6), channel_id=1, source_target_pairs={{0,1},{1,0},{2,3},{3,2},{4,5},{5,4},{6,7},{7,6},{8,9},{9,8},{10,11... | collective-permute-start | bytes 6291464 | tf_op jit(solution)/shard_map/ppermute | solution.py:542
  717.5 32.8 %collective-permute-start.43 = (bf16[512,2048]{1,0:T(8,128)(2,1)}, bf16[512,2048]{1,0:T(8,128)(2,1)}, u32[]{:S(2)}, u32[]{:S(2)}) collective-permute-start(bf16[512,2048]{1,0:T(8,128)(2,1)} %get-tuple-element.221), channel_id=1, source_target_pairs={{0,8},{8,0},{16,24},{24,16},{1,9},{9,1},{17,25},{25,17},{2,10},{10... | collective-permute-start | bytes 6291464 | tf_op jit(solution)/shard_map/ppermute | solution.py:542
  728.6 30.6 %collective-permute-start.47 = (bf16[512,2048]{1,0:T(8,128)(2,1)S(1)}, bf16[512,2048]{1,0:T(8,128)(2,1)}, u32[]{:S(2)}, u32[]{:S(2)}) collective-permute-start(bf16[512,2048]{1,0:T(8,128)(2,1)S(1)} %get-tuple-element.298), channel_id=1, source_target_pairs={{0,8},{8,0},{16,24},{24,16},{1,9},{9,1},{17,25},{25,17},{2,10},{10... | collective-permute-start | bytes 6291464 | tf_op jit(solution)/shard_map/ppermute | solution.py:542
  743.7 47.0 %collective-permute-start.55 = (bf16[2048,512]{1,0:T(8,128)(2,1)}, bf16[2048,512]{1,0:T(8,128)(2,1)}, u32[]{:S(2)}, u32[]{:S(2)}) collective-permute-start(bf16[2048,512]{1,0:T(8,128)(2,1)} %pad_maximum_fusion.16), channel_id=1, source_target_pairs={{0,4},{4,0},{1,5},{5,1},{2,6},{6,2},{3,7},{7,3},{8,12},{12,8},{9,1... | collective-permute-start | bytes 6291464 | tf_op jit(solution)/shard_map/ppermute | solution.py:542
  746.7 54.6 %collective-permute-start.51 = (bf16[2048,512]{1,0:T(8,128)(2,1)}, bf16[2048,512]{1,0:T(8,128)(2,1)}, u32[]{:S(2)}, u32[]{:S(2)}) collective-permute-start(bf16[2048,512]{1,0:T(8,128)(2,1)} %slice.637), channel_id=1, source_target_pairs={{0,16},{8,24},{16,0},{24,8},{1,17},{9,25},{17,1},{25,9},{2,18},{10... | collective-permute-start | bytes 6291464 | tf_op jit(solution)/shard_map/ppermute | solution.py:542
  750.3 128.9 %collective-permute-start.88 = (bf16[512,1024]{1,0:T(8,128)(2,1)}, bf16[512,1024]{1,0:T(8,128)(2,1)}, u32[]{:S(2)}, u32[]{:S(2)}) collective-permute-start(bf16[512,1024]{1,0:T(8,128)(2,1)} %add_convert_fusion.10), channel_id=1, source_target_pairs={{0,2},{1,3},{2,0},{3,1},{4,6},{5,7},{6,4},{7,5},{8,10},{9,11},{10,... | collective-permute-start | bytes 3145736 | tf_op jit(solution)/shard_map/ppermute | solution.py:542
  808.0 93.7 %collective-permute-start.52 = (bf16[1024,512]{1,0:T(8,128)(2,1)}, bf16[1024,512]{1,0:T(8,128)(2,1)}, u32[]{:S(2)}, u32[]{:S(2)}) collective-permute-start(bf16[1024,512]{1,0:T(8,128)(2,1)} %get-tuple-element.311), channel_id=1, source_target_pairs={{0,4},{4,0},{1,5},{5,1},{2,6},{6,2},{3,7},{7,3},{8,12},{12,8},{9,1... | collective-permute-start | bytes 3145736 | tf_op jit(solution)/shard_map/ppermute | solution.py:542
  818.4 79.8 %collective-permute-start.56 = (bf16[1024,512]{1,0:T(8,128)(2,1)}, bf16[1024,512]{1,0:T(8,128)(2,1)}, u32[]{:S(2)}, u32[]{:S(2)}) collective-permute-start(bf16[1024,512]{1,0:T(8,128)(2,1)} %add_convert_fusion.16), channel_id=1, source_target_pairs={{0,16},{8,24},{16,0},{24,8},{1,17},{9,25},{17,1},{25,9},{2,18},{10... | collective-permute-start | bytes 3145736 | tf_op jit(solution)/shard_map/ppermute | solution.py:542
  888.1 59.8 %collective-permute-start.42 = (bf16[512,2048]{1,0:T(8,128)(2,1)}, bf16[512,2048]{1,0:T(8,128)(2,1)}, u32[]{:S(2)}, u32[]{:S(2)}) collective-permute-start(bf16[512,2048]{1,0:T(8,128)(2,1)} %get-tuple-element.217), channel_id=1, source_target_pairs={{0,8},{8,0},{16,24},{24,16},{1,9},{9,1},{17,25},{25,17},{2,10},{10... | collective-permute-start | bytes 6291464 | tf_op jit(solution)/shard_map/ppermute | solution.py:542
  896.4 51.4 %collective-permute-start.44 = (bf16[512,2048]{1,0:T(8,128)(2,1)S(1)}, bf16[512,2048]{1,0:T(8,128)(2,1)}, u32[]{:S(2)}, u32[]{:S(2)}) collective-permute-start(bf16[512,2048]{1,0:T(8,128)(2,1)S(1)} %copy-done.100), channel_id=1, source_target_pairs={{0,1},{1,0},{2,3},{3,2},{4,5},{5,4},{6,7},{7,6},{8,9},{9,8},{10,11... | collective-permute-start | bytes 6291464 | tf_op jit(solution)/shard_map/ppermute | solution.py:542
  897.4 112.3 %collective-permute-start.83 = (bf16[512,2048]{1,0:T(8,128)(2,1)}, bf16[512,2048]{1,0:T(8,128)(2,1)}, u32[]{:S(2)}, u32[]{:S(2)}) collective-permute-start(bf16[512,2048]{1,0:T(8,128)(2,1)} %pad_maximum_fusion.17), channel_id=1, source_target_pairs={{0,1},{1,0},{2,3},{3,2},{4,5},{5,4},{6,7},{7,6},{8,9},{9,8},{10,11... | collective-permute-start | bytes 6291464 | tf_op jit(solution)/shard_map/ppermute | solution.py:542
  898.2 186.8 %collective-permute-start.103 = (bf16[512,1024]{1,0:T(8,128)(2,1)S(1)}, bf16[512,1024]{1,0:T(8,128)(2,1)}, u32[]{:S(2)}, u32[]{:S(2)}) collective-permute-start(bf16[512,1024]{1,0:T(8,128)(2,1)S(1)} %get-tuple-element.289), channel_id=1, source_target_pairs={{0,16},{8,24},{16,0},{24,8},{1,17},{9,25},{17,1},{25,9},{2,18},{10... | collective-permute-start | bytes 3145736 | tf_op jit(solution)/shard_map/ppermute | solution.py:542
  904.3 107.9 %collective-permute-start.61 = (bf16[1024,1024]{1,0:T(8,128)(2,1)}, bf16[1024,1024]{1,0:T(8,128)(2,1)}, u32[]{:S(2)}, u32[]{:S(2)}) collective-permute-start(bf16[1024,1024]{1,0:T(8,128)(2,1)} %get-tuple-element.240), channel_id=1, source_target_pairs={{0,16},{8,24},{16,0},{24,8},{1,17},{9,25},{17,1},{25,9},{2,18},{10... | collective-permute-start | bytes 6291464 | tf_op jit(solution)/shard_map/ppermute | solution.py:542
  947.8 64.4 %collective-permute-start.60 = (bf16[1024,512]{1,0:T(8,128)(2,1)}, bf16[1024,512]{1,0:T(8,128)(2,1)S(1)}, u32[]{:S(2)}, u32[]{:S(2)}) collective-permute-start(bf16[1024,512]{1,0:T(8,128)(2,1)} %add_convert_fusion.15), channel_id=1, source_target_pairs={{0,2},{1,3},{2,0},{3,1},{4,6},{5,7},{6,4},{7,5},{8,10},{9,11},{10,... | collective-permute-start | bytes 3145736 | tf_op jit(solution)/shard_map/ppermute | solution.py:542
  1021.3 66.3 %collective-permute-start.101 = (bf16[1024,512]{1,0:T(8,128)(2,1)S(1)}, bf16[1024,512]{1,0:T(8,128)(2,1)}, u32[]{:S(2)}, u32[]{:S(2)}) collective-permute-start(bf16[1024,512]{1,0:T(8,128)(2,1)S(1)} %get-tuple-element.293), channel_id=1, source_target_pairs={{0,16},{8,24},{16,0},{24,8},{1,17},{9,25},{17,1},{25,9},{2,18},{10... | collective-permute-start | bytes 3145736 | tf_op jit(solution)/shard_map/ppermute | solution.py:542
  1025.7 44.4 %collective-permute-start.76 = (bf16[1024,512]{1,0:T(8,128)(2,1)}, bf16[1024,512]{1,0:T(8,128)(2,1)}, u32[]{:S(2)}, u32[]{:S(2)}) collective-permute-start(bf16[1024,512]{1,0:T(8,128)(2,1)} %slice.709), channel_id=1, source_target_pairs={{0,2},{1,3},{2,0},{3,1},{4,6},{5,7},{6,4},{7,5},{8,10},{9,11},{10,... | collective-permute-start | bytes 3145736 | tf_op jit(solution)/shard_map/ppermute | solution.py:542
  1050.5 51.7 %collective-permute-start.84 = (bf16[512,1024]{1,0:T(8,128)(2,1)}, bf16[512,1024]{1,0:T(8,128)(2,1)}, u32[]{:S(2)}, u32[]{:S(2)}) collective-permute-start(bf16[512,1024]{1,0:T(8,128)(2,1)} %pad_maximum_fusion.35), channel_id=1, source_target_pairs={{0,4},{4,0},{1,5},{5,1},{2,6},{6,2},{3,7},{7,3},{8,12},{12,8},{9,1... | collective-permute-start | bytes 3145736 | tf_op jit(solution)/shard_map/ppermute | solution.py:542
  1063.2 31.6 %collective-permute-start.68 = (bf16[512,1024]{1,0:T(8,128)(2,1)}, bf16[512,1024]{1,0:T(8,128)(2,1)}, u32[]{:S(2)}, u32[]{:S(2)}) collective-permute-start(bf16[512,1024]{1,0:T(8,128)(2,1)} %fusion.38), channel_id=1, source_target_pairs={{0,16},{8,24},{16,0},{24,8},{1,17},{9,25},{17,1},{25,9},{2,18},{10... | collective-permute-start | bytes 3145736 | tf_op jit(solution)/shard_map/ppermute | solution.py:542
  1070.2 41.1 %collective-permute-start.71 = (bf16[768,768]{1,0:T(8,128)(2,1)}, bf16[768,768]{1,0:T(8,128)(2,1)}, u32[]{:S(2)}, u32[]{:S(2)}) collective-permute-start(bf16[768,768]{1,0:T(8,128)(2,1)} %pad_maximum_fusion.26), channel_id=1, source_target_pairs={{0,1},{1,0},{2,3},{3,2},{4,5},{5,4},{6,7},{7,6},{8,9},{9,8},{10,11... | collective-permute-start | bytes 3538952 | tf_op jit(solution)/shard_map/ppermute | solution.py:542
  1087.6 47.5 %collective-permute-start.91 = (bf16[1024,512]{1,0:T(8,128)(2,1)S(1)}, bf16[1024,512]{1,0:T(8,128)(2,1)S(1)}, u32[]{:S(2)}, u32[]{:S(2)}) collective-permute-start(bf16[1024,512]{1,0:T(8,128)(2,1)S(1)} %get-tuple-element.291), channel_id=1, source_target_pairs={{0,16},{8,24},{16,0},{24,8},{1,17},{9,25},{17,1},{25,9},{2,18},{10... | collective-permute-start | bytes 3145736 | tf_op jit(solution)/shard_map/ppermute | solution.py:542
  1094.8 79.2 %collective-permute-start.77 = (bf16[512,2048]{1,0:T(8,128)(2,1)S(1)}, bf16[512,2048]{1,0:T(8,128)(2,1)S(1)}, u32[]{:S(2)}, u32[]{:S(2)}) collective-permute-start(bf16[512,2048]{1,0:T(8,128)(2,1)S(1)} %slice_bitcast_fusion), channel_id=1, source_target_pairs={{0,8},{8,0},{16,24},{24,16},{1,9},{9,1},{17,25},{25,17},{2,10},{10... | collective-permute-start | bytes 6291464 | tf_op jit(solution)/shard_map/ppermute | solution.py:542
  1102.3 93.0 %collective-permute-start.104 = (bf16[2,512,1024]{2,1,0:T(8,128)(2,1)S(1)}, bf16[2,512,1024]{2,1,0:T(8,128)(2,1)S(1)}, u32[]{:S(2)}, u32[]{:S(2)}) collective-permute-start(bf16[2,512,1024]{2,1,0:T(8,128)(2,1)S(1)} %pad_maximum_fusion.23), channel_id=1, source_target_pairs={{0,8},{8,0},{16,24},{24,16},{1,9},{9,1},{17,25},{25,17},{2,10},{10... | collective-permute-start | bytes 6291464 | tf_op jit(solution)/shard_map/ppermute | solution.py:542
  1168.9 51.0 %collective-permute-start.102 = (bf16[2,1024,512]{2,1,0:T(8,128)(2,1)}, bf16[2,1024,512]{2,1,0:T(8,128)(2,1)}, u32[]{:S(2)}, u32[]{:S(2)}) collective-permute-start(bf16[2,1024,512]{2,1,0:T(8,128)(2,1)} %pad_maximum_fusion.22), channel_id=1, source_target_pairs={{0,8},{8,0},{16,24},{24,16},{1,9},{9,1},{17,25},{25,17},{2,10},{10... | collective-permute-start | bytes 6291464 | tf_op jit(solution)/shard_map/ppermute | solution.py:542
  1173.0 143.3 %collective-permute-start.92 = (bf16[2,1024,512]{2,1,0:T(8,128)(2,1)}, bf16[2,1024,512]{2,1,0:T(8,128)(2,1)}, u32[]{:S(2)}, u32[]{:S(2)}) collective-permute-start(bf16[2,1024,512]{2,1,0:T(8,128)(2,1)} %pad_maximum_fusion.18), channel_id=1, source_target_pairs={{0,8},{8,0},{16,24},{24,16},{1,9},{9,1},{17,25},{25,17},{2,10},{10... | collective-permute-start | bytes 6291464 | tf_op jit(solution)/shard_map/ppermute | solution.py:542
  1181.5 27.2 %collective-permute-start.74 = (bf16[1024,256]{1,0:T(8,128)(2,1)}, bf16[1024,256]{1,0:T(8,128)(2,1)}, u32[]{:S(2)}, u32[]{:S(2)}) collective-permute-start(bf16[1024,256]{1,0:T(8,128)(2,1)} %broadcast_select_fusion.5), channel_id=1, source_target_pairs={{0,2},{1,3},{2,0},{3,1},{4,6},{5,7},{6,4},{7,5},{8,10},{9,11},{10,... | collective-permute-start | bytes 1572872 | tf_op jit(solution)/shard_map/ppermute | solution.py:542
  1218.4 74.3 %collective-permute-start.94 = (bf16[1024,128]{1,0:T(8,128)(2,1)}, bf16[1024,128]{1,0:T(8,128)(2,1)}, u32[]{:S(2)}, u32[]{:S(2)}) collective-permute-start(bf16[1024,128]{1,0:T(8,128)(2,1)} %get-tuple-element.409), channel_id=1, source_target_pairs={{0,16},{8,24},{16,0},{24,8},{1,17},{9,25},{17,1},{25,9},{2,18},{10... | collective-permute-start | bytes 786440 | tf_op jit(solution)/shard_map/ppermute | solution.py:542
  1218.9 73.8 %collective-permute-start.96 = (bf16[1024,128]{1,0:T(8,128)(2,1)}, bf16[1024,128]{1,0:T(8,128)(2,1)}, u32[]{:S(2)}, u32[]{:S(2)}) collective-permute-start(bf16[1024,128]{1,0:T(8,128)(2,1)} %get-tuple-element.410), channel_id=1, source_target_pairs={{0,2},{1,3},{2,0},{3,1},{4,6},{5,7},{6,4},{7,5},{8,10},{9,11},{10,... | collective-permute-start | bytes 786440 | tf_op jit(solution)/shard_map/ppermute | solution.py:542
  1224.6 113.7 %collective-permute-start.75 = (bf16[512,1024]{1,0:T(8,128)(2,1)}, bf16[512,1024]{1,0:T(8,128)(2,1)}, u32[]{:S(2)}, u32[]{:S(2)}) collective-permute-start(bf16[512,1024]{1,0:T(8,128)(2,1)} %slice.652), channel_id=1, source_target_pairs={{0,4},{4,0},{1,5},{5,1},{2,6},{6,2},{3,7},{7,3},{8,12},{12,8},{9,1... | collective-permute-start | bytes 3145736 | tf_op jit(solution)/shard_map/ppermute | solution.py:542
  1226.1 112.2 %collective-permute-start.93 = (bf16[512,1024]{1,0:T(8,128)(2,1)}, bf16[512,1024]{1,0:T(8,128)(2,1)}, u32[]{:S(2)}, u32[]{:S(2)}) collective-permute-start(bf16[512,1024]{1,0:T(8,128)(2,1)} %slice.728), channel_id=1, source_target_pairs={{0,4},{4,0},{1,5},{5,1},{2,6},{6,2},{3,7},{7,3},{8,12},{12,8},{9,1... | collective-permute-start | bytes 3145736 | tf_op jit(solution)/shard_map/ppermute | solution.py:542
  1303.8 39.3 %collective-permute-start.98 = (bf16[4,1024,128]{2,1,0:T(8,128)(2,1)S(1)}, bf16[4,1024,128]{2,1,0:T(8,128)(2,1)}, u32[]{:S(2)}, u32[]{:S(2)}) collective-permute-start(bf16[4,1024,128]{2,1,0:T(8,128)(2,1)S(1)} %pad_maximum_fusion.37), channel_id=1, source_target_pairs={{0,8},{8,0},{16,24},{24,16},{1,9},{9,1},{17,25},{25,17},{2,10},{10... | collective-permute-start | bytes 3145736 | tf_op jit(solution)/shard_map/ppermute | solution.py:542
  (162 other events, 3308.4 us)
